TPU v7x, 256 devices: a whole 4x4x8 slice. The times are simulated.
256 devices in a mesh: gx: 8 (over y, core), gy: 32 (over x, z).
Axes of the slice: x: 4, y: 4, z: 8, core: 2. Of those that a mesh axis runs over, the one named last changes fastest.
Arguments:
- rhs: float32 [16, 262144], P(None, ('gx', 'gy')), may hold values from -63 to 63, as said below
- embeddings: float32 [64, 262144], P(None, ('gx', 'gy')), may hold values from -4 to 4
- leaf_order: int32 [256, 1024], P(('gx', 'gy')), may hold values from 0 to 1023, each once within a row
- basis: float32 [64, 262144], P(None, ('gx', 'gy')), may hold values from -0.1875 to 0.1875
- transfer_maps: float32 [5, 256, 64, 64], P(None, ('gx', 'gy')), may hold values from -1 to 1, as said below
- skeletons: float32 [4, 256, 64, 64], P(None, ('gx', 'gy')), may hold values from -1.4 to 1.4, as said below
- top_skeletons: float32 [8, 64, 64], replicated, may hold values from -1.4 to 1.4
- near_lists: int32 [256, 3], P(('gx', 'gy')), may hold values from 0 to 255, as said below
- far_lists: int32 [4, 256], P(None, ('gx', 'gy')), may hold values from 0 to 255, as said below
- top_lists: int32 [8, 4], replicated, may hold values from 0 to 7, as said below
Outputs:
- solution: float32 [16, 262144], P(None, ('gx', 'gy'))
- residual: float32 [16, 262144], P(None, ('gx', 'gy'))
Inputs may be any that keep to these rules, and one draw needn't show every extreme that they name: `rhs`: custom law; entries are products of a random part and positive scales of points, columns and position. `leaf_order`: each row is a permutation of 0 to 1023. `transfer_maps`: rows of leaves with the same ancestor at height h are equal. `skeletons`: rows of leaves with the same ancestor at height h are equal. `near_lists`: row d holds d and the two other leaves of its aligned group of 4 (leaves 4q to 4q + 3) that are not far_lists[0, d], in some order; the relation is symmetric. far_lists[h, d] is c XOR o for the cluster c = d >> h, with o of 1 to 3 the same for all clusters of c's aligned group of 4 at height h; so the relation is symmetric and the partner shares c's group. Leaves with the same ancestor have the same entry. `top_lists`: row c holds c XOR o for 4 distinct nonzero offsets o, the same offsets in every row, one of them 4.
All inputs are finite; a program needn't handle non-finite values.
Results may differ from a plain program's by a relative error of at most 0.0003.
Values sent between devices are 32-bit elements; how exact they have to be, the bound alone decides.
No kernel may reach another device: no remote copies, remote signals or barrier semaphores. Data moves between devices by JAX's collectives and lax.ppermute only.
A program may use at most 128 MiB of HBM per device.

v0:
```python
import math

import jax
import jax.numpy as jnp
from jax import lax
from jax.sharding import PartitionSpec as P

ITERS = 2


highest = lax.Precision.HIGHEST
noise_level = 0.5
length_scale = 2.8
root_five = math.sqrt(5.0)


def swapped(x, axis, stride):
    return lax.ppermute(x, axis, [(i, i ^ 1 << stride) for i in range(lax.axis_size(axis))])


def matern(first_set, second_set):
    cross_dot = lax.dot_general(
        first_set,
        second_set,
        (((0,), (0,)), ((), ())),
        precision=highest,
        preferred_element_type=jnp.float32,
    )
    squares = (
        jnp.sum(first_set * first_set, axis=0)[:, None]
        + jnp.sum(second_set * second_set, axis=0)[None, :]
        - 2.0 * cross_dot
    )
    scaled = root_five * jnp.sqrt(jnp.maximum(squares, 0.0)) / length_scale
    return (1.0 + scaled + scaled * scaled / 3.0) * jnp.exp(-scaled)


def product(first, second):
    return jnp.dot(first, second, precision=highest, preferred_element_type=jnp.float32)


def product_t(first, second):
    return lax.dot_general(
        first,
        second,
        (((1,), (1,)), ((), ())),
        precision=highest,
        preferred_element_type=jnp.float32,
    )


def swap_pieces(pieces, bit):
    widths = [piece.shape[1] for piece in pieces]
    received = swapped(jnp.concatenate(pieces, axis=1), "gy", bit)
    outputs = []
    offset = 0
    for w in widths:
        outputs.append(received[:, offset : offset + w])
        offset = offset + w
    return outputs


def column_total(values):
    return lax.psum(values, ("gx", "gy"))


def local(
    rhs,
    embeddings,
    leaf_order,
    basis,
    transfer_maps,
    skeletons,
    top_skeletons,
    near_lists,
    far_lists,
    top_lists,
):
    row_size = lax.axis_size("gy")
    depth = row_size.bit_length() - 1
    far_depth = far_lists.shape[0]
    columns = rhs.shape[0]
    leaf_size = rhs.shape[1]
    column_index = lax.axis_index("gy")
    top_index = lax.axis_index("gx")
    leaf_index = top_index * row_size + column_index
    leaf_slots = leaf_order[0]
    source = jnp.take(rhs, leaf_slots, axis=1)
    points = jnp.take(embeddings, leaf_slots, axis=1)
    chain_maps = transfer_maps[:, 0]
    chain_skeletons = skeletons[:, 0]
    sibling_points = swap_pieces([points], 0)[0]
    cousin_points = swap_pieces([points, sibling_points], 1)
    group_points = jnp.stack([points, sibling_points] + cousin_points)
    near_slots = jnp.bitwise_xor(near_lists[0], leaf_index)
    near_points = group_points[near_slots]
    far_slots = []
    couplings = []
    for h in range(far_depth):
        own_skeleton = chain_skeletons[h]
        sibling_skeleton = swap_pieces([own_skeleton], h)[0]
        cousin_skeletons = swap_pieces([own_skeleton, sibling_skeleton], h + 1)
        candidates = jnp.stack([own_skeleton, sibling_skeleton] + cousin_skeletons)
        slot = jnp.bitwise_xor(far_lists[h, 0], jnp.right_shift(leaf_index, h))
        far_slots.append(slot)
        couplings.append(matern(own_skeleton, candidates[slot]))
    top_partners = top_lists[top_index]
    top_couplings = jax.vmap(lambda j: matern(top_skeletons[top_index], top_skeletons[j]))(
        top_partners
    )
    row_block = min(512, leaf_size)

    def climb(vector, moment):
        current = moment
        held_pair = None
        near_vectors = [vector]
        partner_moments = []
        for b in range(depth):
            lifted = product(current, chain_maps[b])
            outgoing = [lifted]
            if b < far_depth:
                outgoing.append(current)
            if held_pair is not None:
                outgoing = outgoing + held_pair
            if b < 2:
                outgoing = outgoing + list(near_vectors)
            incoming = swap_pieces(outgoing, b)
            offset = 1
            next_pair = None
            if b < far_depth:
                next_pair = [current, incoming[1]]
                offset = 2
            if held_pair is not None:
                group = jnp.stack(held_pair + incoming[offset : offset + 2])
                partner_moments.append(group[far_slots[b - 1]])
                offset = offset + 2
            if b < 2:
                near_vectors = near_vectors + incoming[offset:]
            held_pair = next_pair
            current = lifted + incoming[0]
        return (current, partner_moments, near_vectors)

    def operate(vector):
        moment = product_t(vector, basis)
        top_moment, partner_moments, near_vectors = climb(vector, moment)
        everyone = lax.all_gather(top_moment[None], "gx", axis=0, tiled=True)
        heads = everyone[top_partners]
        far_field = jnp.einsum("kns,krs->nr", heads, top_couplings, precision=highest)
        for h in reversed(range(depth)):
            far_field = product_t(far_field, chain_maps[h])
            if h < far_depth:
                far_field = far_field + product_t(partner_moments[h], couplings[h])
        far_part = product(far_field, basis)
        group_vectors = jnp.stack(near_vectors)
        near_rows = []
        for row_start in range(0, leaf_size, row_block):
            own_rows = points[:, row_start : row_start + row_block]
            running = jnp.zeros((columns, own_rows.shape[1]), jnp.float32)
            for e in range(near_points.shape[0]):
                kernel = matern(own_rows, near_points[e])
                running = running + product_t(group_vectors[near_slots[e]], kernel)
            near_rows.append(running)
        near_part = jnp.concatenate(near_rows, axis=1)
        return noise_level * vector + near_part + far_part

    iterate = jnp.zeros_like(source)
    remainder = source
    image = operate(remainder)
    norm_now = column_total(jnp.sum(image * image, axis=1))
    direction = image
    for iteration in range(ITERS):
        direction_image = operate(direction)
        step_size = norm_now / column_total(jnp.sum(direction_image * direction_image, axis=1))
        iterate = iterate + step_size[:, None] * direction
        remainder = remainder - step_size[:, None] * direction_image
        if iteration + 1 < ITERS:
            image = operate(remainder)
            norm_next = column_total(jnp.sum(image * image, axis=1))
            direction = image + (norm_next / norm_now)[:, None] * direction
            norm_now = norm_next
    solution = jnp.zeros_like(iterate).at[:, leaf_slots].set(iterate)
    residual = jnp.zeros_like(remainder).at[:, leaf_slots].set(remainder)
    return (solution, residual)


def solution(mesh):
    placed = (
        P(None, ("gx", "gy")),
        P(None, ("gx", "gy")),
        P(("gx", "gy"), None),
        P(None, ("gx", "gy")),
        P(None, ("gx", "gy"), None, None),
        P(None, ("gx", "gy"), None, None),
        P(),
        P(("gx", "gy"), None),
        P(None, ("gx", "gy")),
        P(),
    )
    return jax.shard_map(
        local,
        mesh=mesh,
        in_specs=placed,
        out_specs=(P(None, ("gx", "gy")), P(None, ("gx", "gy"))),
        check_vma=False,
    )
```

profile of v0, /device:TPU:1, one launch (start us, length us, event | category | flops | bytes accessed | tf_op | source)
XLA Modules:
  0.0 539.3 jit_solution(5316988780238232896)
XLA Ops:
  2.5 2.8 gather_fusion
  6.8 2.5 collective-permute-start
  9.5 2.8 gather_fusion.1
  14.0 6.7 %collective-permute-start.9 = (f32[64,64]{1,0:T(8,128)S(1)}, f32[64,64]{1,0:T(8,128)S(1)}, u32[]{:S(2)}, u32[]{:S(2)}) collective-permute-start(f32[64,64]{1,0:T(8,128)S(1)} %get-tuple-element.63), channel_id=1, source_target_pairs={{0,4},{1,5},{2,6},{3,7},{4,0},{5,1},{6,2},{7,3},{8,12},{9,13},{10,... | collective-permute-start | bytes 49160 | tf_op jit(solution)/shard_map/ppermute | solution.py:18
  36.6 2.5 collective-permute-start.8
  43.5 2.6 collective-permute-done.12
  50.2 4.4 collective-permute-done.1
  57.2 4.9 collective-permute-done.4
  69.2 2.4 collective-permute-done.6
  72.4 21.8 %all-gather = f32[128,64]{1,0:T(8,128)S(1)} all-gather(f32[16,64]{1,0:T(8,128)S(1)} %get-tuple-element.142), channel_id=2, replica_groups=mesh['gx'=8,'gy'=32] {'gx'}, dimensions={0}, use_global_device_ids=true | all-gather | bytes 36864 | tf_op jit(solution)/shard_map/all_gather | solution.py:146
  102.7 1.9 gather_fusion.2
  106.5 4.2 exponential_multiply_fusion.5
  110.7 3.1 exponential_multiply_fusion.4
  113.8 3.1 exponential_multiply_fusion.2
  116.9 3.5 exponential_multiply_fusion.1
  120.4 3.1 exponential_multiply_fusion.3
  123.5 3.1 exponential_multiply_fusion
  128.4 1.8 fusion.66
  130.3 1.8 convolution_add_fusion.19
  132.1 2.0 convolution_add_fusion.17
  134.2 1.8 convolution_add_fusion.18
  136.0 1.8 convolution_add_fusion.16
  139.4 3.7 collective-permute-done.15
  144.9 8.9 %collective-permute-done.16 = f32[16,2304]{1,0:T(8,128)S(1)} collective-permute-done((f32[16,2304]{1,0:T(8,128)S(1)}, f32[16,2304]{1,0:T(8,128)S(1)}, u32[]{:S(2)}, u32[]{:S(2)}) %collective-permute-start.16) | collective-permute-done | bytes 147488 | tf_op jit(solution)/shard_map/ppermute | solution.py:18
  153.9 3.5 fusion.60
  157.4 1.8 convolution_add_fusion.15
  159.3 1.8 convolution_add_fusion.14
  162.0 1.9 collective-permute-start.17
  165.7 2.8 collective-permute-done.17
  177.0 15.7 %all-gather.1 = f32[128,64]{1,0:T(8,128)S(1)} all-gather(f32[16,64]{1,0:T(8,128)S(1)} %get-tuple-element.130), channel_id=3, replica_groups=mesh['gx'=8,'gy'=32] {'gx'}, dimensions={0}, use_global_device_ids=true | all-gather | bytes 36864 | tf_op jit(solution)/shard_map/all_gather | solution.py:146
  195.5 74.0 %all-reduce.1 = (f32[16]{0:T(128)S(1)}, f32[16]{0:T(128)S(1)}) all-reduce(f32[16]{0:T(128)} %get-tuple-element.154, f32[16]{0:T(128)S(1)} %get-tuple-element.156), channel_id=1, replica_groups=mesh['gx'=8,'gy'=32] {'gx','gy'}, use_global_device_ids=true, to_apply=%region_16.17 | all-reduce | flops 32 | bytes 256 | tf_op jit(solution)/shard_map/psum | solution.py:64
  275.2 7.0 %collective-permute-done.21 = f32[16,2304]{1,0:T(8,128)S(1)} collective-permute-done((f32[16,2304]{1,0:T(8,128)S(1)}, f32[16,2304]{1,0:T(8,128)S(1)}, u32[]{:S(2)}, u32[]{:S(2)}) %collective-permute-start.21) | collective-permute-done | bytes 147488 | tf_op jit(solution)/shard_map/ppermute | solution.py:18
  282.2 3.5 fusion.52
  285.8 1.8 convolution_add_fusion.11
  287.6 1.8 convolution_add_fusion.10
  290.4 5.5 %collective-permute-start.22 = (f32[16,256]{1,0:T(8,128)S(1)}, f32[16,256]{1,0:T(8,128)S(1)}, u32[]{:S(2)}, u32[]{:S(2)}) collective-permute-start(f32[16,256]{1,0:T(8,128)S(1)} %pad_maximum_fusion.16), channel_id=1, source_target_pairs={{0,4},{1,5},{2,6},{3,7},{4,0},{5,1},{6,2},{7,3},{8,12},{9,13},{10,... | collective-permute-start | bytes 49160 | tf_op jit(solution)/shard_map/ppermute | solution.py:18
  305.4 18.6 %all-gather.2 = f32[128,64]{1,0:T(8,128)S(1)} all-gather(f32[16,64]{1,0:T(8,128)S(1)} %get-tuple-element.118), channel_id=4, replica_groups=mesh['gx'=8,'gy'=32] {'gx'}, dimensions={0}, use_global_device_ids=true | all-gather | bytes 36864 | tf_op jit(solution)/shard_map/all_gather | solution.py:146
  326.8 73.2 %psum.30 = f32[16]{0:T(128)S(1)} all-reduce(f32[16]{0:T(128)S(1)} %get-tuple-element.158), channel_id=1, replica_groups=mesh['gx'=8,'gy'=32] {'gx','gy'}, use_global_device_ids=true, to_apply=%region_20.21 | all-reduce | flops 16 | bytes 128 | tf_op jit(solution)/shard_map/psum | solution.py:64
  402.4 1.9 collective-permute-done.25
  405.5 8.1 %collective-permute-done.26 = f32[16,2304]{1,0:T(8,128)S(1)} collective-permute-done((f32[16,2304]{1,0:T(8,128)S(1)}, f32[16,2304]{1,0:T(8,128)S(1)}, u32[]{:S(2)}, u32[]{:S(2)}) %collective-permute-start.26) | collective-permute-done | bytes 147488 | tf_op jit(solution)/shard_map/ppermute | solution.py:18
  413.7 3.5 fusion.44
  419.1 1.8 convolution_add_fusion.6
  424.1 3.7 collective-permute-done.27
  431.0 2.3 collective-permute-start.29
  435.2 17.5 %all-gather.3 = f32[128,64]{1,0:T(8,128)S(1)} all-gather(f32[16,64]{1,0:T(8,128)S(1)} %get-tuple-element.106), channel_id=5, replica_groups=mesh['gx'=8,'gy'=32] {'gx'}, dimensions={0}, use_global_device_ids=true | all-gather | bytes 36864 | tf_op jit(solution)/shard_map/all_gather | solution.py:146
  455.6 73.4 %psum.31 = f32[16]{0:T(128)S(1)} all-reduce(f32[16]{0:T(128)S(1)} %get-tuple-element.160), channel_id=1, replica_groups=mesh['gx'=8,'gy'=32] {'gx','gy'}, use_global_device_ids=true, to_apply=%region_22.23 | all-reduce | flops 16 | bytes 128 | tf_op jit(solution)/shard_map/psum | solution.py:64
  530.6 3.3 scatter_custom_fusion.1
  534.9 3.3 scatter_custom_fusion
  (335 shorter events, 99.8 us)
Async XLA Ops:
  5.5 16.4 %copy-start.21 = (f32[1024,16]{0,1:T(8,128)}, f32[1024,16]{0,1:T(8,128)S(1)}, u32[]{:S(2)}) copy-start(f32[1024,16]{0,1:T(8,128)S(1)} %copy.29) | copy-start | bytes 196612
  6.2 15.7 %copy-start.32 = (pred[1024]{0:T(1024)(128)(4,1)}, pred[1024]{0:T(1024)(128)(4,1)S(1)}, u32[]{:S(2)}) copy-start(pred[1024]{0:T(1024)(128)(4,1)S(1)} %compare_and_fusion) | copy-start | bytes 3076
  6.5 41.6 %copy-start.29 = (f32[16,64]{1,0:T(8,128)}, f32[16,64]{1,0:T(8,128)S(1)}, u32[]{:S(2)}) copy-start(f32[16,64]{1,0:T(8,128)S(1)} %fusion.362) | copy-start | bytes 12292
  6.8 40.5 %collective-permute-start = (f32[16,1152]{1,0:T(8,128)S(1)}, f32[16,1152]{1,0:T(8,128)S(1)}, u32[]{:S(2)}, u32[]{:S(2)}) collective-permute-start(f32[16,1152]{1,0:T(8,128)S(1)} %concatenate.90), channel_id=1, source_target_pairs={{0,1},{1,0},{2,3},{3,2},{4,5},{5,4},{6,7},{7,6},{8,9},{9,8},{10,11... | collective-permute-start | bytes 221192 | tf_op jit(solution)/shard_map/ppermute | solution.py:18
  12.3 14.1 %copy-start.40 = (s32[4,1]{0,1:T(1,128)S(1)}, s32[4,1]{0,1:T(1,128)}, u32[]{:S(2)}) copy-start(s32[4,1]{0,1:T(1,128)} %param.18) | copy-start | bytes 52
  12.5 56.1 %collective-permute-start.2 = (f32[64,1024]{0,1:T(8,128)S(1)}, f32[64,1024]{0,1:T(8,128)S(1)}, u32[]{:S(2)}, u32[]{:S(2)}) collective-permute-start(f32[64,1024]{0,1:T(8,128)S(1)} %bitcast_select_fusion.1), channel_id=1, source_target_pairs={{0,1},{1,0},{2,3},{3,2},{4,5},{5,4},{6,7},{7,6},{8,9},{9,8},{10,11... | collective-permute-start | bytes 786440 | tf_op jit(solution)/shard_map/ppermute | solution.py:18
  12.7 23.0 %collective-permute-start.7 = (f32[64,64]{1,0:T(8,128)S(1)}, f32[64,64]{1,0:T(8,128)S(1)}, u32[]{:S(2)}, u32[]{:S(2)}) collective-permute-start(f32[64,64]{1,0:T(8,128)S(1)} %get-tuple-element.64), channel_id=1, source_target_pairs={{0,8},{1,9},{2,10},{3,11},{4,12},{5,13},{6,14},{7,15},{8,0},{9,1},... | collective-permute-start | bytes 49160 | tf_op jit(solution)/shard_map/ppermute | solution.py:18
  14.0 22.6 %collective-permute-start.9 = (f32[64,64]{1,0:T(8,128)S(1)}, f32[64,64]{1,0:T(8,128)S(1)}, u32[]{:S(2)}, u32[]{:S(2)}) collective-permute-start(f32[64,64]{1,0:T(8,128)S(1)} %get-tuple-element.63), channel_id=1, source_target_pairs={{0,4},{1,5},{2,6},{3,7},{4,0},{5,1},{6,2},{7,3},{8,12},{9,13},{10,... | collective-permute-start | bytes 49160 | tf_op jit(solution)/shard_map/ppermute | solution.py:18
  20.7 18.5 %collective-permute-start.11 = (f32[64,64]{1,0:T(8,128)S(1)}, f32[64,64]{1,0:T(8,128)S(1)}, u32[]{:S(2)}, u32[]{:S(2)}) collective-permute-start(f32[64,64]{1,0:T(8,128)S(1)} %get-tuple-element.66), channel_id=1, source_target_pairs={{0,2},{1,3},{2,0},{3,1},{4,6},{5,7},{6,4},{7,5},{8,10},{9,11},{10,... | collective-permute-start | bytes 49160 | tf_op jit(solution)/shard_map/ppermute | solution.py:18
  35.7 3.7 collective-permute-start.13
  36.6 4.4 collective-permute-start.8
  39.2 3.3 collective-permute-start.10
  39.4 6.8 %collective-permute-start.12 = (f32[64,128]{1,0:T(8,128)S(1)}, f32[64,128]{1,0:T(8,128)S(1)}, u32[]{:S(2)}, u32[]{:S(2)}) collective-permute-start(f32[64,128]{1,0:T(8,128)S(1)} %pad_maximum_fusion.8), channel_id=1, source_target_pairs={{0,4},{1,5},{2,6},{3,7},{4,0},{5,1},{6,2},{7,3},{8,12},{9,13},{10,... | collective-permute-start | bytes 98312 | tf_op jit(solution)/shard_map/ppermute | solution.py:18
  41.0 6.2 %collective-permute-start.14 = (f32[64,128]{1,0:T(8,128)S(1)}, f32[64,128]{1,0:T(8,128)S(1)}, u32[]{:S(2)}, u32[]{:S(2)}) collective-permute-start(f32[64,128]{1,0:T(8,128)S(1)} %pad_maximum_fusion.9), channel_id=1, source_target_pairs={{0,2},{1,3},{2,0},{3,1},{4,6},{5,7},{6,4},{7,5},{8,10},{9,11},{10,... | collective-permute-start | bytes 98312 | tf_op jit(solution)/shard_map/ppermute | solution.py:18
  48.2 6.5 %collective-permute-start.1 = (f32[16,2304]{1,0:T(8,128)S(1)}, f32[16,2304]{1,0:T(8,128)S(1)}, u32[]{:S(2)}, u32[]{:S(2)}) collective-permute-start(f32[16,2304]{1,0:T(8,128)S(1)} %concatenate.91), channel_id=1, source_target_pairs={{0,2},{1,3},{2,0},{3,1},{4,6},{5,7},{6,4},{7,5},{8,10},{9,11},{10,... | collective-permute-start | bytes 442376 | tf_op jit(solution)/shard_map/ppermute | solution.py:18
  55.6 6.5 %collective-permute-start.4 = (f32[16,256]{1,0:T(8,128)S(1)}, f32[16,256]{1,0:T(8,128)S(1)}, u32[]{:S(2)}, u32[]{:S(2)}) collective-permute-start(f32[16,256]{1,0:T(8,128)S(1)} %pad_maximum_fusion.10), channel_id=1, source_target_pairs={{0,4},{1,5},{2,6},{3,7},{4,0},{5,1},{6,2},{7,3},{8,12},{9,13},{10,... | collective-permute-start | bytes 49160 | tf_op jit(solution)/shard_map/ppermute | solution.py:18
  63.0 2.6 collective-permute-start.5
  67.1 4.4 collective-permute-start.6
  68.7 27.0 %copy-start.20 = (f32[64,1024]{0,1:T(8,128)}, f32[64,1024]{0,1:T(8,128)S(1)}, u32[]{:S(2)}) copy-start(f32[64,1024]{0,1:T(8,128)S(1)} %collective-permute-done.2) | copy-start | bytes 786436
  69.1 29.9 %collective-permute-start.3 = (f32[64,2048]{1,0:T(8,128)S(1)}, f32[64,2048]{1,0:T(8,128)S(1)}, u32[]{:S(2)}, u32[]{:S(2)}) collective-permute-start(f32[64,2048]{1,0:T(8,128)S(1)} %copy.31), channel_id=1, source_target_pairs={{0,2},{1,3},{2,0},{3,1},{4,6},{5,7},{6,4},{7,5},{8,10},{9,11},{10,... | collective-permute-start | bytes 1572872 | tf_op jit(solution)/shard_map/ppermute | solution.py:18
  110.7 15.9 %copy-start.13 = (f32[512,1024]{1,0:T(8,128)}, f32[512,1024]{1,0:T(8,128)S(1)}, u32[]{:S(2)}) copy-start(f32[512,1024]{1,0:T(8,128)S(1)} %exponential_multiply_fusion.5) | copy-start | bytes 6291460
  113.8 16.5 %copy-start.9 = (f32[512,1024]{1,0:T(8,128)}, f32[512,1024]{1,0:T(8,128)S(1)}, u32[]{:S(2)}) copy-start(f32[512,1024]{1,0:T(8,128)S(1)} %exponential_multiply_fusion.4) | copy-start | bytes 6291460
  139.3 3.7 collective-permute-start.15
  144.0 9.8 %collective-permute-start.16 = (f32[16,2304]{1,0:T(8,128)S(1)}, f32[16,2304]{1,0:T(8,128)S(1)}, u32[]{:S(2)}, u32[]{:S(2)}) collective-permute-start(f32[16,2304]{1,0:T(8,128)S(1)} %concatenate.103), channel_id=1, source_target_pairs={{0,2},{1,3},{2,0},{3,1},{4,6},{5,7},{6,4},{7,5},{8,10},{9,11},{10,... | collective-permute-start | bytes 442376 | tf_op jit(solution)/shard_map/ppermute | solution.py:18
  162.0 6.5 %collective-permute-start.17 = (f32[16,256]{1,0:T(8,128)S(1)}, f32[16,256]{1,0:T(8,128)S(1)}, u32[]{:S(2)}, u32[]{:S(2)}) collective-permute-start(f32[16,256]{1,0:T(8,128)S(1)} %pad_maximum_fusion.13), channel_id=1, source_target_pairs={{0,4},{1,5},{2,6},{3,7},{4,0},{5,1},{6,2},{7,3},{8,12},{9,13},{10,... | collective-permute-start | bytes 49160 | tf_op jit(solution)/shard_map/ppermute | solution.py:18
  168.9 25.4 %copy-start.24 = (f32[64,64]{0,1:T(8,128)S(1)}, f32[64,64]{0,1:T(8,128)}, u32[]{:S(2)}) copy-start(f32[64,64]{0,1:T(8,128)} %exponential_multiply_fusion.9) | copy-start | bytes 49156
  168.9 3.7 collective-permute-start.18
  172.5 22.2 %copy-start.25 = (f32[64,64]{0,1:T(8,128)S(1)}, f32[64,64]{0,1:T(8,128)}, u32[]{:S(2)}) copy-start(f32[64,64]{0,1:T(8,128)} %exponential_multiply_fusion.8) | copy-start | bytes 49156
  172.5 22.2 %copy-start.35 = (f32[1,16,64]{2,1,0:T(8,128)S(1)}, f32[1,16,64]{2,1,0:T(8,128)}, u32[]{:S(2)}) copy-start(f32[1,16,64]{2,1,0:T(8,128)} %get-tuple-element.48) | copy-start | bytes 12292
  172.5 22.5 %copy-start.26 = (f32[64,64]{0,1:T(8,128)S(1)}, f32[64,64]{0,1:T(8,128)}, u32[]{:S(2)}) copy-start(f32[64,64]{0,1:T(8,128)} %exponential_multiply_fusion.7) | copy-start | bytes 49156
  172.5 22.5 %copy-start.37 = (f32[1,16,64]{2,1,0:T(8,128)S(1)}, f32[1,16,64]{2,1,0:T(8,128)}, u32[]{:S(2)}) copy-start(f32[1,16,64]{2,1,0:T(8,128)} %get-tuple-element.79) | copy-start | bytes 12292
  172.5 97.0 %copy-start.22 = (f32[1024,16]{0,1:T(8,128)S(1)}, f32[1024,16]{0,1:T(8,128)}, u32[]{:S(2)}) copy-start(f32[1024,16]{0,1:T(8,128)} %copy-done.21) | copy-start | bytes 196612
  172.5 97.0 %copy-start.33 = (pred[1024]{0:T(1024)(128)(4,1)S(1)}, pred[1024]{0:T(1024)(128)(4,1)}, u32[]{:S(2)}) copy-start(pred[1024]{0:T(1024)(128)(4,1)} %copy-done.32) | copy-start | bytes 3076
  172.8 4.1 collective-permute-start.19
  270.6 3.6 collective-permute-start.20
  275.1 7.1 %collective-permute-start.21 = (f32[16,2304]{1,0:T(8,128)S(1)}, f32[16,2304]{1,0:T(8,128)S(1)}, u32[]{:S(2)}, u32[]{:S(2)}) collective-permute-start(f32[16,2304]{1,0:T(8,128)S(1)} %concatenate.109), channel_id=1, source_target_pairs={{0,2},{1,3},{2,0},{3,1},{4,6},{5,7},{6,4},{7,5},{8,10},{9,11},{10,... | collective-permute-start | bytes 442376 | tf_op jit(solution)/shard_map/ppermute | solution.py:18
  290.4 7.3 %collective-permute-start.22 = (f32[16,256]{1,0:T(8,128)S(1)}, f32[16,256]{1,0:T(8,128)S(1)}, u32[]{:S(2)}, u32[]{:S(2)}) collective-permute-start(f32[16,256]{1,0:T(8,128)S(1)} %pad_maximum_fusion.16), channel_id=1, source_target_pairs={{0,4},{1,5},{2,6},{3,7},{4,0},{5,1},{6,2},{7,3},{8,12},{9,13},{10,... | collective-permute-start | bytes 49160 | tf_op jit(solution)/shard_map/ppermute | solution.py:18
  298.0 2.9 collective-permute-start.23
  299.9 26.0 %copy-start.36 = (f32[1,16,64]{2,1,0:T(8,128)S(1)}, f32[1,16,64]{2,1,0:T(8,128)}, u32[]{:S(2)}) copy-start(f32[1,16,64]{2,1,0:T(8,128)} %get-tuple-element.41) | copy-start | bytes 12292
  299.9 26.3 %copy-start.34 = (f32[1,16,64]{2,1,0:T(8,128)S(1)}, f32[1,16,64]{2,1,0:T(8,128)}, u32[]{:S(2)}) copy-start(f32[1,16,64]{2,1,0:T(8,128)} %get-tuple-element.42) | copy-start | bytes 12292
  299.9 26.4 %copy-start.38 = (f32[1,16,64]{2,1,0:T(8,128)S(1)}, f32[1,16,64]{2,1,0:T(8,128)}, u32[]{:S(2)}) copy-start(f32[1,16,64]{2,1,0:T(8,128)} %get-tuple-element.74) | copy-start | bytes 12292
  299.9 100.0 %copy-start.48 = (f32[16]{0:T(128)S(1)}, f32[16]{0:T(128)}, u32[]{:S(2)}) copy-start(f32[16]{0:T(128)} %copy-done.47) | copy-start | bytes 196
  301.2 4.1 collective-permute-start.24
  401.1 3.2 collective-permute-start.25
  404.7 9.0 %collective-permute-start.26 = (f32[16,2304]{1,0:T(8,128)S(1)}, f32[16,2304]{1,0:T(8,128)S(1)}, u32[]{:S(2)}, u32[]{:S(2)}) collective-permute-start(f32[16,2304]{1,0:T(8,128)S(1)} %concatenate.115), channel_id=1, source_target_pairs={{0,2},{1,3},{2,0},{3,1},{4,6},{5,7},{6,4},{7,5},{8,10},{9,11},{10,... | collective-permute-start | bytes 442376 | tf_op jit(solution)/shard_map/ppermute | solution.py:18
  421.3 6.5 %collective-permute-start.27 = (f32[16,256]{1,0:T(8,128)S(1)}, f32[16,256]{1,0:T(8,128)S(1)}, u32[]{:S(2)}, u32[]{:S(2)}) collective-permute-start(f32[16,256]{1,0:T(8,128)S(1)} %pad_maximum_fusion.19), channel_id=1, source_target_pairs={{0,4},{1,5},{2,6},{3,7},{4,0},{5,1},{6,2},{7,3},{8,12},{9,13},{10,... | collective-permute-start | bytes 49160 | tf_op jit(solution)/shard_map/ppermute | solution.py:18
  428.1 2.6 collective-permute-start.28
  431.0 4.1 collective-permute-start.29
  (31 other events, 232.8 us)
where the time goes:
time: 549 us; the launch traced here: 539 us
  blocking collectives  294 us (54%)
  matrix products  87.6 us (16%)
  waiting for transfers between devices  56.8 us (10%)
  starting transfers between devices  44.3 us (8%)
  local copies, waits for them, and re-layouts  28.1 us (5%)
  other arithmetic  18.3 us (3%)
  between operations  9.98 us (2%)
    psum x3, blocking collectives, column_total(): return lax.psum(values, ('gx', 'gy'))  221 us
    all_gather x4, blocking collectives, operate(): everyone = lax.all_gather(top_moment[None], 'gx', axis=0, tiled=True)  73.7 us
    dot_general x64, matrix products, product_t(): lax.dot_general(first, second, (((1,), (1,)), ((), ())), precision=highes...  58.7 us
    ppermute x30, waiting for transfers between devices, swapped(): lax.ppermute(x, axis, [(i, i ^ 1 << stride) for i in range(lax.axis_size(...  56.8 us
    ppermute x30, starting transfers between devices, swapped(): lax.ppermute(x, axis, [(i, i ^ 1 << stride) for i in range(lax.axis_size(...  44.3 us
    dot_general x11, matrix products, matern(): lax.dot_general(first_set, second_set, (((0,), (0,)), ((), ())), precisio...  23.3 us
  transfers between devices with their start and end apart: 30, of which 18 were waited for; matrix products, arithmetic and copies ran while one was open for 7% of the time, Pallas kernels for 0%

commit v1 on v0

v1 whole, which is shorter than its diff:
```python
import functools
import math

import jax
import jax.numpy as jnp
from jax import lax
from jax.experimental import pallas as pl
from jax.experimental.pallas import tpu as pltpu
from jax.sharding import Mesh
from jax.sharding import PartitionSpec as P

F32 = jnp.float32
BF16 = jnp.bfloat16
HIGHEST = lax.Precision.HIGHEST
NOISE = 0.5
SCALE = math.sqrt(5.0) / 2.8
LOG2E = math.log2(math.e)
DEPTH = 208
TILE = 256

Z, X, Y, CORE, O0, O1, O2, O3, TOPS = range(9)


def dot(a, b, ca=1, cb=0, precision=None):
    return lax.dot_general(
        a, b, (((ca,), (cb,)), ((), ())), precision=precision, preferred_element_type=F32
    )


def split(a):
    high = a.astype(BF16)
    return high, (a - high.astype(F32)).astype(BF16)


def stacked(a):
    return jnp.concatenate(split(a), axis=0)


def halves(a):
    n = a.shape[0] // 2
    return a[:n] + a[n:]


def square_sum(v):
    return jnp.broadcast_to(jnp.sum(v * v, axis=1, keepdims=True), (v.shape[0], 64))


def moments(v, weighed, bases, chain):
    both = halves(dot(stacked(v), bases, 1, 1))
    own = both[:, :64] + both[:, 64:]
    lifted = dot(own, chain[:, 0:192], precision=HIGHEST)
    first = jnp.concatenate([square_sum(weighed), lifted[:, 0:64]], axis=1)
    return jnp.concatenate([own, jnp.zeros_like(own)], axis=1), first, lifted[:, 64:192]


def write_moments(extended, out, v, weighed, bases, chain):
    own, first, second = moments(v, weighed, bases[...], chain[...])
    extended[:, 0 : v.shape[1]] = v
    extended[:, v.shape[1] :] = own
    for i in range(out.shape[0]):
        out[i, 0:16, :] = first
        out[i, 16:32, :] = second


def prepare_kernel(scalars, order, basis, maps, skeletons, rhs, bases, chain, out):
    both = stacked(basis[...])
    leaf = basis.shape[1]
    for t in range(leaf // TILE):
        rows = lax.broadcasted_iota(jnp.int32, (TILE, leaf), 0) + t * TILE
        one_hot = jnp.where(rows == order[...], 1.0, 0.0).astype(BF16)
        bases[:, t * TILE : (t + 1) * TILE] = dot(both, one_hot, 1, 1).astype(BF16)
    p1 = maps[0]
    p2 = dot(p1, maps[1], precision=HIGHEST)
    p3 = dot(p2, maps[2], precision=HIGHEST)
    chain[...] = jnp.concatenate([p1, p2, p3, dot(maps[3], maps[4], precision=HIGHEST)], axis=1)
    own, first, second = moments(rhs[...], rhs[...], bases[...], chain[...])
    z = scalars[Z]
    for i in range(out.shape[0]):
        offset = jnp.bitwise_xor(z, i)
        skeleton = jnp.where(offset == 4, skeletons[2], skeletons[0])
        out[i, 0:16, :] = first
        out[i, 16:32, :] = second
        out[i, 32:48, :] = own
        out[i, 48:112, :] = jnp.concatenate([skeleton, skeletons[1]], axis=1)


def matern(first, second):
    turned = first.T
    squares = (
        jnp.sum(turned * turned, axis=1, keepdims=True)
        + jnp.sum(second * second, axis=0, keepdims=True)
        - 2.0 * dot(turned, second, precision=HIGHEST)
    )
    s = SCALE * jnp.sqrt(jnp.maximum(squares, 0.0))
    return (1.0 + s + s * s * (1.0 / 3.0)) * jnp.exp(-s)


def coupling_kernel(scalars, skeletons, from_z, from_x, tops, chain, after, out):
    z, x, core = scalars[Z], scalars[X], scalars[CORE]
    o0, o1, o2, o3 = scalars[O0], scalars[O1], scalars[O2], scalars[O3]
    partners = [
        from_z[jnp.bitwise_xor(z, o0), 48:112, 0:64],
        from_z[jnp.bitwise_xor(z, o1 * 2), 48:112, 64:128],
        from_x[jnp.bitwise_xor(x, o2 // 2), :, 0:64],
        from_x[jnp.bitwise_xor(x, o3), :, 64:128],
    ]
    pieces = []
    for h in range(4):
        coupling = matern(skeletons[h], partners[h])
        if h > 0:
            coupling = dot(chain[:, (h - 1) * 64 : h * 64], coupling, precision=HIGHEST)
        pieces.append(coupling)
    out[:, 0:256] = jnp.concatenate(pieces, axis=1)
    others = []
    masks = []
    for flip in (0, 1):
        for y in range(4):
            side = jnp.bitwise_xor(core, flip)
            others.append(tops[y, side])
            hits = sum((scalars[TOPS + j] == y * 2 + side).astype(F32) for j in range(4))
            masks.append(jnp.full((64, 64), hits, F32))
    top = matern(tops[scalars[Y], core], jnp.concatenate(others, axis=1))
    top = top * jnp.concatenate(masks, axis=1)
    whole = dot(chain[:, 128:192], chain[:, 192:256], precision=HIGHEST)
    out[:, 256:768] = dot(whole, top, precision=HIGHEST)


def three(a):
    high = a.astype(BF16).astype(F32)
    middle = (a - high).astype(BF16).astype(F32)
    return high, middle, a - high - middle


def build_kernel(scalars, own, *refs, choice):
    if choice is None:
        vector_ref, begin, after, whole, near, aug, squares, kernel, sems = refs
        slot = 0
        near[...] = NOISE * begin[...]
    else:
        yes, no, begin, after, previous, whole, near, aug, squares, kernel, sems = refs
        slot = (choice + 1) // 2
        near[...] = begin[...]
        take = scalars[O0] == choice
    leaf = own.shape[1]

    high, low = split(own[...] * SCALE)
    h32, l32 = high.astype(F32), low.astype(F32)
    sums = three(jnp.sum(h32 * h32 + 2.0 * (h32 * l32), axis=0, keepdims=True))
    row = lax.broadcasted_iota(jnp.int32, (16, leaf), 0)
    tail = jnp.where(row < 3, 1.0, 0.0)
    for i in range(3):
        tail = jnp.where(row == 3 + i, sums[i], tail)
    aug[0:64, :] = high
    aug[64:128, :] = low
    aug[128:192, :] = high
    aug[192:208, :] = tail.astype(BF16)

    def tile(t, carry):
        start = pl.multiple_of(t * TILE, TILE)
        cols = pl.ds(start, TILE)
        if choice is None:
            points = own[:, cols]
            vector = vector_ref[:, cols]
        else:
            points = jnp.where(take, yes[0:64, cols], no[0:64, cols])
            vector = jnp.where(take, yes[64:80, cols], no[64:80, cols])
        high, low = split((points * SCALE).T)
        h32, l32 = high.astype(F32), low.astype(F32)
        sums = three(jnp.sum(h32 * h32 + 2.0 * (h32 * l32), axis=1, keepdims=True))
        lane = lax.broadcasted_iota(jnp.int32, (TILE, 16), 1)
        tail = jnp.where((lane >= 3) & (lane < 6), 1.0, 0.0)
        for i in range(3):
            tail = jnp.where(lane == i, sums[i], tail)
        left = jnp.concatenate([-2.0 * h32, -2.0 * h32, -2.0 * l32, tail], axis=1).astype(BF16)
        squares[...] = dot(left, aug[...])
        wide = 512
        tall = 32

        def entries(i, carry):
            r = pl.multiple_of(i * tall, tall)
            for c in range(0, leaf, wide):
                s2 = jnp.maximum(squares[pl.ds(r, tall), c : c + wide], 0.0)
                s = s2 * lax.rsqrt(jnp.maximum(s2, 1e-30))
                value = (1.0 + s + s2 * (1.0 / 3.0)) * jnp.exp2(s * -LOG2E)
                high, low = split(value)
                kernel[t, 0, pl.ds(r, tall), c : c + wide] = high
                kernel[t, 1, pl.ds(r, tall), c : c + wide] = low
            return carry

        lax.fori_loop(0, TILE // tall, entries, 0, unroll=2)
        pair = stacked(vector)
        near[...] += halves(dot(pair, kernel[t, 0]) + dot(pair, kernel[t, 1]))
        pltpu.make_async_copy(kernel.at[t], whole.at[slot, :, cols, :], sems.at[t]).start()
        return carry

    tiles = leaf // TILE
    lax.fori_loop(0, tiles, tile, 0)
    for t in range(tiles):
        rows = pl.ds(t * TILE, TILE)
        pltpu.make_async_copy(kernel.at[t], whole.at[slot, :, rows, :], sems.at[t]).wait()


def near_kernel(scalars, v, v1, v2, v3, kernels, out, held, sems):
    leaf = kernels.shape[2]
    tiles = leaf // TILE
    copies = []
    for e in range(3):
        for t in range(tiles):
            rows = pl.ds(t * TILE, TILE)
            copies.append(
                pltpu.make_async_copy(
                    kernels.at[e, :, rows, :], held.at[e, :, rows, :], sems.at[e * tiles + t]
                )
            )
    for copy in copies:
        copy.start()
    o0 = scalars[O0]
    own = v[:, 0:leaf]
    second = jnp.where(o0 == 1, v2[:, 0:leaf], v1[:, 0:leaf])
    third = jnp.where(o0 == 3, v2[:, 0:leaf], v3[:, 0:leaf])
    total = None
    for e, vector in enumerate((own, second, third)):
        pair = stacked(vector)
        for t in range(tiles):
            rows = slice(t * TILE, (t + 1) * TILE)
            copies[e * tiles + t].wait()
            part = dot(pair[:, rows], held[e, 0, rows, :]) + dot(pair[:, rows], held[e, 1, rows, :])
            total = part if total is None else total + part
    out[:, 0:leaf] = NOISE * own + halves(total)
    out[:, leaf:] = jnp.where(
        o0 == 1, v1[:, leaf:], jnp.where(o0 == 2, v2[:, leaf:], v3[:, leaf:])
    )


def first_middle_kernel(scalars, received, chain, skeletons, after, moved, low, out, pairs):
    middle_kernel(scalars, received, chain, low, out, first=True)
    third = jnp.where(
        scalars[O2] % 2 == 1,
        received[jnp.bitwise_xor(scalars[Z], 4), 48:112, 0:64],
        skeletons[2],
    )
    pair = jnp.concatenate([third, skeletons[3]], axis=1)
    for i in range(pairs.shape[0]):
        pairs[i] = pair


def middle_kernel(scalars, received, chain, low, out, first=False):
    z, o0, o1, o2 = scalars[Z], scalars[O0], scalars[O1], scalars[O2]
    left = lax.broadcasted_iota(jnp.int32, (16, 128), 1) < 64
    sums = [jnp.zeros((16, 128), F32) for _ in range(3)]
    for i in range(received.shape[0]):
        offset = jnp.bitwise_xor(z, i)
        hit1 = offset // 2 == o1
        hit2 = offset // 4 == jnp.bitwise_and(o2, 1)
        sums[0] += jnp.where(left | hit1, received[i, 0:16, :], 0.0)
        sums[1] += jnp.where(~left | hit2, received[i, 16:32, :], 0.0)
        if first:
            sums[2] += jnp.where(offset == o0, received[i, 32:48, :], 0.0)
    low[...] = jnp.concatenate([sums[2][:, 0:64], sums[0][:, 64:128]], axis=1)
    top = dot(sums[1][:, 64:128], chain[:, 192:256], precision=HIGHEST)
    last = jnp.concatenate([top, sums[0][:, 0:64]], axis=1)
    for i in range(out.shape[0]):
        out[i, 0:16, :] = sums[1]
        out[i, 16:32, :] = last


def gather_kernel(scalars, received, *refs):
    high, out = refs[-2:]
    x, y, o2, o3 = scalars[X], scalars[Y], scalars[O2], scalars[O3]
    left = lax.broadcasted_iota(jnp.int32, (16, 128), 1) < 64
    total = jnp.zeros((16, 128), F32)
    for j in range(4):
        top = jnp.zeros((16, 128), F32)
        for i in range(4):
            p = j * 4 + i
            offset = jnp.bitwise_xor(x, i)
            here = y == j
            hit2 = here & (offset == o2 // 2)
            hit3 = here & (offset == o3)
            total += jnp.where((left & hit2) | (~left & hit3), received[p, 0:16, :], 0.0)
            top += received[p, 16:32, :]
        out[j * 16 : (j + 1) * 16, :] = top
    high[...] = total


def apply_far(low, high, mine, other, table, bases, near):
    leaf = bases.shape[1]
    if near.shape[1] > leaf:
        parts = [near[:, leaf : leaf + 64], low[:, 64:128], high[...]]
    else:
        parts = [low[...], high[...]]
    for side in (mine, other):
        parts += [side[j * 16 : (j + 1) * 16, 0:64] for j in range(4)]
    field = dot(jnp.concatenate(parts, axis=1), table[...], 1, 1, precision=HIGHEST)
    pair = stacked(field)
    far = halves(dot(pair, bases[0:64, :]) + dot(pair, bases[64:128, :]))
    total = sum(side[j * 16 : (j + 1) * 16, 64:128] for side in (mine, other) for j in range(4))
    return near[:, 0:leaf] + far, total[:, 0:1]


def first_kernel(low, high, mine, other, table, bases, near, chain, v1, out):
    image, _ = apply_far(low, high, mine, other, table, bases, near)
    write_moments(v1, out, image, image, bases, chain)


def second_kernel(low, high, mine, other, table, bases, near, chain, v2, scaled, sums, out):
    image, norm = apply_far(low, high, mine, other, table, bases, near)
    v2[...] = image
    sums[...] = jnp.broadcast_to(norm, sums.shape)
    write_moments(scaled, out, image / jnp.sqrt(norm), image, bases, chain)


def third_kernel(low, high, mine, other, table, bases, near, chain, v1, sums, image, step, out):
    product, along = apply_far(low, high, mine, other, table, bases, near)
    norm = sums[:, 0:1]
    size = norm / along
    new = v1[:, 0 : product.shape[1]] - (size * jnp.sqrt(norm)) * product
    step[...] = jnp.broadcast_to(size, step.shape)
    write_moments(image, out, new, new, bases, chain)


def diagonal():
    rows = lax.broadcasted_iota(jnp.int32, (16, 128), 0)
    return rows == lax.broadcasted_iota(jnp.int32, (16, 128), 1)


def fourth_kernel(low, high, mine, other, table, bases, near, v2, sums, along, fresh, out):
    product, norm = apply_far(low, high, mine, other, table, bases, near)
    new = product + (norm / sums[:, 0:1]) * v2[...]
    along[...] = new
    fresh[...] = jnp.broadcast_to(norm, fresh.shape)
    share = jnp.sum(new * new, axis=1, keepdims=True)
    line = jnp.sum(jnp.where(diagonal(), share, 0.0), axis=0, keepdims=True)
    for i in range(out.shape[0]):
        out[i] = jnp.broadcast_to(line, (8, 128))


def spread_kernel(received, out):
    total = received[0]
    for i in range(1, received.shape[0]):
        total = total + received[i]
    for i in range(out.shape[0]):
        out[i] = total


def last_kernel(shares, rhs, v1, v2, image, along, sums, fresh, step, iterate, residual):
    leaf = rhs.shape[1]
    norm = fresh[:, 0:1]
    first = step[:, 0:1]
    line = sum(shares[i, 0:1, :] for i in range(shares.shape[0]))
    second = norm / jnp.sum(jnp.where(diagonal(), line, 0.0), axis=1, keepdims=True)
    beta = norm / sums[:, 0:1]
    start = v1[:, 0:leaf]
    iterate[...] = first * start + second * (image[:, 0:leaf] + beta * start)
    residual[...] = rhs[...] - first * v2[...] - second * along[...]


SMEM = pl.BlockSpec(memory_space=pltpu.SMEM)
VMEM = pl.BlockSpec(memory_space=pltpu.VMEM)


def shaped(*shape, dtype=F32):
    return jax.ShapeDtypeStruct(shape, dtype)


MIB = 1024 * 1024
ANY = pl.BlockSpec(memory_space=pl.ANY)


def call(kernel, outs, scalars, arrays, name, after=(), limit=16, flops=100000, scratch=(), alias=None):
    return pl.pallas_call(
        kernel,
        out_shape=outs,
        in_specs=[SMEM] * len(scalars) + [VMEM] * len(arrays) + [ANY] * len(after),
        out_specs=jax.tree.map(lambda a: VMEM if len(a.shape) < 4 else ANY, outs),
        scratch_shapes=list(scratch),
        input_output_aliases=alias or {},
        name=name,
        compiler_params=pltpu.CompilerParams(vmem_limit_bytes=limit * MIB),
        cost_estimate=pl.CostEstimate(flops=flops, bytes_accessed=500000, transcendentals=0),
    )(*scalars, *arrays, *after)


def build(scalars, own, others, choice, near, after, name, kernels=()):
    leaf = own.shape[1]
    tiles = leaf // TILE
    return call(
        functools.partial(build_kernel, choice=choice),
        (shaped(3, 2, leaf, leaf, dtype=BF16), shaped(16, leaf)),
        [scalars],
        [own, *others, near],
        name,
        after=[*after, *kernels],
        limit=50,
        flops=4000000000,
        alias={3 + len(others) + len(after): 0} if kernels else None,
        scratch=[
            pltpu.VMEM((DEPTH, leaf), BF16),
            pltpu.VMEM((TILE, leaf), F32),
            pltpu.VMEM((tiles, 2, TILE, leaf), BF16),
            pltpu.SemaphoreType.DMA((tiles,)),
        ],
    )


def near_product(scalars, vectors, kernels):
    leaf = kernels.shape[2]
    return call(
        near_kernel,
        shaped(*vectors[0].shape),
        [scalars],
        vectors,
        "near",
        after=[kernels],
        limit=50,
        flops=4000000000,
        scratch=[
            pltpu.VMEM((3, 2, leaf, leaf), BF16),
            pltpu.SemaphoreType.DMA((3 * leaf // TILE,)),
        ],
    )


def to_group(v):
    return [lax.ppermute(v, "z", [(i, i ^ o) for i in range(8)]) for o in (1, 2, 3)]


def other_core(v):
    return lax.ppermute(v, "core", [(0, 1), (1, 0)])


def over_z(v):
    return lax.all_to_all(v, "z", 0, 0)


def over_yx(v):
    return lax.all_to_all(v, ("y", "x"), 0, 0)


def local(
    rhs,
    embeddings,
    leaf_order,
    basis,
    transfer_maps,
    skeletons,
    top_skeletons,
    near_lists,
    far_lists,
    top_lists,
):
    y, core, x, z = (lax.axis_index(a) for a in ("y", "core", "x", "z"))
    top = y * 2 + core
    leaf = top * 32 + x * 8 + z
    offsets = jnp.bitwise_xor(
        far_lists[:, 0], jnp.right_shift(leaf, jnp.arange(4, dtype=jnp.int32))
    )
    partners = lax.dynamic_index_in_dim(top_lists, top, 0, keepdims=False)
    scalars = jnp.concatenate([jnp.stack([z, x, y, core]), offsets, partners]).astype(jnp.int32)
    chain_skeletons = skeletons[:, 0]
    tops = top_skeletons.reshape(4, 2, 64, 64)

    moved = to_group(jnp.concatenate([embeddings, rhs], axis=0))
    bases, chain, outgoing = call(
        prepare_kernel,
        (shaped(128, 1024, dtype=BF16), shaped(64, 256), shaped(8, 112, 128)),
        [scalars],
        [leaf_order, basis, transfer_maps[:, 0], chain_skeletons, rhs],
        "prepare",
        limit=50,
    )

    def gather(spread, after):
        high, mine = call(
            gather_kernel,
            (shaped(16, 128), shaped(64, 128)),
            [scalars],
            [spread],
            "gather",
            after=after,
        )
        return high, mine, other_core(mine)

    received = over_z(outgoing)
    kernels, near = build(scalars, embeddings, [rhs], None, rhs, [chain], "build_own")
    low, wide, pairs = call(
        first_middle_kernel,
        (shaped(16, 128), shaped(16, 32, 128), shaped(4, 64, 128)),
        [scalars],
        [received, chain, chain_skeletons],
        "middle",
        after=[near, moved[0]],
    )
    spread = over_yx(wide)
    from_x = lax.all_to_all(pairs, "x", 0, 0)
    kernels, near = build(
        scalars, embeddings, [moved[1], moved[0]], 1, near, [low], "build_a", [kernels]
    )
    high, mine, other = gather(spread, [near, from_x])
    kernels, near = build(
        scalars, embeddings, [moved[1], moved[2]], 3, near, [high], "build_b", [kernels]
    )
    table = call(
        coupling_kernel,
        shaped(64, 768),
        [scalars],
        [chain_skeletons, received, from_x, tops, chain],
        "coupling",
        after=[near],
    )
    far = (low, high, mine, other)

    def operate(extended, outgoing):
        moved = to_group(extended)
        low, wide = call(
            middle_kernel,
            (shaped(16, 128), shaped(16, 32, 128)),
            [scalars],
            [over_z(outgoing), chain],
            "middle",
        )
        near = near_product(scalars, [extended, *moved], kernels)
        high, mine, other = gather(over_yx(wide), [near])
        return low, high, mine, other, table, bases, near

    row = shaped(16, 1024)
    long = shaped(16, 1152)
    thin = shaped(16, 128)
    wire = shaped(8, 32, 128)
    v1, outgoing = call(
        first_kernel,
        (long, wire),
        [],
        [*far, table, bases, near, chain],
        "first",
    )
    v2, scaled, sums, outgoing = call(
        second_kernel, (row, long, thin, wire), [], [*operate(v1, outgoing), chain], "second"
    )
    image, step, outgoing = call(
        third_kernel,
        (long, thin, wire),
        [],
        [*operate(scaled, outgoing), chain, v1, sums],
        "third",
    )
    along, fresh, outgoing = call(
        fourth_kernel,
        (row, thin, shaped(32, 8, 128)),
        [],
        [*operate(image, outgoing), v2, sums],
        "fourth",
    )
    received = lax.all_to_all(outgoing, ("x", "z"), 0, 0)
    wide = call(spread_kernel, shaped(8, 8, 128), [], [received], "spread")
    shares = lax.all_to_all(wide, ("y", "core"), 0, 0)
    return call(
        last_kernel,
        (row, row),
        [],
        [shares, rhs, v1, v2, image, along, sums, fresh, step],
        "last",
    )


def solution(mesh):
    axes = ("y", "core", "x", "z")
    fine = Mesh(mesh.devices.reshape(4, 2, 4, 8), axes)
    placed = (
        P(None, axes),
        P(None, axes),
        P(axes, None),
        P(None, axes),
        P(None, axes, None, None),
        P(None, axes, None, None),
        P(),
        P(axes, None),
        P(None, axes),
        P(),
    )
    return jax.shard_map(
        local,
        mesh=fine,
        in_specs=placed,
        out_specs=(P(None, axes), P(None, axes)),
        check_vma=False,
    )
```

time: 549 us -> 207 us (0.38); the launches traced: 539 us -> 205 us
  blocking collectives: 294 us -> 23.8 us
  matrix products: 87.6 us -> 0 us
  Pallas kernels: 0 us -> 57.2 us
  starting transfers between devices: 44.3 us -> 80 us
  waiting for transfers between devices: 56.8 us -> 35.7 us
  local copies, waits for them, and re-layouts: 28.1 us -> 7.17 us
  other arithmetic: 18.3 us -> 0.66 us
  between operations: 9.98 us -> 0.94 us
    psum x3 -> x0, blocking collectives: 221 us -> none  [column_total(): return lax.psum(values, ('gx', 'gy'))]
    dot_general x103 -> x0, matrix products: 87.6 us -> none  [the longest x64 58.7 us: product_t(): lax.dot_general(first, second, (((1,), (1,)), ((), ())), precision=highes...]
    all_gather x4 -> x0, blocking collectives: 73.7 us -> none  [operate(): everyone = lax.all_gather(top_moment[None], 'gx', axis=0, tiled=True)]
    pallas_call x0 -> x22, Pallas kernels: none -> 57.2 us  [call(): pl.pallas_call(kernel, out_shape=outs, in_specs=[SMEM] * len(scalars) + [...]
    all_to_all x0 -> x9, starting transfers between devices: none -> 46.6 us  [the longest x4 24.5 us: over_z(): return lax.all_to_all(v, 'z', 0, 0)]
    ppermute x30 -> x16, waiting for transfers between devices: 56.8 us -> 13.5 us  [the longest x12 11 us: to_group(): lax.ppermute(v, 'z', [(i, i ^ o) for i in range(8)])]
    all_to_all x0 -> x2, blocking collectives: none -> 23.8 us  [the longest x1 13.5 us: local(): received = lax.all_to_all(outgoing, ('x', 'z'), 0, 0)]
    all_to_all x0 -> x9, waiting for transfers between devices: none -> 22.1 us  [the longest x4 13.8 us: over_z(): return lax.all_to_all(v, 'z', 0, 0)]
  transfers between devices with their start and end apart: 30 -> 25, of which waited for: 18 -> 12; matrix products, arithmetic and copies ran while one was open for 7% -> 0% of each run, Pallas kernels for 0% -> 22%
where the time goes in v1:
time: 207 us; the launch traced here: 205 us
  starting transfers between devices  80 us (39%)
  Pallas kernels  57.2 us (28%)
  waiting for transfers between devices  35.7 us (17%)
  blocking collectives  23.8 us (11%)
  local copies, waits for them, and re-layouts  7.17 us (3%)
    pallas_call x22, Pallas kernels, call(): pl.pallas_call(kernel, out_shape=outs, in_specs=[SMEM] * len(scalars) + [...  57.2 us
    all_to_all x4, starting transfers between devices, over_z(): return lax.all_to_all(v, 'z', 0, 0)  24.5 us
    all_to_all x4, starting transfers between devices, over_yx(): return lax.all_to_all(v, ('y', 'x'), 0, 0)  18.1 us
    ppermute x12, starting transfers between devices, to_group(): lax.ppermute(v, 'z', [(i, i ^ o) for i in range(8)])  17.3 us
    ppermute x4, starting transfers between devices, other_core(): return lax.ppermute(v, 'core', [(0, 1), (1, 0)])  16.1 us
    all_to_all x4, waiting for transfers between devices, over_z(): return lax.all_to_all(v, 'z', 0, 0)  13.8 us
    all_to_all x1, blocking collectives, local(): received = lax.all_to_all(outgoing, ('x', 'z'), 0, 0)  13.5 us
    ppermute x12, waiting for transfers between devices, to_group(): lax.ppermute(v, 'z', [(i, i ^ o) for i in range(8)])  11 us
  transfers between devices with their start and end apart: 25, of which 12 were waited for; matrix products, arithmetic and copies ran while one was open for 0% of the time, Pallas kernels for 22%

profile of v1, /device:TPU:1, one launch (start us, length us, event | category | flops | bytes accessed | tf_op | source)
XLA Modules:
  0.0 205.5 jit_solution(9219060847512928195)
XLA Ops:
  4.0 0.9 copy-done.6
  4.9 0.9 copy-done.9
  6.6 2.8 %prepare.1 = (bf16[128,1024]{1,0:T(8,128)(2,1)S(1)}, f32[64,256]{1,0:T(8,128)S(1)}, f32[8,112,128]{2,1,0:T(8,128)}) custom-call(s32[12]{0:T(128)S(1)} %concatenate.6.scalars, s32[1,1024]{1,0:T(1,128)S(1)} %copy-done.10, f32[64,1024]{1,0:T(8,128)S(1)} %copy-done.6, f32[5,64,64]{2,1,0:T(8,128)S(1)} %bitcast.13, f32[4,64,64]{2,1,0:T(8,128)S(1)} %bitcast.9, ...), custom_call_target="tpu_custom_call" | custom-call | flops 100000 | bytes 500000 | tf_op jit(solution)/shard_map/prepare/pallas_call | solution.py:371
  9.3 9.0 %all-to-all-start = ((f32[8,112,128]{2,1,0:T(8,128)}), f32[8,112,128]{2,1,0:T(8,128)S(1)}, u32[]{:S(2)}, u32[]{:S(2)}) async-start(f32[8,112,128]{2,1,0:T(8,128)} %get-tuple-element.40), calls=%async_computation | async-start | bytes 917504 | tf_op jit(solution)/shard_map/all_to_all | solution.py:433
  18.4 1.0 constant_dynamic-update-slice_fusion.1
  19.3 2.4 %collective-permute-start.1 = (f32[80,1024]{1,0:T(8,128)S(1)}, f32[80,1024]{1,0:T(8,128)S(1)}, u32[]{:S(2)}, u32[]{:S(2)}) collective-permute-start(f32[80,1024]{1,0:T(8,128)S(1)} %constant_dynamic-update-slice_fusion), channel_id=1, source_target_pairs={{0,2},{1,3},{2,0},{3,1},{4,6},{5,7},{6,4},{7,5},{8,10},{9,11},{10,... | collective-permute-start | bytes 983048 | tf_op jit(solution)/shard_map/ppermute | solution.py:425
  21.8 1.2 collective-permute-start
  23.0 0.9 copy-done.7
  23.9 6.9 %build_own.1 = (bf16[3,2,1024,1024]{3,2,1,0:T(8,128)(2,1)}, f32[16,1024]{1,0:T(8,128)S(1)}) custom-call(s32[12]{0:T(128)S(1)} %concatenate.6.scalars, f32[64,1024]{1,0:T(8,128)S(1)} %copy-done.7, f32[16,1024]{1,0:T(8,128)S(1)} %copy-done.3, f32[16,1024]{1,0:T(8,128)S(1)} %copy-done.3, f32[64,256]{1,0:T(8,128)S(1)} %get-tuple-element.41.refs_2_.chain), custom_call_target="tpu_custom_call" | custom-call | flops 4000000000 | bytes 500000 | tf_op jit(solution)/shard_map/build_own/pallas_call | solution.py:371
  30.9 10.9 %collective-permute-done.moved.refs_1_ = f32[80,1024]{1,0:T(8,128)S(1)} collective-permute-done((f32[80,1024]{1,0:T(8,128)S(1)}, f32[80,1024]{1,0:T(8,128)S(1)}, u32[]{:S(2)}, u32[]{:S(2)}) %collective-permute-start) | collective-permute-done | bytes 327712 | tf_op jit(solution)/shard_map/ppermute | solution.py:425
  41.8 1.5 middle.4
  43.3 4.0 %all-to-all-start.2 = ((f32[4,64,128]{2,1,0:T(8,128)}), f32[4,64,128]{2,1,0:T(8,128)S(1)}, u32[]{:S(2)}, u32[]{:S(2)}) async-start(f32[4,64,128]{2,1,0:T(8,128)} %get-tuple-element.47), calls=%async_computation.2 | async-start | bytes 262144 | tf_op jit(solution)/shard_map/all_to_all | solution.py:495
  47.3 2.9 %collective-permute-start.3 = (f32[80,1024]{1,0:T(8,128)S(1)}, f32[80,1024]{1,0:T(8,128)S(1)}, u32[]{:S(2)}, u32[]{:S(2)}) collective-permute-start(f32[80,1024]{1,0:T(8,128)S(1)} %constant_dynamic-update-slice_fusion), channel_id=1, source_target_pairs={{0,3},{1,2},{2,1},{3,0},{4,7},{5,6},{6,5},{7,4},{8,11},{9,10},{10,... | collective-permute-start | bytes 983048 | tf_op jit(solution)/shard_map/ppermute | solution.py:425
  50.3 1.9 all-to-all-done.2.refs_1_.from_x
  52.2 5.1 %all-to-all-start.1 = ((f32[16,32,128]{2,1,0:T(8,128)}), f32[16,32,128]{2,1,0:T(8,128)S(1)}, u32[]{:S(2)}, u32[]{:S(2)}) async-start(f32[16,32,128]{2,1,0:T(8,128)} %get-tuple-element.44), calls=%async_computation.1 | async-start | bytes 524288 | tf_op jit(solution)/shard_map/all_to_all | solution.py:437
  57.3 7.0 %build_a.1 = (bf16[3,2,1024,1024]{3,2,1,0:T(8,128)(2,1)}, f32[16,1024]{1,0:T(8,128)S(1)}) custom-call(s32[12]{0:T(128)S(1)} %concatenate.6.scalars, f32[64,1024]{1,0:T(8,128)S(1)} %copy-done.8, f32[80,1024]{1,0:T(8,128)S(1)} %collective-permute-done.1.refs_0_, f32[80,1024]{1,0:T(8,128)S(1)} %collective-permute-done.moved.refs_1_, ...), custom_call_target="tpu_custom_call", output_to_operand_aliasing={{0}: (6, {})} | custom-call | flops 4000000000 | bytes 500000 | tf_op jit(solution)/shard_map/build_a/pallas_call | solution.py:371
  65.5 4.2 %collective-permute-start.2 = (f32[64,128]{1,0:T(8,128)S(1)}, f32[64,128]{1,0:T(8,128)S(1)}, u32[]{:S(2)}, u32[]{:S(2)}) collective-permute-start(f32[64,128]{1,0:T(8,128)S(1)} %get-tuple-element.49.mine), channel_id=1, source_target_pairs={{0,32},{32,0},{1,33},{33,1},{2,34},{34,2},{3,35},{35,3},{4,36},{36... | collective-permute-start | bytes 98312 | tf_op jit(solution)/shard_map/ppermute | solution.py:429
  69.7 7.0 %build_b.1 = (bf16[3,2,1024,1024]{3,2,1,0:T(8,128)(2,1)}, f32[16,1024]{1,0:T(8,128)S(1)}) custom-call(s32[12]{0:T(128)S(1)} %concatenate.6.scalars, f32[64,1024]{1,0:T(8,128)S(1)} %copy-done.8, f32[80,1024]{1,0:T(8,128)S(1)} %collective-permute-done.1.refs_0_, f32[80,1024]{1,0:T(8,128)S(1)} %collective-permute-done.3.refs_1_, ...), custom_call_target="tpu_custom_call", output_to_operand_aliasing={{0}: (6, {})} | custom-call | flops 4000000000 | bytes 500000 | tf_op jit(solution)/shard_map/build_b/pallas_call | solution.py:371
  76.7 1.7 coupling.1.table
  78.4 1.8 first.1
  80.2 7.7 %all-to-all-start.3 = ((f32[8,32,128]{2,1,0:T(8,128)}), f32[8,32,128]{2,1,0:T(8,128)S(1)}, u32[]{:S(2)}, u32[]{:S(2)}) async-start(f32[8,32,128]{2,1,0:T(8,128)} %get-tuple-element.53), calls=%async_computation.3 | async-start | bytes 262144 | tf_op jit(solution)/shard_map/all_to_all | solution.py:433
  87.9 3.3 %collective-permute-start.6 = (f32[16,1152]{1,0:T(8,128)S(1)}, f32[16,1152]{1,0:T(8,128)S(1)}, u32[]{:S(2)}, u32[]{:S(2)}) collective-permute-start(f32[16,1152]{1,0:T(8,128)S(1)} %get-tuple-element.56.v.v1), channel_id=1, source_target_pairs={{0,3},{1,2},{2,1},{3,0},{4,7},{5,6},{6,5},{7,4},{8,11},{9,10},{10,... | collective-permute-start | bytes 221192 | tf_op jit(solution)/shard_map/ppermute | solution.py:425
  91.4 4.9 %all-to-all-done.3.received = f32[8,32,128]{2,1,0:T(8,128)S(1)} async-done(((f32[8,32,128]{2,1,0:T(8,128)}), f32[8,32,128]{2,1,0:T(8,128)S(1)}, u32[]{:S(2)}, u32[]{:S(2)}) %all-to-all-start.3) | async-done | bytes 131104 | tf_op jit(solution)/shard_map/all_to_all | solution.py:433
  96.4 1.5 middle.5
  97.9 5.3 %all-to-all-start.4 = ((f32[16,32,128]{2,1,0:T(8,128)}), f32[16,32,128]{2,1,0:T(8,128)S(1)}, u32[]{:S(2)}, u32[]{:S(2)}) async-start(f32[16,32,128]{2,1,0:T(8,128)} %get-tuple-element.55), calls=%async_computation.4 | async-start | bytes 524288 | tf_op jit(solution)/shard_map/all_to_all | solution.py:437
  103.2 5.5 %near.3.refs_0_ = f32[16,1152]{1,0:T(8,128)S(1)} custom-call(s32[12]{0:T(128)S(1)} %concatenate.6.scalars, f32[16,1152]{1,0:T(8,128)S(1)} %get-tuple-element.56.v.v1, f32[16,1152]{1,0:T(8,128)S(1)} %collective-permute-done.4.v1, f32[16,1152]{1,0:T(8,128)S(1)} %collective-permute-done.5.v2, f32[16,1152]{1,0:T(8,128)S(1)} %collective-permute-done.6.v3, ...), custom_call_target="tpu_custom_call" | custom-call | flops 4000000000 | bytes 500000 | tf_op jit(solution)/shard_map/near/pallas_call | solution.py:371
  108.8 2.0 all-to-all-done.4.received
  111.3 3.6 %collective-permute-start.7 = (f32[64,128]{1,0:T(8,128)S(1)}, f32[64,128]{1,0:T(8,128)S(1)}, u32[]{:S(2)}, u32[]{:S(2)}) collective-permute-start(f32[64,128]{1,0:T(8,128)S(1)} %get-tuple-element.59.mine), channel_id=1, source_target_pairs={{0,32},{32,0},{1,33},{33,1},{2,34},{34,2},{3,35},{35,3},{4,36},{36... | collective-permute-start | bytes 98312 | tf_op jit(solution)/shard_map/ppermute | solution.py:429
  115.8 1.8 second.1
  117.6 4.0 %all-to-all-start.5 = ((f32[8,32,128]{2,1,0:T(8,128)}), f32[8,32,128]{2,1,0:T(8,128)S(1)}, u32[]{:S(2)}, u32[]{:S(2)}) async-start(f32[8,32,128]{2,1,0:T(8,128)} %get-tuple-element.60), calls=%async_computation.5 | async-start | bytes 262144 | tf_op jit(solution)/shard_map/all_to_all | solution.py:433
  121.6 3.3 %collective-permute-start.10 = (f32[16,1152]{1,0:T(8,128)S(1)}, f32[16,1152]{1,0:T(8,128)S(1)}, u32[]{:S(2)}, u32[]{:S(2)}) collective-permute-start(f32[16,1152]{1,0:T(8,128)S(1)} %get-tuple-element.63.v), channel_id=1, source_target_pairs={{0,3},{1,2},{2,1},{3,0},{4,7},{5,6},{6,5},{7,4},{8,11},{9,10},{10,... | collective-permute-start | bytes 221192 | tf_op jit(solution)/shard_map/ppermute | solution.py:425
  125.2 4.4 %all-to-all-done.5.received = f32[8,32,128]{2,1,0:T(8,128)S(1)} async-done(((f32[8,32,128]{2,1,0:T(8,128)}), f32[8,32,128]{2,1,0:T(8,128)S(1)}, u32[]{:S(2)}, u32[]{:S(2)}) %all-to-all-start.5) | async-done | bytes 131104 | tf_op jit(solution)/shard_map/all_to_all | solution.py:433
  129.7 1.5 middle.6
  131.2 3.8 %all-to-all-start.6 = ((f32[16,32,128]{2,1,0:T(8,128)}), f32[16,32,128]{2,1,0:T(8,128)S(1)}, u32[]{:S(2)}, u32[]{:S(2)}) async-start(f32[16,32,128]{2,1,0:T(8,128)} %get-tuple-element.62), calls=%async_computation.6 | async-start | bytes 524288 | tf_op jit(solution)/shard_map/all_to_all | solution.py:437
  135.0 5.5 %near.4.refs_0_ = f32[16,1152]{1,0:T(8,128)S(1)} custom-call(s32[12]{0:T(128)S(1)} %concatenate.6.scalars, f32[16,1152]{1,0:T(8,128)S(1)} %get-tuple-element.63.v, f32[16,1152]{1,0:T(8,128)S(1)} %collective-permute-done.8.v1, f32[16,1152]{1,0:T(8,128)S(1)} %collective-permute-done.9.v2, f32[16,1152]{1,0:T(8,128)S(1)} %collective-permute-done.10.v3, ...), custom_call_target="tpu_custom_call" | custom-call | flops 4000000000 | bytes 500000 | tf_op jit(solution)/shard_map/near/pallas_call | solution.py:371
  140.6 2.0 all-to-all-done.6.received
  143.1 4.1 %collective-permute-start.11 = (f32[64,128]{1,0:T(8,128)S(1)}, f32[64,128]{1,0:T(8,128)S(1)}, u32[]{:S(2)}, u32[]{:S(2)}) collective-permute-start(f32[64,128]{1,0:T(8,128)S(1)} %get-tuple-element.65.mine), channel_id=1, source_target_pairs={{0,32},{32,0},{1,33},{33,1},{2,34},{34,2},{3,35},{35,3},{4,36},{36... | collective-permute-start | bytes 98312 | tf_op jit(solution)/shard_map/ppermute | solution.py:429
  148.1 1.8 third.1
  149.9 3.8 %all-to-all-start.7 = ((f32[8,32,128]{2,1,0:T(8,128)}), f32[8,32,128]{2,1,0:T(8,128)S(1)}, u32[]{:S(2)}, u32[]{:S(2)}) async-start(f32[8,32,128]{2,1,0:T(8,128)} %get-tuple-element.67), calls=%async_computation.7 | async-start | bytes 262144 | tf_op jit(solution)/shard_map/all_to_all | solution.py:433
  153.7 3.3 %collective-permute-start.14 = (f32[16,1152]{1,0:T(8,128)S(1)}, f32[16,1152]{1,0:T(8,128)S(1)}, u32[]{:S(2)}, u32[]{:S(2)}) collective-permute-start(f32[16,1152]{1,0:T(8,128)S(1)} %get-tuple-element.70.v.image), channel_id=1, source_target_pairs={{0,3},{1,2},{2,1},{3,0},{4,7},{5,6},{6,5},{7,4},{8,11},{9,10},{10,... | collective-permute-start | bytes 221192 | tf_op jit(solution)/shard_map/ppermute | solution.py:425
  157.3 4.4 %all-to-all-done.7.received = f32[8,32,128]{2,1,0:T(8,128)S(1)} async-done(((f32[8,32,128]{2,1,0:T(8,128)}), f32[8,32,128]{2,1,0:T(8,128)S(1)}, u32[]{:S(2)}, u32[]{:S(2)}) %all-to-all-start.7) | async-done | bytes 131104 | tf_op jit(solution)/shard_map/all_to_all | solution.py:433
  161.7 1.5 middle.7
  163.2 3.8 %all-to-all-start.8 = ((f32[16,32,128]{2,1,0:T(8,128)}), f32[16,32,128]{2,1,0:T(8,128)S(1)}, u32[]{:S(2)}, u32[]{:S(2)}) async-start(f32[16,32,128]{2,1,0:T(8,128)} %get-tuple-element.69), calls=%async_computation.8 | async-start | bytes 524288 | tf_op jit(solution)/shard_map/all_to_all | solution.py:437
  167.1 5.5 %near.5.refs_0_ = f32[16,1152]{1,0:T(8,128)S(1)} custom-call(s32[12]{0:T(128)S(1)} %concatenate.6.scalars, f32[16,1152]{1,0:T(8,128)S(1)} %get-tuple-element.70.v.image, f32[16,1152]{1,0:T(8,128)S(1)} %collective-permute-done.12.v1, f32[16,1152]{1,0:T(8,128)S(1)} %collective-permute-done.13.v2, f32[16,1152]{1,0:T(8,128)S(1)} %collective-permute-done.14.v3, ...), custom_call_target="tpu_custom_call" | custom-call | flops 4000000000 | bytes 500000 | tf_op jit(solution)/shard_map/near/pallas_call | solution.py:371
  172.7 2.0 all-to-all-done.8.received
  175.2 4.1 %collective-permute-start.15 = (f32[64,128]{1,0:T(8,128)S(1)}, f32[64,128]{1,0:T(8,128)S(1)}, u32[]{:S(2)}, u32[]{:S(2)}) collective-permute-start(f32[64,128]{1,0:T(8,128)S(1)} %get-tuple-element.72.mine), channel_id=1, source_target_pairs={{0,32},{32,0},{1,33},{33,1},{2,34},{34,2},{3,35},{35,3},{4,36},{36... | collective-permute-start | bytes 98312 | tf_op jit(solution)/shard_map/ppermute | solution.py:429
  180.9 13.5 %all_to_all.55.received = f32[32,8,128]{2,1,0:T(8,128)S(1)} all-to-all(f32[32,8,128]{2,1,0:T(8,128)S(1)} %get-tuple-element.74), channel_id=1, replica_groups=mesh['y'=4,'core'=2,'x'=4,'z'=8] {'x','z'}, dimensions={0} | all-to-all | bytes 262144 | tf_op jit(solution)/shard_map/all_to_all | solution.py:554
  194.4 10.2 %all_to_all.56.shares = f32[8,8,128]{2,1,0:T(8,128)S(1)} all-to-all(f32[8,8,128]{2,1,0:T(8,128)S(1)} %spread.1), channel_id=1, replica_groups=mesh['y'=4,'core'=2,'x'=4,'z'=8] {'y','core'}, dimensions={0} | all-to-all | bytes 65536 | tf_op jit(solution)/shard_map/all_to_all | solution.py:556
  (53 shorter events, 12.0 us)
Async XLA Ops:
  0.6 0.7 copy-start
  2.2 0.9 copy-start.1
  3.2 0.8 copy-start.3
  4.0 0.9 copy-start.6
  4.9 0.9 copy-start.9
  5.9 0.7 copy-start.10
  6.5 35.2 %copy-start.2 = (f32[4,1,64,64]{3,2,1,0:T(8,128)S(1)}, f32[4,1,64,64]{3,2,1,0:T(8,128)}, u32[]{:S(2)}) copy-start(f32[4,1,64,64]{3,2,1,0:T(8,128)} %param.15) | copy-start | bytes 196612
  6.6 50.7 %copy-start.8 = (f32[64,1024]{1,0:T(8,128)S(1)}, f32[64,1024]{1,0:T(8,128)}, u32[]{:S(2)}) copy-start(f32[64,1024]{1,0:T(8,128)} %own.5) | copy-start | bytes 786436
  9.3 32.5 %all-to-all-start = ((f32[8,112,128]{2,1,0:T(8,128)}), f32[8,112,128]{2,1,0:T(8,128)S(1)}, u32[]{:S(2)}, u32[]{:S(2)}) async-start(f32[8,112,128]{2,1,0:T(8,128)} %get-tuple-element.40), calls=%async_computation | async-start | bytes 917504 | tf_op jit(solution)/shard_map/all_to_all | solution.py:433
  19.3 37.9 %collective-permute-start.1 = (f32[80,1024]{1,0:T(8,128)S(1)}, f32[80,1024]{1,0:T(8,128)S(1)}, u32[]{:S(2)}, u32[]{:S(2)}) collective-permute-start(f32[80,1024]{1,0:T(8,128)S(1)} %constant_dynamic-update-slice_fusion), channel_id=1, source_target_pairs={{0,2},{1,3},{2,0},{3,1},{4,6},{5,7},{6,4},{7,5},{8,10},{9,11},{10,... | collective-permute-start | bytes 983048 | tf_op jit(solution)/shard_map/ppermute | solution.py:425
  21.8 20.0 %collective-permute-start = (f32[80,1024]{1,0:T(8,128)S(1)}, f32[80,1024]{1,0:T(8,128)S(1)}, u32[]{:S(2)}, u32[]{:S(2)}) collective-permute-start(f32[80,1024]{1,0:T(8,128)S(1)} %constant_dynamic-update-slice_fusion), channel_id=1, source_target_pairs={{0,1},{1,0},{2,3},{3,2},{4,5},{5,4},{6,7},{7,6},{8,9},{9,8},{10,11... | collective-permute-start | bytes 983048 | tf_op jit(solution)/shard_map/ppermute | solution.py:425
  23.0 0.9 copy-start.7
  43.3 8.8 %all-to-all-start.2 = ((f32[4,64,128]{2,1,0:T(8,128)}), f32[4,64,128]{2,1,0:T(8,128)S(1)}, u32[]{:S(2)}, u32[]{:S(2)}) async-start(f32[4,64,128]{2,1,0:T(8,128)} %get-tuple-element.47), calls=%async_computation.2 | async-start | bytes 262144 | tf_op jit(solution)/shard_map/all_to_all | solution.py:495
  47.3 22.4 %collective-permute-start.3 = (f32[80,1024]{1,0:T(8,128)S(1)}, f32[80,1024]{1,0:T(8,128)S(1)}, u32[]{:S(2)}, u32[]{:S(2)}) collective-permute-start(f32[80,1024]{1,0:T(8,128)S(1)} %constant_dynamic-update-slice_fusion), channel_id=1, source_target_pairs={{0,3},{1,2},{2,1},{3,0},{4,7},{5,6},{6,5},{7,4},{8,11},{9,10},{10,... | collective-permute-start | bytes 983048 | tf_op jit(solution)/shard_map/ppermute | solution.py:425
  52.2 12.7 %all-to-all-start.1 = ((f32[16,32,128]{2,1,0:T(8,128)}), f32[16,32,128]{2,1,0:T(8,128)S(1)}, u32[]{:S(2)}, u32[]{:S(2)}) async-start(f32[16,32,128]{2,1,0:T(8,128)} %get-tuple-element.44), calls=%async_computation.1 | async-start | bytes 524288 | tf_op jit(solution)/shard_map/all_to_all | solution.py:437
  57.3 19.4 %copy-start.5 = (f32[8,64,64]{2,1,0:T(8,128)S(1)}, f32[8,64,64]{2,1,0:T(8,128)}, u32[]{:S(2)}) copy-start(f32[8,64,64]{2,1,0:T(8,128)} %param.16) | copy-start | bytes 393220
  65.5 13.0 %collective-permute-start.2 = (f32[64,128]{1,0:T(8,128)S(1)}, f32[64,128]{1,0:T(8,128)S(1)}, u32[]{:S(2)}, u32[]{:S(2)}) collective-permute-start(f32[64,128]{1,0:T(8,128)S(1)} %get-tuple-element.49.mine), channel_id=1, source_target_pairs={{0,32},{32,0},{1,33},{33,1},{2,34},{34,2},{3,35},{35,3},{4,36},{36... | collective-permute-start | bytes 98312 | tf_op jit(solution)/shard_map/ppermute | solution.py:429
  80.2 16.2 %all-to-all-start.3 = ((f32[8,32,128]{2,1,0:T(8,128)}), f32[8,32,128]{2,1,0:T(8,128)S(1)}, u32[]{:S(2)}, u32[]{:S(2)}) async-start(f32[8,32,128]{2,1,0:T(8,128)} %get-tuple-element.53), calls=%async_computation.3 | async-start | bytes 262144 | tf_op jit(solution)/shard_map/all_to_all | solution.py:433
  87.9 15.3 %collective-permute-start.6 = (f32[16,1152]{1,0:T(8,128)S(1)}, f32[16,1152]{1,0:T(8,128)S(1)}, u32[]{:S(2)}, u32[]{:S(2)}) collective-permute-start(f32[16,1152]{1,0:T(8,128)S(1)} %get-tuple-element.56.v.v1), channel_id=1, source_target_pairs={{0,3},{1,2},{2,1},{3,0},{4,7},{5,6},{6,5},{7,4},{8,11},{9,10},{10,... | collective-permute-start | bytes 221192 | tf_op jit(solution)/shard_map/ppermute | solution.py:425
  91.1 12.1 %collective-permute-start.5 = (f32[16,1152]{1,0:T(8,128)S(1)}, f32[16,1152]{1,0:T(8,128)S(1)}, u32[]{:S(2)}, u32[]{:S(2)}) collective-permute-start(f32[16,1152]{1,0:T(8,128)S(1)} %get-tuple-element.56.v.v1), channel_id=1, source_target_pairs={{0,2},{1,3},{2,0},{3,1},{4,6},{5,7},{6,4},{7,5},{8,10},{9,11},{10,... | collective-permute-start | bytes 221192 | tf_op jit(solution)/shard_map/ppermute | solution.py:425
  91.1 12.1 %collective-permute-start.4 = (f32[16,1152]{1,0:T(8,128)S(1)}, f32[16,1152]{1,0:T(8,128)S(1)}, u32[]{:S(2)}, u32[]{:S(2)}) collective-permute-start(f32[16,1152]{1,0:T(8,128)S(1)} %get-tuple-element.56.v.v1), channel_id=1, source_target_pairs={{0,1},{1,0},{2,3},{3,2},{4,5},{5,4},{6,7},{7,6},{8,9},{9,8},{10,11... | collective-permute-start | bytes 221192 | tf_op jit(solution)/shard_map/ppermute | solution.py:425
  97.9 12.9 %all-to-all-start.4 = ((f32[16,32,128]{2,1,0:T(8,128)}), f32[16,32,128]{2,1,0:T(8,128)S(1)}, u32[]{:S(2)}, u32[]{:S(2)}) async-start(f32[16,32,128]{2,1,0:T(8,128)} %get-tuple-element.55), calls=%async_computation.4 | async-start | bytes 524288 | tf_op jit(solution)/shard_map/all_to_all | solution.py:437
  111.3 4.5 %collective-permute-start.7 = (f32[64,128]{1,0:T(8,128)S(1)}, f32[64,128]{1,0:T(8,128)S(1)}, u32[]{:S(2)}, u32[]{:S(2)}) collective-permute-start(f32[64,128]{1,0:T(8,128)S(1)} %get-tuple-element.59.mine), channel_id=1, source_target_pairs={{0,32},{32,0},{1,33},{33,1},{2,34},{34,2},{3,35},{35,3},{4,36},{36... | collective-permute-start | bytes 98312 | tf_op jit(solution)/shard_map/ppermute | solution.py:429
  117.6 12.1 %all-to-all-start.5 = ((f32[8,32,128]{2,1,0:T(8,128)}), f32[8,32,128]{2,1,0:T(8,128)S(1)}, u32[]{:S(2)}, u32[]{:S(2)}) async-start(f32[8,32,128]{2,1,0:T(8,128)} %get-tuple-element.60), calls=%async_computation.5 | async-start | bytes 262144 | tf_op jit(solution)/shard_map/all_to_all | solution.py:433
  121.6 13.4 %collective-permute-start.10 = (f32[16,1152]{1,0:T(8,128)S(1)}, f32[16,1152]{1,0:T(8,128)S(1)}, u32[]{:S(2)}, u32[]{:S(2)}) collective-permute-start(f32[16,1152]{1,0:T(8,128)S(1)} %get-tuple-element.63.v), channel_id=1, source_target_pairs={{0,3},{1,2},{2,1},{3,0},{4,7},{5,6},{6,5},{7,4},{8,11},{9,10},{10,... | collective-permute-start | bytes 221192 | tf_op jit(solution)/shard_map/ppermute | solution.py:425
  124.9 10.1 %collective-permute-start.9 = (f32[16,1152]{1,0:T(8,128)S(1)}, f32[16,1152]{1,0:T(8,128)S(1)}, u32[]{:S(2)}, u32[]{:S(2)}) collective-permute-start(f32[16,1152]{1,0:T(8,128)S(1)} %get-tuple-element.63.v), channel_id=1, source_target_pairs={{0,2},{1,3},{2,0},{3,1},{4,6},{5,7},{6,4},{7,5},{8,10},{9,11},{10,... | collective-permute-start | bytes 221192 | tf_op jit(solution)/shard_map/ppermute | solution.py:425
  124.9 10.1 %collective-permute-start.8 = (f32[16,1152]{1,0:T(8,128)S(1)}, f32[16,1152]{1,0:T(8,128)S(1)}, u32[]{:S(2)}, u32[]{:S(2)}) collective-permute-start(f32[16,1152]{1,0:T(8,128)S(1)} %get-tuple-element.63.v), channel_id=1, source_target_pairs={{0,1},{1,0},{2,3},{3,2},{4,5},{5,4},{6,7},{7,6},{8,9},{9,8},{10,11... | collective-permute-start | bytes 221192 | tf_op jit(solution)/shard_map/ppermute | solution.py:425
  131.2 11.4 %all-to-all-start.6 = ((f32[16,32,128]{2,1,0:T(8,128)}), f32[16,32,128]{2,1,0:T(8,128)S(1)}, u32[]{:S(2)}, u32[]{:S(2)}) async-start(f32[16,32,128]{2,1,0:T(8,128)} %get-tuple-element.62), calls=%async_computation.6 | async-start | bytes 524288 | tf_op jit(solution)/shard_map/all_to_all | solution.py:437
  140.6 64.1 %copy-start.4 = (f32[16,1024]{1,0:T(8,128)S(1)}, f32[16,1024]{1,0:T(8,128)}, u32[]{:S(2)}) copy-start(f32[16,1024]{1,0:T(8,128)} %rhs.4) | copy-start | bytes 196612
  143.1 5.0 %collective-permute-start.11 = (f32[64,128]{1,0:T(8,128)S(1)}, f32[64,128]{1,0:T(8,128)S(1)}, u32[]{:S(2)}, u32[]{:S(2)}) collective-permute-start(f32[64,128]{1,0:T(8,128)S(1)} %get-tuple-element.65.mine), channel_id=1, source_target_pairs={{0,32},{32,0},{1,33},{33,1},{2,34},{34,2},{3,35},{35,3},{4,36},{36... | collective-permute-start | bytes 98312 | tf_op jit(solution)/shard_map/ppermute | solution.py:429
  149.9 11.8 %all-to-all-start.7 = ((f32[8,32,128]{2,1,0:T(8,128)}), f32[8,32,128]{2,1,0:T(8,128)S(1)}, u32[]{:S(2)}, u32[]{:S(2)}) async-start(f32[8,32,128]{2,1,0:T(8,128)} %get-tuple-element.67), calls=%async_computation.7 | async-start | bytes 262144 | tf_op jit(solution)/shard_map/all_to_all | solution.py:433
  153.7 13.4 %collective-permute-start.14 = (f32[16,1152]{1,0:T(8,128)S(1)}, f32[16,1152]{1,0:T(8,128)S(1)}, u32[]{:S(2)}, u32[]{:S(2)}) collective-permute-start(f32[16,1152]{1,0:T(8,128)S(1)} %get-tuple-element.70.v.image), channel_id=1, source_target_pairs={{0,3},{1,2},{2,1},{3,0},{4,7},{5,6},{6,5},{7,4},{8,11},{9,10},{10,... | collective-permute-start | bytes 221192 | tf_op jit(solution)/shard_map/ppermute | solution.py:425
  157.0 10.1 %collective-permute-start.13 = (f32[16,1152]{1,0:T(8,128)S(1)}, f32[16,1152]{1,0:T(8,128)S(1)}, u32[]{:S(2)}, u32[]{:S(2)}) collective-permute-start(f32[16,1152]{1,0:T(8,128)S(1)} %get-tuple-element.70.v.image), channel_id=1, source_target_pairs={{0,2},{1,3},{2,0},{3,1},{4,6},{5,7},{6,4},{7,5},{8,10},{9,11},{10,... | collective-permute-start | bytes 221192 | tf_op jit(solution)/shard_map/ppermute | solution.py:425
  157.0 10.1 %collective-permute-start.12 = (f32[16,1152]{1,0:T(8,128)S(1)}, f32[16,1152]{1,0:T(8,128)S(1)}, u32[]{:S(2)}, u32[]{:S(2)}) collective-permute-start(f32[16,1152]{1,0:T(8,128)S(1)} %get-tuple-element.70.v.image), channel_id=1, source_target_pairs={{0,1},{1,0},{2,3},{3,2},{4,5},{5,4},{6,7},{7,6},{8,9},{9,8},{10,11... | collective-permute-start | bytes 221192 | tf_op jit(solution)/shard_map/ppermute | solution.py:425
  163.2 11.4 %all-to-all-start.8 = ((f32[16,32,128]{2,1,0:T(8,128)}), f32[16,32,128]{2,1,0:T(8,128)S(1)}, u32[]{:S(2)}, u32[]{:S(2)}) async-start(f32[16,32,128]{2,1,0:T(8,128)} %get-tuple-element.69), calls=%async_computation.8 | async-start | bytes 524288 | tf_op jit(solution)/shard_map/all_to_all | solution.py:437
  175.2 5.0 %collective-permute-start.15 = (f32[64,128]{1,0:T(8,128)S(1)}, f32[64,128]{1,0:T(8,128)S(1)}, u32[]{:S(2)}, u32[]{:S(2)}) collective-permute-start(f32[64,128]{1,0:T(8,128)S(1)} %get-tuple-element.72.mine), channel_id=1, source_target_pairs={{0,32},{32,0},{1,33},{33,1},{2,34},{34,2},{3,35},{35,3},{4,36},{36... | collective-permute-start | bytes 98312 | tf_op jit(solution)/shard_map/ppermute | solution.py:429

commit v2 on v1

v2 whole, which is shorter than its diff:
```python
import functools
import math

import jax
import jax.numpy as jnp
from jax import lax
from jax.experimental import pallas as pl
from jax.experimental.pallas import tpu as pltpu
from jax.sharding import Mesh
from jax.sharding import PartitionSpec as P

F32 = jnp.float32
BF16 = jnp.bfloat16
HIGHEST = lax.Precision.HIGHEST
NOISE = 0.5
SCALE = math.sqrt(5.0) / 2.8
LOG2E = math.log2(math.e)
DEPTH = 208
TILE = 256

Z, X, Y, CORE, O0, O1, O2, O3, TOPS = range(9)


def dot(a, b, ca=1, cb=0, precision=None):
    return lax.dot_general(
        a, b, (((ca,), (cb,)), ((), ())), precision=precision, preferred_element_type=F32
    )


def split(a):
    high = a.astype(BF16)
    return high, (a - high.astype(F32)).astype(BF16)


def stacked(a):
    return jnp.concatenate(split(a), axis=0)


def halves(a):
    n = a.shape[0] // 2
    return a[:n] + a[n:]


def paired(a, axis):
    return jnp.concatenate(split(a), axis=axis)


def times(a, pair):
    both = halves(dot(stacked(a), pair))
    n = both.shape[1] // 2
    return both[:, :n] + both[:, n:]


def times_t(a, pair):
    both = halves(dot(stacked(a), pair, 1, 1))
    n = both.shape[1] // 2
    return both[:, :n] + both[:, n:]


def square_sum(v):
    return jnp.broadcast_to(jnp.sum(v * v, axis=1, keepdims=True), (v.shape[0], 64))


def moments(v, bases, chain):
    own = times_t(v, bases)
    lifted = times(own, chain)
    return jnp.concatenate([own, lifted[:, 0:64]], axis=1), lifted[:, 64:192], lifted[:, 192:256]


def write_moments(extended, out, v, weighed, bases, chain):
    own, middle, top = moments(v, bases[...], chain[...])
    extended[:, 0 : v.shape[1]] = v
    extended[:, v.shape[1] :] = own
    last = jnp.concatenate([top, square_sum(weighed)], axis=1)
    for i in range(out.shape[0]):
        out[i, 0:16, :] = middle
        out[i, 16:32, :] = last


def packed(skeleton):
    return jnp.concatenate([skeleton[0:32], skeleton[32:64]], axis=1)


def unpacked(block):
    return jnp.concatenate([block[:, 0:64], block[:, 64:128]], axis=0)


def skeleton_offsets(scalars):
    o0, o1 = scalars[O0], scalars[O1]
    second = jnp.where(o1 > 1, o1 * 2, jnp.where(o0 == 2, 3, 2))
    return o0, second, jnp.where(o1 == 3, 4, 7)


def prepare_kernel(
    scalars, order, basis, maps, skeletons, rhs, points, bases, chain, tail, wire, all_rows
):
    all_rows[0:64, :] = points[...]
    all_rows[64:80, :] = rhs[...]
    both = stacked(basis[...])
    leaf = basis.shape[1]
    for t in range(leaf // TILE):
        rows = lax.broadcasted_iota(jnp.int32, (TILE, leaf), 0) + t * TILE
        one_hot = jnp.where(rows == order[...], 1.0, 0.0).astype(BF16)
        bases[:, t * TILE : (t + 1) * TILE] = dot(both, one_hot, 1, 1).astype(BF16)
    p1 = maps[0]
    p2 = dot(p1, maps[1], precision=HIGHEST)
    p3 = dot(p2, maps[2], precision=HIGHEST)
    e34 = dot(maps[3], maps[4], precision=HIGHEST)
    p5 = dot(p3, e34, precision=HIGHEST)
    tail[...] = e34
    chain[...] = paired(jnp.concatenate([p1, p2, p3, p5], axis=1), 1)
    own, middle, _ = moments(rhs[...], bases[...], chain[...])
    _, k1, k2 = skeleton_offsets(scalars)
    blocks = [packed(skeletons[h]) for h in range(3)]
    for i in range(wire.shape[0]):
        offset = jnp.bitwise_xor(scalars[Z], i)
        wire[i, 0:16, :] = own
        wire[i, 16:32, :] = middle
        block = jnp.where(offset == k1, blocks[1], blocks[0])
        wire[i, 32:64, :] = jnp.where(offset == k2, blocks[2], block)


def middle_kernel(scalars, received, tail, skeletons, after, low, out, second):
    z, o0, o1, o2 = scalars[Z], scalars[O0], scalars[O1], scalars[O2]
    left = lax.broadcasted_iota(jnp.int32, (16, 128), 1) < 64
    sums = [jnp.zeros((16, 128), F32) for _ in range(2)]
    for i in range(received.shape[0]):
        offset = jnp.bitwise_xor(z, i)
        hit0 = offset == o0
        hit1 = offset // 2 == o1
        hit2 = offset // 4 == jnp.bitwise_and(o2, 1)
        sums[0] += jnp.where((left & hit0) | (~left & hit1), received[i, 0:16, :], 0.0)
        sums[1] += jnp.where(~left | hit2, received[i, 16:32, :], 0.0)
    low[...] = sums[0]
    top = dot(sums[1][:, 64:128], tail[...], precision=HIGHEST)
    last = jnp.concatenate([top, jnp.zeros_like(top)], axis=1)
    for i in range(out.shape[0]):
        out[i, 0:16, :] = sums[1]
        out[i, 16:32, :] = last
        out[i, 32:64, :] = packed(skeletons[3])
    k2 = skeleton_offsets(scalars)[2]
    across = received[jnp.bitwise_xor(z, k2), 32:64, :]
    second[...] = jnp.where(o2 % 2 == 1, across, packed(skeletons[2]))


def matern(first, second):
    turned = first.T
    squares = (
        jnp.sum(turned * turned, axis=1, keepdims=True)
        + jnp.sum(second * second, axis=0, keepdims=True)
        - 2.0 * dot(turned, second, precision=HIGHEST)
    )
    s = SCALE * jnp.sqrt(jnp.maximum(squares, 0.0))
    return (1.0 + s + s * s * (1.0 / 3.0)) * jnp.exp(-s)


def top_kernel(scalars, skeletons, from_yx, tops, tail, out):
    x, y, core = scalars[X], scalars[Y], scalars[CORE]
    partner = unpacked(from_yx[y * 4 + jnp.bitwise_xor(x, scalars[O3]), 32:64, :])
    others = []
    masks = []
    for flip in (0, 1):
        for j in range(4):
            side = jnp.bitwise_xor(core, flip)
            others.append(tops[j, side])
            hits = sum((scalars[TOPS + k] == j * 2 + side).astype(F32) for k in range(4))
            masks.append(jnp.full((64, 64), hits, F32))
    top = matern(tops[y, core], jnp.concatenate(others, axis=1))
    top = dot(tail[...], top * jnp.concatenate(masks, axis=1), precision=HIGHEST)
    out[...] = paired(jnp.concatenate([matern(skeletons[3], partner), top], axis=1), 0)


def low_couplings(scalars, skeletons, from_z, second, chain):
    z = scalars[Z]
    k0, k1, _ = skeleton_offsets(scalars)
    down = chain[:, 0:256].astype(F32) + chain[:, 256:512].astype(F32)
    partners = [from_z[jnp.bitwise_xor(z, k), 32:64, :] for k in (k0, k1)] + [second]
    pieces = []
    for h in range(3):
        coupling = matern(skeletons[h], unpacked(partners[h]))
        if h > 0:
            coupling = dot(down[:, (h - 1) * 64 : h * 64], coupling, precision=HIGHEST)
        pieces.append(coupling)
    return paired(jnp.concatenate(pieces + [down[:, 128:192]], axis=1), 0)


def three(a):
    high = a.astype(BF16).astype(F32)
    middle = (a - high).astype(BF16).astype(F32)
    return high, middle, a - high - middle


def augment(points, target, turned):
    leaf = points.shape[1]
    high, low = split(points * SCALE)
    h32, l32 = high.astype(F32), low.astype(F32)
    sums = three(jnp.sum(h32 * h32 + 2.0 * (h32 * l32), axis=0, keepdims=True))
    row = lax.broadcasted_iota(jnp.int32, (16, leaf), 0)
    first, ones = (0, 3) if turned else (3, 0)
    rest = jnp.where((row >= ones) & (row < ones + 3), 1.0, 0.0)
    for i in range(3):
        rest = jnp.where(row == first + i, sums[i], rest)
    if turned:
        high, low = (-2.0 * h32).astype(BF16), (-2.0 * l32).astype(BF16)
    target[0:64, :] = high
    target[64:128, :] = high if turned else low
    target[128:192, :] = low if turned else high
    target[192:208, :] = rest.astype(BF16)


def entries(squares, kernel):
    wide = 512
    tall = 32
    for r in range(0, squares.shape[0], tall):
        for c in range(0, squares.shape[1], wide):
            s2 = jnp.maximum(squares[r : r + tall, c : c + wide], 1e-30)
            s = s2 * lax.rsqrt(s2)
            value = (1.0 + s + s2 * (1.0 / 3.0)) * jnp.exp2(s * -LOG2E)
            high, low = split(value)
            kernel[0, r : r + tall, c : c + wide] = high
            kernel[1, r : r + tall, c : c + wide] = low


def build_kernel(scalars, own, *refs, choice):
    if choice is None:
        begin, after, whole, near, aug, left, squares, kernel, sems = refs
        both = own[...]
        near[...] = NOISE * begin[...]
        slot = 0
    else:
        yes, no, begin, after, previous, whole, near, aug, left, squares, kernel, sems = refs
        both = jnp.where(scalars[O0] == choice, yes[...], no[...])
        near[...] = begin[...]
        slot = (choice + 1) // 2
    augment(own[0:64, :], aug, False)
    augment(both[0:64, :], left, True)
    pair = stacked(both[64:80, :])
    leaf = own.shape[1]
    tiles = leaf // TILE
    copies = []
    total = None
    squares[0] = dot(left[:, 0:TILE], aug[...], 0, 0)
    for t in range(tiles):
        cols = slice(t * TILE, (t + 1) * TILE)
        if t + 1 < tiles:
            squares[(t + 1) % 2] = dot(left[:, (t + 1) * TILE : (t + 2) * TILE], aug[...], 0, 0)
        entries(squares.at[t % 2], kernel.at[t])
        part = dot(pair[:, cols], kernel[t, 0]) + dot(pair[:, cols], kernel[t, 1])
        total = part if total is None else total + part
        rows = pl.ds(t * TILE, TILE)
        copies.append(
            pltpu.make_async_copy(kernel.at[t], whole.at[slot, :, rows, :], sems.at[t])
        )
        copies[t].start()
    near[...] += halves(total)
    for copy in copies:
        copy.wait()


def near_kernel(scalars, v, v1, v2, v3, kernels, after, out, held, sems):
    leaf = kernels.shape[2]
    tiles = leaf // TILE
    copies = []
    for e in range(3):
        for t in range(tiles):
            rows = pl.ds(t * TILE, TILE)
            copies.append(
                pltpu.make_async_copy(
                    kernels.at[e, :, rows, :], held.at[e, :, rows, :], sems.at[e * tiles + t]
                )
            )
    for copy in copies:
        copy.start()
    o0 = scalars[O0]
    own = v[:, 0:leaf]
    second = jnp.where(o0 == 1, v2[:, 0:leaf], v1[:, 0:leaf])
    third = jnp.where(o0 == 3, v2[:, 0:leaf], v3[:, 0:leaf])
    total = None
    for e, vector in enumerate((own, second, third)):
        pair = stacked(vector)
        for t in range(tiles):
            rows = slice(t * TILE, (t + 1) * TILE)
            copies[e * tiles + t].wait()
            part = dot(pair[:, rows], held[e, 0, rows, :]) + dot(pair[:, rows], held[e, 1, rows, :])
            total = part if total is None else total + part
    out[:, 0:leaf] = NOISE * own + halves(total)
    out[:, leaf:] = jnp.where(
        o0 == 1, v1[:, leaf:], jnp.where(o0 == 2, v2[:, leaf:], v3[:, leaf:])
    )


def gather_kernel(scalars, received, *refs):
    high, out = refs[-2:]
    x, y, o2, o3 = scalars[X], scalars[Y], scalars[O2], scalars[O3]
    left = lax.broadcasted_iota(jnp.int32, (16, 128), 1) < 64
    total = jnp.zeros((16, 128), F32)
    for j in range(4):
        top = jnp.zeros((16, 128), F32)
        for i in range(4):
            p = j * 4 + i
            offset = jnp.bitwise_xor(x, i)
            here = y == j
            hit2 = here & (offset == o2 // 2)
            hit3 = here & (offset == o3)
            total += jnp.where((left & hit2) | (~left & hit3), received[p, 0:16, :], 0.0)
            top += received[p, 16:32, :]
        out[j * 16 : (j + 1) * 16, :] = top
    high[...] = total


def field_at_three(high, mine, other, table):
    parts = [high[:, 64:128]]
    for side in (mine, other):
        parts += [side[j * 16 : (j + 1) * 16, 0:64] for j in range(4)]
    return times_t(jnp.concatenate(parts, axis=1), table[...])


def lower_kernel(high, mine, other, table, own, *refs):
    out = refs[-1]
    start = own.shape[1] - 128
    field = field_at_three(high, mine, other, table)
    norm = sum(side[j * 16 : (j + 1) * 16, 64:128] for side in (mine, other) for j in range(4))
    first = jnp.concatenate([field, norm], axis=1)
    second = jnp.concatenate([own[:, start + 64 :], high[:, 0:64]], axis=1)
    for i in range(out.shape[0]):
        out[i, 0:16, :] = first
        out[i, 16:32, :] = second


def add_far(moments_in, table, bases, near):
    pair = stacked(times_t(moments_in, table[...]))
    far = halves(dot(pair, bases[0:64, :]) + dot(pair, bases[64:128, :]))
    return near[:, 0 : far.shape[1]] + far


def apply_far(scalars, received, table, bases, near):
    leaf = bases.shape[1]
    z, o1, o2 = scalars[Z], scalars[O1], scalars[O2]
    left = lax.broadcasted_iota(jnp.int32, (16, 128), 1) < 64
    sums = [jnp.zeros((16, 128), F32) for _ in range(2)]
    for i in range(received.shape[0]):
        offset = jnp.bitwise_xor(z, i)
        hit1 = offset // 2 == o1
        hit2 = offset // 4 == jnp.bitwise_and(o2, 1)
        sums[0] += received[i, 0:16, :]
        sums[1] += jnp.where((left & hit1) | (~left & hit2), received[i, 16:32, :], 0.0)
    parts = [near[:, leaf : leaf + 64], sums[1], sums[0][:, 0:64]]
    return add_far(jnp.concatenate(parts, axis=1), table, bases, near), sums[0][:, 64:65]


def first_kernel(
    scalars,
    low,
    high,
    mine,
    other,
    top_table,
    from_z,
    second,
    moved,
    skeletons,
    bases,
    near,
    chain,
    table,
    v1,
    out,
):
    across = jnp.where(scalars[O2] > 1, moved[...], second[...])
    table[...] = low_couplings(scalars, skeletons, from_z, across, chain)
    field = field_at_three(high, mine, other, top_table)
    parts = [low[...], high[:, 0:64], field]
    image = add_far(jnp.concatenate(parts, axis=1), table, bases, near)
    write_moments(v1, out, image, image, bases, chain)


def second_kernel(scalars, received, table, bases, near, chain, v2, scaled, sums, out):
    image, norm = apply_far(scalars, received, table, bases, near)
    v2[...] = image
    sums[...] = jnp.broadcast_to(norm, sums.shape)
    write_moments(scaled, out, image / jnp.sqrt(norm), image, bases, chain)


def third_kernel(scalars, received, table, bases, near, chain, v1, sums, image, step, out):
    product, along = apply_far(scalars, received, table, bases, near)
    norm = sums[:, 0:1]
    size = norm / along
    new = v1[:, 0 : product.shape[1]] - (size * jnp.sqrt(norm)) * product
    step[...] = jnp.broadcast_to(size, step.shape)
    write_moments(image, out, new, new, bases, chain)


def diagonal():
    rows = lax.broadcasted_iota(jnp.int32, (16, 128), 0)
    return rows == lax.broadcasted_iota(jnp.int32, (16, 128), 1)


def fourth_kernel(scalars, received, table, bases, near, v2, sums, along, fresh, out):
    product, norm = apply_far(scalars, received, table, bases, near)
    new = product + (norm / sums[:, 0:1]) * v2[...]
    along[...] = new
    fresh[...] = jnp.broadcast_to(norm, fresh.shape)
    share = jnp.sum(new * new, axis=1, keepdims=True)
    line = jnp.sum(jnp.where(diagonal(), share, 0.0), axis=0, keepdims=True)
    for i in range(out.shape[0]):
        out[i] = jnp.broadcast_to(line, (8, 128))


def spread_kernel(received, out):
    total = received[0]
    for i in range(1, received.shape[0]):
        total = total + received[i]
    for i in range(out.shape[0]):
        out[i] = total


def last_kernel(shares, rhs, v1, v2, image, along, sums, fresh, step, iterate, residual):
    leaf = rhs.shape[1]
    norm = fresh[:, 0:1]
    first = step[:, 0:1]
    line = sum(shares[i, 0:1, :] for i in range(shares.shape[0]))
    second = norm / jnp.sum(jnp.where(diagonal(), line, 0.0), axis=1, keepdims=True)
    beta = norm / sums[:, 0:1]
    start = v1[:, 0:leaf]
    iterate[...] = first * start + second * (image[:, 0:leaf] + beta * start)
    residual[...] = rhs[...] - first * v2[...] - second * along[...]


SMEM = pl.BlockSpec(memory_space=pltpu.SMEM)
VMEM = pl.BlockSpec(memory_space=pltpu.VMEM)


def shaped(*shape, dtype=F32):
    return jax.ShapeDtypeStruct(shape, dtype)


MIB = 1024 * 1024
ANY = pl.BlockSpec(memory_space=pl.ANY)


def call(kernel, outs, scalars, arrays, name, after=(), limit=16, flops=100000, scratch=(), alias=None):
    return pl.pallas_call(
        kernel,
        out_shape=outs,
        in_specs=[SMEM] * len(scalars) + [VMEM] * len(arrays) + [ANY] * len(after),
        out_specs=jax.tree.map(lambda a: VMEM if len(a.shape) < 4 else ANY, outs),
        scratch_shapes=list(scratch),
        input_output_aliases=alias or {},
        name=name,
        compiler_params=pltpu.CompilerParams(vmem_limit_bytes=limit * MIB),
        cost_estimate=pl.CostEstimate(flops=flops, bytes_accessed=500000, transcendentals=0),
    )(*scalars, *arrays, *after)


def build(scalars, own, others, choice, near, after, name, kernels=()):
    leaf = own.shape[1]
    tiles = leaf // TILE
    return call(
        functools.partial(build_kernel, choice=choice),
        (shaped(3, 2, leaf, leaf, dtype=BF16), shaped(16, leaf)),
        [scalars],
        [own, *others, near],
        name,
        after=[*after, *kernels],
        limit=50,
        flops=4000000000,
        alias={3 + len(others) + len(after): 0} if kernels else None,
        scratch=[
            pltpu.VMEM((DEPTH, leaf), BF16),
            pltpu.VMEM((DEPTH, leaf), BF16),
            pltpu.VMEM((2, TILE, leaf), F32),
            pltpu.VMEM((tiles, 2, TILE, leaf), BF16),
            pltpu.SemaphoreType.DMA((tiles,)),
        ],
    )


def near_product(scalars, vectors, kernels, after):
    leaf = kernels.shape[2]
    return call(
        near_kernel,
        shaped(*vectors[0].shape),
        [scalars],
        vectors,
        "near",
        after=[kernels, after],
        limit=50,
        flops=4000000000,
        scratch=[
            pltpu.VMEM((3, 2, leaf, leaf), BF16),
            pltpu.SemaphoreType.DMA((3 * leaf // TILE,)),
        ],
    )


def along_z(v, offset):
    return lax.ppermute(v, "z", [(i, i ^ offset) for i in range(8)])


def other_core(v):
    return lax.ppermute(v, "core", [(0, 1), (1, 0)])


def over_z(v):
    return lax.all_to_all(v, "z", 0, 0)


def over_yx(v):
    return lax.all_to_all(v, ("y", "x"), 0, 0)


def local(
    rhs,
    embeddings,
    leaf_order,
    basis,
    transfer_maps,
    skeletons,
    top_skeletons,
    near_lists,
    far_lists,
    top_lists,
):
    y, core, x, z = (lax.axis_index(a) for a in ("y", "core", "x", "z"))
    top = y * 2 + core
    leaf = top * 32 + x * 8 + z
    offsets = jnp.bitwise_xor(
        far_lists[:, 0], jnp.right_shift(leaf, jnp.arange(4, dtype=jnp.int32))
    )
    partners = lax.dynamic_index_in_dim(top_lists, top, 0, keepdims=False)
    scalars = jnp.concatenate([jnp.stack([z, x, y, core]), offsets, partners]).astype(jnp.int32)
    chain_skeletons = skeletons[:, 0]
    tops = top_skeletons.reshape(4, 2, 64, 64)

    row = shaped(16, 1024)
    long = shaped(16, 1152)
    thin = shaped(16, 128)
    wire = shaped(16, 32, 128)
    bases, chain, tail, outgoing, both = call(
        prepare_kernel,
        (
            shaped(128, 1024, dtype=BF16),
            shaped(64, 512, dtype=BF16),
            shaped(64, 64),
            shaped(8, 64, 128),
            shaped(80, 1024),
        ),
        [scalars],
        [leaf_order, basis, transfer_maps[:, 0], chain_skeletons, rhs, embeddings],
        "prepare",
        limit=60,
    )

    def gather(spread, after=()):
        high, mine = call(
            gather_kernel, (thin, shaped(64, 128)), [scalars], [spread], "gather", after=after
        )
        return high, mine, other_core(mine)

    one = along_z(both, 1)
    two = along_z(both, 2)
    three_off = along_z(two, 1)
    from_z = over_z(outgoing)
    kernels, near = build(scalars, both, [], None, rhs, [chain], "build_own")
    low, outgoing, second = call(
        middle_kernel,
        (thin, shaped(16, 64, 128), shaped(32, 128)),
        [scalars],
        [from_z, tail, chain_skeletons],
        "middle",
        after=[near],
    )
    from_yx = over_yx(outgoing)
    moved = lax.ppermute(second, "x", [(i, i ^ 1) for i in range(4)])
    kernels, near = build(scalars, both, [two, one], 1, near, [low], "build_a", [kernels])
    spread = gather(from_yx, [near])
    top_table = call(
        top_kernel,
        shaped(128, 576, dtype=BF16),
        [scalars],
        [chain_skeletons, from_yx, tops, tail],
        "tops",
    )
    kernels, near = build(scalars, both, [two, three_off], 3, near, [low], "build_b", [kernels])
    table, v1, outgoing = call(
        first_kernel,
        (shaped(128, 256, dtype=BF16), long, wire),
        [scalars],
        [low, *spread, top_table, from_z, second, moved, chain_skeletons, bases, near, chain],
        "first",
    )

    def operate(extended, outgoing):
        moved = [along_z(extended, o) for o in (1, 2, 3)]
        spread = gather(over_yx(outgoing))
        lower = call(
            lower_kernel,
            shaped(8, 32, 128),
            [],
            [*spread, top_table, extended],
            "lower",
            after=moved,
        )
        near = near_product(scalars, [extended, *moved], kernels, lower)
        return over_z(lower), table, bases, near

    v2, scaled, sums, outgoing = call(
        second_kernel, (row, long, thin, wire), [scalars], [*operate(v1, outgoing), chain], "second"
    )
    image, step, outgoing = call(
        third_kernel,
        (long, thin, wire),
        [scalars],
        [*operate(scaled, outgoing), chain, v1, sums],
        "third",
    )
    along, fresh, outgoing = call(
        fourth_kernel,
        (row, thin, shaped(32, 8, 128)),
        [scalars],
        [*operate(image, outgoing), v2, sums],
        "fourth",
    )
    received = lax.all_to_all(outgoing, ("x", "z"), 0, 0)
    wide = call(spread_kernel, shaped(8, 8, 128), [], [received], "spread")
    shares = lax.all_to_all(wide, ("y", "core"), 0, 0)
    return call(
        last_kernel,
        (row, row),
        [],
        [shares, rhs, v1, v2, image, along, sums, fresh, step],
        "last",
    )


def solution(mesh):
    axes = ("y", "core", "x", "z")
    fine = Mesh(mesh.devices.reshape(4, 2, 4, 8), axes)
    placed = (
        P(None, axes),
        P(None, axes),
        P(axes, None),
        P(None, axes),
        P(None, axes, None, None),
        P(None, axes, None, None),
        P(),
        P(axes, None),
        P(None, axes),
        P(),
    )
    return jax.shard_map(
        local,
        mesh=fine,
        in_specs=placed,
        out_specs=(P(None, axes), P(None, axes)),
        check_vma=False,
    )
```

time: 207 us -> 181 us (0.87)
  waiting for transfers between devices: 35.7 us -> 21.2 us
  Pallas kernels: 57.2 us -> 50.1 us
  starting transfers between devices: 80 us -> 77.1 us
  local copies, waits for them, and re-layouts: 7.17 us -> 4.73 us
    pallas_call x22, Pallas kernels: 57.2 us -> 50.1 us  [call(): pl.pallas_call(kernel, out_shape=outs, in_specs=[SMEM] * len(scalars) + [...]
    ppermute x12 -> x13, waiting for transfers between devices: 11 us -> 3.9 us  [the longest x12 3.9 us: along_z(): return lax.ppermute(v, 'z', [(i, i ^ offset) for i in range(8)])]
    all_to_all x4, waiting for transfers between devices: 13.8 us -> 6.96 us  [over_z(): return lax.all_to_all(v, 'z', 0, 0)]
    all_to_all x1 -> x0, starting transfers between devices: 4.01 us -> none  [local(): from_x = lax.all_to_all(pairs, 'x', 0, 0)]
    unnamed x23 -> x26, local copies, waits for them, and re-layouts: 6.9 us -> 3.95 us
    ppermute x12 -> x13, starting transfers between devices: 17.3 us -> 19.6 us  [the longest x12 18.4 us: along_z(): return lax.ppermute(v, 'z', [(i, i ^ offset) for i in range(8)])]
    all_to_all x4, waiting for transfers between devices: 6.44 us -> 8.67 us  [over_yx(): return lax.all_to_all(v, ('y', 'x'), 0, 0)]
  transfers between devices with their start and end apart: 25 -> 25, of which waited for: 12 -> 10; matrix products, arithmetic and copies ran while one was open for 0% -> 0% of each run, Pallas kernels for 22% -> 19%
where the time goes in v2:
time: 181 us; the launch traced here: 180 us
  starting transfers between devices  77.1 us (43%)
  Pallas kernels  50.1 us (28%)
  blocking collectives  25.2 us (14%)
  waiting for transfers between devices  21.2 us (12%)
  local copies, waits for them, and re-layouts  4.73 us (3%)
    pallas_call x22, Pallas kernels, call(): pl.pallas_call(kernel, out_shape=outs, in_specs=[SMEM] * len(scalars) + [...  50.1 us
    all_to_all x4, starting transfers between devices, over_z(): return lax.all_to_all(v, 'z', 0, 0)  23 us
    ppermute x12, starting transfers between devices, along_z(): return lax.ppermute(v, 'z', [(i, i ^ offset) for i in range(8)])  18.4 us
    all_to_all x4, starting transfers between devices, over_yx(): return lax.all_to_all(v, ('y', 'x'), 0, 0)  18.4 us
    ppermute x4, starting transfers between devices, other_core(): return lax.ppermute(v, 'core', [(0, 1), (1, 0)])  16.1 us
    all_to_all x1, blocking collectives, local(): received = lax.all_to_all(outgoing, ('x', 'z'), 0, 0)  14 us
    all_to_all x1, blocking collectives, local(): shares = lax.all_to_all(wide, ('y', 'core'), 0, 0)  11.2 us
    all_to_all x4, waiting for transfers between devices, over_yx(): return lax.all_to_all(v, ('y', 'x'), 0, 0)  8.67 us
  transfers between devices with their start and end apart: 25, of which 10 were waited for; matrix products, arithmetic and copies ran while one was open for 0% of the time, Pallas kernels for 19%

profile of v2, /device:TPU:1, one launch (start us, length us, event | category | flops | bytes accessed | tf_op | source)
XLA Modules:
  0.0 179.9 jit_solution(3083424186339003273)
XLA Ops:
  2.8 3.5 %prepare.1 = (bf16[128,1024]{1,0:T(8,128)(2,1)}, bf16[64,512]{1,0:T(8,128)(2,1)}, f32[64,64]{1,0:T(8,128)}, f32[8,64,128]{2,1,0:T(8,128)}, f32[80,1024]{1,0:T(8,128)}) custom-call(s32[12]{0:T(128)} %concatenate.3.scalars, s32[1,1024]{1,0:T(1,128)} %order.1, f32[64,1024]{1,0:T(8,128)} %basis.1, f32[5,64,64]{2,1,0:T(8,128)} %bitcast.14, f32[4,64,64]{2,1,0:T(8,128)} %bitcast.9, ...), custom_call_target="tpu_custom_call" | custom-call | flops 100000 | bytes 500000 | tf_op jit(solution)/shard_map/prepare/pallas_call | solution.py:442
  6.3 9.2 %all-to-all-start = ((f32[8,64,128]{2,1,0:T(8,128)}), f32[8,64,128]{2,1,0:T(8,128)S(1)}, u32[]{:S(2)}, u32[]{:S(2)}) async-start(f32[8,64,128]{2,1,0:T(8,128)} %get-tuple-element.37), calls=%async_computation | async-start | bytes 524288 | tf_op jit(solution)/shard_map/all_to_all | solution.py:505
  15.4 2.4 %collective-permute-start = (f32[80,1024]{1,0:T(8,128)}, f32[80,1024]{1,0:T(8,128)S(1)}, u32[]{:S(2)}, u32[]{:S(2)}) collective-permute-start(f32[80,1024]{1,0:T(8,128)} %get-tuple-element.39.own), channel_id=1, source_target_pairs={{0,2},{1,3},{2,0},{3,1},{4,6},{5,7},{6,4},{7,5},{8,10},{9,11},{10,... | collective-permute-start | bytes 983048 | tf_op jit(solution)/shard_map/ppermute | solution.py:497
  17.8 1.2 collective-permute-start.1
  21.2 1.0 copy-done.11
  22.2 4.1 %build_own.1 = (bf16[3,2,1024,1024]{3,2,1,0:T(8,128)(2,1)}, f32[16,1024]{1,0:T(8,128)S(1)}) custom-call(s32[12]{0:T(128)S(1)} %copy-done.9, f32[80,1024]{1,0:T(8,128)S(1)} %copy-done.11, f32[16,1024]{1,0:T(8,128)S(1)} %copy-done.5, bf16[64,512]{1,0:T(8,128)(2,1)S(1)} %copy-done.3), custom_call_target="tpu_custom_call" | custom-call | flops 4000000000 | bytes 500000 | tf_op jit(solution)/shard_map/build_own/pallas_call | solution.py:442
  26.4 1.6 middle.1
  28.0 6.8 %all-to-all-start.1 = ((f32[16,64,128]{2,1,0:T(8,128)}), f32[16,64,128]{2,1,0:T(8,128)S(1)}, u32[]{:S(2)}, u32[]{:S(2)}) async-start(f32[16,64,128]{2,1,0:T(8,128)} %get-tuple-element.43), calls=%async_computation.1 | async-start | bytes 1048576 | tf_op jit(solution)/shard_map/all_to_all | solution.py:509
  34.8 2.7 %collective-permute-done.refs_0_ = f32[80,1024]{1,0:T(8,128)S(1)} collective-permute-done((f32[80,1024]{1,0:T(8,128)}, f32[80,1024]{1,0:T(8,128)S(1)}, u32[]{:S(2)}, u32[]{:S(2)}) %collective-permute-start) | collective-permute-done | bytes 327712 | tf_op jit(solution)/shard_map/ppermute | solution.py:497
  37.5 1.2 collective-permute-start.3
  38.7 4.2 %build_a.1 = (bf16[3,2,1024,1024]{3,2,1,0:T(8,128)(2,1)}, f32[16,1024]{1,0:T(8,128)S(1)}) custom-call(s32[12]{0:T(128)S(1)} %copy-done.10, f32[80,1024]{1,0:T(8,128)S(1)} %copy-done.12, f32[80,1024]{1,0:T(8,128)S(1)} %collective-permute-done.refs_0_, f32[80,1024]{1,0:T(8,128)S(1)} %collective-permute-done.1.refs_1_, ...), custom_call_target="tpu_custom_call", output_to_operand_aliasing={{0}: (6, {})} | custom-call | flops 4000000000 | bytes 500000 | tf_op jit(solution)/shard_map/build_a/pallas_call | solution.py:442
  44.3 4.5 %collective-permute-start.2 = (f32[64,128]{1,0:T(8,128)S(1)}, f32[64,128]{1,0:T(8,128)S(1)}, u32[]{:S(2)}, u32[]{:S(2)}) collective-permute-start(f32[64,128]{1,0:T(8,128)S(1)} %get-tuple-element.47.mine), channel_id=1, source_target_pairs={{0,32},{32,0},{1,33},{33,1},{2,34},{34,2},{3,35},{35,3},{4,36},{36... | collective-permute-start | bytes 98312 | tf_op jit(solution)/shard_map/ppermute | solution.py:501
  48.9 4.1 %build_b.1 = (bf16[3,2,1024,1024]{3,2,1,0:T(8,128)(2,1)}, f32[16,1024]{1,0:T(8,128)S(1)}) custom-call(s32[12]{0:T(128)S(1)} %copy-done.10, f32[80,1024]{1,0:T(8,128)S(1)} %copy-done.12, f32[80,1024]{1,0:T(8,128)S(1)} %collective-permute-done.refs_0_, f32[80,1024]{1,0:T(8,128)S(1)} %collective-permute-done.4.refs_1_, ...), custom_call_target="tpu_custom_call", output_to_operand_aliasing={{0}: (6, {})} | custom-call | flops 4000000000 | bytes 500000 | tf_op jit(solution)/shard_map/build_b/pallas_call | solution.py:442
  53.0 1.3 tops.1.top_table.table
  54.3 2.9 %first.1 = (bf16[128,256]{1,0:T(8,128)(2,1)S(1)}, f32[16,1152]{1,0:T(8,128)S(1)}, f32[16,32,128]{2,1,0:T(8,128)}) custom-call(s32[12]{0:T(128)S(1)} %copy-done.10, f32[16,128]{1,0:T(8,128)S(1)} %get-tuple-element.42.refs_3_.low, f32[16,128]{1,0:T(8,128)S(1)} %get-tuple-element.46.high, f32[64,128]{1,0:T(8,128)S(1)} %get-tuple-element.47.mine, ...), custom_call_target="tpu_custom_call" | custom-call | flops 100000 | bytes 500000 | tf_op jit(solution)/shard_map/first/pallas_call | solution.py:442
  57.2 3.7 %all-to-all-start.2 = ((f32[16,32,128]{2,1,0:T(8,128)}), f32[16,32,128]{2,1,0:T(8,128)S(1)}, u32[]{:S(2)}, u32[]{:S(2)}) async-start(f32[16,32,128]{2,1,0:T(8,128)} %get-tuple-element.52), calls=%async_computation.2 | async-start | bytes 524288 | tf_op jit(solution)/shard_map/all_to_all | solution.py:509
  60.9 1.6 collective-permute-start.6
  62.5 5.8 %collective-permute-start.7 = (f32[16,1152]{1,0:T(8,128)S(1)}, f32[16,1152]{1,0:T(8,128)S(1)}, u32[]{:S(2)}, u32[]{:S(2)}) collective-permute-start(f32[16,1152]{1,0:T(8,128)S(1)} %get-tuple-element.55.own.v.v1), channel_id=1, source_target_pairs={{0,2},{1,3},{2,0},{3,1},{4,6},{5,7},{6,4},{7,5},{8,10},{9,11},{10,... | collective-permute-start | bytes 221192 | tf_op jit(solution)/shard_map/ppermute | solution.py:497
  69.1 3.2 %collective-permute-start.5 = (f32[64,128]{1,0:T(8,128)S(1)}, f32[64,128]{1,0:T(8,128)S(1)}, u32[]{:S(2)}, u32[]{:S(2)}) collective-permute-start(f32[64,128]{1,0:T(8,128)S(1)} %get-tuple-element.54.mine), channel_id=1, source_target_pairs={{0,32},{32,0},{1,33},{33,1},{2,34},{34,2},{3,35},{35,3},{4,36},{36... | collective-permute-start | bytes 98312 | tf_op jit(solution)/shard_map/ppermute | solution.py:501
  72.4 1.2 collective-permute-done.8.refs_2_.v3
  73.5 1.0 lower.3.after
  74.5 6.8 %all-to-all-start.3 = ((f32[8,32,128]{2,1,0:T(8,128)}), f32[8,32,128]{2,1,0:T(8,128)S(1)}, u32[]{:S(2)}, u32[]{:S(2)}) async-start(f32[8,32,128]{2,1,0:T(8,128)} %lower.3.after), calls=%async_computation.3 | async-start | bytes 262144 | tf_op jit(solution)/shard_map/all_to_all | solution.py:505
  81.3 5.5 %near.3 = f32[16,1152]{1,0:T(8,128)S(1)} custom-call(s32[12]{0:T(128)S(1)} %copy-done.10, f32[16,1152]{1,0:T(8,128)S(1)} %get-tuple-element.55.own.v.v1, f32[16,1152]{1,0:T(8,128)S(1)} %collective-permute-done.6.refs_0_.v1, f32[16,1152]{1,0:T(8,128)S(1)} %collective-permute-done.7.refs_1_.v2, f32[16,1152]{1,0:T(8,128)S(1)} %collective-permute-done.8.refs_2_.v3, ...), custom_call_target="tpu_custom_call" | custom-call | flops 4000000000 | bytes 500000 | tf_op jit(solution)/shard_map/near/pallas_call | solution.py:442
  86.8 2.4 %all-to-all-done.3.received = f32[8,32,128]{2,1,0:T(8,128)S(1)} async-done(((f32[8,32,128]{2,1,0:T(8,128)}), f32[8,32,128]{2,1,0:T(8,128)S(1)}, u32[]{:S(2)}, u32[]{:S(2)}) %all-to-all-start.3) | async-done | bytes 131104 | tf_op jit(solution)/shard_map/all_to_all | solution.py:505
  89.2 2.3 %second.1 = (f32[16,1024]{1,0:T(8,128)S(1)}, f32[16,1152]{1,0:T(8,128)S(1)}, f32[16,128]{1,0:T(8,128)S(1)}, f32[16,32,128]{2,1,0:T(8,128)}) custom-call(s32[12]{0:T(128)S(1)} %copy-done.10, f32[8,32,128]{2,1,0:T(8,128)S(1)} %all-to-all-done.3.received, bf16[128,256]{1,0:T(8,128)(2,1)S(1)} %get-tuple-element.56.table, bf16[128,1024]{1,0:T(8,128)(2,1)S(1)} %copy-done.1, ...), custom_call_target="tpu_custom_call" | custom-call | flops 100000 | bytes 500000 | tf_op jit(solution)/shard_map/second/pallas_call | solution.py:442
  91.5 4.3 %all-to-all-start.4 = ((f32[16,32,128]{2,1,0:T(8,128)}), f32[16,32,128]{2,1,0:T(8,128)S(1)}, u32[]{:S(2)}, u32[]{:S(2)}) async-start(f32[16,32,128]{2,1,0:T(8,128)} %get-tuple-element.58), calls=%async_computation.4 | async-start | bytes 524288 | tf_op jit(solution)/shard_map/all_to_all | solution.py:509
  96.2 0.9 collective-permute-start.11
  97.1 2.4 %collective-permute-start.12 = (f32[16,1152]{1,0:T(8,128)S(1)}, f32[16,1152]{1,0:T(8,128)S(1)}, u32[]{:S(2)}, u32[]{:S(2)}) collective-permute-start(f32[16,1152]{1,0:T(8,128)S(1)} %get-tuple-element.61.own.v), channel_id=1, source_target_pairs={{0,3},{1,2},{2,1},{3,0},{4,7},{5,6},{6,5},{7,4},{8,11},{9,10},{10,... | collective-permute-start | bytes 221192 | tf_op jit(solution)/shard_map/ppermute | solution.py:497
  99.5 3.9 %all-to-all-done.4.received = f32[16,32,128]{2,1,0:T(8,128)S(1)} async-done(((f32[16,32,128]{2,1,0:T(8,128)}), f32[16,32,128]{2,1,0:T(8,128)S(1)}, u32[]{:S(2)}, u32[]{:S(2)}) %all-to-all-start.4) | async-done | bytes 262176 | tf_op jit(solution)/shard_map/all_to_all | solution.py:509
  104.0 4.1 %collective-permute-start.9 = (f32[64,128]{1,0:T(8,128)S(1)}, f32[64,128]{1,0:T(8,128)S(1)}, u32[]{:S(2)}, u32[]{:S(2)}) collective-permute-start(f32[64,128]{1,0:T(8,128)S(1)} %get-tuple-element.60.mine), channel_id=1, source_target_pairs={{0,32},{32,0},{1,33},{33,1},{2,34},{34,2},{3,35},{35,3},{4,36},{36... | collective-permute-start | bytes 98312 | tf_op jit(solution)/shard_map/ppermute | solution.py:501
  108.1 0.8 collective-permute-done.9.other
  109.0 1.0 lower.4.after
  110.0 3.6 %all-to-all-start.5 = ((f32[8,32,128]{2,1,0:T(8,128)}), f32[8,32,128]{2,1,0:T(8,128)S(1)}, u32[]{:S(2)}, u32[]{:S(2)}) async-start(f32[8,32,128]{2,1,0:T(8,128)} %lower.4.after), calls=%async_computation.5 | async-start | bytes 262144 | tf_op jit(solution)/shard_map/all_to_all | solution.py:505
  113.6 5.5 %near.4 = f32[16,1152]{1,0:T(8,128)S(1)} custom-call(s32[12]{0:T(128)S(1)} %copy-done.10, f32[16,1152]{1,0:T(8,128)S(1)} %get-tuple-element.61.own.v, f32[16,1152]{1,0:T(8,128)S(1)} %collective-permute-done.10.refs_0_.v1, f32[16,1152]{1,0:T(8,128)S(1)} %collective-permute-done.11.refs_1_.v2, f32[16,1152]{1,0:T(8,128)S(1)} %collective-permute-done.12.refs_2_.v3, ...), custom_call_target="tpu_custom_call" | custom-call | flops 4000000000 | bytes 500000 | tf_op jit(solution)/shard_map/near/pallas_call | solution.py:442
  119.1 2.2 %all-to-all-done.5.received = f32[8,32,128]{2,1,0:T(8,128)S(1)} async-done(((f32[8,32,128]{2,1,0:T(8,128)}), f32[8,32,128]{2,1,0:T(8,128)S(1)}, u32[]{:S(2)}, u32[]{:S(2)}) %all-to-all-start.5) | async-done | bytes 131104 | tf_op jit(solution)/shard_map/all_to_all | solution.py:505
  121.3 2.3 %third.1 = (f32[16,1152]{1,0:T(8,128)S(1)}, f32[16,128]{1,0:T(8,128)S(1)}, f32[16,32,128]{2,1,0:T(8,128)}) custom-call(s32[12]{0:T(128)S(1)} %copy-done.10, f32[8,32,128]{2,1,0:T(8,128)S(1)} %all-to-all-done.5.received, bf16[128,256]{1,0:T(8,128)(2,1)S(1)} %get-tuple-element.56.table, bf16[128,1024]{1,0:T(8,128)(2,1)S(1)} %copy-done.1, f32[16,1152]{1,0:T(8,128)S(1)} %near.4, ...), custom_call_target="tpu_custom_call" | custom-call | flops 100000 | bytes 500000 | tf_op jit(solution)/shard_map/third/pallas_call | solution.py:442
  123.6 3.5 %all-to-all-start.6 = ((f32[16,32,128]{2,1,0:T(8,128)}), f32[16,32,128]{2,1,0:T(8,128)S(1)}, u32[]{:S(2)}, u32[]{:S(2)}) async-start(f32[16,32,128]{2,1,0:T(8,128)} %get-tuple-element.63), calls=%async_computation.6 | async-start | bytes 524288 | tf_op jit(solution)/shard_map/all_to_all | solution.py:509
  127.4 1.0 collective-permute-start.15
  128.4 2.3 %collective-permute-start.16 = (f32[16,1152]{1,0:T(8,128)S(1)}, f32[16,1152]{1,0:T(8,128)S(1)}, u32[]{:S(2)}, u32[]{:S(2)}) collective-permute-start(f32[16,1152]{1,0:T(8,128)S(1)} %get-tuple-element.66.own.v.image), channel_id=1, source_target_pairs={{0,3},{1,2},{2,1},{3,0},{4,7},{5,6},{6,5},{7,4},{8,11},{9,10},{10,... | collective-permute-start | bytes 221192 | tf_op jit(solution)/shard_map/ppermute | solution.py:497
  130.8 3.9 %all-to-all-done.6.received = f32[16,32,128]{2,1,0:T(8,128)S(1)} async-done(((f32[16,32,128]{2,1,0:T(8,128)}), f32[16,32,128]{2,1,0:T(8,128)S(1)}, u32[]{:S(2)}, u32[]{:S(2)}) %all-to-all-start.6) | async-done | bytes 262176 | tf_op jit(solution)/shard_map/all_to_all | solution.py:509
  135.3 4.2 %collective-permute-start.13 = (f32[64,128]{1,0:T(8,128)S(1)}, f32[64,128]{1,0:T(8,128)S(1)}, u32[]{:S(2)}, u32[]{:S(2)}) collective-permute-start(f32[64,128]{1,0:T(8,128)S(1)} %get-tuple-element.65.mine), channel_id=1, source_target_pairs={{0,32},{32,0},{1,33},{33,1},{2,34},{34,2},{3,35},{35,3},{4,36},{36... | collective-permute-start | bytes 98312 | tf_op jit(solution)/shard_map/ppermute | solution.py:501
  140.4 1.0 lower.5.after
  141.3 3.4 %all-to-all-start.7 = ((f32[8,32,128]{2,1,0:T(8,128)}), f32[8,32,128]{2,1,0:T(8,128)S(1)}, u32[]{:S(2)}, u32[]{:S(2)}) async-start(f32[8,32,128]{2,1,0:T(8,128)} %lower.5.after), calls=%async_computation.7 | async-start | bytes 262144 | tf_op jit(solution)/shard_map/all_to_all | solution.py:505
  144.7 5.5 %near.5 = f32[16,1152]{1,0:T(8,128)S(1)} custom-call(s32[12]{0:T(128)S(1)} %copy-done.10, f32[16,1152]{1,0:T(8,128)S(1)} %get-tuple-element.66.own.v.image, f32[16,1152]{1,0:T(8,128)S(1)} %collective-permute-done.14.refs_0_.v1, f32[16,1152]{1,0:T(8,128)S(1)} %collective-permute-done.15.refs_1_.v2, f32[16,1152]{1,0:T(8,128)S(1)} %collective-permute-done.16.refs_2_.v3, ...), custom_call_target="tpu_custom_call" | custom-call | flops 4000000000 | bytes 500000 | tf_op jit(solution)/shard_map/near/pallas_call | solution.py:442
  150.3 2.4 %all-to-all-done.7.received = f32[8,32,128]{2,1,0:T(8,128)S(1)} async-done(((f32[8,32,128]{2,1,0:T(8,128)}), f32[8,32,128]{2,1,0:T(8,128)S(1)}, u32[]{:S(2)}, u32[]{:S(2)}) %all-to-all-start.7) | async-done | bytes 131104 | tf_op jit(solution)/shard_map/all_to_all | solution.py:505
  152.7 1.2 fourth.1
  153.8 14.0 %all_to_all.50.received = f32[32,8,128]{2,1,0:T(8,128)S(1)} all-to-all(f32[32,8,128]{2,1,0:T(8,128)S(1)} %get-tuple-element.68), channel_id=1, replica_groups=mesh['y'=4,'core'=2,'x'=4,'z'=8] {'x','z'}, dimensions={0} | all-to-all | bytes 262144 | tf_op jit(solution)/shard_map/all_to_all | solution.py:624
  167.9 11.2 %all_to_all.51.shares = f32[8,8,128]{2,1,0:T(8,128)S(1)} all-to-all(f32[8,8,128]{2,1,0:T(8,128)S(1)} %spread.1), channel_id=1, replica_groups=mesh['y'=4,'core'=2,'x'=4,'z'=8] {'y','core'}, dimensions={0} | all-to-all | bytes 65536 | tf_op jit(solution)/shard_map/all_to_all | solution.py:626
  (55 shorter events, 10.2 us)
Async XLA Ops:
  0.6 0.7 copy-start
  0.6 25.7 %copy-start.2 = (f32[4,1,64,64]{3,2,1,0:T(8,128)S(1)}, f32[4,1,64,64]{3,2,1,0:T(8,128)}, u32[]{:S(2)}) copy-start(f32[4,1,64,64]{3,2,1,0:T(8,128)} %param.15) | copy-start | bytes 196612
  2.8 23.6 %copy-start.10 = (s32[12]{0:T(128)S(1)}, s32[12]{0:T(128)}, u32[]{:S(2)}) copy-start(s32[12]{0:T(128)} %concatenate.3.scalars) | copy-start | bytes 148
  6.2 20.1 %copy-start.8 = (f32[64,64]{1,0:T(8,128)S(1)}, f32[64,64]{1,0:T(8,128)}, u32[]{:S(2)}) copy-start(f32[64,64]{1,0:T(8,128)} %get-tuple-element.38.tail) | copy-start | bytes 49156
  6.2 32.4 %copy-start.12 = (f32[80,1024]{1,0:T(8,128)S(1)}, f32[80,1024]{1,0:T(8,128)}, u32[]{:S(2)}) copy-start(f32[80,1024]{1,0:T(8,128)} %get-tuple-element.39.own) | copy-start | bytes 983044
  6.3 20.1 %all-to-all-start = ((f32[8,64,128]{2,1,0:T(8,128)}), f32[8,64,128]{2,1,0:T(8,128)S(1)}, u32[]{:S(2)}, u32[]{:S(2)}) async-start(f32[8,64,128]{2,1,0:T(8,128)} %get-tuple-element.37), calls=%async_computation | async-start | bytes 524288 | tf_op jit(solution)/shard_map/all_to_all | solution.py:505
  15.4 22.1 %collective-permute-start = (f32[80,1024]{1,0:T(8,128)}, f32[80,1024]{1,0:T(8,128)S(1)}, u32[]{:S(2)}, u32[]{:S(2)}) collective-permute-start(f32[80,1024]{1,0:T(8,128)} %get-tuple-element.39.own), channel_id=1, source_target_pairs={{0,2},{1,3},{2,0},{3,1},{4,6},{5,7},{6,4},{7,5},{8,10},{9,11},{10,... | collective-permute-start | bytes 983048 | tf_op jit(solution)/shard_map/ppermute | solution.py:497
  17.8 20.9 %collective-permute-start.1 = (f32[80,1024]{1,0:T(8,128)}, f32[80,1024]{1,0:T(8,128)S(1)}, u32[]{:S(2)}, u32[]{:S(2)}) collective-permute-start(f32[80,1024]{1,0:T(8,128)} %get-tuple-element.39.own), channel_id=1, source_target_pairs={{0,1},{1,0},{2,3},{3,2},{4,5},{5,4},{6,7},{7,6},{8,9},{9,8},{10,11... | collective-permute-start | bytes 983048 | tf_op jit(solution)/shard_map/ppermute | solution.py:497
  19.0 0.8 copy-start.3
  19.8 0.8 copy-start.5
  20.6 0.6 copy-start.9
  21.2 1.0 copy-start.11
  28.0 15.8 %all-to-all-start.1 = ((f32[16,64,128]{2,1,0:T(8,128)}), f32[16,64,128]{2,1,0:T(8,128)S(1)}, u32[]{:S(2)}, u32[]{:S(2)}) async-start(f32[16,64,128]{2,1,0:T(8,128)} %get-tuple-element.43), calls=%async_computation.1 | async-start | bytes 1048576 | tf_op jit(solution)/shard_map/all_to_all | solution.py:509
  37.5 11.4 %collective-permute-start.4 = (f32[80,1024]{1,0:T(8,128)S(1)}, f32[80,1024]{1,0:T(8,128)S(1)}, u32[]{:S(2)}, u32[]{:S(2)}) collective-permute-start(f32[80,1024]{1,0:T(8,128)S(1)} %collective-permute-done.refs_0_), channel_id=1, source_target_pairs={{0,1},{1,0},{2,3},{3,2},{4,5},{5,4},{6,7},{7,6},{8,9},{9,8},{10,11... | collective-permute-start | bytes 983048 | tf_op jit(solution)/shard_map/ppermute | solution.py:497
  37.5 16.8 %collective-permute-start.3 = (f32[32,128]{1,0:T(8,128)S(1)}, f32[32,128]{1,0:T(8,128)S(1)}, u32[]{:S(2)}, u32[]{:S(2)}) collective-permute-start(f32[32,128]{1,0:T(8,128)S(1)} %get-tuple-element.48.second), channel_id=1, source_target_pairs={{0,8},{8,0},{16,24},{24,16},{1,9},{9,1},{17,25},{25,17},{2,10},{10... | collective-permute-start | bytes 49160 | tf_op jit(solution)/shard_map/ppermute | solution.py:574
  38.7 14.3 %copy-start.7 = (f32[8,64,64]{2,1,0:T(8,128)S(1)}, f32[8,64,64]{2,1,0:T(8,128)}, u32[]{:S(2)}) copy-start(f32[8,64,64]{2,1,0:T(8,128)} %param.16) | copy-start | bytes 393220
  38.7 15.6 %copy-start.1 = (bf16[128,1024]{1,0:T(8,128)(2,1)S(1)}, bf16[128,1024]{1,0:T(8,128)(2,1)}, u32[]{:S(2)}) copy-start(bf16[128,1024]{1,0:T(8,128)(2,1)} %get-tuple-element.49.bases) | copy-start | bytes 786436
  38.7 15.6 %copy-start.4 = (bf16[64,512]{1,0:T(8,128)(2,1)S(1)}, bf16[64,512]{1,0:T(8,128)(2,1)}, u32[]{:S(2)}) copy-start(bf16[64,512]{1,0:T(8,128)(2,1)} %get-tuple-element.40.refs_1_.chain) | copy-start | bytes 196612
  44.3 10.0 %collective-permute-start.2 = (f32[64,128]{1,0:T(8,128)S(1)}, f32[64,128]{1,0:T(8,128)S(1)}, u32[]{:S(2)}, u32[]{:S(2)}) collective-permute-start(f32[64,128]{1,0:T(8,128)S(1)} %get-tuple-element.47.mine), channel_id=1, source_target_pairs={{0,32},{32,0},{1,33},{33,1},{2,34},{34,2},{3,35},{35,3},{4,36},{36... | collective-permute-start | bytes 98312 | tf_op jit(solution)/shard_map/ppermute | solution.py:501
  57.2 11.3 %all-to-all-start.2 = ((f32[16,32,128]{2,1,0:T(8,128)}), f32[16,32,128]{2,1,0:T(8,128)S(1)}, u32[]{:S(2)}, u32[]{:S(2)}) async-start(f32[16,32,128]{2,1,0:T(8,128)} %get-tuple-element.52), calls=%async_computation.2 | async-start | bytes 524288 | tf_op jit(solution)/shard_map/all_to_all | solution.py:509
  60.9 11.4 %collective-permute-start.6 = (f32[16,1152]{1,0:T(8,128)S(1)}, f32[16,1152]{1,0:T(8,128)S(1)}, u32[]{:S(2)}, u32[]{:S(2)}) collective-permute-start(f32[16,1152]{1,0:T(8,128)S(1)} %get-tuple-element.55.own.v.v1), channel_id=1, source_target_pairs={{0,1},{1,0},{2,3},{3,2},{4,5},{5,4},{6,7},{7,6},{8,9},{9,8},{10,11... | collective-permute-start | bytes 221192 | tf_op jit(solution)/shard_map/ppermute | solution.py:497
  62.5 9.8 %collective-permute-start.7 = (f32[16,1152]{1,0:T(8,128)S(1)}, f32[16,1152]{1,0:T(8,128)S(1)}, u32[]{:S(2)}, u32[]{:S(2)}) collective-permute-start(f32[16,1152]{1,0:T(8,128)S(1)} %get-tuple-element.55.own.v.v1), channel_id=1, source_target_pairs={{0,2},{1,3},{2,0},{3,1},{4,6},{5,7},{6,4},{7,5},{8,10},{9,11},{10,... | collective-permute-start | bytes 221192 | tf_op jit(solution)/shard_map/ppermute | solution.py:497
  68.3 5.2 %collective-permute-start.8 = (f32[16,1152]{1,0:T(8,128)S(1)}, f32[16,1152]{1,0:T(8,128)S(1)}, u32[]{:S(2)}, u32[]{:S(2)}) collective-permute-start(f32[16,1152]{1,0:T(8,128)S(1)} %get-tuple-element.55.own.v.v1), channel_id=1, source_target_pairs={{0,3},{1,2},{2,1},{3,0},{4,7},{5,6},{6,5},{7,4},{8,11},{9,10},{10,... | collective-permute-start | bytes 221192 | tf_op jit(solution)/shard_map/ppermute | solution.py:497
  69.1 4.4 %collective-permute-start.5 = (f32[64,128]{1,0:T(8,128)S(1)}, f32[64,128]{1,0:T(8,128)S(1)}, u32[]{:S(2)}, u32[]{:S(2)}) collective-permute-start(f32[64,128]{1,0:T(8,128)S(1)} %get-tuple-element.54.mine), channel_id=1, source_target_pairs={{0,32},{32,0},{1,33},{33,1},{2,34},{34,2},{3,35},{35,3},{4,36},{36... | collective-permute-start | bytes 98312 | tf_op jit(solution)/shard_map/ppermute | solution.py:501
  74.5 14.7 %all-to-all-start.3 = ((f32[8,32,128]{2,1,0:T(8,128)}), f32[8,32,128]{2,1,0:T(8,128)S(1)}, u32[]{:S(2)}, u32[]{:S(2)}) async-start(f32[8,32,128]{2,1,0:T(8,128)} %lower.3.after), calls=%async_computation.3 | async-start | bytes 262144 | tf_op jit(solution)/shard_map/all_to_all | solution.py:505
  91.5 11.9 %all-to-all-start.4 = ((f32[16,32,128]{2,1,0:T(8,128)}), f32[16,32,128]{2,1,0:T(8,128)S(1)}, u32[]{:S(2)}, u32[]{:S(2)}) async-start(f32[16,32,128]{2,1,0:T(8,128)} %get-tuple-element.58), calls=%async_computation.4 | async-start | bytes 524288 | tf_op jit(solution)/shard_map/all_to_all | solution.py:509
  95.9 12.3 %collective-permute-start.10 = (f32[16,1152]{1,0:T(8,128)S(1)}, f32[16,1152]{1,0:T(8,128)S(1)}, u32[]{:S(2)}, u32[]{:S(2)}) collective-permute-start(f32[16,1152]{1,0:T(8,128)S(1)} %get-tuple-element.61.own.v), channel_id=1, source_target_pairs={{0,1},{1,0},{2,3},{3,2},{4,5},{5,4},{6,7},{7,6},{8,9},{9,8},{10,11... | collective-permute-start | bytes 221192 | tf_op jit(solution)/shard_map/ppermute | solution.py:497
  96.2 11.9 %collective-permute-start.11 = (f32[16,1152]{1,0:T(8,128)S(1)}, f32[16,1152]{1,0:T(8,128)S(1)}, u32[]{:S(2)}, u32[]{:S(2)}) collective-permute-start(f32[16,1152]{1,0:T(8,128)S(1)} %get-tuple-element.61.own.v), channel_id=1, source_target_pairs={{0,2},{1,3},{2,0},{3,1},{4,6},{5,7},{6,4},{7,5},{8,10},{9,11},{10,... | collective-permute-start | bytes 221192 | tf_op jit(solution)/shard_map/ppermute | solution.py:497
  97.1 11.1 %collective-permute-start.12 = (f32[16,1152]{1,0:T(8,128)S(1)}, f32[16,1152]{1,0:T(8,128)S(1)}, u32[]{:S(2)}, u32[]{:S(2)}) collective-permute-start(f32[16,1152]{1,0:T(8,128)S(1)} %get-tuple-element.61.own.v), channel_id=1, source_target_pairs={{0,3},{1,2},{2,1},{3,0},{4,7},{5,6},{6,5},{7,4},{8,11},{9,10},{10,... | collective-permute-start | bytes 221192 | tf_op jit(solution)/shard_map/ppermute | solution.py:497
  104.0 5.0 %collective-permute-start.9 = (f32[64,128]{1,0:T(8,128)S(1)}, f32[64,128]{1,0:T(8,128)S(1)}, u32[]{:S(2)}, u32[]{:S(2)}) collective-permute-start(f32[64,128]{1,0:T(8,128)S(1)} %get-tuple-element.60.mine), channel_id=1, source_target_pairs={{0,32},{32,0},{1,33},{33,1},{2,34},{34,2},{3,35},{35,3},{4,36},{36... | collective-permute-start | bytes 98312 | tf_op jit(solution)/shard_map/ppermute | solution.py:501
  110.0 11.3 %all-to-all-start.5 = ((f32[8,32,128]{2,1,0:T(8,128)}), f32[8,32,128]{2,1,0:T(8,128)S(1)}, u32[]{:S(2)}, u32[]{:S(2)}) async-start(f32[8,32,128]{2,1,0:T(8,128)} %lower.4.after), calls=%async_computation.5 | async-start | bytes 262144 | tf_op jit(solution)/shard_map/all_to_all | solution.py:505
  119.1 60.0 %copy-start.6 = (f32[16,1024]{1,0:T(8,128)S(1)}, f32[16,1024]{1,0:T(8,128)}, u32[]{:S(2)}) copy-start(f32[16,1024]{1,0:T(8,128)} %rhs.4) | copy-start | bytes 196612
  123.6 11.1 %all-to-all-start.6 = ((f32[16,32,128]{2,1,0:T(8,128)}), f32[16,32,128]{2,1,0:T(8,128)S(1)}, u32[]{:S(2)}, u32[]{:S(2)}) async-start(f32[16,32,128]{2,1,0:T(8,128)} %get-tuple-element.63), calls=%async_computation.6 | async-start | bytes 524288 | tf_op jit(solution)/shard_map/all_to_all | solution.py:509
  127.1 12.4 %collective-permute-start.14 = (f32[16,1152]{1,0:T(8,128)S(1)}, f32[16,1152]{1,0:T(8,128)S(1)}, u32[]{:S(2)}, u32[]{:S(2)}) collective-permute-start(f32[16,1152]{1,0:T(8,128)S(1)} %get-tuple-element.66.own.v.image), channel_id=1, source_target_pairs={{0,1},{1,0},{2,3},{3,2},{4,5},{5,4},{6,7},{7,6},{8,9},{9,8},{10,11... | collective-permute-start | bytes 221192 | tf_op jit(solution)/shard_map/ppermute | solution.py:497
  127.4 12.1 %collective-permute-start.15 = (f32[16,1152]{1,0:T(8,128)S(1)}, f32[16,1152]{1,0:T(8,128)S(1)}, u32[]{:S(2)}, u32[]{:S(2)}) collective-permute-start(f32[16,1152]{1,0:T(8,128)S(1)} %get-tuple-element.66.own.v.image), channel_id=1, source_target_pairs={{0,2},{1,3},{2,0},{3,1},{4,6},{5,7},{6,4},{7,5},{8,10},{9,11},{10,... | collective-permute-start | bytes 221192 | tf_op jit(solution)/shard_map/ppermute | solution.py:497
  128.4 11.1 %collective-permute-start.16 = (f32[16,1152]{1,0:T(8,128)S(1)}, f32[16,1152]{1,0:T(8,128)S(1)}, u32[]{:S(2)}, u32[]{:S(2)}) collective-permute-start(f32[16,1152]{1,0:T(8,128)S(1)} %get-tuple-element.66.own.v.image), channel_id=1, source_target_pairs={{0,3},{1,2},{2,1},{3,0},{4,7},{5,6},{6,5},{7,4},{8,11},{9,10},{10,... | collective-permute-start | bytes 221192 | tf_op jit(solution)/shard_map/ppermute | solution.py:497
  135.3 5.1 %collective-permute-start.13 = (f32[64,128]{1,0:T(8,128)S(1)}, f32[64,128]{1,0:T(8,128)S(1)}, u32[]{:S(2)}, u32[]{:S(2)}) collective-permute-start(f32[64,128]{1,0:T(8,128)S(1)} %get-tuple-element.65.mine), channel_id=1, source_target_pairs={{0,32},{32,0},{1,33},{33,1},{2,34},{34,2},{3,35},{35,3},{4,36},{36... | collective-permute-start | bytes 98312 | tf_op jit(solution)/shard_map/ppermute | solution.py:501
  141.3 11.3 %all-to-all-start.7 = ((f32[8,32,128]{2,1,0:T(8,128)}), f32[8,32,128]{2,1,0:T(8,128)S(1)}, u32[]{:S(2)}, u32[]{:S(2)}) async-start(f32[8,32,128]{2,1,0:T(8,128)} %lower.5.after), calls=%async_computation.7 | async-start | bytes 262144 | tf_op jit(solution)/shard_map/all_to_all | solution.py:505

commit v3 on v2

--- a/solution.py
+++ b/solution.py
@@ -18,7 +18,7 @@
 DEPTH = 208
 TILE = 256
 
-Z, X, Y, CORE, O0, O1, O2, O3, TOPS = range(9)
+Z, X, Y, CORE, O0, O1, O2, O3 = range(8)
 
 
 def dot(a, b, ca=1, cb=0, precision=None):
@@ -39,6 +39,12 @@
 def halves(a):
     n = a.shape[0] // 2
     return a[:n] + a[n:]
+
+
+def places(partners):
+    y, core, x, z = (lax.axis_index(a) for a in ("y", "core", "x", "z"))
+    leaf = ((y * 2 + core) * 4 + x) * 8 + z
+    return [z, x, y, core] + [jnp.bitwise_xor(partners[h], leaf // 2**h) for h in range(4)]
 
 
 def paired(a, axis):
@@ -91,11 +97,7 @@
     return o0, second, jnp.where(o1 == 3, 4, 7)
 
 
-def prepare_kernel(
-    scalars, order, basis, maps, skeletons, rhs, points, bases, chain, tail, wire, all_rows
-):
-    all_rows[0:64, :] = points[...]
-    all_rows[64:80, :] = rhs[...]
+def prepare_kernel(scalars, order, basis, maps, skeletons, rhs, bases, chain, tail, wire):
     both = stacked(basis[...])
     leaf = basis.shape[1]
     for t in range(leaf // TILE):
@@ -154,7 +156,7 @@
     return (1.0 + s + s * s * (1.0 / 3.0)) * jnp.exp(-s)
 
 
-def top_kernel(scalars, skeletons, from_yx, tops, tail, out):
+def top_kernel(scalars, listed, skeletons, from_yx, tops, tail, out):
     x, y, core = scalars[X], scalars[Y], scalars[CORE]
     partner = unpacked(from_yx[y * 4 + jnp.bitwise_xor(x, scalars[O3]), 32:64, :])
     others = []
@@ -163,15 +165,16 @@
         for j in range(4):
             side = jnp.bitwise_xor(core, flip)
             others.append(tops[j, side])
-            hits = sum((scalars[TOPS + k] == j * 2 + side).astype(F32) for k in range(4))
+            hits = sum((listed[k] == j * 2 + side).astype(F32) for k in range(4))
             masks.append(jnp.full((64, 64), hits, F32))
     top = matern(tops[y, core], jnp.concatenate(others, axis=1))
     top = dot(tail[...], top * jnp.concatenate(masks, axis=1), precision=HIGHEST)
     out[...] = paired(jnp.concatenate([matern(skeletons[3], partner), top], axis=1), 0)
 
 
-def low_couplings(scalars, skeletons, from_z, second, chain):
+def low_kernel(scalars, skeletons, from_z, second, moved, chain, out):
     z = scalars[Z]
+    second = jnp.where(scalars[O2] > 1, moved[...], second[...])
     k0, k1, _ = skeleton_offsets(scalars)
     down = chain[:, 0:256].astype(F32) + chain[:, 256:512].astype(F32)
     partners = [from_z[jnp.bitwise_xor(z, k), 32:64, :] for k in (k0, k1)] + [second]
@@ -181,7 +184,7 @@
         if h > 0:
             coupling = dot(down[:, (h - 1) * 64 : h * 64], coupling, precision=HIGHEST)
         pieces.append(coupling)
-    return paired(jnp.concatenate(pieces + [down[:, 128:192]], axis=1), 0)
+    out[...] = paired(jnp.concatenate(pieces + [down[:, 128:192]], axis=1), 0)
 
 
 def three(a):
@@ -223,12 +226,13 @@
 
 def build_kernel(scalars, own, *refs, choice):
     if choice is None:
-        begin, after, whole, near, aug, left, squares, kernel, sems = refs
+        whole, near, aug, left, squares, kernel, sems = refs[-7:]
         both = own[...]
-        near[...] = NOISE * begin[...]
+        near[...] = NOISE * own[64:80, :]
         slot = 0
     else:
-        yes, no, begin, after, previous, whole, near, aug, left, squares, kernel, sems = refs
+        yes, no, begin = refs[:3]
+        whole, near, aug, left, squares, kernel, sems = refs[-7:]
         both = jnp.where(scalars[O0] == choice, yes[...], no[...])
         near[...] = begin[...]
         slot = (choice + 1) // 2
@@ -348,26 +352,7 @@
     return add_far(jnp.concatenate(parts, axis=1), table, bases, near), sums[0][:, 64:65]
 
 
-def first_kernel(
-    scalars,
-    low,
-    high,
-    mine,
-    other,
-    top_table,
-    from_z,
-    second,
-    moved,
-    skeletons,
-    bases,
-    near,
-    chain,
-    table,
-    v1,
-    out,
-):
-    across = jnp.where(scalars[O2] > 1, moved[...], second[...])
-    table[...] = low_couplings(scalars, skeletons, from_z, across, chain)
+def first_kernel(low, high, mine, other, top_table, table, bases, near, chain, v1, out):
     field = field_at_three(high, mine, other, top_table)
     parts = [low[...], high[:, 0:64], field]
     image = add_far(jnp.concatenate(parts, axis=1), table, bases, near)
@@ -439,8 +424,11 @@
 
 
 def call(kernel, outs, scalars, arrays, name, after=(), limit=16, flops=100000, scratch=(), alias=None):
+    body = kernel
+    if scalars:
+        body = lambda far, *refs: kernel(places(far), *refs)
     return pl.pallas_call(
-        kernel,
+        body,
         out_shape=outs,
         in_specs=[SMEM] * len(scalars) + [VMEM] * len(arrays) + [ANY] * len(after),
         out_specs=jax.tree.map(lambda a: VMEM if len(a.shape) < 4 else ANY, outs),
@@ -459,7 +447,7 @@
         functools.partial(build_kernel, choice=choice),
         (shaped(3, 2, leaf, leaf, dtype=BF16), shaped(16, leaf)),
         [scalars],
-        [own, *others, near],
+        [own, *others, *([] if near is None else [near])],
         name,
         after=[*after, *kernels],
         limit=50,
@@ -521,14 +509,9 @@
     far_lists,
     top_lists,
 ):
-    y, core, x, z = (lax.axis_index(a) for a in ("y", "core", "x", "z"))
-    top = y * 2 + core
-    leaf = top * 32 + x * 8 + z
-    offsets = jnp.bitwise_xor(
-        far_lists[:, 0], jnp.right_shift(leaf, jnp.arange(4, dtype=jnp.int32))
-    )
-    partners = lax.dynamic_index_in_dim(top_lists, top, 0, keepdims=False)
-    scalars = jnp.concatenate([jnp.stack([z, x, y, core]), offsets, partners]).astype(jnp.int32)
+    top = lax.axis_index("y") * 2 + lax.axis_index("core")
+    listed = lax.dynamic_index_in_dim(top_lists, top, 0, keepdims=False)
+    scalars = far_lists[:, 0]
     chain_skeletons = skeletons[:, 0]
     tops = top_skeletons.reshape(4, 2, 64, 64)
 
@@ -536,17 +519,20 @@
     long = shaped(16, 1152)
     thin = shaped(16, 128)
     wire = shaped(16, 32, 128)
-    bases, chain, tail, outgoing, both = call(
+    both = jnp.concatenate([embeddings, rhs], axis=0)
+    one = along_z(both, 1)
+    two = along_z(both, 2)
+    three_off = along_z(two, 1)
+    bases, chain, tail, outgoing = call(
         prepare_kernel,
         (
             shaped(128, 1024, dtype=BF16),
             shaped(64, 512, dtype=BF16),
             shaped(64, 64),
             shaped(8, 64, 128),
-            shaped(80, 1024),
         ),
         [scalars],
-        [leaf_order, basis, transfer_maps[:, 0], chain_skeletons, rhs, embeddings],
+        [leaf_order, basis, transfer_maps[:, 0], chain_skeletons, rhs],
         "prepare",
         limit=60,
     )
@@ -557,11 +543,8 @@
         )
         return high, mine, other_core(mine)
 
-    one = along_z(both, 1)
-    two = along_z(both, 2)
-    three_off = along_z(two, 1)
     from_z = over_z(outgoing)
-    kernels, near = build(scalars, both, [], None, rhs, [chain], "build_own")
+    kernels, near = build(scalars, both, [], None, None, [two], "build_own")
     low, outgoing, second = call(
         middle_kernel,
         (thin, shaped(16, 64, 128), shaped(32, 128)),
@@ -572,21 +555,30 @@
     )
     from_yx = over_yx(outgoing)
     moved = lax.ppermute(second, "x", [(i, i ^ 1) for i in range(4)])
-    kernels, near = build(scalars, both, [two, one], 1, near, [low], "build_a", [kernels])
-    spread = gather(from_yx, [near])
+    kernels, near = build(
+        scalars, both, [two, one], 1, near, [low, three_off], "build_a", [kernels]
+    )
+    kernels, near = build(scalars, both, [two, three_off], 3, near, [low], "build_b", [kernels])
+    table = call(
+        low_kernel,
+        shaped(128, 256, dtype=BF16),
+        [scalars],
+        [chain_skeletons, from_z, second, moved, chain],
+        "couplings",
+    )
+    spread = gather(from_yx, [near, table])
     top_table = call(
         top_kernel,
         shaped(128, 576, dtype=BF16),
-        [scalars],
+        [scalars, listed],
         [chain_skeletons, from_yx, tops, tail],
         "tops",
     )
-    kernels, near = build(scalars, both, [two, three_off], 3, near, [low], "build_b", [kernels])
-    table, v1, outgoing = call(
+    v1, outgoing = call(
         first_kernel,
-        (shaped(128, 256, dtype=BF16), long, wire),
-        [scalars],
-        [low, *spread, top_table, from_z, second, moved, chain_skeletons, bases, near, chain],
+        (long, wire),
+        [],
+        [low, *spread, top_table, table, bases, near, chain],
         "first",
     )
 

time: 181 us -> 182 us (level)
  waiting for transfers between devices: 21.2 us -> 24.1 us
  local copies, waits for them, and re-layouts: 4.73 us -> 2.73 us
    ppermute x12, starting transfers between devices: 18.4 us -> 23.3 us  [along_z(): return lax.ppermute(v, 'z', [(i, i ^ offset) for i in range(8)])]
    ppermute x4, starting transfers between devices: 16.1 us -> 11.4 us  [other_core(): return lax.ppermute(v, 'core', [(0, 1), (1, 0)])]
    all_to_all x4, starting transfers between devices: 18.4 us -> 21.1 us  [over_yx(): return lax.all_to_all(v, ('y', 'x'), 0, 0)]
    all_to_all x4, starting transfers between devices: 23 us -> 20.4 us  [over_z(): return lax.all_to_all(v, 'z', 0, 0)]
    unnamed x26 -> x19, local copies, waits for them, and re-layouts: 3.95 us -> 1.7 us
    pallas_call x22 -> x23, Pallas kernels: 50.1 us -> 50.3 us  [call(): pl.pallas_call(body, out_shape=outs, in_specs=[SMEM] * len(scalars) + [VM...]
  transfers between devices with their start and end apart: 25 -> 25, of which waited for: 10 -> 11; matrix products, arithmetic and copies ran while one was open for 0% -> 0% of each run, Pallas kernels for 19% -> 21%
where the time goes in v3:
time: 182 us; the launch traced here: 181 us
  starting transfers between devices  77.3 us (42%)
  Pallas kernels  50.3 us (28%)
  blocking collectives  25.2 us (14%)
  waiting for transfers between devices  24.1 us (13%)
  local copies, waits for them, and re-layouts  2.73 us (2%)
    pallas_call x23, Pallas kernels, call(): pl.pallas_call(body, out_shape=outs, in_specs=[SMEM] * len(scalars) + [VM...  50.3 us
    ppermute x12, starting transfers between devices, along_z(): return lax.ppermute(v, 'z', [(i, i ^ offset) for i in range(8)])  23.3 us
    all_to_all x4, starting transfers between devices, over_yx(): return lax.all_to_all(v, ('y', 'x'), 0, 0)  21.1 us
    all_to_all x4, starting transfers between devices, over_z(): return lax.all_to_all(v, 'z', 0, 0)  20.4 us
    all_to_all x1, blocking collectives, local(): received = lax.all_to_all(outgoing, ('x', 'z'), 0, 0)  14 us
    ppermute x4, starting transfers between devices, other_core(): return lax.ppermute(v, 'core', [(0, 1), (1, 0)])  11.4 us
    all_to_all x1, blocking collectives, local(): shares = lax.all_to_all(wide, ('y', 'core'), 0, 0)  11.2 us
    all_to_all x4, waiting for transfers between devices, over_yx(): return lax.all_to_all(v, ('y', 'x'), 0, 0)  10.2 us
  transfers between devices with their start and end apart: 25, of which 11 were waited for; matrix products, arithmetic and copies ran while one was open for 0% of the time, Pallas kernels for 21%

profile of v3, /device:TPU:1, one launch (start us, length us, event | category | flops | bytes accessed | tf_op | source)
XLA Modules:
  0.0 180.6 jit_solution(3414549869437404092)
XLA Ops:
  0.7 1.0 constant_dynamic-update-slice_fusion.1
  2.5 3.8 %collective-permute-start = (f32[80,1024]{1,0:T(8,128)S(1)}, f32[80,1024]{1,0:T(8,128)S(1)}, u32[]{:S(2)}, u32[]{:S(2)}) collective-permute-start(f32[80,1024]{1,0:T(8,128)S(1)} %constant_dynamic-update-slice_fusion.refs_0_), channel_id=1, source_target_pairs={{0,2},{1,3},{2,0},{3,1},{4,6},{5,7},{6,4},{7,5},{8,10},{9,11},{10,... | collective-permute-start | bytes 983048 | tf_op jit(solution)/shard_map/ppermute | solution.py:485
  6.3 3.3 %prepare.1 = (bf16[128,1024]{1,0:T(8,128)(2,1)}, bf16[64,512]{1,0:T(8,128)(2,1)}, f32[64,64]{1,0:T(8,128)}, f32[8,64,128]{2,1,0:T(8,128)}) custom-call(s32[4]{0:T(128)} %bitcast.9, s32[1,1024]{1,0:T(1,128)} %refs_0_.1, f32[64,1024]{1,0:T(8,128)} %refs_1_.1, f32[5,64,64]{2,1,0:T(8,128)} %bitcast.26, f32[4,64,64]{2,1,0:T(8,128)} %bitcast.4, f32[16,1024]{1,0:T(8,128)} %rhs.2), custom_call_target="tpu_custom_call" | custom-call | flops 100000 | bytes 500000 | tf_op jit(solution)/shard_map/prepare/pallas_call | solution.py:430
  9.6 6.5 %all-to-all-start = ((f32[8,64,128]{2,1,0:T(8,128)}), f32[8,64,128]{2,1,0:T(8,128)S(1)}, u32[]{:S(2)}, u32[]{:S(2)}) async-start(f32[8,64,128]{2,1,0:T(8,128)} %get-tuple-element.35), calls=%async_computation | async-start | bytes 524288 | tf_op jit(solution)/shard_map/all_to_all | solution.py:493
  16.1 1.5 collective-permute-start.2
  17.6 2.5 %collective-permute-done.refs_1_ = f32[80,1024]{1,0:T(8,128)S(1)} collective-permute-done((f32[80,1024]{1,0:T(8,128)S(1)}, f32[80,1024]{1,0:T(8,128)S(1)}, u32[]{:S(2)}, u32[]{:S(2)}) %collective-permute-start) | collective-permute-done | bytes 327712 | tf_op jit(solution)/shard_map/ppermute | solution.py:485
  20.1 4.5 %collective-permute-start.1 = (f32[80,1024]{1,0:T(8,128)S(1)}, f32[80,1024]{1,0:T(8,128)S(1)}, u32[]{:S(2)}, u32[]{:S(2)}) collective-permute-start(f32[80,1024]{1,0:T(8,128)S(1)} %collective-permute-done.refs_1_), channel_id=1, source_target_pairs={{0,1},{1,0},{2,3},{3,2},{4,5},{5,4},{6,7},{7,6},{8,9},{9,8},{10,11... | collective-permute-start | bytes 983048 | tf_op jit(solution)/shard_map/ppermute | solution.py:485
  25.3 4.1 %build_own.1 = (bf16[3,2,1024,1024]{3,2,1,0:T(8,128)(2,1)}, f32[16,1024]{1,0:T(8,128)S(1)}) custom-call(s32[4]{0:T(128)S(1)} %bitcast.10, f32[80,1024]{1,0:T(8,128)S(1)} %constant_dynamic-update-slice_fusion.refs_0_, f32[80,1024]{1,0:T(8,128)S(1)} %collective-permute-done.refs_1_), custom_call_target="tpu_custom_call" | custom-call | flops 4000000000 | bytes 500000 | tf_op jit(solution)/shard_map/build_own/pallas_call | solution.py:430
  29.4 1.7 middle.1
  31.1 1.2 collective-permute-start.3
  32.3 6.5 %all-to-all-start.1 = ((f32[16,64,128]{2,1,0:T(8,128)}), f32[16,64,128]{2,1,0:T(8,128)S(1)}, u32[]{:S(2)}, u32[]{:S(2)}) async-start(f32[16,64,128]{2,1,0:T(8,128)} %get-tuple-element.39), calls=%async_computation.1 | async-start | bytes 1048576 | tf_op jit(solution)/shard_map/all_to_all | solution.py:497
  38.8 1.1 couplings.1.refs_2_.table.refs_1_
  39.9 1.1 collective-permute-done.1.refs_5_.refs_2_
  41.0 4.2 %build_a.1 = (bf16[3,2,1024,1024]{3,2,1,0:T(8,128)(2,1)}, f32[16,1024]{1,0:T(8,128)S(1)}) custom-call(s32[4]{0:T(128)S(1)} %bitcast.13, f32[80,1024]{1,0:T(8,128)S(1)} %constant_dynamic-update-slice_fusion.refs_0_, f32[80,1024]{1,0:T(8,128)S(1)} %collective-permute-done.refs_1_, ...), custom_call_target="tpu_custom_call", output_to_operand_aliasing={{0}: (7, {})} | custom-call | flops 4000000000 | bytes 500000 | tf_op jit(solution)/shard_map/build_a/pallas_call | solution.py:430
  45.2 4.1 %build_b.1 = (bf16[3,2,1024,1024]{3,2,1,0:T(8,128)(2,1)}, f32[16,1024]{1,0:T(8,128)S(1)}) custom-call(s32[4]{0:T(128)S(1)} %bitcast.14, f32[80,1024]{1,0:T(8,128)S(1)} %constant_dynamic-update-slice_fusion.refs_0_, f32[80,1024]{1,0:T(8,128)S(1)} %collective-permute-done.refs_1_, ...), custom_call_target="tpu_custom_call", output_to_operand_aliasing={{0}: (6, {})} | custom-call | flops 4000000000 | bytes 500000 | tf_op jit(solution)/shard_map/build_b/pallas_call | solution.py:430
  50.0 2.2 %collective-permute-start.4 = (f32[64,128]{1,0:T(8,128)S(1)}, f32[64,128]{1,0:T(8,128)S(1)}, u32[]{:S(2)}, u32[]{:S(2)}) collective-permute-start(f32[64,128]{1,0:T(8,128)S(1)} %get-tuple-element.47.mine), channel_id=1, source_target_pairs={{0,32},{32,0},{1,33},{33,1},{2,34},{34,2},{3,35},{35,3},{4,36},{36... | collective-permute-start | bytes 98312 | tf_op jit(solution)/shard_map/ppermute | solution.py:489
  52.4 1.3 tops.1.top_table.table
  53.7 2.0 %first.1 = (f32[16,1152]{1,0:T(8,128)S(1)}, f32[16,32,128]{2,1,0:T(8,128)}) custom-call(f32[16,128]{1,0:T(8,128)S(1)} %get-tuple-element.38.refs_4_.low, f32[16,128]{1,0:T(8,128)S(1)} %get-tuple-element.46.high, f32[64,128]{1,0:T(8,128)S(1)} %get-tuple-element.47.mine, f32[64,128]{1,0:T(8,128)S(1)} %collective-permute-done.4.other, ...), custom_call_target="tpu_custom_call" | custom-call | flops 100000 | bytes 500000 | tf_op jit(solution)/shard_map/first/pallas_call | solution.py:430
  55.7 5.9 %all-to-all-start.2 = ((f32[16,32,128]{2,1,0:T(8,128)}), f32[16,32,128]{2,1,0:T(8,128)S(1)}, u32[]{:S(2)}, u32[]{:S(2)}) async-start(f32[16,32,128]{2,1,0:T(8,128)} %get-tuple-element.49), calls=%async_computation.2 | async-start | bytes 524288 | tf_op jit(solution)/shard_map/all_to_all | solution.py:497
  61.6 4.0 %collective-permute-start.6 = (f32[16,1152]{1,0:T(8,128)S(1)}, f32[16,1152]{1,0:T(8,128)S(1)}, u32[]{:S(2)}, u32[]{:S(2)}) collective-permute-start(f32[16,1152]{1,0:T(8,128)S(1)} %get-tuple-element.52.own.refs_0_.refs_5_.v1), channel_id=1, source_target_pairs={{0,1},{1,0},{2,3},{3,2},{4,5},{5,4},{6,7},{7,6},{8,9},{9,8},{10,11... | collective-permute-start | bytes 221192 | tf_op jit(solution)/shard_map/ppermute | solution.py:485
  65.6 2.2 %collective-permute-start.8 = (f32[16,1152]{1,0:T(8,128)S(1)}, f32[16,1152]{1,0:T(8,128)S(1)}, u32[]{:S(2)}, u32[]{:S(2)}) collective-permute-start(f32[16,1152]{1,0:T(8,128)S(1)} %get-tuple-element.52.own.refs_0_.refs_5_.v1), channel_id=1, source_target_pairs={{0,3},{1,2},{2,1},{3,0},{4,7},{5,6},{6,5},{7,4},{8,11},{9,10},{10,... | collective-permute-start | bytes 221192 | tf_op jit(solution)/shard_map/ppermute | solution.py:485
  67.8 2.3 %all-to-all-done.2.refs_0_ = f32[16,32,128]{2,1,0:T(8,128)S(1)} async-done(((f32[16,32,128]{2,1,0:T(8,128)}), f32[16,32,128]{2,1,0:T(8,128)S(1)}, u32[]{:S(2)}, u32[]{:S(2)}) %all-to-all-start.2) | async-done | bytes 262176 | tf_op jit(solution)/shard_map/all_to_all | solution.py:497
  70.7 1.2 collective-permute-start.5
  71.9 1.4 collective-permute-done.7.refs_1_.refs_2_
  73.4 1.0 lower.3.refs_5_
  74.3 7.0 %all-to-all-start.3 = ((f32[8,32,128]{2,1,0:T(8,128)}), f32[8,32,128]{2,1,0:T(8,128)S(1)}, u32[]{:S(2)}, u32[]{:S(2)}) async-start(f32[8,32,128]{2,1,0:T(8,128)} %lower.3.refs_5_), calls=%async_computation.3 | async-start | bytes 262144 | tf_op jit(solution)/shard_map/all_to_all | solution.py:493
  81.3 5.5 %near.3.refs_3_ = f32[16,1152]{1,0:T(8,128)S(1)} custom-call(s32[4]{0:T(128)S(1)} %bitcast.18, f32[16,1152]{1,0:T(8,128)S(1)} %get-tuple-element.52.own.refs_0_.refs_5_.v1, f32[16,1152]{1,0:T(8,128)S(1)} %collective-permute-done.6.refs_0_.refs_1_, f32[16,1152]{1,0:T(8,128)S(1)} %collective-permute-done.7.refs_1_.refs_2_, ...), custom_call_target="tpu_custom_call" | custom-call | flops 4000000000 | bytes 500000 | tf_op jit(solution)/shard_map/near/pallas_call | solution.py:430
  86.9 2.4 %all-to-all-done.3.refs_0_ = f32[8,32,128]{2,1,0:T(8,128)S(1)} async-done(((f32[8,32,128]{2,1,0:T(8,128)}), f32[8,32,128]{2,1,0:T(8,128)S(1)}, u32[]{:S(2)}, u32[]{:S(2)}) %all-to-all-start.3) | async-done | bytes 131104 | tf_op jit(solution)/shard_map/all_to_all | solution.py:493
  89.3 2.3 %second.1 = (f32[16,1024]{1,0:T(8,128)S(1)}, f32[16,1152]{1,0:T(8,128)S(1)}, f32[16,128]{1,0:T(8,128)S(1)}, f32[16,32,128]{2,1,0:T(8,128)}) custom-call(s32[4]{0:T(128)S(1)} %bitcast.19, f32[8,32,128]{2,1,0:T(8,128)S(1)} %all-to-all-done.3.refs_0_, bf16[128,256]{1,0:T(8,128)(2,1)S(1)} %couplings.1.refs_2_.table.refs_1_, bf16[128,1024]{1,0:T(8,128)(2,1)S(1)} %copy-done.1, ...), custom_call_target="tpu_custom_call" | custom-call | flops 100000 | bytes 500000 | tf_op jit(solution)/shard_map/second/pallas_call | solution.py:430
  91.6 5.2 %all-to-all-start.4 = ((f32[16,32,128]{2,1,0:T(8,128)}), f32[16,32,128]{2,1,0:T(8,128)S(1)}, u32[]{:S(2)}, u32[]{:S(2)}) async-start(f32[16,32,128]{2,1,0:T(8,128)} %get-tuple-element.54), calls=%async_computation.4 | async-start | bytes 524288 | tf_op jit(solution)/shard_map/all_to_all | solution.py:497
  98.0 2.5 %collective-permute-start.12 = (f32[16,1152]{1,0:T(8,128)S(1)}, f32[16,1152]{1,0:T(8,128)S(1)}, u32[]{:S(2)}, u32[]{:S(2)}) collective-permute-start(f32[16,1152]{1,0:T(8,128)S(1)} %get-tuple-element.57.own.refs_0_), channel_id=1, source_target_pairs={{0,3},{1,2},{2,1},{3,0},{4,7},{5,6},{6,5},{7,4},{8,11},{9,10},{10,... | collective-permute-start | bytes 221192 | tf_op jit(solution)/shard_map/ppermute | solution.py:485
  100.4 4.0 %all-to-all-done.4.refs_0_ = f32[16,32,128]{2,1,0:T(8,128)S(1)} async-done(((f32[16,32,128]{2,1,0:T(8,128)}), f32[16,32,128]{2,1,0:T(8,128)S(1)}, u32[]{:S(2)}, u32[]{:S(2)}) %all-to-all-start.4) | async-done | bytes 262176 | tf_op jit(solution)/shard_map/all_to_all | solution.py:497
  105.0 3.8 %collective-permute-start.9 = (f32[64,128]{1,0:T(8,128)S(1)}, f32[64,128]{1,0:T(8,128)S(1)}, u32[]{:S(2)}, u32[]{:S(2)}) collective-permute-start(f32[64,128]{1,0:T(8,128)S(1)} %get-tuple-element.56.mine), channel_id=1, source_target_pairs={{0,32},{32,0},{1,33},{33,1},{2,34},{34,2},{3,35},{35,3},{4,36},{36... | collective-permute-start | bytes 98312 | tf_op jit(solution)/shard_map/ppermute | solution.py:489
  110.6 3.4 %all-to-all-start.5 = ((f32[8,32,128]{2,1,0:T(8,128)}), f32[8,32,128]{2,1,0:T(8,128)S(1)}, u32[]{:S(2)}, u32[]{:S(2)}) async-start(f32[8,32,128]{2,1,0:T(8,128)} %lower.4.refs_5_), calls=%async_computation.5 | async-start | bytes 262144 | tf_op jit(solution)/shard_map/all_to_all | solution.py:493
  114.0 5.5 %near.4.refs_3_ = f32[16,1152]{1,0:T(8,128)S(1)} custom-call(s32[4]{0:T(128)S(1)} %bitcast.21, f32[16,1152]{1,0:T(8,128)S(1)} %get-tuple-element.57.own.refs_0_, f32[16,1152]{1,0:T(8,128)S(1)} %collective-permute-done.10.refs_0_.refs_1_, f32[16,1152]{1,0:T(8,128)S(1)} %collective-permute-done.11.refs_1_.refs_2_, ...), custom_call_target="tpu_custom_call" | custom-call | flops 4000000000 | bytes 500000 | tf_op jit(solution)/shard_map/near/pallas_call | solution.py:430
  119.5 2.4 %all-to-all-done.5.refs_0_ = f32[8,32,128]{2,1,0:T(8,128)S(1)} async-done(((f32[8,32,128]{2,1,0:T(8,128)}), f32[8,32,128]{2,1,0:T(8,128)S(1)}, u32[]{:S(2)}, u32[]{:S(2)}) %all-to-all-start.5) | async-done | bytes 131104 | tf_op jit(solution)/shard_map/all_to_all | solution.py:493
  121.9 2.3 %third.1 = (f32[16,1152]{1,0:T(8,128)S(1)}, f32[16,128]{1,0:T(8,128)S(1)}, f32[16,32,128]{2,1,0:T(8,128)}) custom-call(s32[4]{0:T(128)S(1)} %bitcast.22, f32[8,32,128]{2,1,0:T(8,128)S(1)} %all-to-all-done.5.refs_0_, bf16[128,256]{1,0:T(8,128)(2,1)S(1)} %couplings.1.refs_2_.table.refs_1_, bf16[128,1024]{1,0:T(8,128)(2,1)S(1)} %copy-done.1, ...), custom_call_target="tpu_custom_call" | custom-call | flops 100000 | bytes 500000 | tf_op jit(solution)/shard_map/third/pallas_call | solution.py:430
  124.2 3.5 %all-to-all-start.6 = ((f32[16,32,128]{2,1,0:T(8,128)}), f32[16,32,128]{2,1,0:T(8,128)S(1)}, u32[]{:S(2)}, u32[]{:S(2)}) async-start(f32[16,32,128]{2,1,0:T(8,128)} %get-tuple-element.59), calls=%async_computation.6 | async-start | bytes 524288 | tf_op jit(solution)/shard_map/all_to_all | solution.py:497
  127.9 1.1 collective-permute-start.15
  129.1 2.4 %collective-permute-start.16 = (f32[16,1152]{1,0:T(8,128)S(1)}, f32[16,1152]{1,0:T(8,128)S(1)}, u32[]{:S(2)}, u32[]{:S(2)}) collective-permute-start(f32[16,1152]{1,0:T(8,128)S(1)} %get-tuple-element.62.own.refs_0_.image), channel_id=1, source_target_pairs={{0,3},{1,2},{2,1},{3,0},{4,7},{5,6},{6,5},{7,4},{8,11},{9,10},{10,... | collective-permute-start | bytes 221192 | tf_op jit(solution)/shard_map/ppermute | solution.py:485
  131.4 3.9 %all-to-all-done.6.refs_0_ = f32[16,32,128]{2,1,0:T(8,128)S(1)} async-done(((f32[16,32,128]{2,1,0:T(8,128)}), f32[16,32,128]{2,1,0:T(8,128)S(1)}, u32[]{:S(2)}, u32[]{:S(2)}) %all-to-all-start.6) | async-done | bytes 262176 | tf_op jit(solution)/shard_map/all_to_all | solution.py:497
  135.9 4.2 %collective-permute-start.13 = (f32[64,128]{1,0:T(8,128)S(1)}, f32[64,128]{1,0:T(8,128)S(1)}, u32[]{:S(2)}, u32[]{:S(2)}) collective-permute-start(f32[64,128]{1,0:T(8,128)S(1)} %get-tuple-element.61.mine), channel_id=1, source_target_pairs={{0,32},{32,0},{1,33},{33,1},{2,34},{34,2},{3,35},{35,3},{4,36},{36... | collective-permute-start | bytes 98312 | tf_op jit(solution)/shard_map/ppermute | solution.py:489
  142.0 3.4 %all-to-all-start.7 = ((f32[8,32,128]{2,1,0:T(8,128)}), f32[8,32,128]{2,1,0:T(8,128)S(1)}, u32[]{:S(2)}, u32[]{:S(2)}) async-start(f32[8,32,128]{2,1,0:T(8,128)} %lower.5.refs_5_), calls=%async_computation.7 | async-start | bytes 262144 | tf_op jit(solution)/shard_map/all_to_all | solution.py:493
  145.4 5.5 %near.5.refs_3_ = f32[16,1152]{1,0:T(8,128)S(1)} custom-call(s32[4]{0:T(128)S(1)} %bitcast.24, f32[16,1152]{1,0:T(8,128)S(1)} %get-tuple-element.62.own.refs_0_.image, f32[16,1152]{1,0:T(8,128)S(1)} %collective-permute-done.14.refs_0_.refs_1_, f32[16,1152]{1,0:T(8,128)S(1)} %collective-permute-done.15.refs_1_.refs_2_, ...), custom_call_target="tpu_custom_call" | custom-call | flops 4000000000 | bytes 500000 | tf_op jit(solution)/shard_map/near/pallas_call | solution.py:430
  151.0 2.4 %all-to-all-done.7.refs_0_ = f32[8,32,128]{2,1,0:T(8,128)S(1)} async-done(((f32[8,32,128]{2,1,0:T(8,128)}), f32[8,32,128]{2,1,0:T(8,128)S(1)}, u32[]{:S(2)}, u32[]{:S(2)}) %all-to-all-start.7) | async-done | bytes 131104 | tf_op jit(solution)/shard_map/all_to_all | solution.py:493
  153.3 1.2 fourth.1
  154.5 14.0 %all_to_all.50.received = f32[32,8,128]{2,1,0:T(8,128)S(1)} all-to-all(f32[32,8,128]{2,1,0:T(8,128)S(1)} %get-tuple-element.64), channel_id=1, replica_groups=mesh['y'=4,'core'=2,'x'=4,'z'=8] {'x','z'}, dimensions={0} | all-to-all | bytes 262144 | tf_op jit(solution)/shard_map/all_to_all | solution.py:616
  168.6 11.2 %all_to_all.51.shares = f32[8,8,128]{2,1,0:T(8,128)S(1)} all-to-all(f32[8,8,128]{2,1,0:T(8,128)S(1)} %spread.1), channel_id=1, replica_groups=mesh['y'=4,'core'=2,'x'=4,'z'=8] {'y','core'}, dimensions={0} | all-to-all | bytes 65536 | tf_op jit(solution)/shard_map/all_to_all | solution.py:618
  (48 shorter events, 9.9 us)
Async XLA Ops:
  0.6 51.5 %copy-start = (s32[8,4]{0,1:T(4,128)S(1)}, s32[8,4]{0,1:T(4,128)}, u32[]{:S(2)}) copy-start(s32[8,4]{0,1:T(4,128)} %param.18) | copy-start | bytes 388
  0.6 28.8 %copy-start.2 = (f32[4,1,64,64]{3,2,1,0:T(8,128)S(1)}, f32[4,1,64,64]{3,2,1,0:T(8,128)}, u32[]{:S(2)}) copy-start(f32[4,1,64,64]{3,2,1,0:T(8,128)} %param.15) | copy-start | bytes 196612
  2.5 17.6 %collective-permute-start = (f32[80,1024]{1,0:T(8,128)S(1)}, f32[80,1024]{1,0:T(8,128)S(1)}, u32[]{:S(2)}, u32[]{:S(2)}) collective-permute-start(f32[80,1024]{1,0:T(8,128)S(1)} %constant_dynamic-update-slice_fusion.refs_0_), channel_id=1, source_target_pairs={{0,2},{1,3},{2,0},{3,1},{4,6},{5,7},{6,4},{7,5},{8,10},{9,11},{10,... | collective-permute-start | bytes 983048 | tf_op jit(solution)/shard_map/ppermute | solution.py:485
  9.6 19.8 %copy-start.6 = (f32[64,64]{1,0:T(8,128)S(1)}, f32[64,64]{1,0:T(8,128)}, u32[]{:S(2)}) copy-start(f32[64,64]{1,0:T(8,128)} %get-tuple-element.36.refs_1_.refs_4_) | copy-start | bytes 49156
  9.6 29.2 %copy-start.3 = (bf16[64,512]{1,0:T(8,128)(2,1)S(1)}, bf16[64,512]{1,0:T(8,128)(2,1)}, u32[]{:S(2)}) copy-start(bf16[64,512]{1,0:T(8,128)(2,1)} %get-tuple-element.45.refs_4_.chain) | copy-start | bytes 196612
  9.6 19.8 %all-to-all-start = ((f32[8,64,128]{2,1,0:T(8,128)}), f32[8,64,128]{2,1,0:T(8,128)S(1)}, u32[]{:S(2)}, u32[]{:S(2)}) async-start(f32[8,64,128]{2,1,0:T(8,128)} %get-tuple-element.35), calls=%async_computation | async-start | bytes 524288 | tf_op jit(solution)/shard_map/all_to_all | solution.py:493
  16.1 23.8 %collective-permute-start.2 = (f32[80,1024]{1,0:T(8,128)S(1)}, f32[80,1024]{1,0:T(8,128)S(1)}, u32[]{:S(2)}, u32[]{:S(2)}) collective-permute-start(f32[80,1024]{1,0:T(8,128)S(1)} %constant_dynamic-update-slice_fusion.refs_0_), channel_id=1, source_target_pairs={{0,1},{1,0},{2,3},{3,2},{4,5},{5,4},{6,7},{7,6},{8,9},{9,8},{10,11... | collective-permute-start | bytes 983048 | tf_op jit(solution)/shard_map/ppermute | solution.py:485
  20.1 20.9 %collective-permute-start.1 = (f32[80,1024]{1,0:T(8,128)S(1)}, f32[80,1024]{1,0:T(8,128)S(1)}, u32[]{:S(2)}, u32[]{:S(2)}) collective-permute-start(f32[80,1024]{1,0:T(8,128)S(1)} %collective-permute-done.refs_1_), channel_id=1, source_target_pairs={{0,1},{1,0},{2,3},{3,2},{4,5},{5,4},{6,7},{7,6},{8,9},{9,8},{10,11... | collective-permute-start | bytes 983048 | tf_op jit(solution)/shard_map/ppermute | solution.py:485
  24.6 0.7 copy-start.7
  31.1 7.7 %collective-permute-start.3 = (f32[32,128]{1,0:T(8,128)S(1)}, f32[32,128]{1,0:T(8,128)S(1)}, u32[]{:S(2)}, u32[]{:S(2)}) collective-permute-start(f32[32,128]{1,0:T(8,128)S(1)} %get-tuple-element.44.refs_2_), channel_id=1, source_target_pairs={{0,8},{8,0},{16,24},{24,16},{1,9},{9,1},{17,25},{25,17},{2,10},{10... | collective-permute-start | bytes 49160 | tf_op jit(solution)/shard_map/ppermute | solution.py:557
  32.3 17.0 %all-to-all-start.1 = ((f32[16,64,128]{2,1,0:T(8,128)}), f32[16,64,128]{2,1,0:T(8,128)S(1)}, u32[]{:S(2)}, u32[]{:S(2)}) async-start(f32[16,64,128]{2,1,0:T(8,128)} %get-tuple-element.39), calls=%async_computation.1 | async-start | bytes 1048576 | tf_op jit(solution)/shard_map/all_to_all | solution.py:497
  41.0 11.4 %copy-start.5 = (f32[8,64,64]{2,1,0:T(8,128)S(1)}, f32[8,64,64]{2,1,0:T(8,128)}, u32[]{:S(2)}) copy-start(f32[8,64,64]{2,1,0:T(8,128)} %param.16) | copy-start | bytes 393220
  41.0 11.4 %copy-start.8 = (s32[4,1]{0,1:T(1,128)S(1)}, s32[4,1]{0,1:T(1,128)}, u32[]{:S(2)}) copy-start(s32[4,1]{0,1:T(1,128)} %param.17) | copy-start | bytes 52
  41.0 12.7 %copy-start.1 = (bf16[128,1024]{1,0:T(8,128)(2,1)S(1)}, bf16[128,1024]{1,0:T(8,128)(2,1)}, u32[]{:S(2)}) copy-start(bf16[128,1024]{1,0:T(8,128)(2,1)} %get-tuple-element.48.bases.refs_2_) | copy-start | bytes 786436
  50.0 3.7 %collective-permute-start.4 = (f32[64,128]{1,0:T(8,128)S(1)}, f32[64,128]{1,0:T(8,128)S(1)}, u32[]{:S(2)}, u32[]{:S(2)}) collective-permute-start(f32[64,128]{1,0:T(8,128)S(1)} %get-tuple-element.47.mine), channel_id=1, source_target_pairs={{0,32},{32,0},{1,33},{33,1},{2,34},{34,2},{3,35},{35,3},{4,36},{36... | collective-permute-start | bytes 98312 | tf_op jit(solution)/shard_map/ppermute | solution.py:489
  55.7 14.4 %all-to-all-start.2 = ((f32[16,32,128]{2,1,0:T(8,128)}), f32[16,32,128]{2,1,0:T(8,128)S(1)}, u32[]{:S(2)}, u32[]{:S(2)}) async-start(f32[16,32,128]{2,1,0:T(8,128)} %get-tuple-element.49), calls=%async_computation.2 | async-start | bytes 524288 | tf_op jit(solution)/shard_map/all_to_all | solution.py:497
  61.6 10.3 %collective-permute-start.6 = (f32[16,1152]{1,0:T(8,128)S(1)}, f32[16,1152]{1,0:T(8,128)S(1)}, u32[]{:S(2)}, u32[]{:S(2)}) collective-permute-start(f32[16,1152]{1,0:T(8,128)S(1)} %get-tuple-element.52.own.refs_0_.refs_5_.v1), channel_id=1, source_target_pairs={{0,1},{1,0},{2,3},{3,2},{4,5},{5,4},{6,7},{7,6},{8,9},{9,8},{10,11... | collective-permute-start | bytes 221192 | tf_op jit(solution)/shard_map/ppermute | solution.py:485
  65.6 7.8 %collective-permute-start.7 = (f32[16,1152]{1,0:T(8,128)S(1)}, f32[16,1152]{1,0:T(8,128)S(1)}, u32[]{:S(2)}, u32[]{:S(2)}) collective-permute-start(f32[16,1152]{1,0:T(8,128)S(1)} %get-tuple-element.52.own.refs_0_.refs_5_.v1), channel_id=1, source_target_pairs={{0,2},{1,3},{2,0},{3,1},{4,6},{5,7},{6,4},{7,5},{8,10},{9,11},{10,... | collective-permute-start | bytes 221192 | tf_op jit(solution)/shard_map/ppermute | solution.py:485
  65.6 7.8 %collective-permute-start.8 = (f32[16,1152]{1,0:T(8,128)S(1)}, f32[16,1152]{1,0:T(8,128)S(1)}, u32[]{:S(2)}, u32[]{:S(2)}) collective-permute-start(f32[16,1152]{1,0:T(8,128)S(1)} %get-tuple-element.52.own.refs_0_.refs_5_.v1), channel_id=1, source_target_pairs={{0,3},{1,2},{2,1},{3,0},{4,7},{5,6},{6,5},{7,4},{8,11},{9,10},{10,... | collective-permute-start | bytes 221192 | tf_op jit(solution)/shard_map/ppermute | solution.py:485
  70.7 2.7 %collective-permute-start.5 = (f32[64,128]{1,0:T(8,128)S(1)}, f32[64,128]{1,0:T(8,128)S(1)}, u32[]{:S(2)}, u32[]{:S(2)}) collective-permute-start(f32[64,128]{1,0:T(8,128)S(1)} %get-tuple-element.51.mine), channel_id=1, source_target_pairs={{0,32},{32,0},{1,33},{33,1},{2,34},{34,2},{3,35},{35,3},{4,36},{36... | collective-permute-start | bytes 98312 | tf_op jit(solution)/shard_map/ppermute | solution.py:489
  74.3 15.0 %all-to-all-start.3 = ((f32[8,32,128]{2,1,0:T(8,128)}), f32[8,32,128]{2,1,0:T(8,128)S(1)}, u32[]{:S(2)}, u32[]{:S(2)}) async-start(f32[8,32,128]{2,1,0:T(8,128)} %lower.3.refs_5_), calls=%async_computation.3 | async-start | bytes 262144 | tf_op jit(solution)/shard_map/all_to_all | solution.py:493
  91.6 12.8 %all-to-all-start.4 = ((f32[16,32,128]{2,1,0:T(8,128)}), f32[16,32,128]{2,1,0:T(8,128)S(1)}, u32[]{:S(2)}, u32[]{:S(2)}) async-start(f32[16,32,128]{2,1,0:T(8,128)} %get-tuple-element.54), calls=%async_computation.4 | async-start | bytes 524288 | tf_op jit(solution)/shard_map/all_to_all | solution.py:497
  96.8 12.0 %collective-permute-start.10 = (f32[16,1152]{1,0:T(8,128)S(1)}, f32[16,1152]{1,0:T(8,128)S(1)}, u32[]{:S(2)}, u32[]{:S(2)}) collective-permute-start(f32[16,1152]{1,0:T(8,128)S(1)} %get-tuple-element.57.own.refs_0_), channel_id=1, source_target_pairs={{0,1},{1,0},{2,3},{3,2},{4,5},{5,4},{6,7},{7,6},{8,9},{9,8},{10,11... | collective-permute-start | bytes 221192 | tf_op jit(solution)/shard_map/ppermute | solution.py:485
  97.1 11.7 %collective-permute-start.11 = (f32[16,1152]{1,0:T(8,128)S(1)}, f32[16,1152]{1,0:T(8,128)S(1)}, u32[]{:S(2)}, u32[]{:S(2)}) collective-permute-start(f32[16,1152]{1,0:T(8,128)S(1)} %get-tuple-element.57.own.refs_0_), channel_id=1, source_target_pairs={{0,2},{1,3},{2,0},{3,1},{4,6},{5,7},{6,4},{7,5},{8,10},{9,11},{10,... | collective-permute-start | bytes 221192 | tf_op jit(solution)/shard_map/ppermute | solution.py:485
  98.0 10.8 %collective-permute-start.12 = (f32[16,1152]{1,0:T(8,128)S(1)}, f32[16,1152]{1,0:T(8,128)S(1)}, u32[]{:S(2)}, u32[]{:S(2)}) collective-permute-start(f32[16,1152]{1,0:T(8,128)S(1)} %get-tuple-element.57.own.refs_0_), channel_id=1, source_target_pairs={{0,3},{1,2},{2,1},{3,0},{4,7},{5,6},{6,5},{7,4},{8,11},{9,10},{10,... | collective-permute-start | bytes 221192 | tf_op jit(solution)/shard_map/ppermute | solution.py:485
  105.0 4.6 %collective-permute-start.9 = (f32[64,128]{1,0:T(8,128)S(1)}, f32[64,128]{1,0:T(8,128)S(1)}, u32[]{:S(2)}, u32[]{:S(2)}) collective-permute-start(f32[64,128]{1,0:T(8,128)S(1)} %get-tuple-element.56.mine), channel_id=1, source_target_pairs={{0,32},{32,0},{1,33},{33,1},{2,34},{34,2},{3,35},{35,3},{4,36},{36... | collective-permute-start | bytes 98312 | tf_op jit(solution)/shard_map/ppermute | solution.py:489
  110.6 11.3 %all-to-all-start.5 = ((f32[8,32,128]{2,1,0:T(8,128)}), f32[8,32,128]{2,1,0:T(8,128)S(1)}, u32[]{:S(2)}, u32[]{:S(2)}) async-start(f32[8,32,128]{2,1,0:T(8,128)} %lower.4.refs_5_), calls=%async_computation.5 | async-start | bytes 262144 | tf_op jit(solution)/shard_map/all_to_all | solution.py:493
  119.5 60.2 %copy-start.4 = (f32[16,1024]{1,0:T(8,128)S(1)}, f32[16,1024]{1,0:T(8,128)}, u32[]{:S(2)}) copy-start(f32[16,1024]{1,0:T(8,128)} %rhs.2) | copy-start | bytes 196612
  124.2 11.1 %all-to-all-start.6 = ((f32[16,32,128]{2,1,0:T(8,128)}), f32[16,32,128]{2,1,0:T(8,128)S(1)}, u32[]{:S(2)}, u32[]{:S(2)}) async-start(f32[16,32,128]{2,1,0:T(8,128)} %get-tuple-element.59), calls=%async_computation.6 | async-start | bytes 524288 | tf_op jit(solution)/shard_map/all_to_all | solution.py:497
  127.8 12.4 %collective-permute-start.14 = (f32[16,1152]{1,0:T(8,128)S(1)}, f32[16,1152]{1,0:T(8,128)S(1)}, u32[]{:S(2)}, u32[]{:S(2)}) collective-permute-start(f32[16,1152]{1,0:T(8,128)S(1)} %get-tuple-element.62.own.refs_0_.image), channel_id=1, source_target_pairs={{0,1},{1,0},{2,3},{3,2},{4,5},{5,4},{6,7},{7,6},{8,9},{9,8},{10,11... | collective-permute-start | bytes 221192 | tf_op jit(solution)/shard_map/ppermute | solution.py:485
  127.9 12.3 %collective-permute-start.15 = (f32[16,1152]{1,0:T(8,128)S(1)}, f32[16,1152]{1,0:T(8,128)S(1)}, u32[]{:S(2)}, u32[]{:S(2)}) collective-permute-start(f32[16,1152]{1,0:T(8,128)S(1)} %get-tuple-element.62.own.refs_0_.image), channel_id=1, source_target_pairs={{0,2},{1,3},{2,0},{3,1},{4,6},{5,7},{6,4},{7,5},{8,10},{9,11},{10,... | collective-permute-start | bytes 221192 | tf_op jit(solution)/shard_map/ppermute | solution.py:485
  129.1 11.1 %collective-permute-start.16 = (f32[16,1152]{1,0:T(8,128)S(1)}, f32[16,1152]{1,0:T(8,128)S(1)}, u32[]{:S(2)}, u32[]{:S(2)}) collective-permute-start(f32[16,1152]{1,0:T(8,128)S(1)} %get-tuple-element.62.own.refs_0_.image), channel_id=1, source_target_pairs={{0,3},{1,2},{2,1},{3,0},{4,7},{5,6},{6,5},{7,4},{8,11},{9,10},{10,... | collective-permute-start | bytes 221192 | tf_op jit(solution)/shard_map/ppermute | solution.py:485
  135.9 5.1 %collective-permute-start.13 = (f32[64,128]{1,0:T(8,128)S(1)}, f32[64,128]{1,0:T(8,128)S(1)}, u32[]{:S(2)}, u32[]{:S(2)}) collective-permute-start(f32[64,128]{1,0:T(8,128)S(1)} %get-tuple-element.61.mine), channel_id=1, source_target_pairs={{0,32},{32,0},{1,33},{33,1},{2,34},{34,2},{3,35},{35,3},{4,36},{36... | collective-permute-start | bytes 98312 | tf_op jit(solution)/shard_map/ppermute | solution.py:489
  142.0 11.3 %all-to-all-start.7 = ((f32[8,32,128]{2,1,0:T(8,128)}), f32[8,32,128]{2,1,0:T(8,128)S(1)}, u32[]{:S(2)}, u32[]{:S(2)}) async-start(f32[8,32,128]{2,1,0:T(8,128)} %lower.5.refs_5_), calls=%async_computation.7 | async-start | bytes 262144 | tf_op jit(solution)/shard_map/all_to_all | solution.py:493

commit v4 on v3

--- a/solution.py
+++ b/solution.py
@@ -97,7 +97,9 @@
     return o0, second, jnp.where(o1 == 3, 4, 7)
 
 
-def prepare_kernel(scalars, order, basis, maps, skeletons, rhs, bases, chain, tail, wire):
+def prepare_kernel(
+    scalars, order, basis, maps, skeletons, rhs, bases, chain, tail, own, wire, second
+):
     both = stacked(basis[...])
     leaf = basis.shape[1]
     for t in range(leaf // TILE):
@@ -111,38 +113,14 @@
     p5 = dot(p3, e34, precision=HIGHEST)
     tail[...] = e34
     chain[...] = paired(jnp.concatenate([p1, p2, p3, p5], axis=1), 1)
-    own, middle, _ = moments(rhs[...], bases[...], chain[...])
-    _, k1, k2 = skeleton_offsets(scalars)
-    blocks = [packed(skeletons[h]) for h in range(3)]
+    first, middle, top = moments(rhs[...], bases[...], chain[...])
+    own[...] = first
+    last = jnp.concatenate([top, jnp.zeros_like(top)], axis=1)
     for i in range(wire.shape[0]):
-        offset = jnp.bitwise_xor(scalars[Z], i)
-        wire[i, 0:16, :] = own
-        wire[i, 16:32, :] = middle
-        block = jnp.where(offset == k1, blocks[1], blocks[0])
-        wire[i, 32:64, :] = jnp.where(offset == k2, blocks[2], block)
-
-
-def middle_kernel(scalars, received, tail, skeletons, after, low, out, second):
-    z, o0, o1, o2 = scalars[Z], scalars[O0], scalars[O1], scalars[O2]
-    left = lax.broadcasted_iota(jnp.int32, (16, 128), 1) < 64
-    sums = [jnp.zeros((16, 128), F32) for _ in range(2)]
-    for i in range(received.shape[0]):
-        offset = jnp.bitwise_xor(z, i)
-        hit0 = offset == o0
-        hit1 = offset // 2 == o1
-        hit2 = offset // 4 == jnp.bitwise_and(o2, 1)
-        sums[0] += jnp.where((left & hit0) | (~left & hit1), received[i, 0:16, :], 0.0)
-        sums[1] += jnp.where(~left | hit2, received[i, 16:32, :], 0.0)
-    low[...] = sums[0]
-    top = dot(sums[1][:, 64:128], tail[...], precision=HIGHEST)
-    last = jnp.concatenate([top, jnp.zeros_like(top)], axis=1)
-    for i in range(out.shape[0]):
-        out[i, 0:16, :] = sums[1]
-        out[i, 16:32, :] = last
-        out[i, 32:64, :] = packed(skeletons[3])
-    k2 = skeleton_offsets(scalars)[2]
-    across = received[jnp.bitwise_xor(z, k2), 32:64, :]
-    second[...] = jnp.where(o2 % 2 == 1, across, packed(skeletons[2]))
+        wire[i, 0:16, :] = middle
+        wire[i, 16:32, :] = last
+        wire[i, 32:64, :] = packed(skeletons[3])
+    second[...] = packed(skeletons[2])
 
 
 def matern(first, second):
@@ -172,19 +150,19 @@
     out[...] = paired(jnp.concatenate([matern(skeletons[3], partner), top], axis=1), 0)
 
 
-def low_kernel(scalars, skeletons, from_z, second, moved, chain, out):
+def low_couplings(scalars, skeletons, from_z, chain):
     z = scalars[Z]
-    second = jnp.where(scalars[O2] > 1, moved[...], second[...])
-    k0, k1, _ = skeleton_offsets(scalars)
     down = chain[:, 0:256].astype(F32) + chain[:, 256:512].astype(F32)
-    partners = [from_z[jnp.bitwise_xor(z, k), 32:64, :] for k in (k0, k1)] + [second]
     pieces = []
-    for h in range(3):
-        coupling = matern(skeletons[h], unpacked(partners[h]))
+    for h, offset in enumerate(skeleton_offsets(scalars)):
+        if h == 2:
+            offset = jnp.where(scalars[O2] % 2 == 1, offset, 0)
+        partner = unpacked(from_z[jnp.bitwise_xor(z, offset), 48:80, :])
+        coupling = matern(skeletons[h], partner)
         if h > 0:
             coupling = dot(down[:, (h - 1) * 64 : h * 64], coupling, precision=HIGHEST)
         pieces.append(coupling)
-    out[...] = paired(jnp.concatenate(pieces + [down[:, 128:192]], axis=1), 0)
+    return paired(jnp.concatenate(pieces + [down[:, 128:192]], axis=1), 0)
 
 
 def three(a):
@@ -312,17 +290,13 @@
     high[...] = total
 
 
-def field_at_three(high, mine, other, table):
+def lower_kernel(high, mine, other, table, own, *refs):
+    out = refs[-1]
+    start = own.shape[1] - 128
     parts = [high[:, 64:128]]
     for side in (mine, other):
         parts += [side[j * 16 : (j + 1) * 16, 0:64] for j in range(4)]
-    return times_t(jnp.concatenate(parts, axis=1), table[...])
-
-
-def lower_kernel(high, mine, other, table, own, *refs):
-    out = refs[-1]
-    start = own.shape[1] - 128
-    field = field_at_three(high, mine, other, table)
+    field = times_t(jnp.concatenate(parts, axis=1), table[...])
     norm = sum(side[j * 16 : (j + 1) * 16, 64:128] for side in (mine, other) for j in range(4))
     first = jnp.concatenate([field, norm], axis=1)
     second = jnp.concatenate([own[:, start + 64 :], high[:, 0:64]], axis=1)
@@ -331,31 +305,42 @@
         out[i, 16:32, :] = second
 
 
-def add_far(moments_in, table, bases, near):
-    pair = stacked(times_t(moments_in, table[...]))
-    far = halves(dot(pair, bases[0:64, :]) + dot(pair, bases[64:128, :]))
-    return near[:, 0 : far.shape[1]] + far
+def first_lower_kernel(scalars, high, mine, other, table, own, skeletons, second, moved, out):
+    lower_kernel(high, mine, other, table, own, out)
+    _, k1, k2 = skeleton_offsets(scalars)
+    third = jnp.where(scalars[O2] > 1, moved[...], second[...])
+    blocks = [packed(skeletons[0]), packed(skeletons[1]), third]
+    for i in range(out.shape[0]):
+        offset = jnp.bitwise_xor(scalars[Z], i)
+        block = jnp.where(offset == k1, blocks[1], blocks[0])
+        out[i, 32:48, :] = own[...]
+        out[i, 48:80, :] = jnp.where((offset == k2) | (offset == 0), blocks[2], block)
 
 
 def apply_far(scalars, received, table, bases, near):
     leaf = bases.shape[1]
-    z, o1, o2 = scalars[Z], scalars[O1], scalars[O2]
+    z, o0, o1, o2 = scalars[Z], scalars[O0], scalars[O1], scalars[O2]
     left = lax.broadcasted_iota(jnp.int32, (16, 128), 1) < 64
-    sums = [jnp.zeros((16, 128), F32) for _ in range(2)]
+    sums = [jnp.zeros((16, 128), F32) for _ in range(3)]
     for i in range(received.shape[0]):
         offset = jnp.bitwise_xor(z, i)
         hit1 = offset // 2 == o1
         hit2 = offset // 4 == jnp.bitwise_and(o2, 1)
         sums[0] += received[i, 0:16, :]
         sums[1] += jnp.where((left & hit1) | (~left & hit2), received[i, 16:32, :], 0.0)
-    parts = [near[:, leaf : leaf + 64], sums[1], sums[0][:, 0:64]]
-    return add_far(jnp.concatenate(parts, axis=1), table, bases, near), sums[0][:, 64:65]
-
-
-def first_kernel(low, high, mine, other, top_table, table, bases, near, chain, v1, out):
-    field = field_at_three(high, mine, other, top_table)
-    parts = [low[...], high[:, 0:64], field]
-    image = add_far(jnp.concatenate(parts, axis=1), table, bases, near)
+        if received.shape[1] > 32:
+            sums[2] += jnp.where(offset == o0, received[i, 32:48, :], 0.0)
+    moment = sums[2] if received.shape[1] > 32 else near[:, leaf : leaf + 128]
+    parts = [moment[:, 0:64], sums[1], sums[0][:, 0:64]]
+    field = times_t(jnp.concatenate(parts, axis=1), table[...])
+    pair = stacked(field)
+    far = halves(dot(pair, bases[0:64, :]) + dot(pair, bases[64:128, :]))
+    return near[:, 0:leaf] + far, sums[0][:, 64:65]
+
+
+def first_kernel(scalars, received, skeletons, bases, near, chain, table, v1, out):
+    table[...] = low_couplings(scalars, skeletons, received, chain)
+    image, _ = apply_far(scalars, received, table, bases, near)
     write_moments(v1, out, image, image, bases, chain)
 
 
@@ -387,23 +372,14 @@
     fresh[...] = jnp.broadcast_to(norm, fresh.shape)
     share = jnp.sum(new * new, axis=1, keepdims=True)
     line = jnp.sum(jnp.where(diagonal(), share, 0.0), axis=0, keepdims=True)
-    for i in range(out.shape[0]):
-        out[i] = jnp.broadcast_to(line, (8, 128))
-
-
-def spread_kernel(received, out):
-    total = received[0]
-    for i in range(1, received.shape[0]):
-        total = total + received[i]
-    for i in range(out.shape[0]):
-        out[i] = total
+    out[...] = jnp.broadcast_to(line, out.shape)
 
 
 def last_kernel(shares, rhs, v1, v2, image, along, sums, fresh, step, iterate, residual):
     leaf = rhs.shape[1]
     norm = fresh[:, 0:1]
     first = step[:, 0:1]
-    line = sum(shares[i, 0:1, :] for i in range(shares.shape[0]))
+    line = jnp.sum(shares[...], axis=0, keepdims=True)
     second = norm / jnp.sum(jnp.where(diagonal(), line, 0.0), axis=1, keepdims=True)
     beta = norm / sums[:, 0:1]
     start = v1[:, 0:leaf]
@@ -424,9 +400,12 @@
 
 
 def call(kernel, outs, scalars, arrays, name, after=(), limit=16, flops=100000, scratch=(), alias=None):
-    body = kernel
-    if scalars:
-        body = lambda far, *refs: kernel(places(far), *refs)
+    def body(*refs):
+        if scalars:
+            kernel(places(refs[0]), *refs[1:])
+        else:
+            kernel(*refs)
+
     return pl.pallas_call(
         body,
         out_shape=outs,
@@ -523,13 +502,15 @@
     one = along_z(both, 1)
     two = along_z(both, 2)
     three_off = along_z(two, 1)
-    bases, chain, tail, outgoing = call(
+    bases, chain, tail, own, outgoing, second = call(
         prepare_kernel,
         (
             shaped(128, 1024, dtype=BF16),
             shaped(64, 512, dtype=BF16),
             shaped(64, 64),
-            shaped(8, 64, 128),
+            thin,
+            shaped(16, 64, 128),
+            shaped(32, 128),
         ),
         [scalars],
         [leaf_order, basis, transfer_maps[:, 0], chain_skeletons, rhs],
@@ -543,30 +524,10 @@
         )
         return high, mine, other_core(mine)
 
-    from_z = over_z(outgoing)
     kernels, near = build(scalars, both, [], None, None, [two], "build_own")
-    low, outgoing, second = call(
-        middle_kernel,
-        (thin, shaped(16, 64, 128), shaped(32, 128)),
-        [scalars],
-        [from_z, tail, chain_skeletons],
-        "middle",
-        after=[near],
-    )
     from_yx = over_yx(outgoing)
-    moved = lax.ppermute(second, "x", [(i, i ^ 1) for i in range(4)])
-    kernels, near = build(
-        scalars, both, [two, one], 1, near, [low, three_off], "build_a", [kernels]
-    )
-    kernels, near = build(scalars, both, [two, three_off], 3, near, [low], "build_b", [kernels])
-    table = call(
-        low_kernel,
-        shaped(128, 256, dtype=BF16),
-        [scalars],
-        [chain_skeletons, from_z, second, moved, chain],
-        "couplings",
-    )
-    spread = gather(from_yx, [near, table])
+    second_moved = lax.ppermute(second, "x", [(i, i ^ 1) for i in range(4)])
+    spread = gather(from_yx, [near])
     top_table = call(
         top_kernel,
         shaped(128, 576, dtype=BF16),
@@ -574,11 +535,24 @@
         [chain_skeletons, from_yx, tops, tail],
         "tops",
     )
-    v1, outgoing = call(
+    outgoing = call(
+        first_lower_kernel,
+        shaped(8, 80, 128),
+        [scalars],
+        [*spread, top_table, own, chain_skeletons, second, second_moved],
+        "lower",
+    )
+    kernels, near = build(
+        scalars, both, [two, one], 1, near, [outgoing], "build_a", [kernels]
+    )
+    kernels, near = build(
+        scalars, both, [two, three_off], 3, near, [outgoing], "build_b", [kernels]
+    )
+    table, v1, outgoing = call(
         first_kernel,
-        (long, wire),
-        [],
-        [low, *spread, top_table, table, bases, near, chain],
+        (shaped(128, 256, dtype=BF16), long, wire),
+        [scalars],
+        [over_z(outgoing), chain_skeletons, bases, near, chain],
         "first",
     )
 
@@ -608,14 +582,12 @@
     )
     along, fresh, outgoing = call(
         fourth_kernel,
-        (row, thin, shaped(32, 8, 128)),
+        (row, thin, shaped(256, 128)),
         [scalars],
         [*operate(image, outgoing), v2, sums],
         "fourth",
     )
-    received = lax.all_to_all(outgoing, ("x", "z"), 0, 0)
-    wide = call(spread_kernel, shaped(8, 8, 128), [], [received], "spread")
-    shares = lax.all_to_all(wide, ("y", "core"), 0, 0)
+    shares = lax.all_to_all(outgoing, ("y", "core", "x", "z"), 0, 0, tiled=True)
     return call(
         last_kernel,
         (row, row),

time: 182 us -> 174 us (0.956)
  starting transfers between devices: 77.3 us -> 68.8 us
  waiting for transfers between devices: 24.1 us -> 28.6 us
  blocking collectives: 25.2 us -> 21.7 us
    ppermute x12, starting transfers between devices: 23.3 us -> 18.2 us  [along_z(): return lax.ppermute(v, 'z', [(i, i ^ offset) for i in range(8)])]
    all_to_all x4, starting transfers between devices: 20.4 us -> 15.7 us  [over_z(): return lax.all_to_all(v, 'z', 0, 0)]
    all_to_all x4, waiting for transfers between devices: 10.2 us -> 13.9 us  [over_yx(): return lax.all_to_all(v, ('y', 'x'), 0, 0)]
    all_to_all x2 -> x1, blocking collectives: 25.2 us -> 21.7 us  [local(): shares = lax.all_to_all(outgoing, ('y', 'core', 'x', 'z'), 0, 0, tiled=True)]
    ppermute x4, starting transfers between devices: 11.4 us -> 14.7 us  [other_core(): return lax.ppermute(v, 'core', [(0, 1), (1, 0)])]
    ppermute x12, waiting for transfers between devices: 5.07 us -> 1.8 us  [along_z(): return lax.ppermute(v, 'z', [(i, i ^ offset) for i in range(8)])]
    all_to_all x4, waiting for transfers between devices: 7.15 us -> 10.3 us  [over_z(): return lax.all_to_all(v, 'z', 0, 0)]
    pallas_call x23 -> x21, Pallas kernels: 50.3 us -> 49.8 us  [call(): pl.pallas_call(body, out_shape=outs, in_specs=[SMEM] * len(scalars) + [VM...]
  transfers between devices with their start and end apart: 25 -> 25, of which waited for: 11 -> 12; matrix products, arithmetic and copies ran while one was open for 0% -> 0% of each run, Pallas kernels for 21% -> 22%
where the time goes in v4:
time: 174 us; the launch traced here: 173 us
  starting transfers between devices  68.8 us (40%)
  Pallas kernels  49.8 us (29%)
  waiting for transfers between devices  28.6 us (16%)
  blocking collectives  21.7 us (12%)
  local copies, waits for them, and re-layouts  2.76 us (2%)
    pallas_call x21, Pallas kernels, call(): pl.pallas_call(body, out_shape=outs, in_specs=[SMEM] * len(scalars) + [VM...  49.8 us
    all_to_all x1, blocking collectives, local(): shares = lax.all_to_all(outgoing, ('y', 'core', 'x', 'z'), 0, 0, tiled=True)  21.7 us
    all_to_all x4, starting transfers between devices, over_yx(): return lax.all_to_all(v, ('y', 'x'), 0, 0)  19.9 us
    ppermute x12, starting transfers between devices, along_z(): return lax.ppermute(v, 'z', [(i, i ^ offset) for i in range(8)])  18.2 us
    all_to_all x4, starting transfers between devices, over_z(): return lax.all_to_all(v, 'z', 0, 0)  15.7 us
    ppermute x4, starting transfers between devices, other_core(): return lax.ppermute(v, 'core', [(0, 1), (1, 0)])  14.7 us
    all_to_all x4, waiting for transfers between devices, over_yx(): return lax.all_to_all(v, ('y', 'x'), 0, 0)  13.9 us
    all_to_all x4, waiting for transfers between devices, over_z(): return lax.all_to_all(v, 'z', 0, 0)  10.3 us
  transfers between devices with their start and end apart: 25, of which 12 were waited for; matrix products, arithmetic and copies ran while one was open for 0% of the time, Pallas kernels for 22%

profile of v4, /device:TPU:1, one launch (start us, length us, event | category | flops | bytes accessed | tf_op | source)
XLA Modules:
  0.0 172.6 jit_solution(8388767811044131813)
XLA Ops:
  0.7 1.0 constant_dynamic-update-slice_fusion.1
  2.5 3.8 %collective-permute-start = (f32[80,1024]{1,0:T(8,128)S(1)}, f32[80,1024]{1,0:T(8,128)S(1)}, u32[]{:S(2)}, u32[]{:S(2)}) collective-permute-start(f32[80,1024]{1,0:T(8,128)S(1)} %constant_dynamic-update-slice_fusion.refs_1_), channel_id=1, source_target_pairs={{0,2},{1,3},{2,0},{3,1},{4,6},{5,7},{6,4},{7,5},{8,10},{9,11},{10,... | collective-permute-start | bytes 983048 | tf_op jit(solution)/shard_map/ppermute | solution.py:464
  6.4 3.3 %prepare.1 = (bf16[128,1024]{1,0:T(8,128)(2,1)}, bf16[64,512]{1,0:T(8,128)(2,1)}, f32[64,64]{1,0:T(8,128)}, f32[16,128]{1,0:T(8,128)}, f32[16,64,128]{2,1,0:T(8,128)}, /*index=5*/f32[32,128]{1,0:T(8,128)}) custom-call(s32[4]{0:T(128)} %bitcast.15, s32[1,1024]{1,0:T(1,128)} %refs_1_.2, f32[64,1024]{1,0:T(8,128)} %refs_2_.1, f32[5,64,64]{2,1,0:T(8,128)} %bitcast.32, ...), custom_call_target="tpu_custom_call" | custom-call | flops 100000 | bytes 500000 | tf_op jit(solution)/shard_map/prepare/pallas_call | solution.py:409
  9.7 6.9 %all-to-all-start = ((f32[16,64,128]{2,1,0:T(8,128)}), f32[16,64,128]{2,1,0:T(8,128)S(1)}, u32[]{:S(2)}, u32[]{:S(2)}) async-start(f32[16,64,128]{2,1,0:T(8,128)} %get-tuple-element.35), calls=%async_computation | async-start | bytes 1048576 | tf_op jit(solution)/shard_map/all_to_all | solution.py:476
  16.6 1.7 %collective-permute-start.4 = (f32[80,1024]{1,0:T(8,128)S(1)}, f32[80,1024]{1,0:T(8,128)S(1)}, u32[]{:S(2)}, u32[]{:S(2)}) collective-permute-start(f32[80,1024]{1,0:T(8,128)S(1)} %constant_dynamic-update-slice_fusion.refs_1_), channel_id=1, source_target_pairs={{0,1},{1,0},{2,3},{3,2},{4,5},{5,4},{6,7},{7,6},{8,9},{9,8},{10,11... | collective-permute-start | bytes 983048 | tf_op jit(solution)/shard_map/ppermute | solution.py:464
  18.4 1.8 %collective-permute-done.refs_2_ = f32[80,1024]{1,0:T(8,128)S(1)} collective-permute-done((f32[80,1024]{1,0:T(8,128)S(1)}, f32[80,1024]{1,0:T(8,128)S(1)}, u32[]{:S(2)}, u32[]{:S(2)}) %collective-permute-start) | collective-permute-done | bytes 327712 | tf_op jit(solution)/shard_map/ppermute | solution.py:464
  20.8 4.1 %build_own.1 = (bf16[3,2,1024,1024]{3,2,1,0:T(8,128)(2,1)}, f32[16,1024]{1,0:T(8,128)S(1)}) custom-call(s32[4]{0:T(128)S(1)} %bitcast.16, f32[80,1024]{1,0:T(8,128)S(1)} %constant_dynamic-update-slice_fusion.refs_1_, f32[80,1024]{1,0:T(8,128)S(1)} %collective-permute-done.refs_2_), custom_call_target="tpu_custom_call" | custom-call | flops 4000000000 | bytes 500000 | tf_op jit(solution)/shard_map/build_own/pallas_call | solution.py:409
  24.9 2.1 %all-to-all-done.refs_1_.refs_3_ = f32[16,64,128]{2,1,0:T(8,128)S(1)} async-done(((f32[16,64,128]{2,1,0:T(8,128)}), f32[16,64,128]{2,1,0:T(8,128)S(1)}, u32[]{:S(2)}, u32[]{:S(2)}) %all-to-all-start) | async-done | bytes 524320 | tf_op jit(solution)/shard_map/all_to_all | solution.py:476
  27.6 2.2 %collective-permute-start.1 = (f32[64,128]{1,0:T(8,128)S(1)}, f32[64,128]{1,0:T(8,128)S(1)}, u32[]{:S(2)}, u32[]{:S(2)}) collective-permute-start(f32[64,128]{1,0:T(8,128)S(1)} %get-tuple-element.38.refs_2_), channel_id=1, source_target_pairs={{0,32},{32,0},{1,33},{33,1},{2,34},{34,2},{3,35},{35,3},{4,36},{36... | collective-permute-start | bytes 98312 | tf_op jit(solution)/shard_map/ppermute | solution.py:468
  30.3 1.7 collective-permute-start.3
  32.1 1.3 tops.1.refs_4_.refs_3_
  33.4 1.6 lower.4.refs_5_
  34.9 5.5 %all-to-all-start.1 = ((f32[8,80,128]{2,1,0:T(8,128)}), f32[8,80,128]{2,1,0:T(8,128)S(1)}, u32[]{:S(2)}, u32[]{:S(2)}) async-start(f32[8,80,128]{2,1,0:T(8,128)} %lower.4.refs_5_), calls=%async_computation.1 | async-start | bytes 655360 | tf_op jit(solution)/shard_map/all_to_all | solution.py:472
  40.5 4.2 %build_a.1 = (bf16[3,2,1024,1024]{3,2,1,0:T(8,128)(2,1)}, f32[16,1024]{1,0:T(8,128)S(1)}) custom-call(s32[4]{0:T(128)S(1)} %bitcast.20, f32[80,1024]{1,0:T(8,128)S(1)} %constant_dynamic-update-slice_fusion.refs_1_, f32[80,1024]{1,0:T(8,128)S(1)} %collective-permute-done.refs_2_, ...), custom_call_target="tpu_custom_call", output_to_operand_aliasing={{0}: (6, {})} | custom-call | flops 4000000000 | bytes 500000 | tf_op jit(solution)/shard_map/build_a/pallas_call | solution.py:409
  44.7 4.2 %build_b.1 = (bf16[3,2,1024,1024]{3,2,1,0:T(8,128)(2,1)}, f32[16,1024]{1,0:T(8,128)S(1)}) custom-call(s32[4]{0:T(128)S(1)} %bitcast.21, f32[80,1024]{1,0:T(8,128)S(1)} %constant_dynamic-update-slice_fusion.refs_1_, f32[80,1024]{1,0:T(8,128)S(1)} %collective-permute-done.refs_2_, ...), custom_call_target="tpu_custom_call", output_to_operand_aliasing={{0}: (6, {})} | custom-call | flops 4000000000 | bytes 500000 | tf_op jit(solution)/shard_map/build_b/pallas_call | solution.py:409
  48.8 2.7 %all-to-all-done.1.refs_1_ = f32[8,80,128]{2,1,0:T(8,128)S(1)} async-done(((f32[8,80,128]{2,1,0:T(8,128)}), f32[8,80,128]{2,1,0:T(8,128)S(1)}, u32[]{:S(2)}, u32[]{:S(2)}) %all-to-all-start.1) | async-done | bytes 327712 | tf_op jit(solution)/shard_map/all_to_all | solution.py:472
  51.6 2.7 %first.1 = (bf16[128,256]{1,0:T(8,128)(2,1)S(1)}, f32[16,1152]{1,0:T(8,128)S(1)}, f32[16,32,128]{2,1,0:T(8,128)}) custom-call(s32[4]{0:T(128)S(1)} %bitcast.22, f32[8,80,128]{2,1,0:T(8,128)S(1)} %all-to-all-done.1.refs_1_, f32[4,64,64]{2,1,0:T(8,128)S(1)} %bitcast.11, bf16[128,1024]{1,0:T(8,128)(2,1)S(1)} %copy-done.1, ...), custom_call_target="tpu_custom_call" | custom-call | flops 100000 | bytes 500000 | tf_op jit(solution)/shard_map/first/pallas_call | solution.py:409
  54.3 6.0 %all-to-all-start.2 = ((f32[16,32,128]{2,1,0:T(8,128)}), f32[16,32,128]{2,1,0:T(8,128)S(1)}, u32[]{:S(2)}, u32[]{:S(2)}) async-start(f32[16,32,128]{2,1,0:T(8,128)} %get-tuple-element.48), calls=%async_computation.2 | async-start | bytes 524288 | tf_op jit(solution)/shard_map/all_to_all | solution.py:476
  60.4 1.0 collective-permute-start.7
  61.4 2.5 %collective-permute-start.8 = (f32[16,1152]{1,0:T(8,128)S(1)}, f32[16,1152]{1,0:T(8,128)S(1)}, u32[]{:S(2)}, u32[]{:S(2)}) collective-permute-start(f32[16,1152]{1,0:T(8,128)S(1)} %get-tuple-element.51.refs_4_.refs_1_.refs_6_.refs_2_), channel_id=1, source_target_pairs={{0,3},{1,2},{2,1},{3,0},{4,7},{5,6},{6,5},{7,4},{8,11},{9,10},{10,... | collective-permute-start | bytes 221192 | tf_op jit(solution)/shard_map/ppermute | solution.py:464
  63.9 3.9 %all-to-all-done.2.refs_1_ = f32[16,32,128]{2,1,0:T(8,128)S(1)} async-done(((f32[16,32,128]{2,1,0:T(8,128)}), f32[16,32,128]{2,1,0:T(8,128)S(1)}, u32[]{:S(2)}, u32[]{:S(2)}) %all-to-all-start.2) | async-done | bytes 262176 | tf_op jit(solution)/shard_map/all_to_all | solution.py:476
  68.4 4.5 %collective-permute-start.5 = (f32[64,128]{1,0:T(8,128)S(1)}, f32[64,128]{1,0:T(8,128)S(1)}, u32[]{:S(2)}, u32[]{:S(2)}) collective-permute-start(f32[64,128]{1,0:T(8,128)S(1)} %get-tuple-element.50.refs_1_), channel_id=1, source_target_pairs={{0,32},{32,0},{1,33},{33,1},{2,34},{34,2},{3,35},{35,3},{4,36},{36... | collective-permute-start | bytes 98312 | tf_op jit(solution)/shard_map/ppermute | solution.py:468
  73.8 0.9 lower.5.refs_6_
  74.7 3.4 %all-to-all-start.3 = ((f32[8,32,128]{2,1,0:T(8,128)}), f32[8,32,128]{2,1,0:T(8,128)S(1)}, u32[]{:S(2)}, u32[]{:S(2)}) async-start(f32[8,32,128]{2,1,0:T(8,128)} %lower.5.refs_6_), calls=%async_computation.3 | async-start | bytes 262144 | tf_op jit(solution)/shard_map/all_to_all | solution.py:472
  78.1 5.5 %near.3.refs_4_ = f32[16,1152]{1,0:T(8,128)S(1)} custom-call(s32[4]{0:T(128)S(1)} %bitcast.24, f32[16,1152]{1,0:T(8,128)S(1)} %get-tuple-element.51.refs_4_.refs_1_.refs_6_.refs_2_, f32[16,1152]{1,0:T(8,128)S(1)} %collective-permute-done.6.refs_5_.refs_2_, f32[16,1152]{1,0:T(8,128)S(1)} %collective-permute-done.7.refs_6_.refs_3_, ...), custom_call_target="tpu_custom_call" | custom-call | flops 4000000000 | bytes 500000 | tf_op jit(solution)/shard_map/near/pallas_call | solution.py:409
  83.7 2.8 %all-to-all-done.3.refs_1_ = f32[8,32,128]{2,1,0:T(8,128)S(1)} async-done(((f32[8,32,128]{2,1,0:T(8,128)}), f32[8,32,128]{2,1,0:T(8,128)S(1)}, u32[]{:S(2)}, u32[]{:S(2)}) %all-to-all-start.3) | async-done | bytes 131104 | tf_op jit(solution)/shard_map/all_to_all | solution.py:472
  86.5 2.3 %second.1 = (f32[16,1024]{1,0:T(8,128)S(1)}, f32[16,1152]{1,0:T(8,128)S(1)}, f32[16,128]{1,0:T(8,128)S(1)}, f32[16,32,128]{2,1,0:T(8,128)}) custom-call(s32[4]{0:T(128)S(1)} %bitcast.25, f32[8,32,128]{2,1,0:T(8,128)S(1)} %all-to-all-done.3.refs_1_, bf16[128,256]{1,0:T(8,128)(2,1)S(1)} %get-tuple-element.52.refs_2_, bf16[128,1024]{1,0:T(8,128)(2,1)S(1)} %copy-done.1, ...), custom_call_target="tpu_custom_call" | custom-call | flops 100000 | bytes 500000 | tf_op jit(solution)/shard_map/second/pallas_call | solution.py:409
  88.8 3.5 %all-to-all-start.4 = ((f32[16,32,128]{2,1,0:T(8,128)}), f32[16,32,128]{2,1,0:T(8,128)S(1)}, u32[]{:S(2)}, u32[]{:S(2)}) async-start(f32[16,32,128]{2,1,0:T(8,128)} %get-tuple-element.54), calls=%async_computation.4 | async-start | bytes 524288 | tf_op jit(solution)/shard_map/all_to_all | solution.py:476
  93.3 2.7 %collective-permute-start.12 = (f32[16,1152]{1,0:T(8,128)S(1)}, f32[16,1152]{1,0:T(8,128)S(1)}, u32[]{:S(2)}, u32[]{:S(2)}) collective-permute-start(f32[16,1152]{1,0:T(8,128)S(1)} %get-tuple-element.57.refs_4_.refs_1_), channel_id=1, source_target_pairs={{0,3},{1,2},{2,1},{3,0},{4,7},{5,6},{6,5},{7,4},{8,11},{9,10},{10,... | collective-permute-start | bytes 221192 | tf_op jit(solution)/shard_map/ppermute | solution.py:464
  95.9 4.0 %all-to-all-done.4.refs_1_ = f32[16,32,128]{2,1,0:T(8,128)S(1)} async-done(((f32[16,32,128]{2,1,0:T(8,128)}), f32[16,32,128]{2,1,0:T(8,128)S(1)}, u32[]{:S(2)}, u32[]{:S(2)}) %all-to-all-start.4) | async-done | bytes 262176 | tf_op jit(solution)/shard_map/all_to_all | solution.py:476
  100.6 3.8 %collective-permute-start.9 = (f32[64,128]{1,0:T(8,128)S(1)}, f32[64,128]{1,0:T(8,128)S(1)}, u32[]{:S(2)}, u32[]{:S(2)}) collective-permute-start(f32[64,128]{1,0:T(8,128)S(1)} %get-tuple-element.56.refs_1_), channel_id=1, source_target_pairs={{0,32},{32,0},{1,33},{33,1},{2,34},{34,2},{3,35},{35,3},{4,36},{36... | collective-permute-start | bytes 98312 | tf_op jit(solution)/shard_map/ppermute | solution.py:468
  105.2 0.9 lower.6.refs_6_
  106.1 3.4 %all-to-all-start.5 = ((f32[8,32,128]{2,1,0:T(8,128)}), f32[8,32,128]{2,1,0:T(8,128)S(1)}, u32[]{:S(2)}, u32[]{:S(2)}) async-start(f32[8,32,128]{2,1,0:T(8,128)} %lower.6.refs_6_), calls=%async_computation.5 | async-start | bytes 262144 | tf_op jit(solution)/shard_map/all_to_all | solution.py:472
  109.5 5.5 %near.4.refs_4_ = f32[16,1152]{1,0:T(8,128)S(1)} custom-call(s32[4]{0:T(128)S(1)} %bitcast.27, f32[16,1152]{1,0:T(8,128)S(1)} %get-tuple-element.57.refs_4_.refs_1_, f32[16,1152]{1,0:T(8,128)S(1)} %collective-permute-done.10.refs_5_.refs_2_, f32[16,1152]{1,0:T(8,128)S(1)} %collective-permute-done.11.refs_6_.refs_3_, ...), custom_call_target="tpu_custom_call" | custom-call | flops 4000000000 | bytes 500000 | tf_op jit(solution)/shard_map/near/pallas_call | solution.py:409
  115.1 2.4 %all-to-all-done.5.refs_1_ = f32[8,32,128]{2,1,0:T(8,128)S(1)} async-done(((f32[8,32,128]{2,1,0:T(8,128)}), f32[8,32,128]{2,1,0:T(8,128)S(1)}, u32[]{:S(2)}, u32[]{:S(2)}) %all-to-all-start.5) | async-done | bytes 131104 | tf_op jit(solution)/shard_map/all_to_all | solution.py:472
  117.5 2.3 %third.1 = (f32[16,1152]{1,0:T(8,128)S(1)}, f32[16,128]{1,0:T(8,128)S(1)}, f32[16,32,128]{2,1,0:T(8,128)}) custom-call(s32[4]{0:T(128)S(1)} %bitcast.28, f32[8,32,128]{2,1,0:T(8,128)S(1)} %all-to-all-done.5.refs_1_, bf16[128,256]{1,0:T(8,128)(2,1)S(1)} %get-tuple-element.52.refs_2_, bf16[128,1024]{1,0:T(8,128)(2,1)S(1)} %copy-done.1, ...), custom_call_target="tpu_custom_call" | custom-call | flops 100000 | bytes 500000 | tf_op jit(solution)/shard_map/third/pallas_call | solution.py:409
  119.8 3.5 %all-to-all-start.6 = ((f32[16,32,128]{2,1,0:T(8,128)}), f32[16,32,128]{2,1,0:T(8,128)S(1)}, u32[]{:S(2)}, u32[]{:S(2)}) async-start(f32[16,32,128]{2,1,0:T(8,128)} %get-tuple-element.59), calls=%async_computation.6 | async-start | bytes 524288 | tf_op jit(solution)/shard_map/all_to_all | solution.py:476
  123.5 1.1 collective-permute-start.15
  124.6 2.4 %collective-permute-start.16 = (f32[16,1152]{1,0:T(8,128)S(1)}, f32[16,1152]{1,0:T(8,128)S(1)}, u32[]{:S(2)}, u32[]{:S(2)}) collective-permute-start(f32[16,1152]{1,0:T(8,128)S(1)} %get-tuple-element.62.refs_4_.refs_1_), channel_id=1, source_target_pairs={{0,3},{1,2},{2,1},{3,0},{4,7},{5,6},{6,5},{7,4},{8,11},{9,10},{10,... | collective-permute-start | bytes 221192 | tf_op jit(solution)/shard_map/ppermute | solution.py:464
  126.9 3.9 %all-to-all-done.6.refs_1_ = f32[16,32,128]{2,1,0:T(8,128)S(1)} async-done(((f32[16,32,128]{2,1,0:T(8,128)}), f32[16,32,128]{2,1,0:T(8,128)S(1)}, u32[]{:S(2)}, u32[]{:S(2)}) %all-to-all-start.6) | async-done | bytes 262176 | tf_op jit(solution)/shard_map/all_to_all | solution.py:476
  131.5 4.2 %collective-permute-start.13 = (f32[64,128]{1,0:T(8,128)S(1)}, f32[64,128]{1,0:T(8,128)S(1)}, u32[]{:S(2)}, u32[]{:S(2)}) collective-permute-start(f32[64,128]{1,0:T(8,128)S(1)} %get-tuple-element.61.refs_1_), channel_id=1, source_target_pairs={{0,32},{32,0},{1,33},{33,1},{2,34},{34,2},{3,35},{35,3},{4,36},{36... | collective-permute-start | bytes 98312 | tf_op jit(solution)/shard_map/ppermute | solution.py:468
  136.6 0.9 lower.7.refs_6_
  137.5 3.4 %all-to-all-start.7 = ((f32[8,32,128]{2,1,0:T(8,128)}), f32[8,32,128]{2,1,0:T(8,128)S(1)}, u32[]{:S(2)}, u32[]{:S(2)}) async-start(f32[8,32,128]{2,1,0:T(8,128)} %lower.7.refs_6_), calls=%async_computation.7 | async-start | bytes 262144 | tf_op jit(solution)/shard_map/all_to_all | solution.py:472
  140.9 5.5 %near.5.refs_4_ = f32[16,1152]{1,0:T(8,128)S(1)} custom-call(s32[4]{0:T(128)S(1)} %bitcast.30, f32[16,1152]{1,0:T(8,128)S(1)} %get-tuple-element.62.refs_4_.refs_1_, f32[16,1152]{1,0:T(8,128)S(1)} %collective-permute-done.14.refs_5_.refs_2_, f32[16,1152]{1,0:T(8,128)S(1)} %collective-permute-done.15.refs_6_.refs_3_, ...), custom_call_target="tpu_custom_call" | custom-call | flops 4000000000 | bytes 500000 | tf_op jit(solution)/shard_map/near/pallas_call | solution.py:409
  146.5 2.4 %all-to-all-done.7.refs_1_ = f32[8,32,128]{2,1,0:T(8,128)S(1)} async-done(((f32[8,32,128]{2,1,0:T(8,128)}), f32[8,32,128]{2,1,0:T(8,128)S(1)}, u32[]{:S(2)}, u32[]{:S(2)}) %all-to-all-start.7) | async-done | bytes 131104 | tf_op jit(solution)/shard_map/all_to_all | solution.py:472
  148.9 1.2 fourth.1
  150.0 21.7 %all_to_all.51 = f32[256,1,128]{2,1,0:T(1,128)S(1)} all-to-all(f32[256,1,128]{2,1,0:T(1,128)S(1)} %bitcast.14), channel_id=1, replica_groups=mesh['y'=4,'core'=2,'x'=4,'z'=8] {'y','core','x','z'}, dimensions={0} | all-to-all | bytes 262144 | tf_op jit(solution)/shard_map/all_to_all | solution.py:590
  171.8 0.9 last.1
  (49 shorter events, 8.3 us)
Async XLA Ops:
  0.6 29.5 %copy-start = (s32[8,4]{0,1:T(4,128)S(1)}, s32[8,4]{0,1:T(4,128)}, u32[]{:S(2)}) copy-start(s32[8,4]{0,1:T(4,128)} %param.18) | copy-start | bytes 388
  0.6 39.8 %copy-start.7 = (s32[4,1]{0,1:T(1,128)S(1)}, s32[4,1]{0,1:T(1,128)}, u32[]{:S(2)}) copy-start(s32[4,1]{0,1:T(1,128)} %param.17) | copy-start | bytes 52
  0.7 31.4 %copy-start.2 = (f32[4,1,64,64]{3,2,1,0:T(8,128)S(1)}, f32[4,1,64,64]{3,2,1,0:T(8,128)}, u32[]{:S(2)}) copy-start(f32[4,1,64,64]{3,2,1,0:T(8,128)} %param.15) | copy-start | bytes 196612
  0.7 31.4 %copy-start.5 = (f32[8,64,64]{2,1,0:T(8,128)S(1)}, f32[8,64,64]{2,1,0:T(8,128)}, u32[]{:S(2)}) copy-start(f32[8,64,64]{2,1,0:T(8,128)} %param.16) | copy-start | bytes 393220
  2.5 17.6 %collective-permute-start = (f32[80,1024]{1,0:T(8,128)S(1)}, f32[80,1024]{1,0:T(8,128)S(1)}, u32[]{:S(2)}, u32[]{:S(2)}) collective-permute-start(f32[80,1024]{1,0:T(8,128)S(1)} %constant_dynamic-update-slice_fusion.refs_1_), channel_id=1, source_target_pairs={{0,2},{1,3},{2,0},{3,1},{4,6},{5,7},{6,4},{7,5},{8,10},{9,11},{10,... | collective-permute-start | bytes 983048 | tf_op jit(solution)/shard_map/ppermute | solution.py:464
  9.7 20.1 %copy-start.9 = (f32[32,128]{1,0:T(8,128)S(1)}, f32[32,128]{1,0:T(8,128)}, u32[]{:S(2)}) copy-start(f32[32,128]{1,0:T(8,128)} %get-tuple-element.41.refs_7_) | copy-start | bytes 49156
  9.7 22.3 %copy-start.8 = (f32[64,64]{1,0:T(8,128)S(1)}, f32[64,64]{1,0:T(8,128)}, u32[]{:S(2)}) copy-start(f32[64,64]{1,0:T(8,128)} %get-tuple-element.39.refs_5_) | copy-start | bytes 49156
  9.7 23.6 %copy-start.10 = (f32[16,128]{1,0:T(8,128)S(1)}, f32[16,128]{1,0:T(8,128)}, u32[]{:S(2)}) copy-start(f32[16,128]{1,0:T(8,128)} %get-tuple-element.40.refs_5_) | copy-start | bytes 24580
  9.7 17.3 %all-to-all-start = ((f32[16,64,128]{2,1,0:T(8,128)}), f32[16,64,128]{2,1,0:T(8,128)S(1)}, u32[]{:S(2)}, u32[]{:S(2)}) async-start(f32[16,64,128]{2,1,0:T(8,128)} %get-tuple-element.35), calls=%async_computation | async-start | bytes 1048576 | tf_op jit(solution)/shard_map/all_to_all | solution.py:476
  16.6 23.8 %collective-permute-start.4 = (f32[80,1024]{1,0:T(8,128)S(1)}, f32[80,1024]{1,0:T(8,128)S(1)}, u32[]{:S(2)}, u32[]{:S(2)}) collective-permute-start(f32[80,1024]{1,0:T(8,128)S(1)} %constant_dynamic-update-slice_fusion.refs_1_), channel_id=1, source_target_pairs={{0,1},{1,0},{2,3},{3,2},{4,5},{5,4},{6,7},{7,6},{8,9},{9,8},{10,11... | collective-permute-start | bytes 983048 | tf_op jit(solution)/shard_map/ppermute | solution.py:464
  20.1 0.7 copy-start.6
  27.6 5.7 %collective-permute-start.1 = (f32[64,128]{1,0:T(8,128)S(1)}, f32[64,128]{1,0:T(8,128)S(1)}, u32[]{:S(2)}, u32[]{:S(2)}) collective-permute-start(f32[64,128]{1,0:T(8,128)S(1)} %get-tuple-element.38.refs_2_), channel_id=1, source_target_pairs={{0,32},{32,0},{1,33},{33,1},{2,34},{34,2},{3,35},{35,3},{4,36},{36... | collective-permute-start | bytes 98312 | tf_op jit(solution)/shard_map/ppermute | solution.py:468
  29.8 3.5 %collective-permute-start.2 = (f32[32,128]{1,0:T(8,128)S(1)}, f32[32,128]{1,0:T(8,128)S(1)}, u32[]{:S(2)}, u32[]{:S(2)}) collective-permute-start(f32[32,128]{1,0:T(8,128)S(1)} %copy-done.9), channel_id=1, source_target_pairs={{0,8},{8,0},{16,24},{24,16},{1,9},{9,1},{17,25},{25,17},{2,10},{10... | collective-permute-start | bytes 49160 | tf_op jit(solution)/shard_map/ppermute | solution.py:529
  30.3 14.3 %collective-permute-start.3 = (f32[80,1024]{1,0:T(8,128)S(1)}, f32[80,1024]{1,0:T(8,128)S(1)}, u32[]{:S(2)}, u32[]{:S(2)}) collective-permute-start(f32[80,1024]{1,0:T(8,128)S(1)} %collective-permute-done.refs_2_), channel_id=1, source_target_pairs={{0,1},{1,0},{2,3},{3,2},{4,5},{5,4},{6,7},{7,6},{8,9},{9,8},{10,11... | collective-permute-start | bytes 983048 | tf_op jit(solution)/shard_map/ppermute | solution.py:464
  34.9 16.6 %all-to-all-start.1 = ((f32[8,80,128]{2,1,0:T(8,128)}), f32[8,80,128]{2,1,0:T(8,128)S(1)}, u32[]{:S(2)}, u32[]{:S(2)}) async-start(f32[8,80,128]{2,1,0:T(8,128)} %lower.4.refs_5_), calls=%async_computation.1 | async-start | bytes 655360 | tf_op jit(solution)/shard_map/all_to_all | solution.py:472
  40.4 11.1 %copy-start.1 = (bf16[128,1024]{1,0:T(8,128)(2,1)S(1)}, bf16[128,1024]{1,0:T(8,128)(2,1)}, u32[]{:S(2)}) copy-start(bf16[128,1024]{1,0:T(8,128)(2,1)} %get-tuple-element.42.refs_3_) | copy-start | bytes 786436
  40.4 11.1 %copy-start.3 = (bf16[64,512]{1,0:T(8,128)(2,1)S(1)}, bf16[64,512]{1,0:T(8,128)(2,1)}, u32[]{:S(2)}) copy-start(bf16[64,512]{1,0:T(8,128)(2,1)} %get-tuple-element.47.refs_5_) | copy-start | bytes 196612
  54.3 13.5 %all-to-all-start.2 = ((f32[16,32,128]{2,1,0:T(8,128)}), f32[16,32,128]{2,1,0:T(8,128)S(1)}, u32[]{:S(2)}, u32[]{:S(2)}) async-start(f32[16,32,128]{2,1,0:T(8,128)} %get-tuple-element.48), calls=%async_computation.2 | async-start | bytes 524288 | tf_op jit(solution)/shard_map/all_to_all | solution.py:476
  60.3 12.7 %collective-permute-start.6 = (f32[16,1152]{1,0:T(8,128)S(1)}, f32[16,1152]{1,0:T(8,128)S(1)}, u32[]{:S(2)}, u32[]{:S(2)}) collective-permute-start(f32[16,1152]{1,0:T(8,128)S(1)} %get-tuple-element.51.refs_4_.refs_1_.refs_6_.refs_2_), channel_id=1, source_target_pairs={{0,1},{1,0},{2,3},{3,2},{4,5},{5,4},{6,7},{7,6},{8,9},{9,8},{10,11... | collective-permute-start | bytes 221192 | tf_op jit(solution)/shard_map/ppermute | solution.py:464
  60.4 12.6 %collective-permute-start.7 = (f32[16,1152]{1,0:T(8,128)S(1)}, f32[16,1152]{1,0:T(8,128)S(1)}, u32[]{:S(2)}, u32[]{:S(2)}) collective-permute-start(f32[16,1152]{1,0:T(8,128)S(1)} %get-tuple-element.51.refs_4_.refs_1_.refs_6_.refs_2_), channel_id=1, source_target_pairs={{0,2},{1,3},{2,0},{3,1},{4,6},{5,7},{6,4},{7,5},{8,10},{9,11},{10,... | collective-permute-start | bytes 221192 | tf_op jit(solution)/shard_map/ppermute | solution.py:464
  61.4 11.5 %collective-permute-start.8 = (f32[16,1152]{1,0:T(8,128)S(1)}, f32[16,1152]{1,0:T(8,128)S(1)}, u32[]{:S(2)}, u32[]{:S(2)}) collective-permute-start(f32[16,1152]{1,0:T(8,128)S(1)} %get-tuple-element.51.refs_4_.refs_1_.refs_6_.refs_2_), channel_id=1, source_target_pairs={{0,3},{1,2},{2,1},{3,0},{4,7},{5,6},{6,5},{7,4},{8,11},{9,10},{10,... | collective-permute-start | bytes 221192 | tf_op jit(solution)/shard_map/ppermute | solution.py:464
  68.4 5.4 %collective-permute-start.5 = (f32[64,128]{1,0:T(8,128)S(1)}, f32[64,128]{1,0:T(8,128)S(1)}, u32[]{:S(2)}, u32[]{:S(2)}) collective-permute-start(f32[64,128]{1,0:T(8,128)S(1)} %get-tuple-element.50.refs_1_), channel_id=1, source_target_pairs={{0,32},{32,0},{1,33},{33,1},{2,34},{34,2},{3,35},{35,3},{4,36},{36... | collective-permute-start | bytes 98312 | tf_op jit(solution)/shard_map/ppermute | solution.py:468
  74.7 11.7 %all-to-all-start.3 = ((f32[8,32,128]{2,1,0:T(8,128)}), f32[8,32,128]{2,1,0:T(8,128)S(1)}, u32[]{:S(2)}, u32[]{:S(2)}) async-start(f32[8,32,128]{2,1,0:T(8,128)} %lower.5.refs_6_), calls=%async_computation.3 | async-start | bytes 262144 | tf_op jit(solution)/shard_map/all_to_all | solution.py:472
  88.8 11.2 %all-to-all-start.4 = ((f32[16,32,128]{2,1,0:T(8,128)}), f32[16,32,128]{2,1,0:T(8,128)S(1)}, u32[]{:S(2)}, u32[]{:S(2)}) async-start(f32[16,32,128]{2,1,0:T(8,128)} %get-tuple-element.54), calls=%async_computation.4 | async-start | bytes 524288 | tf_op jit(solution)/shard_map/all_to_all | solution.py:476
  92.3 12.0 %collective-permute-start.10 = (f32[16,1152]{1,0:T(8,128)S(1)}, f32[16,1152]{1,0:T(8,128)S(1)}, u32[]{:S(2)}, u32[]{:S(2)}) collective-permute-start(f32[16,1152]{1,0:T(8,128)S(1)} %get-tuple-element.57.refs_4_.refs_1_), channel_id=1, source_target_pairs={{0,1},{1,0},{2,3},{3,2},{4,5},{5,4},{6,7},{7,6},{8,9},{9,8},{10,11... | collective-permute-start | bytes 221192 | tf_op jit(solution)/shard_map/ppermute | solution.py:464
  92.4 11.9 %collective-permute-start.11 = (f32[16,1152]{1,0:T(8,128)S(1)}, f32[16,1152]{1,0:T(8,128)S(1)}, u32[]{:S(2)}, u32[]{:S(2)}) collective-permute-start(f32[16,1152]{1,0:T(8,128)S(1)} %get-tuple-element.57.refs_4_.refs_1_), channel_id=1, source_target_pairs={{0,2},{1,3},{2,0},{3,1},{4,6},{5,7},{6,4},{7,5},{8,10},{9,11},{10,... | collective-permute-start | bytes 221192 | tf_op jit(solution)/shard_map/ppermute | solution.py:464
  93.3 11.1 %collective-permute-start.12 = (f32[16,1152]{1,0:T(8,128)S(1)}, f32[16,1152]{1,0:T(8,128)S(1)}, u32[]{:S(2)}, u32[]{:S(2)}) collective-permute-start(f32[16,1152]{1,0:T(8,128)S(1)} %get-tuple-element.57.refs_4_.refs_1_), channel_id=1, source_target_pairs={{0,3},{1,2},{2,1},{3,0},{4,7},{5,6},{6,5},{7,4},{8,11},{9,10},{10,... | collective-permute-start | bytes 221192 | tf_op jit(solution)/shard_map/ppermute | solution.py:464
  100.6 4.6 %collective-permute-start.9 = (f32[64,128]{1,0:T(8,128)S(1)}, f32[64,128]{1,0:T(8,128)S(1)}, u32[]{:S(2)}, u32[]{:S(2)}) collective-permute-start(f32[64,128]{1,0:T(8,128)S(1)} %get-tuple-element.56.refs_1_), channel_id=1, source_target_pairs={{0,32},{32,0},{1,33},{33,1},{2,34},{34,2},{3,35},{35,3},{4,36},{36... | collective-permute-start | bytes 98312 | tf_op jit(solution)/shard_map/ppermute | solution.py:468
  106.1 11.3 %all-to-all-start.5 = ((f32[8,32,128]{2,1,0:T(8,128)}), f32[8,32,128]{2,1,0:T(8,128)S(1)}, u32[]{:S(2)}, u32[]{:S(2)}) async-start(f32[8,32,128]{2,1,0:T(8,128)} %lower.6.refs_6_), calls=%async_computation.5 | async-start | bytes 262144 | tf_op jit(solution)/shard_map/all_to_all | solution.py:472
  115.1 56.7 %copy-start.4 = (f32[16,1024]{1,0:T(8,128)S(1)}, f32[16,1024]{1,0:T(8,128)}, u32[]{:S(2)}) copy-start(f32[16,1024]{1,0:T(8,128)} %refs_1_.3) | copy-start | bytes 196612
  119.8 11.1 %all-to-all-start.6 = ((f32[16,32,128]{2,1,0:T(8,128)}), f32[16,32,128]{2,1,0:T(8,128)S(1)}, u32[]{:S(2)}, u32[]{:S(2)}) async-start(f32[16,32,128]{2,1,0:T(8,128)} %get-tuple-element.59), calls=%async_computation.6 | async-start | bytes 524288 | tf_op jit(solution)/shard_map/all_to_all | solution.py:476
  123.3 12.4 %collective-permute-start.14 = (f32[16,1152]{1,0:T(8,128)S(1)}, f32[16,1152]{1,0:T(8,128)S(1)}, u32[]{:S(2)}, u32[]{:S(2)}) collective-permute-start(f32[16,1152]{1,0:T(8,128)S(1)} %get-tuple-element.62.refs_4_.refs_1_), channel_id=1, source_target_pairs={{0,1},{1,0},{2,3},{3,2},{4,5},{5,4},{6,7},{7,6},{8,9},{9,8},{10,11... | collective-permute-start | bytes 221192 | tf_op jit(solution)/shard_map/ppermute | solution.py:464
  123.5 12.3 %collective-permute-start.15 = (f32[16,1152]{1,0:T(8,128)S(1)}, f32[16,1152]{1,0:T(8,128)S(1)}, u32[]{:S(2)}, u32[]{:S(2)}) collective-permute-start(f32[16,1152]{1,0:T(8,128)S(1)} %get-tuple-element.62.refs_4_.refs_1_), channel_id=1, source_target_pairs={{0,2},{1,3},{2,0},{3,1},{4,6},{5,7},{6,4},{7,5},{8,10},{9,11},{10,... | collective-permute-start | bytes 221192 | tf_op jit(solution)/shard_map/ppermute | solution.py:464
  124.6 11.1 %collective-permute-start.16 = (f32[16,1152]{1,0:T(8,128)S(1)}, f32[16,1152]{1,0:T(8,128)S(1)}, u32[]{:S(2)}, u32[]{:S(2)}) collective-permute-start(f32[16,1152]{1,0:T(8,128)S(1)} %get-tuple-element.62.refs_4_.refs_1_), channel_id=1, source_target_pairs={{0,3},{1,2},{2,1},{3,0},{4,7},{5,6},{6,5},{7,4},{8,11},{9,10},{10,... | collective-permute-start | bytes 221192 | tf_op jit(solution)/shard_map/ppermute | solution.py:464
  131.5 5.1 %collective-permute-start.13 = (f32[64,128]{1,0:T(8,128)S(1)}, f32[64,128]{1,0:T(8,128)S(1)}, u32[]{:S(2)}, u32[]{:S(2)}) collective-permute-start(f32[64,128]{1,0:T(8,128)S(1)} %get-tuple-element.61.refs_1_), channel_id=1, source_target_pairs={{0,32},{32,0},{1,33},{33,1},{2,34},{34,2},{3,35},{35,3},{4,36},{36... | collective-permute-start | bytes 98312 | tf_op jit(solution)/shard_map/ppermute | solution.py:468
  137.5 11.3 %all-to-all-start.7 = ((f32[8,32,128]{2,1,0:T(8,128)}), f32[8,32,128]{2,1,0:T(8,128)S(1)}, u32[]{:S(2)}, u32[]{:S(2)}) async-start(f32[8,32,128]{2,1,0:T(8,128)} %lower.7.refs_6_), calls=%async_computation.7 | async-start | bytes 262144 | tf_op jit(solution)/shard_map/all_to_all | solution.py:472

commit v5 on v4

--- a/solution.py
+++ b/solution.py
@@ -67,20 +67,27 @@
     return jnp.broadcast_to(jnp.sum(v * v, axis=1, keepdims=True), (v.shape[0], 64))
 
 
-def moments(v, bases, chain):
-    own = times_t(v, bases)
+def lift(own, chain):
     lifted = times(own, chain)
     return jnp.concatenate([own, lifted[:, 0:64]], axis=1), lifted[:, 64:192], lifted[:, 192:256]
 
 
-def write_moments(extended, out, v, weighed, bases, chain):
-    own, middle, top = moments(v, bases[...], chain[...])
+def send(block, out, sems):
+    copies = [pltpu.make_async_copy(block, out.at[i], sems.at[i]) for i in range(out.shape[0])]
+    for copy in copies:
+        copy.start()
+    return copies
+
+
+def write_moments(extended, out, block, sems, v, own, weighed, chain):
+    first, middle, top = lift(own, chain[...])
+    block[0:16, :] = middle
+    block[16:32, :] = jnp.concatenate([top, square_sum(weighed)], axis=1)
+    copies = send(block, out, sems)
     extended[:, 0 : v.shape[1]] = v
-    extended[:, v.shape[1] :] = own
-    last = jnp.concatenate([top, square_sum(weighed)], axis=1)
-    for i in range(out.shape[0]):
-        out[i, 0:16, :] = middle
-        out[i, 16:32, :] = last
+    extended[:, v.shape[1] :] = first
+    for copy in copies:
+        copy.wait()
 
 
 def packed(skeleton):
@@ -98,7 +105,7 @@
 
 
 def prepare_kernel(
-    scalars, order, basis, maps, skeletons, rhs, bases, chain, tail, own, wire, second
+    scalars, order, basis, maps, skeletons, rhs, bases, chain, tail, gram, own, wire, second
 ):
     both = stacked(basis[...])
     leaf = basis.shape[1]
@@ -113,7 +120,10 @@
     p5 = dot(p3, e34, precision=HIGHEST)
     tail[...] = e34
     chain[...] = paired(jnp.concatenate([p1, p2, p3, p5], axis=1), 1)
-    first, middle, top = moments(rhs[...], bases[...], chain[...])
+    products = dot(bases[...], bases[...], 1, 1)
+    products = halves(products[:, 0:64] + products[:, 64:128])
+    gram[...] = paired(products, 1)
+    first, middle, top = lift(times_t(rhs[...], bases[...]), chain[...])
     own[...] = first
     last = jnp.concatenate([top, jnp.zeros_like(top)], axis=1)
     for i in range(wire.shape[0]):
@@ -157,7 +167,7 @@
     for h, offset in enumerate(skeleton_offsets(scalars)):
         if h == 2:
             offset = jnp.where(scalars[O2] % 2 == 1, offset, 0)
-        partner = unpacked(from_z[jnp.bitwise_xor(z, offset), 48:80, :])
+        partner = unpacked(from_z[jnp.bitwise_xor(z, offset), 32:64, :])
         coupling = matern(skeletons[h], partner)
         if h > 0:
             coupling = dot(down[:, (h - 1) * 64 : h * 64], coupling, precision=HIGHEST)
@@ -239,7 +249,7 @@
         copy.wait()
 
 
-def near_kernel(scalars, v, v1, v2, v3, kernels, after, out, held, sems):
+def near_kernel(scalars, v, v1, v2, v3, bases, kernels, after, out, held, sems):
     leaf = kernels.shape[2]
     tiles = leaf // TILE
     copies = []
@@ -265,10 +275,10 @@
             copies[e * tiles + t].wait()
             part = dot(pair[:, rows], held[e, 0, rows, :]) + dot(pair[:, rows], held[e, 1, rows, :])
             total = part if total is None else total + part
-    out[:, 0:leaf] = NOISE * own + halves(total)
-    out[:, leaf:] = jnp.where(
-        o0 == 1, v1[:, leaf:], jnp.where(o0 == 2, v2[:, leaf:], v3[:, leaf:])
-    )
+    result = NOISE * own + halves(total)
+    partner = jnp.where(o0 == 1, v1[:, leaf:], jnp.where(o0 == 2, v2[:, leaf:], v3[:, leaf:]))
+    out[:, 0:leaf] = result
+    out[:, leaf:] = jnp.concatenate([partner[:, 0:64], times_t(result, bases[...])], axis=1)
 
 
 def gather_kernel(scalars, received, *refs):
@@ -290,74 +300,96 @@
     high[...] = total
 
 
-def lower_kernel(high, mine, other, table, own, *refs):
-    out = refs[-1]
+def lower_blocks(high, mine, other, table, own):
     start = own.shape[1] - 128
     parts = [high[:, 64:128]]
     for side in (mine, other):
         parts += [side[j * 16 : (j + 1) * 16, 0:64] for j in range(4)]
     field = times_t(jnp.concatenate(parts, axis=1), table[...])
+    return field, jnp.concatenate([own[:, start + 64 :], high[:, 0:64]], axis=1)
+
+
+def lower_kernel(high, mine, other, table, own, *refs):
+    out, block, sems = refs[-3:]
+    field, second = lower_blocks(high, mine, other, table, own)
     norm = sum(side[j * 16 : (j + 1) * 16, 64:128] for side in (mine, other) for j in range(4))
-    first = jnp.concatenate([field, norm], axis=1)
-    second = jnp.concatenate([own[:, start + 64 :], high[:, 0:64]], axis=1)
-    for i in range(out.shape[0]):
-        out[i, 0:16, :] = first
-        out[i, 16:32, :] = second
+    block[0:16, :] = jnp.concatenate([field, norm], axis=1)
+    block[16:32, :] = second
+    for copy in send(block, out, sems):
+        copy.wait()
 
 
 def first_lower_kernel(scalars, high, mine, other, table, own, skeletons, second, moved, out):
-    lower_kernel(high, mine, other, table, own, out)
+    field, lifted = lower_blocks(high, mine, other, table, own)
+    first = jnp.concatenate([field, own[:, 0:64]], axis=1)
     _, k1, k2 = skeleton_offsets(scalars)
     third = jnp.where(scalars[O2] > 1, moved[...], second[...])
     blocks = [packed(skeletons[0]), packed(skeletons[1]), third]
     for i in range(out.shape[0]):
         offset = jnp.bitwise_xor(scalars[Z], i)
         block = jnp.where(offset == k1, blocks[1], blocks[0])
-        out[i, 32:48, :] = own[...]
-        out[i, 48:80, :] = jnp.where((offset == k2) | (offset == 0), blocks[2], block)
+        out[i, 0:16, :] = first
+        out[i, 16:32, :] = lifted
+        out[i, 32:64, :] = jnp.where((offset == k2) | (offset == 0), blocks[2], block)
 
 
 def apply_far(scalars, received, table, bases, near):
     leaf = bases.shape[1]
     z, o0, o1, o2 = scalars[Z], scalars[O0], scalars[O1], scalars[O2]
+    start = received.shape[1] > 32
     left = lax.broadcasted_iota(jnp.int32, (16, 128), 1) < 64
-    sums = [jnp.zeros((16, 128), F32) for _ in range(3)]
+    sums = [jnp.zeros((16, 128), F32) for _ in range(2)]
     for i in range(received.shape[0]):
         offset = jnp.bitwise_xor(z, i)
         hit1 = offset // 2 == o1
         hit2 = offset // 4 == jnp.bitwise_and(o2, 1)
-        sums[0] += received[i, 0:16, :]
+        block = received[i, 0:16, :]
+        sums[0] += jnp.where(left | (offset == o0), block, 0.0) if start else block
         sums[1] += jnp.where((left & hit1) | (~left & hit2), received[i, 16:32, :], 0.0)
-        if received.shape[1] > 32:
-            sums[2] += jnp.where(offset == o0, received[i, 32:48, :], 0.0)
-    moment = sums[2] if received.shape[1] > 32 else near[:, leaf : leaf + 128]
-    parts = [moment[:, 0:64], sums[1], sums[0][:, 0:64]]
+    moment = sums[0][:, 64:128] if start else near[:, leaf : leaf + 64]
+    parts = [moment, sums[1], sums[0][:, 0:64]]
     field = times_t(jnp.concatenate(parts, axis=1), table[...])
     pair = stacked(field)
     far = halves(dot(pair, bases[0:64, :]) + dot(pair, bases[64:128, :]))
-    return near[:, 0:leaf] + far, sums[0][:, 64:65]
-
-
-def first_kernel(scalars, received, skeletons, bases, near, chain, table, v1, out):
+    return near[:, 0:leaf] + far, sums[0][:, 64:65], field
+
+
+def moment_of(near, field, gram):
+    return near[:, near.shape[1] - 64 :] + times(field, gram[...])
+
+
+def first_kernel(
+    scalars, received, skeletons, bases, near, chain, table, v1, out, block, sems
+):
     table[...] = low_couplings(scalars, skeletons, received, chain)
-    image, _ = apply_far(scalars, received, table, bases, near)
-    write_moments(v1, out, image, image, bases, chain)
-
-
-def second_kernel(scalars, received, table, bases, near, chain, v2, scaled, sums, out):
-    image, norm = apply_far(scalars, received, table, bases, near)
+    image, _, _ = apply_far(scalars, received, table, bases, near)
+    own = times_t(image, bases[...])
+    write_moments(v1, out, block, sems, image, own, image, chain)
+
+
+def second_kernel(
+    scalars, received, table, bases, near, gram, chain, v2, scaled, sums, out, block, sems
+):
+    image, norm, field = apply_far(scalars, received, table, bases, near)
     v2[...] = image
     sums[...] = jnp.broadcast_to(norm, sums.shape)
-    write_moments(scaled, out, image / jnp.sqrt(norm), image, bases, chain)
-
-
-def third_kernel(scalars, received, table, bases, near, chain, v1, sums, image, step, out):
-    product, along = apply_far(scalars, received, table, bases, near)
+    size = 1.0 / jnp.sqrt(norm)
+    own = moment_of(near, field, gram) * size
+    write_moments(scaled, out, block, sems, image * size, own, image, chain)
+
+
+def third_kernel(
+    scalars, received, table, bases, near, gram, chain, v1, sums, image, step, out, block, sems
+):
+    product, along, field = apply_far(scalars, received, table, bases, near)
+    leaf = product.shape[1]
     norm = sums[:, 0:1]
     size = norm / along
-    new = v1[:, 0 : product.shape[1]] - (size * jnp.sqrt(norm)) * product
+    back = size * jnp.sqrt(norm)
+    new = v1[:, 0:leaf] - back * product
+    own = v1[:, leaf : leaf + 64] - back * moment_of(near, field, gram)
     step[...] = jnp.broadcast_to(size, step.shape)
-    write_moments(image, out, new, new, bases, chain)
+    write_moments(image, out, block, sems, new, own, new, chain)
 
 
 def diagonal():
@@ -366,7 +398,7 @@
 
 
 def fourth_kernel(scalars, received, table, bases, near, v2, sums, along, fresh, out):
-    product, norm = apply_far(scalars, received, table, bases, near)
+    product, norm, _ = apply_far(scalars, received, table, bases, near)
     new = product + (norm / sums[:, 0:1]) * v2[...]
     along[...] = new
     fresh[...] = jnp.broadcast_to(norm, fresh.shape)
@@ -410,13 +442,17 @@
         body,
         out_shape=outs,
         in_specs=[SMEM] * len(scalars) + [VMEM] * len(arrays) + [ANY] * len(after),
-        out_specs=jax.tree.map(lambda a: VMEM if len(a.shape) < 4 else ANY, outs),
+        out_specs=jax.tree.map(lambda a: ANY if len(a.shape) == 4 or a.shape[1:] == (32, 128) else VMEM, outs),
         scratch_shapes=list(scratch),
         input_output_aliases=alias or {},
         name=name,
         compiler_params=pltpu.CompilerParams(vmem_limit_bytes=limit * MIB),
         cost_estimate=pl.CostEstimate(flops=flops, bytes_accessed=500000, transcendentals=0),
     )(*scalars, *arrays, *after)
+
+
+def block(copies):
+    return [pltpu.VMEM((32, 128), F32), pltpu.SemaphoreType.DMA((copies,))]
 
 
 def build(scalars, own, others, choice, near, after, name, kernels=()):
@@ -442,13 +478,13 @@
     )
 
 
-def near_product(scalars, vectors, kernels, after):
+def near_product(scalars, vectors, bases, kernels, after):
     leaf = kernels.shape[2]
     return call(
         near_kernel,
         shaped(*vectors[0].shape),
         [scalars],
-        vectors,
+        [*vectors, bases],
         "near",
         after=[kernels, after],
         limit=50,
@@ -502,12 +538,13 @@
     one = along_z(both, 1)
     two = along_z(both, 2)
     three_off = along_z(two, 1)
-    bases, chain, tail, own, outgoing, second = call(
+    bases, chain, tail, gram, own, outgoing, second = call(
         prepare_kernel,
         (
             shaped(128, 1024, dtype=BF16),
             shaped(64, 512, dtype=BF16),
             shaped(64, 64),
+            shaped(64, 128, dtype=BF16),
             thin,
             shaped(16, 64, 128),
             shaped(32, 128),
@@ -537,7 +574,7 @@
     )
     outgoing = call(
         first_lower_kernel,
-        shaped(8, 80, 128),
+        shaped(8, 64, 128),
         [scalars],
         [*spread, top_table, own, chain_skeletons, second, second_moved],
         "lower",
@@ -554,6 +591,7 @@
         [scalars],
         [over_z(outgoing), chain_skeletons, bases, near, chain],
         "first",
+        scratch=block(16),
     )
 
     def operate(extended, outgoing):
@@ -566,19 +604,26 @@
             [*spread, top_table, extended],
             "lower",
             after=moved,
+            scratch=block(8),
         )
-        near = near_product(scalars, [extended, *moved], kernels, lower)
+        near = near_product(scalars, [extended, *moved], bases, kernels, lower)
         return over_z(lower), table, bases, near
 
     v2, scaled, sums, outgoing = call(
-        second_kernel, (row, long, thin, wire), [scalars], [*operate(v1, outgoing), chain], "second"
+        second_kernel,
+        (row, long, thin, wire),
+        [scalars],
+        [*operate(v1, outgoing), gram, chain],
+        "second",
+        scratch=block(16),
     )
     image, step, outgoing = call(
         third_kernel,
         (long, thin, wire),
         [scalars],
-        [*operate(scaled, outgoing), chain, v1, sums],
+        [*operate(scaled, outgoing), gram, chain, v1, sums],
         "third",
+        scratch=block(16),
     )
     along, fresh, outgoing = call(
         fourth_kernel,

time: 174 us -> 173 us (level)
  waiting for transfers between devices: 28.6 us -> 26.3 us
    all_to_all x4, waiting for transfers between devices: 10.3 us -> 7.93 us  [over_z(): return lax.all_to_all(v, 'z', 0, 0)]
  transfers between devices with their start and end apart: 25 -> 25, of which waited for: 12 -> 12; matrix products, arithmetic and copies ran while one was open for 0% -> 0% of each run, Pallas kernels for 22% -> 23%
where the time goes in v5:
time: 173 us; the launch traced here: 172 us
  starting transfers between devices  69 us (40%)
  Pallas kernels  51.3 us (30%)
  waiting for transfers between devices  26.3 us (15%)
  blocking collectives  21.7 us (13%)
  local copies, waits for them, and re-layouts  2.76 us (2%)
    pallas_call x21, Pallas kernels, call(): pl.pallas_call(body, out_shape=outs, in_specs=[SMEM] * len(scalars) + [VM...  51.3 us
    all_to_all x1, blocking collectives, local(): shares = lax.all_to_all(outgoing, ('y', 'core', 'x', 'z'), 0, 0, tiled=True)  21.7 us
    all_to_all x4, starting transfers between devices, over_yx(): return lax.all_to_all(v, ('y', 'x'), 0, 0)  19.6 us
    ppermute x12, starting transfers between devices, along_z(): return lax.ppermute(v, 'z', [(i, i ^ offset) for i in range(8)])  18.2 us
    all_to_all x4, starting transfers between devices, over_z(): return lax.all_to_all(v, 'z', 0, 0)  16.8 us
    all_to_all x4, waiting for transfers between devices, over_yx(): return lax.all_to_all(v, ('y', 'x'), 0, 0)  14.2 us
    ppermute x4, starting transfers between devices, other_core(): return lax.ppermute(v, 'core', [(0, 1), (1, 0)])  14 us
    all_to_all x4, waiting for transfers between devices, over_z(): return lax.all_to_all(v, 'z', 0, 0)  7.93 us
  transfers between devices with their start and end apart: 25, of which 12 were waited for; matrix products, arithmetic and copies ran while one was open for 0% of the time, Pallas kernels for 23%

profile of v5, /device:TPU:1, one launch (start us, length us, event | category | flops | bytes accessed | tf_op | source)
XLA Modules:
  0.0 172.1 jit_solution(6027008776441781125)
XLA Ops:
  0.7 1.0 constant_dynamic-update-slice_fusion.1
  2.5 3.8 %collective-permute-start = (f32[80,1024]{1,0:T(8,128)S(1)}, f32[80,1024]{1,0:T(8,128)S(1)}, u32[]{:S(2)}, u32[]{:S(2)}) collective-permute-start(f32[80,1024]{1,0:T(8,128)S(1)} %constant_dynamic-update-slice_fusion.refs_1_), channel_id=1, source_target_pairs={{0,2},{1,3},{2,0},{3,1},{4,6},{5,7},{6,4},{7,5},{8,10},{9,11},{10,... | collective-permute-start | bytes 983048 | tf_op jit(solution)/shard_map/ppermute | solution.py:500
  6.4 3.5 %prepare.1 = (bf16[128,1024]{1,0:T(8,128)(2,1)}, bf16[64,512]{1,0:T(8,128)(2,1)}, f32[64,64]{1,0:T(8,128)}, bf16[64,128]{1,0:T(8,128)(2,1)}, f32[16,128]{1,0:T(8...) custom-call(s32[4]{0:T(128)} %bitcast.15, s32[1,1024]{1,0:T(1,128)} %refs_1_.2, f32[64,1024]{1,0:T(8,128)} %refs_2_.1, ...), custom_call_target="tpu_custom_call" | custom-call | flops 100000 | bytes 500000 | tf_op jit(solution)/shard_map/prepare/pallas_call | solution.py:441
  9.9 6.9 %all-to-all-start = ((f32[16,64,128]{2,1,0:T(8,128)}), f32[16,64,128]{2,1,0:T(8,128)S(1)}, u32[]{:S(2)}, u32[]{:S(2)}) async-start(f32[16,64,128]{2,1,0:T(8,128)} %get-tuple-element.36), calls=%async_computation | async-start | bytes 1048576 | tf_op jit(solution)/shard_map/all_to_all | solution.py:512
  16.8 1.7 %collective-permute-start.4 = (f32[80,1024]{1,0:T(8,128)S(1)}, f32[80,1024]{1,0:T(8,128)S(1)}, u32[]{:S(2)}, u32[]{:S(2)}) collective-permute-start(f32[80,1024]{1,0:T(8,128)S(1)} %constant_dynamic-update-slice_fusion.refs_1_), channel_id=1, source_target_pairs={{0,1},{1,0},{2,3},{3,2},{4,5},{5,4},{6,7},{7,6},{8,9},{9,8},{10,11... | collective-permute-start | bytes 983048 | tf_op jit(solution)/shard_map/ppermute | solution.py:500
  18.5 1.6 collective-permute-done.refs_2_
  20.8 4.1 %build_own.1 = (bf16[3,2,1024,1024]{3,2,1,0:T(8,128)(2,1)}, f32[16,1024]{1,0:T(8,128)S(1)}) custom-call(s32[4]{0:T(128)S(1)} %bitcast.16, f32[80,1024]{1,0:T(8,128)S(1)} %constant_dynamic-update-slice_fusion.refs_1_, f32[80,1024]{1,0:T(8,128)S(1)} %collective-permute-done.refs_2_), custom_call_target="tpu_custom_call" | custom-call | flops 4000000000 | bytes 500000 | tf_op jit(solution)/shard_map/build_own/pallas_call | solution.py:441
  24.9 2.3 %all-to-all-done.refs_1_.refs_3_ = f32[16,64,128]{2,1,0:T(8,128)S(1)} async-done(((f32[16,64,128]{2,1,0:T(8,128)}), f32[16,64,128]{2,1,0:T(8,128)S(1)}, u32[]{:S(2)}, u32[]{:S(2)}) %all-to-all-start) | async-done | bytes 524320 | tf_op jit(solution)/shard_map/all_to_all | solution.py:512
  27.8 2.2 %collective-permute-start.1 = (f32[64,128]{1,0:T(8,128)S(1)}, f32[64,128]{1,0:T(8,128)S(1)}, u32[]{:S(2)}, u32[]{:S(2)}) collective-permute-start(f32[64,128]{1,0:T(8,128)S(1)} %get-tuple-element.39.refs_2_), channel_id=1, source_target_pairs={{0,32},{32,0},{1,33},{33,1},{2,34},{34,2},{3,35},{35,3},{4,36},{36... | collective-permute-start | bytes 98312 | tf_op jit(solution)/shard_map/ppermute | solution.py:504
  30.5 1.7 collective-permute-start.3
  32.2 1.3 tops.1.refs_4_.refs_3_
  33.5 1.6 lower.4.refs_5_
  35.1 5.5 %all-to-all-start.1 = ((f32[8,64,128]{2,1,0:T(8,128)}), f32[8,64,128]{2,1,0:T(8,128)S(1)}, u32[]{:S(2)}, u32[]{:S(2)}) async-start(f32[8,64,128]{2,1,0:T(8,128)} %lower.4.refs_5_), calls=%async_computation.1 | async-start | bytes 524288 | tf_op jit(solution)/shard_map/all_to_all | solution.py:508
  40.6 4.2 %build_a.1 = (bf16[3,2,1024,1024]{3,2,1,0:T(8,128)(2,1)}, f32[16,1024]{1,0:T(8,128)S(1)}) custom-call(s32[4]{0:T(128)S(1)} %bitcast.20, f32[80,1024]{1,0:T(8,128)S(1)} %constant_dynamic-update-slice_fusion.refs_1_, f32[80,1024]{1,0:T(8,128)S(1)} %collective-permute-done.refs_2_, ...), custom_call_target="tpu_custom_call", output_to_operand_aliasing={{0}: (6, {})} | custom-call | flops 4000000000 | bytes 500000 | tf_op jit(solution)/shard_map/build_a/pallas_call | solution.py:441
  44.8 4.2 %build_b.1 = (bf16[3,2,1024,1024]{3,2,1,0:T(8,128)(2,1)}, f32[16,1024]{1,0:T(8,128)S(1)}) custom-call(s32[4]{0:T(128)S(1)} %bitcast.21, f32[80,1024]{1,0:T(8,128)S(1)} %constant_dynamic-update-slice_fusion.refs_1_, f32[80,1024]{1,0:T(8,128)S(1)} %collective-permute-done.refs_2_, ...), custom_call_target="tpu_custom_call", output_to_operand_aliasing={{0}: (6, {})} | custom-call | flops 4000000000 | bytes 500000 | tf_op jit(solution)/shard_map/build_b/pallas_call | solution.py:441
  49.0 1.8 %all-to-all-done.1.refs_1_ = f32[8,64,128]{2,1,0:T(8,128)S(1)} async-done(((f32[8,64,128]{2,1,0:T(8,128)}), f32[8,64,128]{2,1,0:T(8,128)S(1)}, u32[]{:S(2)}, u32[]{:S(2)}) %all-to-all-start.1) | async-done | bytes 262176 | tf_op jit(solution)/shard_map/all_to_all | solution.py:508
  50.8 2.8 %first.1 = (bf16[128,256]{1,0:T(8,128)(2,1)S(1)}, f32[16,1152]{1,0:T(8,128)S(1)}, f32[16,32,128]{2,1,0:T(8,128)}) custom-call(s32[4]{0:T(128)S(1)} %bitcast.22, f32[8,64,128]{2,1,0:T(8,128)S(1)} %all-to-all-done.1.refs_1_, f32[4,64,64]{2,1,0:T(8,128)S(1)} %bitcast.11, bf16[128,1024]{1,0:T(8,128)(2,1)S(1)} %copy-done.1, ...), custom_call_target="tpu_custom_call" | custom-call | flops 100000 | bytes 500000 | tf_op jit(solution)/shard_map/first/pallas_call | solution.py:441
  53.6 5.7 %all-to-all-start.2 = ((f32[16,32,128]{2,1,0:T(8,128)}), f32[16,32,128]{2,1,0:T(8,128)S(1)}, u32[]{:S(2)}, u32[]{:S(2)}) async-start(f32[16,32,128]{2,1,0:T(8,128)} %get-tuple-element.49), calls=%async_computation.2 | async-start | bytes 524288 | tf_op jit(solution)/shard_map/all_to_all | solution.py:512
  59.4 1.9 %collective-permute-start.7 = (f32[16,1152]{1,0:T(8,128)S(1)}, f32[16,1152]{1,0:T(8,128)S(1)}, u32[]{:S(2)}, u32[]{:S(2)}) collective-permute-start(f32[16,1152]{1,0:T(8,128)S(1)} %get-tuple-element.52.refs_4_.refs_1_.refs_7_.refs_2_), channel_id=1, source_target_pairs={{0,2},{1,3},{2,0},{3,1},{4,6},{5,7},{6,4},{7,5},{8,10},{9,11},{10,... | collective-permute-start | bytes 221192 | tf_op jit(solution)/shard_map/ppermute | solution.py:500
  61.2 1.7 collective-permute-start.8
  62.9 3.9 %all-to-all-done.2.refs_1_ = f32[16,32,128]{2,1,0:T(8,128)S(1)} async-done(((f32[16,32,128]{2,1,0:T(8,128)}), f32[16,32,128]{2,1,0:T(8,128)S(1)}, u32[]{:S(2)}, u32[]{:S(2)}) %all-to-all-start.2) | async-done | bytes 262176 | tf_op jit(solution)/shard_map/all_to_all | solution.py:512
  67.4 4.2 %collective-permute-start.5 = (f32[64,128]{1,0:T(8,128)S(1)}, f32[64,128]{1,0:T(8,128)S(1)}, u32[]{:S(2)}, u32[]{:S(2)}) collective-permute-start(f32[64,128]{1,0:T(8,128)S(1)} %get-tuple-element.51.refs_1_), channel_id=1, source_target_pairs={{0,32},{32,0},{1,33},{33,1},{2,34},{34,2},{3,35},{35,3},{4,36},{36... | collective-permute-start | bytes 98312 | tf_op jit(solution)/shard_map/ppermute | solution.py:504
  72.5 1.0 lower.5.refs_7_
  73.6 3.8 %all-to-all-start.3 = ((f32[8,32,128]{2,1,0:T(8,128)}), f32[8,32,128]{2,1,0:T(8,128)S(1)}, u32[]{:S(2)}, u32[]{:S(2)}) async-start(f32[8,32,128]{2,1,0:T(8,128)} %lower.5.refs_7_), calls=%async_computation.3 | async-start | bytes 262144 | tf_op jit(solution)/shard_map/all_to_all | solution.py:508
  77.4 5.9 %near.3.refs_4_ = f32[16,1152]{1,0:T(8,128)S(1)} custom-call(s32[4]{0:T(128)S(1)} %bitcast.24, f32[16,1152]{1,0:T(8,128)S(1)} %get-tuple-element.52.refs_4_.refs_1_.refs_7_.refs_2_, f32[16,1152]{1,0:T(8,128)S(1)} %collective-permute-done.6.refs_5_.refs_2_, f32[16,1152]{1,0:T(8,128)S(1)} %collective-permute-done.7.refs_6_.refs_3_, ...), custom_call_target="tpu_custom_call" | custom-call | flops 4000000000 | bytes 500000 | tf_op jit(solution)/shard_map/near/pallas_call | solution.py:441
  83.3 2.1 %all-to-all-done.3.refs_1_ = f32[8,32,128]{2,1,0:T(8,128)S(1)} async-done(((f32[8,32,128]{2,1,0:T(8,128)}), f32[8,32,128]{2,1,0:T(8,128)S(1)}, u32[]{:S(2)}, u32[]{:S(2)}) %all-to-all-start.3) | async-done | bytes 131104 | tf_op jit(solution)/shard_map/all_to_all | solution.py:508
  85.4 2.3 %second.1 = (f32[16,1024]{1,0:T(8,128)S(1)}, f32[16,1152]{1,0:T(8,128)S(1)}, f32[16,128]{1,0:T(8,128)S(1)}, f32[16,32,128]{2,1,0:T(8,128)}) custom-call(s32[4]{0:T(128)S(1)} %bitcast.25, f32[8,32,128]{2,1,0:T(8,128)S(1)} %all-to-all-done.3.refs_1_, bf16[128,256]{1,0:T(8,128)(2,1)S(1)} %get-tuple-element.53.refs_2_, bf16[128,1024]{1,0:T(8,128)(2,1)S(1)} %copy-done.1, ...), custom_call_target="tpu_custom_call" | custom-call | flops 100000 | bytes 500000 | tf_op jit(solution)/shard_map/second/pallas_call | solution.py:441
  87.7 3.5 %all-to-all-start.4 = ((f32[16,32,128]{2,1,0:T(8,128)}), f32[16,32,128]{2,1,0:T(8,128)S(1)}, u32[]{:S(2)}, u32[]{:S(2)}) async-start(f32[16,32,128]{2,1,0:T(8,128)} %get-tuple-element.56), calls=%async_computation.4 | async-start | bytes 524288 | tf_op jit(solution)/shard_map/all_to_all | solution.py:512
  91.3 1.4 collective-permute-start.11
  92.8 2.0 %collective-permute-start.12 = (f32[16,1152]{1,0:T(8,128)S(1)}, f32[16,1152]{1,0:T(8,128)S(1)}, u32[]{:S(2)}, u32[]{:S(2)}) collective-permute-start(f32[16,1152]{1,0:T(8,128)S(1)} %get-tuple-element.59.refs_4_.refs_1_), channel_id=1, source_target_pairs={{0,3},{1,2},{2,1},{3,0},{4,7},{5,6},{6,5},{7,4},{8,11},{9,10},{10,... | collective-permute-start | bytes 221192 | tf_op jit(solution)/shard_map/ppermute | solution.py:500
  94.8 4.0 %all-to-all-done.4.refs_1_ = f32[16,32,128]{2,1,0:T(8,128)S(1)} async-done(((f32[16,32,128]{2,1,0:T(8,128)}), f32[16,32,128]{2,1,0:T(8,128)S(1)}, u32[]{:S(2)}, u32[]{:S(2)}) %all-to-all-start.4) | async-done | bytes 262176 | tf_op jit(solution)/shard_map/all_to_all | solution.py:512
  99.4 3.8 %collective-permute-start.9 = (f32[64,128]{1,0:T(8,128)S(1)}, f32[64,128]{1,0:T(8,128)S(1)}, u32[]{:S(2)}, u32[]{:S(2)}) collective-permute-start(f32[64,128]{1,0:T(8,128)S(1)} %get-tuple-element.58.refs_1_), channel_id=1, source_target_pairs={{0,32},{32,0},{1,33},{33,1},{2,34},{34,2},{3,35},{35,3},{4,36},{36... | collective-permute-start | bytes 98312 | tf_op jit(solution)/shard_map/ppermute | solution.py:504
  104.1 1.0 lower.6.refs_7_
  105.1 3.8 %all-to-all-start.5 = ((f32[8,32,128]{2,1,0:T(8,128)}), f32[8,32,128]{2,1,0:T(8,128)S(1)}, u32[]{:S(2)}, u32[]{:S(2)}) async-start(f32[8,32,128]{2,1,0:T(8,128)} %lower.6.refs_7_), calls=%async_computation.5 | async-start | bytes 262144 | tf_op jit(solution)/shard_map/all_to_all | solution.py:508
  108.9 5.9 %near.4.refs_4_ = f32[16,1152]{1,0:T(8,128)S(1)} custom-call(s32[4]{0:T(128)S(1)} %bitcast.27, f32[16,1152]{1,0:T(8,128)S(1)} %get-tuple-element.59.refs_4_.refs_1_, f32[16,1152]{1,0:T(8,128)S(1)} %collective-permute-done.10.refs_5_.refs_2_, f32[16,1152]{1,0:T(8,128)S(1)} %collective-permute-done.11.refs_6_.refs_3_, ...), custom_call_target="tpu_custom_call" | custom-call | flops 4000000000 | bytes 500000 | tf_op jit(solution)/shard_map/near/pallas_call | solution.py:441
  114.7 2.0 %all-to-all-done.5.refs_1_ = f32[8,32,128]{2,1,0:T(8,128)S(1)} async-done(((f32[8,32,128]{2,1,0:T(8,128)}), f32[8,32,128]{2,1,0:T(8,128)S(1)}, u32[]{:S(2)}, u32[]{:S(2)}) %all-to-all-start.5) | async-done | bytes 131104 | tf_op jit(solution)/shard_map/all_to_all | solution.py:508
  116.8 2.3 %third.1 = (f32[16,1152]{1,0:T(8,128)S(1)}, f32[16,128]{1,0:T(8,128)S(1)}, f32[16,32,128]{2,1,0:T(8,128)}) custom-call(s32[4]{0:T(128)S(1)} %bitcast.28, f32[8,32,128]{2,1,0:T(8,128)S(1)} %all-to-all-done.5.refs_1_, bf16[128,256]{1,0:T(8,128)(2,1)S(1)} %get-tuple-element.53.refs_2_, bf16[128,1024]{1,0:T(8,128)(2,1)S(1)} %copy-done.1, ...), custom_call_target="tpu_custom_call" | custom-call | flops 100000 | bytes 500000 | tf_op jit(solution)/shard_map/third/pallas_call | solution.py:441
  119.1 3.5 %all-to-all-start.6 = ((f32[16,32,128]{2,1,0:T(8,128)}), f32[16,32,128]{2,1,0:T(8,128)S(1)}, u32[]{:S(2)}, u32[]{:S(2)}) async-start(f32[16,32,128]{2,1,0:T(8,128)} %get-tuple-element.61), calls=%async_computation.6 | async-start | bytes 524288 | tf_op jit(solution)/shard_map/all_to_all | solution.py:512
  122.8 1.4 collective-permute-start.15
  124.3 2.0 %collective-permute-start.16 = (f32[16,1152]{1,0:T(8,128)S(1)}, f32[16,1152]{1,0:T(8,128)S(1)}, u32[]{:S(2)}, u32[]{:S(2)}) collective-permute-start(f32[16,1152]{1,0:T(8,128)S(1)} %get-tuple-element.64.refs_4_.refs_1_), channel_id=1, source_target_pairs={{0,3},{1,2},{2,1},{3,0},{4,7},{5,6},{6,5},{7,4},{8,11},{9,10},{10,... | collective-permute-start | bytes 221192 | tf_op jit(solution)/shard_map/ppermute | solution.py:500
  126.3 4.0 %all-to-all-done.6.refs_1_ = f32[16,32,128]{2,1,0:T(8,128)S(1)} async-done(((f32[16,32,128]{2,1,0:T(8,128)}), f32[16,32,128]{2,1,0:T(8,128)S(1)}, u32[]{:S(2)}, u32[]{:S(2)}) %all-to-all-start.6) | async-done | bytes 262176 | tf_op jit(solution)/shard_map/all_to_all | solution.py:512
  130.9 3.8 %collective-permute-start.13 = (f32[64,128]{1,0:T(8,128)S(1)}, f32[64,128]{1,0:T(8,128)S(1)}, u32[]{:S(2)}, u32[]{:S(2)}) collective-permute-start(f32[64,128]{1,0:T(8,128)S(1)} %get-tuple-element.63.refs_1_), channel_id=1, source_target_pairs={{0,32},{32,0},{1,33},{33,1},{2,34},{34,2},{3,35},{35,3},{4,36},{36... | collective-permute-start | bytes 98312 | tf_op jit(solution)/shard_map/ppermute | solution.py:504
  135.6 1.0 lower.7.refs_7_
  136.6 3.8 %all-to-all-start.7 = ((f32[8,32,128]{2,1,0:T(8,128)}), f32[8,32,128]{2,1,0:T(8,128)S(1)}, u32[]{:S(2)}, u32[]{:S(2)}) async-start(f32[8,32,128]{2,1,0:T(8,128)} %lower.7.refs_7_), calls=%async_computation.7 | async-start | bytes 262144 | tf_op jit(solution)/shard_map/all_to_all | solution.py:508
  140.4 5.9 %near.5.refs_4_ = f32[16,1152]{1,0:T(8,128)S(1)} custom-call(s32[4]{0:T(128)S(1)} %bitcast.30, f32[16,1152]{1,0:T(8,128)S(1)} %get-tuple-element.64.refs_4_.refs_1_, f32[16,1152]{1,0:T(8,128)S(1)} %collective-permute-done.14.refs_5_.refs_2_, f32[16,1152]{1,0:T(8,128)S(1)} %collective-permute-done.15.refs_6_.refs_3_, ...), custom_call_target="tpu_custom_call" | custom-call | flops 4000000000 | bytes 500000 | tf_op jit(solution)/shard_map/near/pallas_call | solution.py:441
  146.2 2.1 %all-to-all-done.7.refs_1_ = f32[8,32,128]{2,1,0:T(8,128)S(1)} async-done(((f32[8,32,128]{2,1,0:T(8,128)}), f32[8,32,128]{2,1,0:T(8,128)S(1)}, u32[]{:S(2)}, u32[]{:S(2)}) %all-to-all-start.7) | async-done | bytes 131104 | tf_op jit(solution)/shard_map/all_to_all | solution.py:508
  148.3 1.2 fourth.1
  149.5 21.7 %all_to_all.51 = f32[256,1,128]{2,1,0:T(1,128)S(1)} all-to-all(f32[256,1,128]{2,1,0:T(1,128)S(1)} %bitcast.14), channel_id=1, replica_groups=mesh['y'=4,'core'=2,'x'=4,'z'=8] {'y','core','x','z'}, dimensions={0} | all-to-all | bytes 262144 | tf_op jit(solution)/shard_map/all_to_all | solution.py:635
  (51 shorter events, 8.3 us)
Async XLA Ops:
  0.6 29.7 %copy-start = (s32[8,4]{0,1:T(4,128)S(1)}, s32[8,4]{0,1:T(4,128)}, u32[]{:S(2)}) copy-start(s32[8,4]{0,1:T(4,128)} %param.18) | copy-start | bytes 388
  0.6 31.6 %copy-start.8 = (s32[4,1]{0,1:T(1,128)S(1)}, s32[4,1]{0,1:T(1,128)}, u32[]{:S(2)}) copy-start(s32[4,1]{0,1:T(1,128)} %param.17) | copy-start | bytes 52
  0.7 31.6 %copy-start.2 = (f32[4,1,64,64]{3,2,1,0:T(8,128)S(1)}, f32[4,1,64,64]{3,2,1,0:T(8,128)}, u32[]{:S(2)}) copy-start(f32[4,1,64,64]{3,2,1,0:T(8,128)} %param.15) | copy-start | bytes 196612
  0.7 31.6 %copy-start.5 = (f32[8,64,64]{2,1,0:T(8,128)S(1)}, f32[8,64,64]{2,1,0:T(8,128)}, u32[]{:S(2)}) copy-start(f32[8,64,64]{2,1,0:T(8,128)} %param.16) | copy-start | bytes 393220
  2.5 17.6 %collective-permute-start = (f32[80,1024]{1,0:T(8,128)S(1)}, f32[80,1024]{1,0:T(8,128)S(1)}, u32[]{:S(2)}, u32[]{:S(2)}) collective-permute-start(f32[80,1024]{1,0:T(8,128)S(1)} %constant_dynamic-update-slice_fusion.refs_1_), channel_id=1, source_target_pairs={{0,2},{1,3},{2,0},{3,1},{4,6},{5,7},{6,4},{7,5},{8,10},{9,11},{10,... | collective-permute-start | bytes 983048 | tf_op jit(solution)/shard_map/ppermute | solution.py:500
  9.9 20.1 %copy-start.10 = (f32[32,128]{1,0:T(8,128)S(1)}, f32[32,128]{1,0:T(8,128)}, u32[]{:S(2)}) copy-start(f32[32,128]{1,0:T(8,128)} %get-tuple-element.42.refs_7_) | copy-start | bytes 49156
  9.9 22.3 %copy-start.9 = (f32[64,64]{1,0:T(8,128)S(1)}, f32[64,64]{1,0:T(8,128)}, u32[]{:S(2)}) copy-start(f32[64,64]{1,0:T(8,128)} %get-tuple-element.40.refs_5_) | copy-start | bytes 49156
  9.9 23.6 %copy-start.11 = (f32[16,128]{1,0:T(8,128)S(1)}, f32[16,128]{1,0:T(8,128)}, u32[]{:S(2)}) copy-start(f32[16,128]{1,0:T(8,128)} %get-tuple-element.41.refs_5_) | copy-start | bytes 24580
  9.9 17.3 %all-to-all-start = ((f32[16,64,128]{2,1,0:T(8,128)}), f32[16,64,128]{2,1,0:T(8,128)S(1)}, u32[]{:S(2)}, u32[]{:S(2)}) async-start(f32[16,64,128]{2,1,0:T(8,128)} %get-tuple-element.36), calls=%async_computation | async-start | bytes 1048576 | tf_op jit(solution)/shard_map/all_to_all | solution.py:512
  16.8 23.8 %collective-permute-start.4 = (f32[80,1024]{1,0:T(8,128)S(1)}, f32[80,1024]{1,0:T(8,128)S(1)}, u32[]{:S(2)}, u32[]{:S(2)}) collective-permute-start(f32[80,1024]{1,0:T(8,128)S(1)} %constant_dynamic-update-slice_fusion.refs_1_), channel_id=1, source_target_pairs={{0,1},{1,0},{2,3},{3,2},{4,5},{5,4},{6,7},{7,6},{8,9},{9,8},{10,11... | collective-permute-start | bytes 983048 | tf_op jit(solution)/shard_map/ppermute | solution.py:500
  20.1 0.7 copy-start.7
  27.8 5.7 %collective-permute-start.1 = (f32[64,128]{1,0:T(8,128)S(1)}, f32[64,128]{1,0:T(8,128)S(1)}, u32[]{:S(2)}, u32[]{:S(2)}) collective-permute-start(f32[64,128]{1,0:T(8,128)S(1)} %get-tuple-element.39.refs_2_), channel_id=1, source_target_pairs={{0,32},{32,0},{1,33},{33,1},{2,34},{34,2},{3,35},{35,3},{4,36},{36... | collective-permute-start | bytes 98312 | tf_op jit(solution)/shard_map/ppermute | solution.py:504
  30.0 3.5 %collective-permute-start.2 = (f32[32,128]{1,0:T(8,128)S(1)}, f32[32,128]{1,0:T(8,128)S(1)}, u32[]{:S(2)}, u32[]{:S(2)}) collective-permute-start(f32[32,128]{1,0:T(8,128)S(1)} %copy-done.10), channel_id=1, source_target_pairs={{0,8},{8,0},{16,24},{24,16},{1,9},{9,1},{17,25},{25,17},{2,10},{10... | collective-permute-start | bytes 49160 | tf_op jit(solution)/shard_map/ppermute | solution.py:566
  30.5 14.3 %collective-permute-start.3 = (f32[80,1024]{1,0:T(8,128)S(1)}, f32[80,1024]{1,0:T(8,128)S(1)}, u32[]{:S(2)}, u32[]{:S(2)}) collective-permute-start(f32[80,1024]{1,0:T(8,128)S(1)} %collective-permute-done.refs_2_), channel_id=1, source_target_pairs={{0,1},{1,0},{2,3},{3,2},{4,5},{5,4},{6,7},{7,6},{8,9},{9,8},{10,11... | collective-permute-start | bytes 983048 | tf_op jit(solution)/shard_map/ppermute | solution.py:500
  35.1 15.7 %all-to-all-start.1 = ((f32[8,64,128]{2,1,0:T(8,128)}), f32[8,64,128]{2,1,0:T(8,128)S(1)}, u32[]{:S(2)}, u32[]{:S(2)}) async-start(f32[8,64,128]{2,1,0:T(8,128)} %lower.4.refs_5_), calls=%async_computation.1 | async-start | bytes 524288 | tf_op jit(solution)/shard_map/all_to_all | solution.py:508
  40.6 10.2 %copy-start.1 = (bf16[128,1024]{1,0:T(8,128)(2,1)S(1)}, bf16[128,1024]{1,0:T(8,128)(2,1)}, u32[]{:S(2)}) copy-start(bf16[128,1024]{1,0:T(8,128)(2,1)} %get-tuple-element.43.refs_3_.refs_5_) | copy-start | bytes 786436
  40.6 10.2 %copy-start.4 = (bf16[64,512]{1,0:T(8,128)(2,1)S(1)}, bf16[64,512]{1,0:T(8,128)(2,1)}, u32[]{:S(2)}) copy-start(bf16[64,512]{1,0:T(8,128)(2,1)} %get-tuple-element.48.refs_5_.refs_6_) | copy-start | bytes 196612
  44.8 40.5 %copy-start.6 = (bf16[64,128]{1,0:T(8,128)(2,1)S(1)}, bf16[64,128]{1,0:T(8,128)(2,1)}, u32[]{:S(2)}) copy-start(bf16[64,128]{1,0:T(8,128)(2,1)} %get-tuple-element.55.refs_5_) | copy-start | bytes 49156
  53.6 13.2 %all-to-all-start.2 = ((f32[16,32,128]{2,1,0:T(8,128)}), f32[16,32,128]{2,1,0:T(8,128)S(1)}, u32[]{:S(2)}, u32[]{:S(2)}) async-start(f32[16,32,128]{2,1,0:T(8,128)} %get-tuple-element.49), calls=%async_computation.2 | async-start | bytes 524288 | tf_op jit(solution)/shard_map/all_to_all | solution.py:512
  59.3 12.4 %collective-permute-start.6 = (f32[16,1152]{1,0:T(8,128)S(1)}, f32[16,1152]{1,0:T(8,128)S(1)}, u32[]{:S(2)}, u32[]{:S(2)}) collective-permute-start(f32[16,1152]{1,0:T(8,128)S(1)} %get-tuple-element.52.refs_4_.refs_1_.refs_7_.refs_2_), channel_id=1, source_target_pairs={{0,1},{1,0},{2,3},{3,2},{4,5},{5,4},{6,7},{7,6},{8,9},{9,8},{10,11... | collective-permute-start | bytes 221192 | tf_op jit(solution)/shard_map/ppermute | solution.py:500
  59.4 12.3 %collective-permute-start.7 = (f32[16,1152]{1,0:T(8,128)S(1)}, f32[16,1152]{1,0:T(8,128)S(1)}, u32[]{:S(2)}, u32[]{:S(2)}) collective-permute-start(f32[16,1152]{1,0:T(8,128)S(1)} %get-tuple-element.52.refs_4_.refs_1_.refs_7_.refs_2_), channel_id=1, source_target_pairs={{0,2},{1,3},{2,0},{3,1},{4,6},{5,7},{6,4},{7,5},{8,10},{9,11},{10,... | collective-permute-start | bytes 221192 | tf_op jit(solution)/shard_map/ppermute | solution.py:500
  61.2 10.4 %collective-permute-start.8 = (f32[16,1152]{1,0:T(8,128)S(1)}, f32[16,1152]{1,0:T(8,128)S(1)}, u32[]{:S(2)}, u32[]{:S(2)}) collective-permute-start(f32[16,1152]{1,0:T(8,128)S(1)} %get-tuple-element.52.refs_4_.refs_1_.refs_7_.refs_2_), channel_id=1, source_target_pairs={{0,3},{1,2},{2,1},{3,0},{4,7},{5,6},{6,5},{7,4},{8,11},{9,10},{10,... | collective-permute-start | bytes 221192 | tf_op jit(solution)/shard_map/ppermute | solution.py:500
  67.4 5.1 %collective-permute-start.5 = (f32[64,128]{1,0:T(8,128)S(1)}, f32[64,128]{1,0:T(8,128)S(1)}, u32[]{:S(2)}, u32[]{:S(2)}) collective-permute-start(f32[64,128]{1,0:T(8,128)S(1)} %get-tuple-element.51.refs_1_), channel_id=1, source_target_pairs={{0,32},{32,0},{1,33},{33,1},{2,34},{34,2},{3,35},{35,3},{4,36},{36... | collective-permute-start | bytes 98312 | tf_op jit(solution)/shard_map/ppermute | solution.py:504
  73.6 11.8 %all-to-all-start.3 = ((f32[8,32,128]{2,1,0:T(8,128)}), f32[8,32,128]{2,1,0:T(8,128)S(1)}, u32[]{:S(2)}, u32[]{:S(2)}) async-start(f32[8,32,128]{2,1,0:T(8,128)} %lower.5.refs_7_), calls=%async_computation.3 | async-start | bytes 262144 | tf_op jit(solution)/shard_map/all_to_all | solution.py:508
  87.7 11.2 %all-to-all-start.4 = ((f32[16,32,128]{2,1,0:T(8,128)}), f32[16,32,128]{2,1,0:T(8,128)S(1)}, u32[]{:S(2)}, u32[]{:S(2)}) async-start(f32[16,32,128]{2,1,0:T(8,128)} %get-tuple-element.56), calls=%async_computation.4 | async-start | bytes 524288 | tf_op jit(solution)/shard_map/all_to_all | solution.py:512
  91.2 12.0 %collective-permute-start.10 = (f32[16,1152]{1,0:T(8,128)S(1)}, f32[16,1152]{1,0:T(8,128)S(1)}, u32[]{:S(2)}, u32[]{:S(2)}) collective-permute-start(f32[16,1152]{1,0:T(8,128)S(1)} %get-tuple-element.59.refs_4_.refs_1_), channel_id=1, source_target_pairs={{0,1},{1,0},{2,3},{3,2},{4,5},{5,4},{6,7},{7,6},{8,9},{9,8},{10,11... | collective-permute-start | bytes 221192 | tf_op jit(solution)/shard_map/ppermute | solution.py:500
  91.3 11.9 %collective-permute-start.11 = (f32[16,1152]{1,0:T(8,128)S(1)}, f32[16,1152]{1,0:T(8,128)S(1)}, u32[]{:S(2)}, u32[]{:S(2)}) collective-permute-start(f32[16,1152]{1,0:T(8,128)S(1)} %get-tuple-element.59.refs_4_.refs_1_), channel_id=1, source_target_pairs={{0,2},{1,3},{2,0},{3,1},{4,6},{5,7},{6,4},{7,5},{8,10},{9,11},{10,... | collective-permute-start | bytes 221192 | tf_op jit(solution)/shard_map/ppermute | solution.py:500
  92.8 10.4 %collective-permute-start.12 = (f32[16,1152]{1,0:T(8,128)S(1)}, f32[16,1152]{1,0:T(8,128)S(1)}, u32[]{:S(2)}, u32[]{:S(2)}) collective-permute-start(f32[16,1152]{1,0:T(8,128)S(1)} %get-tuple-element.59.refs_4_.refs_1_), channel_id=1, source_target_pairs={{0,3},{1,2},{2,1},{3,0},{4,7},{5,6},{6,5},{7,4},{8,11},{9,10},{10,... | collective-permute-start | bytes 221192 | tf_op jit(solution)/shard_map/ppermute | solution.py:500
  99.4 4.6 %collective-permute-start.9 = (f32[64,128]{1,0:T(8,128)S(1)}, f32[64,128]{1,0:T(8,128)S(1)}, u32[]{:S(2)}, u32[]{:S(2)}) collective-permute-start(f32[64,128]{1,0:T(8,128)S(1)} %get-tuple-element.58.refs_1_), channel_id=1, source_target_pairs={{0,32},{32,0},{1,33},{33,1},{2,34},{34,2},{3,35},{35,3},{4,36},{36... | collective-permute-start | bytes 98312 | tf_op jit(solution)/shard_map/ppermute | solution.py:504
  105.1 11.7 %all-to-all-start.5 = ((f32[8,32,128]{2,1,0:T(8,128)}), f32[8,32,128]{2,1,0:T(8,128)S(1)}, u32[]{:S(2)}, u32[]{:S(2)}) async-start(f32[8,32,128]{2,1,0:T(8,128)} %lower.6.refs_7_), calls=%async_computation.5 | async-start | bytes 262144 | tf_op jit(solution)/shard_map/all_to_all | solution.py:508
  114.7 56.5 %copy-start.3 = (f32[16,1024]{1,0:T(8,128)S(1)}, f32[16,1024]{1,0:T(8,128)}, u32[]{:S(2)}) copy-start(f32[16,1024]{1,0:T(8,128)} %refs_1_.3) | copy-start | bytes 196612
  119.1 11.2 %all-to-all-start.6 = ((f32[16,32,128]{2,1,0:T(8,128)}), f32[16,32,128]{2,1,0:T(8,128)S(1)}, u32[]{:S(2)}, u32[]{:S(2)}) async-start(f32[16,32,128]{2,1,0:T(8,128)} %get-tuple-element.61), calls=%async_computation.6 | async-start | bytes 524288 | tf_op jit(solution)/shard_map/all_to_all | solution.py:512
  122.6 12.1 %collective-permute-start.14 = (f32[16,1152]{1,0:T(8,128)S(1)}, f32[16,1152]{1,0:T(8,128)S(1)}, u32[]{:S(2)}, u32[]{:S(2)}) collective-permute-start(f32[16,1152]{1,0:T(8,128)S(1)} %get-tuple-element.64.refs_4_.refs_1_), channel_id=1, source_target_pairs={{0,1},{1,0},{2,3},{3,2},{4,5},{5,4},{6,7},{7,6},{8,9},{9,8},{10,11... | collective-permute-start | bytes 221192 | tf_op jit(solution)/shard_map/ppermute | solution.py:500
  122.8 11.9 %collective-permute-start.15 = (f32[16,1152]{1,0:T(8,128)S(1)}, f32[16,1152]{1,0:T(8,128)S(1)}, u32[]{:S(2)}, u32[]{:S(2)}) collective-permute-start(f32[16,1152]{1,0:T(8,128)S(1)} %get-tuple-element.64.refs_4_.refs_1_), channel_id=1, source_target_pairs={{0,2},{1,3},{2,0},{3,1},{4,6},{5,7},{6,4},{7,5},{8,10},{9,11},{10,... | collective-permute-start | bytes 221192 | tf_op jit(solution)/shard_map/ppermute | solution.py:500
  124.3 10.5 %collective-permute-start.16 = (f32[16,1152]{1,0:T(8,128)S(1)}, f32[16,1152]{1,0:T(8,128)S(1)}, u32[]{:S(2)}, u32[]{:S(2)}) collective-permute-start(f32[16,1152]{1,0:T(8,128)S(1)} %get-tuple-element.64.refs_4_.refs_1_), channel_id=1, source_target_pairs={{0,3},{1,2},{2,1},{3,0},{4,7},{5,6},{6,5},{7,4},{8,11},{9,10},{10,... | collective-permute-start | bytes 221192 | tf_op jit(solution)/shard_map/ppermute | solution.py:500
  130.9 4.7 %collective-permute-start.13 = (f32[64,128]{1,0:T(8,128)S(1)}, f32[64,128]{1,0:T(8,128)S(1)}, u32[]{:S(2)}, u32[]{:S(2)}) collective-permute-start(f32[64,128]{1,0:T(8,128)S(1)} %get-tuple-element.63.refs_1_), channel_id=1, source_target_pairs={{0,32},{32,0},{1,33},{33,1},{2,34},{34,2},{3,35},{35,3},{4,36},{36... | collective-permute-start | bytes 98312 | tf_op jit(solution)/shard_map/ppermute | solution.py:504
  136.6 11.7 %all-to-all-start.7 = ((f32[8,32,128]{2,1,0:T(8,128)}), f32[8,32,128]{2,1,0:T(8,128)S(1)}, u32[]{:S(2)}, u32[]{:S(2)}) async-start(f32[8,32,128]{2,1,0:T(8,128)} %lower.7.refs_7_), calls=%async_computation.7 | async-start | bytes 262144 | tf_op jit(solution)/shard_map/all_to_all | solution.py:508

commit v6 on v5

--- a/solution.py
+++ b/solution.py
@@ -72,22 +72,14 @@
     return jnp.concatenate([own, lifted[:, 0:64]], axis=1), lifted[:, 64:192], lifted[:, 192:256]
 
 
-def send(block, out, sems):
-    copies = [pltpu.make_async_copy(block, out.at[i], sems.at[i]) for i in range(out.shape[0])]
-    for copy in copies:
-        copy.start()
-    return copies
-
-
-def write_moments(extended, out, block, sems, v, own, weighed, chain):
+def write_moments(extended, out, v, own, weighed, chain):
     first, middle, top = lift(own, chain[...])
-    block[0:16, :] = middle
-    block[16:32, :] = jnp.concatenate([top, square_sum(weighed)], axis=1)
-    copies = send(block, out, sems)
+    last = jnp.concatenate([top, square_sum(weighed)], axis=1)
+    for i in range(out.shape[0]):
+        out[i, 0:16, :] = middle
+        out[i, 16:32, :] = last
     extended[:, 0 : v.shape[1]] = v
     extended[:, v.shape[1] :] = first
-    for copy in copies:
-        copy.wait()
 
 
 def packed(skeleton):
@@ -310,13 +302,13 @@
 
 
 def lower_kernel(high, mine, other, table, own, *refs):
-    out, block, sems = refs[-3:]
+    out = refs[-1]
     field, second = lower_blocks(high, mine, other, table, own)
     norm = sum(side[j * 16 : (j + 1) * 16, 64:128] for side in (mine, other) for j in range(4))
-    block[0:16, :] = jnp.concatenate([field, norm], axis=1)
-    block[16:32, :] = second
-    for copy in send(block, out, sems):
-        copy.wait()
+    first = jnp.concatenate([field, norm], axis=1)
+    for i in range(out.shape[0]):
+        out[i, 0:16, :] = first
+        out[i, 16:32, :] = second
 
 
 def first_lower_kernel(scalars, high, mine, other, table, own, skeletons, second, moved, out):
@@ -359,27 +351,27 @@
 
 
 def first_kernel(
-    scalars, received, skeletons, bases, near, chain, table, v1, out, block, sems
+    scalars, received, skeletons, bases, near, chain, table, v1, out
 ):
     table[...] = low_couplings(scalars, skeletons, received, chain)
     image, _, _ = apply_far(scalars, received, table, bases, near)
     own = times_t(image, bases[...])
-    write_moments(v1, out, block, sems, image, own, image, chain)
+    write_moments(v1, out, image, own, image, chain)
 
 
 def second_kernel(
-    scalars, received, table, bases, near, gram, chain, v2, scaled, sums, out, block, sems
+    scalars, received, table, bases, near, gram, chain, v2, scaled, sums, out
 ):
     image, norm, field = apply_far(scalars, received, table, bases, near)
     v2[...] = image
     sums[...] = jnp.broadcast_to(norm, sums.shape)
     size = 1.0 / jnp.sqrt(norm)
     own = moment_of(near, field, gram) * size
-    write_moments(scaled, out, block, sems, image * size, own, image, chain)
+    write_moments(scaled, out, image * size, own, image, chain)
 
 
 def third_kernel(
-    scalars, received, table, bases, near, gram, chain, v1, sums, image, step, out, block, sems
+    scalars, received, table, bases, near, gram, chain, v1, sums, image, step, out
 ):
     product, along, field = apply_far(scalars, received, table, bases, near)
     leaf = product.shape[1]
@@ -389,7 +381,7 @@
     new = v1[:, 0:leaf] - back * product
     own = v1[:, leaf : leaf + 64] - back * moment_of(near, field, gram)
     step[...] = jnp.broadcast_to(size, step.shape)
-    write_moments(image, out, block, sems, new, own, new, chain)
+    write_moments(image, out, new, own, new, chain)
 
 
 def diagonal():
@@ -442,17 +434,13 @@
         body,
         out_shape=outs,
         in_specs=[SMEM] * len(scalars) + [VMEM] * len(arrays) + [ANY] * len(after),
-        out_specs=jax.tree.map(lambda a: ANY if len(a.shape) == 4 or a.shape[1:] == (32, 128) else VMEM, outs),
+        out_specs=jax.tree.map(lambda a: ANY if len(a.shape) == 4 else VMEM, outs),
         scratch_shapes=list(scratch),
         input_output_aliases=alias or {},
         name=name,
         compiler_params=pltpu.CompilerParams(vmem_limit_bytes=limit * MIB),
         cost_estimate=pl.CostEstimate(flops=flops, bytes_accessed=500000, transcendentals=0),
     )(*scalars, *arrays, *after)
-
-
-def block(copies):
-    return [pltpu.VMEM((32, 128), F32), pltpu.SemaphoreType.DMA((copies,))]
 
 
 def build(scalars, own, others, choice, near, after, name, kernels=()):
@@ -564,7 +552,7 @@
     kernels, near = build(scalars, both, [], None, None, [two], "build_own")
     from_yx = over_yx(outgoing)
     second_moved = lax.ppermute(second, "x", [(i, i ^ 1) for i in range(4)])
-    spread = gather(from_yx, [near])
+    spread = gather(from_yx, [near, second_moved])
     top_table = call(
         top_kernel,
         shaped(128, 576, dtype=BF16),
@@ -580,7 +568,7 @@
         "lower",
     )
     kernels, near = build(
-        scalars, both, [two, one], 1, near, [outgoing], "build_a", [kernels]
+        scalars, both, [two, one], 1, near, [outgoing, three_off], "build_a", [kernels]
     )
     kernels, near = build(
         scalars, both, [two, three_off], 3, near, [outgoing], "build_b", [kernels]
@@ -591,7 +579,6 @@
         [scalars],
         [over_z(outgoing), chain_skeletons, bases, near, chain],
         "first",
-        scratch=block(16),
     )
 
     def operate(extended, outgoing):
@@ -604,7 +591,6 @@
             [*spread, top_table, extended],
             "lower",
             after=moved,
-            scratch=block(8),
         )
         near = near_product(scalars, [extended, *moved], bases, kernels, lower)
         return over_z(lower), table, bases, near
@@ -615,7 +601,6 @@
         [scalars],
         [*operate(v1, outgoing), gram, chain],
         "second",
-        scratch=block(16),
     )
     image, step, outgoing = call(
         third_kernel,
@@ -623,7 +608,6 @@
         [scalars],
         [*operate(scaled, outgoing), gram, chain, v1, sums],
         "third",
-        scratch=block(16),
     )
     along, fresh, outgoing = call(
         fourth_kernel,

time: 173 us -> 172 us (level)
    all_to_all x4, waiting for transfers between devices: 7.93 us -> 10.5 us  [over_z(): return lax.all_to_all(v, 'z', 0, 0)]
    ppermute x4, starting transfers between devices: 14 us -> 11.6 us  [other_core(): return lax.ppermute(v, 'core', [(0, 1), (1, 0)])]
    all_to_all x4, waiting for transfers between devices: 14.2 us -> 12.5 us  [over_yx(): return lax.all_to_all(v, ('y', 'x'), 0, 0)]
where the time goes in v6:
time: 172 us; the launch traced here: 171 us
  starting transfers between devices  68.4 us (40%)
  Pallas kernels  50.7 us (29%)
  waiting for transfers between devices  25.9 us (15%)
  blocking collectives  21.8 us (13%)
  local copies, waits for them, and re-layouts  2.76 us (2%)
    pallas_call x21, Pallas kernels, call(): pl.pallas_call(body, out_shape=outs, in_specs=[SMEM] * len(scalars) + [VM...  50.7 us
    all_to_all x1, blocking collectives, local(): shares = lax.all_to_all(outgoing, ('y', 'core', 'x', 'z'), 0, 0, tiled=True)  21.8 us
    all_to_all x4, starting transfers between devices, over_yx(): return lax.all_to_all(v, ('y', 'x'), 0, 0)  19.9 us
    ppermute x12, starting transfers between devices, along_z(): return lax.ppermute(v, 'z', [(i, i ^ offset) for i in range(8)])  18.3 us
    all_to_all x4, starting transfers between devices, over_z(): return lax.all_to_all(v, 'z', 0, 0)  17.3 us
    all_to_all x4, waiting for transfers between devices, over_yx(): return lax.all_to_all(v, ('y', 'x'), 0, 0)  12.5 us
    ppermute x4, starting transfers between devices, other_core(): return lax.ppermute(v, 'core', [(0, 1), (1, 0)])  11.6 us
    all_to_all x4, waiting for transfers between devices, over_z(): return lax.all_to_all(v, 'z', 0, 0)  10.5 us
  transfers between devices with their start and end apart: 25, of which 12 were waited for; matrix products, arithmetic and copies ran while one was open for 0% of the time, Pallas kernels for 23%

profile of v6, /device:TPU:1, one launch (start us, length us, event | category | flops | bytes accessed | tf_op | source)
XLA Modules:
  0.0 170.6 jit_solution(156291626134289774)
XLA Ops:
  0.7 1.0 constant_dynamic-update-slice_fusion.1
  2.5 3.8 %collective-permute-start = (f32[80,1024]{1,0:T(8,128)S(1)}, f32[80,1024]{1,0:T(8,128)S(1)}, u32[]{:S(2)}, u32[]{:S(2)}) collective-permute-start(f32[80,1024]{1,0:T(8,128)S(1)} %constant_dynamic-update-slice_fusion.refs_1_), channel_id=1, source_target_pairs={{0,2},{1,3},{2,0},{3,1},{4,6},{5,7},{6,4},{7,5},{8,10},{9,11},{10,... | collective-permute-start | bytes 983048 | tf_op jit(solution)/shard_map/ppermute | solution.py:488
  6.4 3.5 %prepare.1 = (bf16[128,1024]{1,0:T(8,128)(2,1)}, bf16[64,512]{1,0:T(8,128)(2,1)}, f32[64,64]{1,0:T(8,128)}, bf16[64,128]{1,0:T(8,128)(2,1)}, f32[16,128]{1,0:T(8...) custom-call(s32[4]{0:T(128)} %bitcast.15, s32[1,1024]{1,0:T(1,128)} %refs_1_.2, f32[64,1024]{1,0:T(8,128)} %refs_2_.1, ...), custom_call_target="tpu_custom_call" | custom-call | flops 100000 | bytes 500000 | tf_op jit(solution)/shard_map/prepare/pallas_call | solution.py:433
  9.9 6.9 %all-to-all-start = ((f32[16,64,128]{2,1,0:T(8,128)}), f32[16,64,128]{2,1,0:T(8,128)S(1)}, u32[]{:S(2)}, u32[]{:S(2)}) async-start(f32[16,64,128]{2,1,0:T(8,128)} %get-tuple-element.36), calls=%async_computation | async-start | bytes 1048576 | tf_op jit(solution)/shard_map/all_to_all | solution.py:500
  16.8 1.7 %collective-permute-start.4 = (f32[80,1024]{1,0:T(8,128)S(1)}, f32[80,1024]{1,0:T(8,128)S(1)}, u32[]{:S(2)}, u32[]{:S(2)}) collective-permute-start(f32[80,1024]{1,0:T(8,128)S(1)} %constant_dynamic-update-slice_fusion.refs_1_), channel_id=1, source_target_pairs={{0,1},{1,0},{2,3},{3,2},{4,5},{5,4},{6,7},{7,6},{8,9},{9,8},{10,11... | collective-permute-start | bytes 983048 | tf_op jit(solution)/shard_map/ppermute | solution.py:488
  18.5 1.3 collective-permute-start.1
  20.1 1.9 %collective-permute-start.3 = (f32[80,1024]{1,0:T(8,128)S(1)}, f32[80,1024]{1,0:T(8,128)S(1)}, u32[]{:S(2)}, u32[]{:S(2)}) collective-permute-start(f32[80,1024]{1,0:T(8,128)S(1)} %collective-permute-done.refs_2_), channel_id=1, source_target_pairs={{0,1},{1,0},{2,3},{3,2},{4,5},{5,4},{6,7},{7,6},{8,9},{9,8},{10,11... | collective-permute-start | bytes 983048 | tf_op jit(solution)/shard_map/ppermute | solution.py:488
  22.7 4.1 %build_own.1 = (bf16[3,2,1024,1024]{3,2,1,0:T(8,128)(2,1)}, f32[16,1024]{1,0:T(8,128)S(1)}) custom-call(s32[4]{0:T(128)S(1)} %bitcast.16, f32[80,1024]{1,0:T(8,128)S(1)} %constant_dynamic-update-slice_fusion.refs_1_, f32[80,1024]{1,0:T(8,128)S(1)} %collective-permute-done.refs_2_), custom_call_target="tpu_custom_call" | custom-call | flops 4000000000 | bytes 500000 | tf_op jit(solution)/shard_map/build_own/pallas_call | solution.py:433
  27.8 2.4 %collective-permute-start.2 = (f32[64,128]{1,0:T(8,128)S(1)}, f32[64,128]{1,0:T(8,128)S(1)}, u32[]{:S(2)}, u32[]{:S(2)}) collective-permute-start(f32[64,128]{1,0:T(8,128)S(1)} %get-tuple-element.40.refs_2_), channel_id=1, source_target_pairs={{0,32},{32,0},{1,33},{33,1},{2,34},{34,2},{3,35},{35,3},{4,36},{36... | collective-permute-start | bytes 98312 | tf_op jit(solution)/shard_map/ppermute | solution.py:492
  30.4 1.3 tops.1.refs_4_.refs_3_
  31.7 1.6 lower.4.refs_5_
  33.3 6.4 %all-to-all-start.1 = ((f32[8,64,128]{2,1,0:T(8,128)}), f32[8,64,128]{2,1,0:T(8,128)S(1)}, u32[]{:S(2)}, u32[]{:S(2)}) async-start(f32[8,64,128]{2,1,0:T(8,128)} %lower.4.refs_5_), calls=%async_computation.1 | async-start | bytes 524288 | tf_op jit(solution)/shard_map/all_to_all | solution.py:496
  39.7 4.2 %build_a.1 = (bf16[3,2,1024,1024]{3,2,1,0:T(8,128)(2,1)}, f32[16,1024]{1,0:T(8,128)S(1)}) custom-call(s32[4]{0:T(128)S(1)} %bitcast.20, f32[80,1024]{1,0:T(8,128)S(1)} %constant_dynamic-update-slice_fusion.refs_1_, f32[80,1024]{1,0:T(8,128)S(1)} %collective-permute-done.refs_2_, ...), custom_call_target="tpu_custom_call", output_to_operand_aliasing={{0}: (7, {})} | custom-call | flops 4000000000 | bytes 500000 | tf_op jit(solution)/shard_map/build_a/pallas_call | solution.py:433
  43.9 4.2 %build_b.1 = (bf16[3,2,1024,1024]{3,2,1,0:T(8,128)(2,1)}, f32[16,1024]{1,0:T(8,128)S(1)}) custom-call(s32[4]{0:T(128)S(1)} %bitcast.21, f32[80,1024]{1,0:T(8,128)S(1)} %constant_dynamic-update-slice_fusion.refs_1_, f32[80,1024]{1,0:T(8,128)S(1)} %collective-permute-done.refs_2_, ...), custom_call_target="tpu_custom_call", output_to_operand_aliasing={{0}: (6, {})} | custom-call | flops 4000000000 | bytes 500000 | tf_op jit(solution)/shard_map/build_b/pallas_call | solution.py:433
  48.1 4.0 %all-to-all-done.1.refs_1_ = f32[8,64,128]{2,1,0:T(8,128)S(1)} async-done(((f32[8,64,128]{2,1,0:T(8,128)}), f32[8,64,128]{2,1,0:T(8,128)S(1)}, u32[]{:S(2)}, u32[]{:S(2)}) %all-to-all-start.1) | async-done | bytes 262176 | tf_op jit(solution)/shard_map/all_to_all | solution.py:496
  52.0 2.7 %first.1 = (bf16[128,256]{1,0:T(8,128)(2,1)S(1)}, f32[16,1152]{1,0:T(8,128)S(1)}, f32[16,32,128]{2,1,0:T(8,128)}) custom-call(s32[4]{0:T(128)S(1)} %bitcast.22, f32[8,64,128]{2,1,0:T(8,128)S(1)} %all-to-all-done.1.refs_1_, f32[4,64,64]{2,1,0:T(8,128)S(1)} %bitcast.11, bf16[128,1024]{1,0:T(8,128)(2,1)S(1)} %copy-done.1, ...), custom_call_target="tpu_custom_call" | custom-call | flops 100000 | bytes 500000 | tf_op jit(solution)/shard_map/first/pallas_call | solution.py:433
  54.7 5.9 %all-to-all-start.2 = ((f32[16,32,128]{2,1,0:T(8,128)}), f32[16,32,128]{2,1,0:T(8,128)S(1)}, u32[]{:S(2)}, u32[]{:S(2)}) async-start(f32[16,32,128]{2,1,0:T(8,128)} %get-tuple-element.49), calls=%async_computation.2 | async-start | bytes 524288 | tf_op jit(solution)/shard_map/all_to_all | solution.py:500
  60.9 3.4 %collective-permute-start.6 = (f32[16,1152]{1,0:T(8,128)S(1)}, f32[16,1152]{1,0:T(8,128)S(1)}, u32[]{:S(2)}, u32[]{:S(2)}) collective-permute-start(f32[16,1152]{1,0:T(8,128)S(1)} %get-tuple-element.52.refs_4_.refs_1_.refs_7_.refs_2_), channel_id=1, source_target_pairs={{0,1},{1,0},{2,3},{3,2},{4,5},{5,4},{6,7},{7,6},{8,9},{9,8},{10,11... | collective-permute-start | bytes 221192 | tf_op jit(solution)/shard_map/ppermute | solution.py:488
  64.3 4.4 %all-to-all-done.2.refs_1_ = f32[16,32,128]{2,1,0:T(8,128)S(1)} async-done(((f32[16,32,128]{2,1,0:T(8,128)}), f32[16,32,128]{2,1,0:T(8,128)S(1)}, u32[]{:S(2)}, u32[]{:S(2)}) %all-to-all-start.2) | async-done | bytes 262176 | tf_op jit(solution)/shard_map/all_to_all | solution.py:500
  69.3 1.7 %collective-permute-start.5 = (f32[64,128]{1,0:T(8,128)S(1)}, f32[64,128]{1,0:T(8,128)S(1)}, u32[]{:S(2)}, u32[]{:S(2)}) collective-permute-start(f32[64,128]{1,0:T(8,128)S(1)} %get-tuple-element.51.refs_1_), channel_id=1, source_target_pairs={{0,32},{32,0},{1,33},{33,1},{2,34},{34,2},{3,35},{35,3},{4,36},{36... | collective-permute-start | bytes 98312 | tf_op jit(solution)/shard_map/ppermute | solution.py:492
  71.0 0.8 collective-permute-done.5.refs_2_
  71.9 1.0 lower.5.refs_7_
  72.8 3.4 %all-to-all-start.3 = ((f32[8,32,128]{2,1,0:T(8,128)}), f32[8,32,128]{2,1,0:T(8,128)S(1)}, u32[]{:S(2)}, u32[]{:S(2)}) async-start(f32[8,32,128]{2,1,0:T(8,128)} %lower.5.refs_7_), calls=%async_computation.3 | async-start | bytes 262144 | tf_op jit(solution)/shard_map/all_to_all | solution.py:496
  76.2 5.9 %near.3.refs_4_ = f32[16,1152]{1,0:T(8,128)S(1)} custom-call(s32[4]{0:T(128)S(1)} %bitcast.24, f32[16,1152]{1,0:T(8,128)S(1)} %get-tuple-element.52.refs_4_.refs_1_.refs_7_.refs_2_, f32[16,1152]{1,0:T(8,128)S(1)} %collective-permute-done.6.refs_5_.refs_2_, f32[16,1152]{1,0:T(8,128)S(1)} %collective-permute-done.7.refs_6_.refs_3_, ...), custom_call_target="tpu_custom_call" | custom-call | flops 4000000000 | bytes 500000 | tf_op jit(solution)/shard_map/near/pallas_call | solution.py:433
  82.1 2.5 %all-to-all-done.3.refs_1_ = f32[8,32,128]{2,1,0:T(8,128)S(1)} async-done(((f32[8,32,128]{2,1,0:T(8,128)}), f32[8,32,128]{2,1,0:T(8,128)S(1)}, u32[]{:S(2)}, u32[]{:S(2)}) %all-to-all-start.3) | async-done | bytes 131104 | tf_op jit(solution)/shard_map/all_to_all | solution.py:496
  84.5 2.2 %second.1 = (f32[16,1024]{1,0:T(8,128)S(1)}, f32[16,1152]{1,0:T(8,128)S(1)}, f32[16,128]{1,0:T(8,128)S(1)}, f32[16,32,128]{2,1,0:T(8,128)}) custom-call(s32[4]{0:T(128)S(1)} %bitcast.25, f32[8,32,128]{2,1,0:T(8,128)S(1)} %all-to-all-done.3.refs_1_, bf16[128,256]{1,0:T(8,128)(2,1)S(1)} %get-tuple-element.53.refs_2_, bf16[128,1024]{1,0:T(8,128)(2,1)S(1)} %copy-done.1, ...), custom_call_target="tpu_custom_call" | custom-call | flops 100000 | bytes 500000 | tf_op jit(solution)/shard_map/second/pallas_call | solution.py:433
  86.7 3.5 %all-to-all-start.4 = ((f32[16,32,128]{2,1,0:T(8,128)}), f32[16,32,128]{2,1,0:T(8,128)S(1)}, u32[]{:S(2)}, u32[]{:S(2)}) async-start(f32[16,32,128]{2,1,0:T(8,128)} %get-tuple-element.56), calls=%async_computation.4 | async-start | bytes 524288 | tf_op jit(solution)/shard_map/all_to_all | solution.py:500
  91.6 2.3 %collective-permute-start.10 = (f32[16,1152]{1,0:T(8,128)S(1)}, f32[16,1152]{1,0:T(8,128)S(1)}, u32[]{:S(2)}, u32[]{:S(2)}) collective-permute-start(f32[16,1152]{1,0:T(8,128)S(1)} %get-tuple-element.59.refs_4_.refs_1_), channel_id=1, source_target_pairs={{0,1},{1,0},{2,3},{3,2},{4,5},{5,4},{6,7},{7,6},{8,9},{9,8},{10,11... | collective-permute-start | bytes 221192 | tf_op jit(solution)/shard_map/ppermute | solution.py:488
  93.9 3.9 %all-to-all-done.4.refs_1_ = f32[16,32,128]{2,1,0:T(8,128)S(1)} async-done(((f32[16,32,128]{2,1,0:T(8,128)}), f32[16,32,128]{2,1,0:T(8,128)S(1)}, u32[]{:S(2)}, u32[]{:S(2)}) %all-to-all-start.4) | async-done | bytes 262176 | tf_op jit(solution)/shard_map/all_to_all | solution.py:500
  98.4 3.8 %collective-permute-start.9 = (f32[64,128]{1,0:T(8,128)S(1)}, f32[64,128]{1,0:T(8,128)S(1)}, u32[]{:S(2)}, u32[]{:S(2)}) collective-permute-start(f32[64,128]{1,0:T(8,128)S(1)} %get-tuple-element.58.refs_1_), channel_id=1, source_target_pairs={{0,32},{32,0},{1,33},{33,1},{2,34},{34,2},{3,35},{35,3},{4,36},{36... | collective-permute-start | bytes 98312 | tf_op jit(solution)/shard_map/ppermute | solution.py:492
  103.0 1.0 lower.6.refs_7_
  104.0 3.8 %all-to-all-start.5 = ((f32[8,32,128]{2,1,0:T(8,128)}), f32[8,32,128]{2,1,0:T(8,128)S(1)}, u32[]{:S(2)}, u32[]{:S(2)}) async-start(f32[8,32,128]{2,1,0:T(8,128)} %lower.6.refs_7_), calls=%async_computation.5 | async-start | bytes 262144 | tf_op jit(solution)/shard_map/all_to_all | solution.py:496
  107.7 5.9 %near.4.refs_4_ = f32[16,1152]{1,0:T(8,128)S(1)} custom-call(s32[4]{0:T(128)S(1)} %bitcast.27, f32[16,1152]{1,0:T(8,128)S(1)} %get-tuple-element.59.refs_4_.refs_1_, f32[16,1152]{1,0:T(8,128)S(1)} %collective-permute-done.10.refs_5_.refs_2_, f32[16,1152]{1,0:T(8,128)S(1)} %collective-permute-done.11.refs_6_.refs_3_, ...), custom_call_target="tpu_custom_call" | custom-call | flops 4000000000 | bytes 500000 | tf_op jit(solution)/shard_map/near/pallas_call | solution.py:433
  113.6 2.0 %all-to-all-done.5.refs_1_ = f32[8,32,128]{2,1,0:T(8,128)S(1)} async-done(((f32[8,32,128]{2,1,0:T(8,128)}), f32[8,32,128]{2,1,0:T(8,128)S(1)}, u32[]{:S(2)}, u32[]{:S(2)}) %all-to-all-start.5) | async-done | bytes 131104 | tf_op jit(solution)/shard_map/all_to_all | solution.py:496
  115.6 2.2 %third.1 = (f32[16,1152]{1,0:T(8,128)S(1)}, f32[16,128]{1,0:T(8,128)S(1)}, f32[16,32,128]{2,1,0:T(8,128)}) custom-call(s32[4]{0:T(128)S(1)} %bitcast.28, f32[8,32,128]{2,1,0:T(8,128)S(1)} %all-to-all-done.5.refs_1_, bf16[128,256]{1,0:T(8,128)(2,1)S(1)} %get-tuple-element.53.refs_2_, bf16[128,1024]{1,0:T(8,128)(2,1)S(1)} %copy-done.1, ...), custom_call_target="tpu_custom_call" | custom-call | flops 100000 | bytes 500000 | tf_op jit(solution)/shard_map/third/pallas_call | solution.py:433
  117.8 3.5 %all-to-all-start.6 = ((f32[16,32,128]{2,1,0:T(8,128)}), f32[16,32,128]{2,1,0:T(8,128)S(1)}, u32[]{:S(2)}, u32[]{:S(2)}) async-start(f32[16,32,128]{2,1,0:T(8,128)} %get-tuple-element.61), calls=%async_computation.6 | async-start | bytes 524288 | tf_op jit(solution)/shard_map/all_to_all | solution.py:500
  121.4 1.3 collective-permute-start.16
  122.7 2.3 %collective-permute-start.14 = (f32[16,1152]{1,0:T(8,128)S(1)}, f32[16,1152]{1,0:T(8,128)S(1)}, u32[]{:S(2)}, u32[]{:S(2)}) collective-permute-start(f32[16,1152]{1,0:T(8,128)S(1)} %get-tuple-element.64.refs_4_.refs_1_), channel_id=1, source_target_pairs={{0,1},{1,0},{2,3},{3,2},{4,5},{5,4},{6,7},{7,6},{8,9},{9,8},{10,11... | collective-permute-start | bytes 221192 | tf_op jit(solution)/shard_map/ppermute | solution.py:488
  125.0 3.9 %all-to-all-done.6.refs_1_ = f32[16,32,128]{2,1,0:T(8,128)S(1)} async-done(((f32[16,32,128]{2,1,0:T(8,128)}), f32[16,32,128]{2,1,0:T(8,128)S(1)}, u32[]{:S(2)}, u32[]{:S(2)}) %all-to-all-start.6) | async-done | bytes 262176 | tf_op jit(solution)/shard_map/all_to_all | solution.py:500
  129.5 3.8 %collective-permute-start.13 = (f32[64,128]{1,0:T(8,128)S(1)}, f32[64,128]{1,0:T(8,128)S(1)}, u32[]{:S(2)}, u32[]{:S(2)}) collective-permute-start(f32[64,128]{1,0:T(8,128)S(1)} %get-tuple-element.63.refs_1_), channel_id=1, source_target_pairs={{0,32},{32,0},{1,33},{33,1},{2,34},{34,2},{3,35},{35,3},{4,36},{36... | collective-permute-start | bytes 98312 | tf_op jit(solution)/shard_map/ppermute | solution.py:492
  133.3 0.8 collective-permute-done.13.refs_2_
  134.1 1.0 lower.7.refs_7_
  135.1 3.8 %all-to-all-start.7 = ((f32[8,32,128]{2,1,0:T(8,128)}), f32[8,32,128]{2,1,0:T(8,128)S(1)}, u32[]{:S(2)}, u32[]{:S(2)}) async-start(f32[8,32,128]{2,1,0:T(8,128)} %lower.7.refs_7_), calls=%async_computation.7 | async-start | bytes 262144 | tf_op jit(solution)/shard_map/all_to_all | solution.py:496
  138.8 5.9 %near.5.refs_4_ = f32[16,1152]{1,0:T(8,128)S(1)} custom-call(s32[4]{0:T(128)S(1)} %bitcast.30, f32[16,1152]{1,0:T(8,128)S(1)} %get-tuple-element.64.refs_4_.refs_1_, f32[16,1152]{1,0:T(8,128)S(1)} %collective-permute-done.14.refs_5_.refs_2_, f32[16,1152]{1,0:T(8,128)S(1)} %collective-permute-done.15.refs_6_.refs_3_, ...), custom_call_target="tpu_custom_call" | custom-call | flops 4000000000 | bytes 500000 | tf_op jit(solution)/shard_map/near/pallas_call | solution.py:433
  144.7 2.1 %all-to-all-done.7.refs_1_ = f32[8,32,128]{2,1,0:T(8,128)S(1)} async-done(((f32[8,32,128]{2,1,0:T(8,128)}), f32[8,32,128]{2,1,0:T(8,128)S(1)}, u32[]{:S(2)}, u32[]{:S(2)}) %all-to-all-start.7) | async-done | bytes 131104 | tf_op jit(solution)/shard_map/all_to_all | solution.py:496
  146.7 1.2 fourth.1
  147.9 21.8 %all_to_all.51 = f32[256,1,128]{2,1,0:T(1,128)S(1)} all-to-all(f32[256,1,128]{2,1,0:T(1,128)S(1)} %bitcast.14), channel_id=1, replica_groups=mesh['y'=4,'core'=2,'x'=4,'z'=8] {'y','core','x','z'}, dimensions={0} | all-to-all | bytes 262144 | tf_op jit(solution)/shard_map/all_to_all | solution.py:619
  169.7 0.9 last.1
  (51 shorter events, 7.2 us)
Async XLA Ops:
  0.6 29.6 %copy-start = (s32[8,4]{0,1:T(4,128)S(1)}, s32[8,4]{0,1:T(4,128)}, u32[]{:S(2)}) copy-start(s32[8,4]{0,1:T(4,128)} %param.18) | copy-start | bytes 388
  0.6 29.7 %copy-start.8 = (s32[4,1]{0,1:T(1,128)S(1)}, s32[4,1]{0,1:T(1,128)}, u32[]{:S(2)}) copy-start(s32[4,1]{0,1:T(1,128)} %param.17) | copy-start | bytes 52
  0.7 29.7 %copy-start.2 = (f32[4,1,64,64]{3,2,1,0:T(8,128)S(1)}, f32[4,1,64,64]{3,2,1,0:T(8,128)}, u32[]{:S(2)}) copy-start(f32[4,1,64,64]{3,2,1,0:T(8,128)} %param.15) | copy-start | bytes 196612
  0.7 29.7 %copy-start.5 = (f32[8,64,64]{2,1,0:T(8,128)S(1)}, f32[8,64,64]{2,1,0:T(8,128)}, u32[]{:S(2)}) copy-start(f32[8,64,64]{2,1,0:T(8,128)} %param.16) | copy-start | bytes 393220
  2.5 17.6 %collective-permute-start = (f32[80,1024]{1,0:T(8,128)S(1)}, f32[80,1024]{1,0:T(8,128)S(1)}, u32[]{:S(2)}, u32[]{:S(2)}) collective-permute-start(f32[80,1024]{1,0:T(8,128)S(1)} %constant_dynamic-update-slice_fusion.refs_1_), channel_id=1, source_target_pairs={{0,2},{1,3},{2,0},{3,1},{4,6},{5,7},{6,4},{7,5},{8,10},{9,11},{10,... | collective-permute-start | bytes 983048 | tf_op jit(solution)/shard_map/ppermute | solution.py:488
  9.9 20.5 %copy-start.9 = (f32[64,64]{1,0:T(8,128)S(1)}, f32[64,64]{1,0:T(8,128)}, u32[]{:S(2)}) copy-start(f32[64,64]{1,0:T(8,128)} %get-tuple-element.41.refs_5_) | copy-start | bytes 49156
  9.9 21.8 %copy-start.10 = (f32[32,128]{1,0:T(8,128)S(1)}, f32[32,128]{1,0:T(8,128)}, u32[]{:S(2)}) copy-start(f32[32,128]{1,0:T(8,128)} %get-tuple-element.38.refs_7_) | copy-start | bytes 49156
  9.9 21.8 %copy-start.11 = (f32[16,128]{1,0:T(8,128)S(1)}, f32[16,128]{1,0:T(8,128)}, u32[]{:S(2)}) copy-start(f32[16,128]{1,0:T(8,128)} %get-tuple-element.42.refs_5_) | copy-start | bytes 24580
  9.9 17.3 %all-to-all-start = ((f32[16,64,128]{2,1,0:T(8,128)}), f32[16,64,128]{2,1,0:T(8,128)S(1)}, u32[]{:S(2)}, u32[]{:S(2)}) async-start(f32[16,64,128]{2,1,0:T(8,128)} %get-tuple-element.36), calls=%async_computation | async-start | bytes 1048576 | tf_op jit(solution)/shard_map/all_to_all | solution.py:500
  16.8 22.8 %collective-permute-start.4 = (f32[80,1024]{1,0:T(8,128)S(1)}, f32[80,1024]{1,0:T(8,128)S(1)}, u32[]{:S(2)}, u32[]{:S(2)}) collective-permute-start(f32[80,1024]{1,0:T(8,128)S(1)} %constant_dynamic-update-slice_fusion.refs_1_), channel_id=1, source_target_pairs={{0,1},{1,0},{2,3},{3,2},{4,5},{5,4},{6,7},{7,6},{8,9},{9,8},{10,11... | collective-permute-start | bytes 983048 | tf_op jit(solution)/shard_map/ppermute | solution.py:488
  18.5 8.3 %collective-permute-start.1 = (f32[32,128]{1,0:T(8,128)}, f32[32,128]{1,0:T(8,128)S(1)}, u32[]{:S(2)}, u32[]{:S(2)}) collective-permute-start(f32[32,128]{1,0:T(8,128)} %get-tuple-element.38.refs_7_), channel_id=1, source_target_pairs={{0,8},{8,0},{16,24},{24,16},{1,9},{9,1},{17,25},{25,17},{2,10},{10... | collective-permute-start | bytes 49160 | tf_op jit(solution)/shard_map/ppermute | solution.py:554
  20.1 19.5 %collective-permute-start.3 = (f32[80,1024]{1,0:T(8,128)S(1)}, f32[80,1024]{1,0:T(8,128)S(1)}, u32[]{:S(2)}, u32[]{:S(2)}) collective-permute-start(f32[80,1024]{1,0:T(8,128)S(1)} %collective-permute-done.refs_2_), channel_id=1, source_target_pairs={{0,1},{1,0},{2,3},{3,2},{4,5},{5,4},{6,7},{7,6},{8,9},{9,8},{10,11... | collective-permute-start | bytes 983048 | tf_op jit(solution)/shard_map/ppermute | solution.py:488
  22.1 0.7 copy-start.7
  27.8 3.9 %collective-permute-start.2 = (f32[64,128]{1,0:T(8,128)S(1)}, f32[64,128]{1,0:T(8,128)S(1)}, u32[]{:S(2)}, u32[]{:S(2)}) collective-permute-start(f32[64,128]{1,0:T(8,128)S(1)} %get-tuple-element.40.refs_2_), channel_id=1, source_target_pairs={{0,32},{32,0},{1,33},{33,1},{2,34},{34,2},{3,35},{35,3},{4,36},{36... | collective-permute-start | bytes 98312 | tf_op jit(solution)/shard_map/ppermute | solution.py:492
  33.3 18.8 %all-to-all-start.1 = ((f32[8,64,128]{2,1,0:T(8,128)}), f32[8,64,128]{2,1,0:T(8,128)S(1)}, u32[]{:S(2)}, u32[]{:S(2)}) async-start(f32[8,64,128]{2,1,0:T(8,128)} %lower.4.refs_5_), calls=%async_computation.1 | async-start | bytes 524288 | tf_op jit(solution)/shard_map/all_to_all | solution.py:496
  39.7 12.4 %copy-start.1 = (bf16[128,1024]{1,0:T(8,128)(2,1)S(1)}, bf16[128,1024]{1,0:T(8,128)(2,1)}, u32[]{:S(2)}) copy-start(bf16[128,1024]{1,0:T(8,128)(2,1)} %get-tuple-element.43.refs_3_.refs_5_) | copy-start | bytes 786436
  39.7 12.3 %copy-start.4 = (bf16[64,512]{1,0:T(8,128)(2,1)S(1)}, bf16[64,512]{1,0:T(8,128)(2,1)}, u32[]{:S(2)}) copy-start(bf16[64,512]{1,0:T(8,128)(2,1)} %get-tuple-element.48.refs_5_.refs_6_) | copy-start | bytes 196612
  43.9 40.7 %copy-start.6 = (bf16[64,128]{1,0:T(8,128)(2,1)S(1)}, bf16[64,128]{1,0:T(8,128)(2,1)}, u32[]{:S(2)}) copy-start(bf16[64,128]{1,0:T(8,128)(2,1)} %get-tuple-element.55.refs_5_) | copy-start | bytes 49156
  54.7 14.0 %all-to-all-start.2 = ((f32[16,32,128]{2,1,0:T(8,128)}), f32[16,32,128]{2,1,0:T(8,128)S(1)}, u32[]{:S(2)}, u32[]{:S(2)}) async-start(f32[16,32,128]{2,1,0:T(8,128)} %get-tuple-element.49), calls=%async_computation.2 | async-start | bytes 524288 | tf_op jit(solution)/shard_map/all_to_all | solution.py:500
  60.7 10.3 %collective-permute-start.8 = (f32[16,1152]{1,0:T(8,128)S(1)}, f32[16,1152]{1,0:T(8,128)S(1)}, u32[]{:S(2)}, u32[]{:S(2)}) collective-permute-start(f32[16,1152]{1,0:T(8,128)S(1)} %get-tuple-element.52.refs_4_.refs_1_.refs_7_.refs_2_), channel_id=1, source_target_pairs={{0,3},{1,2},{2,1},{3,0},{4,7},{5,6},{6,5},{7,4},{8,11},{9,10},{10,... | collective-permute-start | bytes 221192 | tf_op jit(solution)/shard_map/ppermute | solution.py:488
  60.8 10.2 %collective-permute-start.7 = (f32[16,1152]{1,0:T(8,128)S(1)}, f32[16,1152]{1,0:T(8,128)S(1)}, u32[]{:S(2)}, u32[]{:S(2)}) collective-permute-start(f32[16,1152]{1,0:T(8,128)S(1)} %get-tuple-element.52.refs_4_.refs_1_.refs_7_.refs_2_), channel_id=1, source_target_pairs={{0,2},{1,3},{2,0},{3,1},{4,6},{5,7},{6,4},{7,5},{8,10},{9,11},{10,... | collective-permute-start | bytes 221192 | tf_op jit(solution)/shard_map/ppermute | solution.py:488
  60.9 10.1 %collective-permute-start.6 = (f32[16,1152]{1,0:T(8,128)S(1)}, f32[16,1152]{1,0:T(8,128)S(1)}, u32[]{:S(2)}, u32[]{:S(2)}) collective-permute-start(f32[16,1152]{1,0:T(8,128)S(1)} %get-tuple-element.52.refs_4_.refs_1_.refs_7_.refs_2_), channel_id=1, source_target_pairs={{0,1},{1,0},{2,3},{3,2},{4,5},{5,4},{6,7},{7,6},{8,9},{9,8},{10,11... | collective-permute-start | bytes 221192 | tf_op jit(solution)/shard_map/ppermute | solution.py:488
  69.3 2.6 %collective-permute-start.5 = (f32[64,128]{1,0:T(8,128)S(1)}, f32[64,128]{1,0:T(8,128)S(1)}, u32[]{:S(2)}, u32[]{:S(2)}) collective-permute-start(f32[64,128]{1,0:T(8,128)S(1)} %get-tuple-element.51.refs_1_), channel_id=1, source_target_pairs={{0,32},{32,0},{1,33},{33,1},{2,34},{34,2},{3,35},{35,3},{4,36},{36... | collective-permute-start | bytes 98312 | tf_op jit(solution)/shard_map/ppermute | solution.py:492
  72.8 11.7 %all-to-all-start.3 = ((f32[8,32,128]{2,1,0:T(8,128)}), f32[8,32,128]{2,1,0:T(8,128)S(1)}, u32[]{:S(2)}, u32[]{:S(2)}) async-start(f32[8,32,128]{2,1,0:T(8,128)} %lower.5.refs_7_), calls=%async_computation.3 | async-start | bytes 262144 | tf_op jit(solution)/shard_map/all_to_all | solution.py:496
  86.7 11.0 %all-to-all-start.4 = ((f32[16,32,128]{2,1,0:T(8,128)}), f32[16,32,128]{2,1,0:T(8,128)S(1)}, u32[]{:S(2)}, u32[]{:S(2)}) async-start(f32[16,32,128]{2,1,0:T(8,128)} %get-tuple-element.56), calls=%async_computation.4 | async-start | bytes 524288 | tf_op jit(solution)/shard_map/all_to_all | solution.py:500
  90.3 11.9 %collective-permute-start.12 = (f32[16,1152]{1,0:T(8,128)S(1)}, f32[16,1152]{1,0:T(8,128)S(1)}, u32[]{:S(2)}, u32[]{:S(2)}) collective-permute-start(f32[16,1152]{1,0:T(8,128)S(1)} %get-tuple-element.59.refs_4_.refs_1_), channel_id=1, source_target_pairs={{0,3},{1,2},{2,1},{3,0},{4,7},{5,6},{6,5},{7,4},{8,11},{9,10},{10,... | collective-permute-start | bytes 221192 | tf_op jit(solution)/shard_map/ppermute | solution.py:488
  91.1 11.1 %collective-permute-start.11 = (f32[16,1152]{1,0:T(8,128)S(1)}, f32[16,1152]{1,0:T(8,128)S(1)}, u32[]{:S(2)}, u32[]{:S(2)}) collective-permute-start(f32[16,1152]{1,0:T(8,128)S(1)} %get-tuple-element.59.refs_4_.refs_1_), channel_id=1, source_target_pairs={{0,2},{1,3},{2,0},{3,1},{4,6},{5,7},{6,4},{7,5},{8,10},{9,11},{10,... | collective-permute-start | bytes 221192 | tf_op jit(solution)/shard_map/ppermute | solution.py:488
  91.6 10.6 %collective-permute-start.10 = (f32[16,1152]{1,0:T(8,128)S(1)}, f32[16,1152]{1,0:T(8,128)S(1)}, u32[]{:S(2)}, u32[]{:S(2)}) collective-permute-start(f32[16,1152]{1,0:T(8,128)S(1)} %get-tuple-element.59.refs_4_.refs_1_), channel_id=1, source_target_pairs={{0,1},{1,0},{2,3},{3,2},{4,5},{5,4},{6,7},{7,6},{8,9},{9,8},{10,11... | collective-permute-start | bytes 221192 | tf_op jit(solution)/shard_map/ppermute | solution.py:488
  98.4 4.6 %collective-permute-start.9 = (f32[64,128]{1,0:T(8,128)S(1)}, f32[64,128]{1,0:T(8,128)S(1)}, u32[]{:S(2)}, u32[]{:S(2)}) collective-permute-start(f32[64,128]{1,0:T(8,128)S(1)} %get-tuple-element.58.refs_1_), channel_id=1, source_target_pairs={{0,32},{32,0},{1,33},{33,1},{2,34},{34,2},{3,35},{35,3},{4,36},{36... | collective-permute-start | bytes 98312 | tf_op jit(solution)/shard_map/ppermute | solution.py:492
  104.0 11.7 %all-to-all-start.5 = ((f32[8,32,128]{2,1,0:T(8,128)}), f32[8,32,128]{2,1,0:T(8,128)S(1)}, u32[]{:S(2)}, u32[]{:S(2)}) async-start(f32[8,32,128]{2,1,0:T(8,128)} %lower.6.refs_7_), calls=%async_computation.5 | async-start | bytes 262144 | tf_op jit(solution)/shard_map/all_to_all | solution.py:496
  113.6 56.1 %copy-start.3 = (f32[16,1024]{1,0:T(8,128)S(1)}, f32[16,1024]{1,0:T(8,128)}, u32[]{:S(2)}) copy-start(f32[16,1024]{1,0:T(8,128)} %refs_1_.3) | copy-start | bytes 196612
  117.8 11.1 %all-to-all-start.6 = ((f32[16,32,128]{2,1,0:T(8,128)}), f32[16,32,128]{2,1,0:T(8,128)S(1)}, u32[]{:S(2)}, u32[]{:S(2)}) async-start(f32[16,32,128]{2,1,0:T(8,128)} %get-tuple-element.61), calls=%async_computation.6 | async-start | bytes 524288 | tf_op jit(solution)/shard_map/all_to_all | solution.py:500
  121.4 11.9 %collective-permute-start.16 = (f32[16,1152]{1,0:T(8,128)S(1)}, f32[16,1152]{1,0:T(8,128)S(1)}, u32[]{:S(2)}, u32[]{:S(2)}) collective-permute-start(f32[16,1152]{1,0:T(8,128)S(1)} %get-tuple-element.64.refs_4_.refs_1_), channel_id=1, source_target_pairs={{0,3},{1,2},{2,1},{3,0},{4,7},{5,6},{6,5},{7,4},{8,11},{9,10},{10,... | collective-permute-start | bytes 221192 | tf_op jit(solution)/shard_map/ppermute | solution.py:488
  122.7 10.6 %collective-permute-start.15 = (f32[16,1152]{1,0:T(8,128)S(1)}, f32[16,1152]{1,0:T(8,128)S(1)}, u32[]{:S(2)}, u32[]{:S(2)}) collective-permute-start(f32[16,1152]{1,0:T(8,128)S(1)} %get-tuple-element.64.refs_4_.refs_1_), channel_id=1, source_target_pairs={{0,2},{1,3},{2,0},{3,1},{4,6},{5,7},{6,4},{7,5},{8,10},{9,11},{10,... | collective-permute-start | bytes 221192 | tf_op jit(solution)/shard_map/ppermute | solution.py:488
  122.7 10.6 %collective-permute-start.14 = (f32[16,1152]{1,0:T(8,128)S(1)}, f32[16,1152]{1,0:T(8,128)S(1)}, u32[]{:S(2)}, u32[]{:S(2)}) collective-permute-start(f32[16,1152]{1,0:T(8,128)S(1)} %get-tuple-element.64.refs_4_.refs_1_), channel_id=1, source_target_pairs={{0,1},{1,0},{2,3},{3,2},{4,5},{5,4},{6,7},{7,6},{8,9},{9,8},{10,11... | collective-permute-start | bytes 221192 | tf_op jit(solution)/shard_map/ppermute | solution.py:488
  129.5 4.6 %collective-permute-start.13 = (f32[64,128]{1,0:T(8,128)S(1)}, f32[64,128]{1,0:T(8,128)S(1)}, u32[]{:S(2)}, u32[]{:S(2)}) collective-permute-start(f32[64,128]{1,0:T(8,128)S(1)} %get-tuple-element.63.refs_1_), channel_id=1, source_target_pairs={{0,32},{32,0},{1,33},{33,1},{2,34},{34,2},{3,35},{35,3},{4,36},{36... | collective-permute-start | bytes 98312 | tf_op jit(solution)/shard_map/ppermute | solution.py:492
  135.1 11.7 %all-to-all-start.7 = ((f32[8,32,128]{2,1,0:T(8,128)}), f32[8,32,128]{2,1,0:T(8,128)S(1)}, u32[]{:S(2)}, u32[]{:S(2)}) async-start(f32[8,32,128]{2,1,0:T(8,128)} %lower.7.refs_7_), calls=%async_computation.7 | async-start | bytes 262144 | tf_op jit(solution)/shard_map/all_to_all | solution.py:496

commit v7 on v6

--- a/solution.py
+++ b/solution.py
@@ -17,6 +17,7 @@
 LOG2E = math.log2(math.e)
 DEPTH = 208
 TILE = 256
+AHEAD = 4
 
 Z, X, Y, CORE, O0, O1, O2, O3 = range(8)
 
@@ -253,7 +254,7 @@
                     kernels.at[e, :, rows, :], held.at[e, :, rows, :], sems.at[e * tiles + t]
                 )
             )
-    for copy in copies:
+    for copy in copies[:AHEAD]:
         copy.start()
     o0 = scalars[O0]
     own = v[:, 0:leaf]
@@ -265,6 +266,8 @@
         for t in range(tiles):
             rows = slice(t * TILE, (t + 1) * TILE)
             copies[e * tiles + t].wait()
+            if e * tiles + t + AHEAD < len(copies):
+                copies[e * tiles + t + AHEAD].start()
             part = dot(pair[:, rows], held[e, 0, rows, :]) + dot(pair[:, rows], held[e, 1, rows, :])
             total = part if total is None else total + part
     result = NOISE * own + halves(total)

time: 172 us -> 173 us (level)
  no operation moved by 1% of the time
where the time goes in v7:
time: 173 us; the launch traced here: 172 us
  starting transfers between devices  69.1 us (40%)
  Pallas kernels  52.1 us (30%)
  waiting for transfers between devices  24.5 us (14%)
  blocking collectives  22.5 us (13%)
  local copies, waits for them, and re-layouts  2.76 us (2%)
    pallas_call x21, Pallas kernels, call(): pl.pallas_call(body, out_shape=outs, in_specs=[SMEM] * len(scalars) + [VM...  52.1 us
    all_to_all x1, blocking collectives, local(): shares = lax.all_to_all(outgoing, ('y', 'core', 'x', 'z'), 0, 0, tiled=True)  22.5 us
    all_to_all x4, starting transfers between devices, over_yx(): return lax.all_to_all(v, ('y', 'x'), 0, 0)  19.9 us
    ppermute x12, starting transfers between devices, along_z(): return lax.ppermute(v, 'z', [(i, i ^ offset) for i in range(8)])  18.3 us
    all_to_all x4, starting transfers between devices, over_z(): return lax.all_to_all(v, 'z', 0, 0)  18.2 us
    all_to_all x4, waiting for transfers between devices, over_yx(): return lax.all_to_all(v, ('y', 'x'), 0, 0)  12.5 us
    ppermute x4, starting transfers between devices, other_core(): return lax.ppermute(v, 'core', [(0, 1), (1, 0)])  11.4 us
    all_to_all x4, waiting for transfers between devices, over_z(): return lax.all_to_all(v, 'z', 0, 0)  9.14 us
  transfers between devices with their start and end apart: 25, of which 12 were waited for; matrix products, arithmetic and copies ran while one was open for 0% of the time, Pallas kernels for 23%

profile of v7, /device:TPU:1, one launch (start us, length us, event | category | flops | bytes accessed | tf_op | source)
XLA Modules:
  0.0 172.0 jit_solution(6153506002605027969)
XLA Ops:
  0.7 1.0 constant_dynamic-update-slice_fusion.1
  2.5 3.8 %collective-permute-start = (f32[80,1024]{1,0:T(8,128)S(1)}, f32[80,1024]{1,0:T(8,128)S(1)}, u32[]{:S(2)}, u32[]{:S(2)}) collective-permute-start(f32[80,1024]{1,0:T(8,128)S(1)} %constant_dynamic-update-slice_fusion.refs_1_), channel_id=1, source_target_pairs={{0,2},{1,3},{2,0},{3,1},{4,6},{5,7},{6,4},{7,5},{8,10},{9,11},{10,... | collective-permute-start | bytes 983048 | tf_op jit(solution)/shard_map/ppermute | solution.py:491
  6.4 3.5 %prepare.1 = (bf16[128,1024]{1,0:T(8,128)(2,1)}, bf16[64,512]{1,0:T(8,128)(2,1)}, f32[64,64]{1,0:T(8,128)}, bf16[64,128]{1,0:T(8,128)(2,1)}, f32[16,128]{1,0:T(8...) custom-call(s32[4]{0:T(128)} %bitcast.15, s32[1,1024]{1,0:T(1,128)} %refs_1_.2, f32[64,1024]{1,0:T(8,128)} %refs_2_.1, ...), custom_call_target="tpu_custom_call" | custom-call | flops 100000 | bytes 500000 | tf_op jit(solution)/shard_map/prepare/pallas_call | solution.py:436
  9.9 6.9 %all-to-all-start = ((f32[16,64,128]{2,1,0:T(8,128)}), f32[16,64,128]{2,1,0:T(8,128)S(1)}, u32[]{:S(2)}, u32[]{:S(2)}) async-start(f32[16,64,128]{2,1,0:T(8,128)} %get-tuple-element.36), calls=%async_computation | async-start | bytes 1048576 | tf_op jit(solution)/shard_map/all_to_all | solution.py:503
  16.8 1.7 %collective-permute-start.4 = (f32[80,1024]{1,0:T(8,128)S(1)}, f32[80,1024]{1,0:T(8,128)S(1)}, u32[]{:S(2)}, u32[]{:S(2)}) collective-permute-start(f32[80,1024]{1,0:T(8,128)S(1)} %constant_dynamic-update-slice_fusion.refs_1_), channel_id=1, source_target_pairs={{0,1},{1,0},{2,3},{3,2},{4,5},{5,4},{6,7},{7,6},{8,9},{9,8},{10,11... | collective-permute-start | bytes 983048 | tf_op jit(solution)/shard_map/ppermute | solution.py:491
  18.5 1.3 collective-permute-start.1
  20.1 1.9 %collective-permute-start.3 = (f32[80,1024]{1,0:T(8,128)S(1)}, f32[80,1024]{1,0:T(8,128)S(1)}, u32[]{:S(2)}, u32[]{:S(2)}) collective-permute-start(f32[80,1024]{1,0:T(8,128)S(1)} %collective-permute-done.refs_2_), channel_id=1, source_target_pairs={{0,1},{1,0},{2,3},{3,2},{4,5},{5,4},{6,7},{7,6},{8,9},{9,8},{10,11... | collective-permute-start | bytes 983048 | tf_op jit(solution)/shard_map/ppermute | solution.py:491
  22.7 4.1 %build_own.1 = (bf16[3,2,1024,1024]{3,2,1,0:T(8,128)(2,1)}, f32[16,1024]{1,0:T(8,128)S(1)}) custom-call(s32[4]{0:T(128)S(1)} %bitcast.16, f32[80,1024]{1,0:T(8,128)S(1)} %constant_dynamic-update-slice_fusion.refs_1_, f32[80,1024]{1,0:T(8,128)S(1)} %collective-permute-done.refs_2_), custom_call_target="tpu_custom_call" | custom-call | flops 4000000000 | bytes 500000 | tf_op jit(solution)/shard_map/build_own/pallas_call | solution.py:436
  27.8 2.4 %collective-permute-start.2 = (f32[64,128]{1,0:T(8,128)S(1)}, f32[64,128]{1,0:T(8,128)S(1)}, u32[]{:S(2)}, u32[]{:S(2)}) collective-permute-start(f32[64,128]{1,0:T(8,128)S(1)} %get-tuple-element.40.refs_2_), channel_id=1, source_target_pairs={{0,32},{32,0},{1,33},{33,1},{2,34},{34,2},{3,35},{35,3},{4,36},{36... | collective-permute-start | bytes 98312 | tf_op jit(solution)/shard_map/ppermute | solution.py:495
  30.4 1.3 tops.1.refs_4_.refs_3_
  31.7 1.6 lower.4.refs_5_
  33.3 6.4 %all-to-all-start.1 = ((f32[8,64,128]{2,1,0:T(8,128)}), f32[8,64,128]{2,1,0:T(8,128)S(1)}, u32[]{:S(2)}, u32[]{:S(2)}) async-start(f32[8,64,128]{2,1,0:T(8,128)} %lower.4.refs_5_), calls=%async_computation.1 | async-start | bytes 524288 | tf_op jit(solution)/shard_map/all_to_all | solution.py:499
  39.7 4.2 %build_a.1 = (bf16[3,2,1024,1024]{3,2,1,0:T(8,128)(2,1)}, f32[16,1024]{1,0:T(8,128)S(1)}) custom-call(s32[4]{0:T(128)S(1)} %bitcast.20, f32[80,1024]{1,0:T(8,128)S(1)} %constant_dynamic-update-slice_fusion.refs_1_, f32[80,1024]{1,0:T(8,128)S(1)} %collective-permute-done.refs_2_, ...), custom_call_target="tpu_custom_call", output_to_operand_aliasing={{0}: (7, {})} | custom-call | flops 4000000000 | bytes 500000 | tf_op jit(solution)/shard_map/build_a/pallas_call | solution.py:436
  43.9 4.2 %build_b.1 = (bf16[3,2,1024,1024]{3,2,1,0:T(8,128)(2,1)}, f32[16,1024]{1,0:T(8,128)S(1)}) custom-call(s32[4]{0:T(128)S(1)} %bitcast.21, f32[80,1024]{1,0:T(8,128)S(1)} %constant_dynamic-update-slice_fusion.refs_1_, f32[80,1024]{1,0:T(8,128)S(1)} %collective-permute-done.refs_2_, ...), custom_call_target="tpu_custom_call", output_to_operand_aliasing={{0}: (6, {})} | custom-call | flops 4000000000 | bytes 500000 | tf_op jit(solution)/shard_map/build_b/pallas_call | solution.py:436
  48.1 4.0 %all-to-all-done.1.refs_1_ = f32[8,64,128]{2,1,0:T(8,128)S(1)} async-done(((f32[8,64,128]{2,1,0:T(8,128)}), f32[8,64,128]{2,1,0:T(8,128)S(1)}, u32[]{:S(2)}, u32[]{:S(2)}) %all-to-all-start.1) | async-done | bytes 262176 | tf_op jit(solution)/shard_map/all_to_all | solution.py:499
  52.0 2.7 %first.1 = (bf16[128,256]{1,0:T(8,128)(2,1)S(1)}, f32[16,1152]{1,0:T(8,128)S(1)}, f32[16,32,128]{2,1,0:T(8,128)}) custom-call(s32[4]{0:T(128)S(1)} %bitcast.22, f32[8,64,128]{2,1,0:T(8,128)S(1)} %all-to-all-done.1.refs_1_, f32[4,64,64]{2,1,0:T(8,128)S(1)} %bitcast.11, bf16[128,1024]{1,0:T(8,128)(2,1)S(1)} %copy-done.1, ...), custom_call_target="tpu_custom_call" | custom-call | flops 100000 | bytes 500000 | tf_op jit(solution)/shard_map/first/pallas_call | solution.py:436
  54.7 5.9 %all-to-all-start.2 = ((f32[16,32,128]{2,1,0:T(8,128)}), f32[16,32,128]{2,1,0:T(8,128)S(1)}, u32[]{:S(2)}, u32[]{:S(2)}) async-start(f32[16,32,128]{2,1,0:T(8,128)} %get-tuple-element.49), calls=%async_computation.2 | async-start | bytes 524288 | tf_op jit(solution)/shard_map/all_to_all | solution.py:503
  60.9 3.4 %collective-permute-start.6 = (f32[16,1152]{1,0:T(8,128)S(1)}, f32[16,1152]{1,0:T(8,128)S(1)}, u32[]{:S(2)}, u32[]{:S(2)}) collective-permute-start(f32[16,1152]{1,0:T(8,128)S(1)} %get-tuple-element.52.refs_4_.refs_1_.refs_7_.refs_2_), channel_id=1, source_target_pairs={{0,1},{1,0},{2,3},{3,2},{4,5},{5,4},{6,7},{7,6},{8,9},{9,8},{10,11... | collective-permute-start | bytes 221192 | tf_op jit(solution)/shard_map/ppermute | solution.py:491
  64.3 4.4 %all-to-all-done.2.refs_1_ = f32[16,32,128]{2,1,0:T(8,128)S(1)} async-done(((f32[16,32,128]{2,1,0:T(8,128)}), f32[16,32,128]{2,1,0:T(8,128)S(1)}, u32[]{:S(2)}, u32[]{:S(2)}) %all-to-all-start.2) | async-done | bytes 262176 | tf_op jit(solution)/shard_map/all_to_all | solution.py:503
  69.3 1.7 collective-permute-start.5
  71.9 1.0 lower.5.refs_7_
  72.8 3.4 %all-to-all-start.3 = ((f32[8,32,128]{2,1,0:T(8,128)}), f32[8,32,128]{2,1,0:T(8,128)S(1)}, u32[]{:S(2)}, u32[]{:S(2)}) async-start(f32[8,32,128]{2,1,0:T(8,128)} %lower.5.refs_7_), calls=%async_computation.3 | async-start | bytes 262144 | tf_op jit(solution)/shard_map/all_to_all | solution.py:499
  76.2 6.3 %near.3.refs_4_ = f32[16,1152]{1,0:T(8,128)S(1)} custom-call(s32[4]{0:T(128)S(1)} %bitcast.24, f32[16,1152]{1,0:T(8,128)S(1)} %get-tuple-element.52.refs_4_.refs_1_.refs_7_.refs_2_, f32[16,1152]{1,0:T(8,128)S(1)} %collective-permute-done.6.refs_5_.refs_2_, f32[16,1152]{1,0:T(8,128)S(1)} %collective-permute-done.7.refs_6_.refs_3_, ...), custom_call_target="tpu_custom_call" | custom-call | flops 4000000000 | bytes 500000 | tf_op jit(solution)/shard_map/near/pallas_call | solution.py:436
  82.5 2.0 %all-to-all-done.3.refs_1_ = f32[8,32,128]{2,1,0:T(8,128)S(1)} async-done(((f32[8,32,128]{2,1,0:T(8,128)}), f32[8,32,128]{2,1,0:T(8,128)S(1)}, u32[]{:S(2)}, u32[]{:S(2)}) %all-to-all-start.3) | async-done | bytes 131104 | tf_op jit(solution)/shard_map/all_to_all | solution.py:499
  84.5 2.2 %second.1 = (f32[16,1024]{1,0:T(8,128)S(1)}, f32[16,1152]{1,0:T(8,128)S(1)}, f32[16,128]{1,0:T(8,128)S(1)}, f32[16,32,128]{2,1,0:T(8,128)}) custom-call(s32[4]{0:T(128)S(1)} %bitcast.25, f32[8,32,128]{2,1,0:T(8,128)S(1)} %all-to-all-done.3.refs_1_, bf16[128,256]{1,0:T(8,128)(2,1)S(1)} %get-tuple-element.53.refs_2_, bf16[128,1024]{1,0:T(8,128)(2,1)S(1)} %copy-done.1, ...), custom_call_target="tpu_custom_call" | custom-call | flops 100000 | bytes 500000 | tf_op jit(solution)/shard_map/second/pallas_call | solution.py:436
  86.7 3.5 %all-to-all-start.4 = ((f32[16,32,128]{2,1,0:T(8,128)}), f32[16,32,128]{2,1,0:T(8,128)S(1)}, u32[]{:S(2)}, u32[]{:S(2)}) async-start(f32[16,32,128]{2,1,0:T(8,128)} %get-tuple-element.56), calls=%async_computation.4 | async-start | bytes 524288 | tf_op jit(solution)/shard_map/all_to_all | solution.py:503
  90.3 1.3 collective-permute-start.12
  91.6 2.3 %collective-permute-start.10 = (f32[16,1152]{1,0:T(8,128)S(1)}, f32[16,1152]{1,0:T(8,128)S(1)}, u32[]{:S(2)}, u32[]{:S(2)}) collective-permute-start(f32[16,1152]{1,0:T(8,128)S(1)} %get-tuple-element.59.refs_4_.refs_1_), channel_id=1, source_target_pairs={{0,1},{1,0},{2,3},{3,2},{4,5},{5,4},{6,7},{7,6},{8,9},{9,8},{10,11... | collective-permute-start | bytes 221192 | tf_op jit(solution)/shard_map/ppermute | solution.py:491
  93.9 3.9 %all-to-all-done.4.refs_1_ = f32[16,32,128]{2,1,0:T(8,128)S(1)} async-done(((f32[16,32,128]{2,1,0:T(8,128)}), f32[16,32,128]{2,1,0:T(8,128)S(1)}, u32[]{:S(2)}, u32[]{:S(2)}) %all-to-all-start.4) | async-done | bytes 262176 | tf_op jit(solution)/shard_map/all_to_all | solution.py:503
  98.4 3.8 %collective-permute-start.9 = (f32[64,128]{1,0:T(8,128)S(1)}, f32[64,128]{1,0:T(8,128)S(1)}, u32[]{:S(2)}, u32[]{:S(2)}) collective-permute-start(f32[64,128]{1,0:T(8,128)S(1)} %get-tuple-element.58.refs_1_), channel_id=1, source_target_pairs={{0,32},{32,0},{1,33},{33,1},{2,34},{34,2},{3,35},{35,3},{4,36},{36... | collective-permute-start | bytes 98312 | tf_op jit(solution)/shard_map/ppermute | solution.py:495
  103.0 1.0 lower.6.refs_7_
  104.0 4.2 %all-to-all-start.5 = ((f32[8,32,128]{2,1,0:T(8,128)}), f32[8,32,128]{2,1,0:T(8,128)S(1)}, u32[]{:S(2)}, u32[]{:S(2)}) async-start(f32[8,32,128]{2,1,0:T(8,128)} %lower.6.refs_7_), calls=%async_computation.5 | async-start | bytes 262144 | tf_op jit(solution)/shard_map/all_to_all | solution.py:499
  108.2 6.3 %near.4.refs_4_ = f32[16,1152]{1,0:T(8,128)S(1)} custom-call(s32[4]{0:T(128)S(1)} %bitcast.27, f32[16,1152]{1,0:T(8,128)S(1)} %get-tuple-element.59.refs_4_.refs_1_, f32[16,1152]{1,0:T(8,128)S(1)} %collective-permute-done.10.refs_5_.refs_2_, f32[16,1152]{1,0:T(8,128)S(1)} %collective-permute-done.11.refs_6_.refs_3_, ...), custom_call_target="tpu_custom_call" | custom-call | flops 4000000000 | bytes 500000 | tf_op jit(solution)/shard_map/near/pallas_call | solution.py:436
  114.5 1.6 all-to-all-done.5.refs_1_
  116.1 2.2 %third.1 = (f32[16,1152]{1,0:T(8,128)S(1)}, f32[16,128]{1,0:T(8,128)S(1)}, f32[16,32,128]{2,1,0:T(8,128)}) custom-call(s32[4]{0:T(128)S(1)} %bitcast.28, f32[8,32,128]{2,1,0:T(8,128)S(1)} %all-to-all-done.5.refs_1_, bf16[128,256]{1,0:T(8,128)(2,1)S(1)} %get-tuple-element.53.refs_2_, bf16[128,1024]{1,0:T(8,128)(2,1)S(1)} %copy-done.1, ...), custom_call_target="tpu_custom_call" | custom-call | flops 100000 | bytes 500000 | tf_op jit(solution)/shard_map/third/pallas_call | solution.py:436
  118.3 3.5 %all-to-all-start.6 = ((f32[16,32,128]{2,1,0:T(8,128)}), f32[16,32,128]{2,1,0:T(8,128)S(1)}, u32[]{:S(2)}, u32[]{:S(2)}) async-start(f32[16,32,128]{2,1,0:T(8,128)} %get-tuple-element.61), calls=%async_computation.6 | async-start | bytes 524288 | tf_op jit(solution)/shard_map/all_to_all | solution.py:503
  121.8 1.8 %collective-permute-start.16 = (f32[16,1152]{1,0:T(8,128)S(1)}, f32[16,1152]{1,0:T(8,128)S(1)}, u32[]{:S(2)}, u32[]{:S(2)}) collective-permute-start(f32[16,1152]{1,0:T(8,128)S(1)} %get-tuple-element.64.refs_4_.refs_1_), channel_id=1, source_target_pairs={{0,3},{1,2},{2,1},{3,0},{4,7},{5,6},{6,5},{7,4},{8,11},{9,10},{10,... | collective-permute-start | bytes 221192 | tf_op jit(solution)/shard_map/ppermute | solution.py:491
  123.6 1.9 %collective-permute-start.14 = (f32[16,1152]{1,0:T(8,128)S(1)}, f32[16,1152]{1,0:T(8,128)S(1)}, u32[]{:S(2)}, u32[]{:S(2)}) collective-permute-start(f32[16,1152]{1,0:T(8,128)S(1)} %get-tuple-element.64.refs_4_.refs_1_), channel_id=1, source_target_pairs={{0,1},{1,0},{2,3},{3,2},{4,5},{5,4},{6,7},{7,6},{8,9},{9,8},{10,11... | collective-permute-start | bytes 221192 | tf_op jit(solution)/shard_map/ppermute | solution.py:491
  125.5 3.9 %all-to-all-done.6.refs_1_ = f32[16,32,128]{2,1,0:T(8,128)S(1)} async-done(((f32[16,32,128]{2,1,0:T(8,128)}), f32[16,32,128]{2,1,0:T(8,128)S(1)}, u32[]{:S(2)}, u32[]{:S(2)}) %all-to-all-start.6) | async-done | bytes 262176 | tf_op jit(solution)/shard_map/all_to_all | solution.py:503
  129.9 3.6 %collective-permute-start.13 = (f32[64,128]{1,0:T(8,128)S(1)}, f32[64,128]{1,0:T(8,128)S(1)}, u32[]{:S(2)}, u32[]{:S(2)}) collective-permute-start(f32[64,128]{1,0:T(8,128)S(1)} %get-tuple-element.63.refs_1_), channel_id=1, source_target_pairs={{0,32},{32,0},{1,33},{33,1},{2,34},{34,2},{3,35},{35,3},{4,36},{36... | collective-permute-start | bytes 98312 | tf_op jit(solution)/shard_map/ppermute | solution.py:495
  133.5 0.8 collective-permute-done.13.refs_2_
  134.4 1.0 lower.7.refs_7_
  135.3 4.2 %all-to-all-start.7 = ((f32[8,32,128]{2,1,0:T(8,128)}), f32[8,32,128]{2,1,0:T(8,128)S(1)}, u32[]{:S(2)}, u32[]{:S(2)}) async-start(f32[8,32,128]{2,1,0:T(8,128)} %lower.7.refs_7_), calls=%async_computation.7 | async-start | bytes 262144 | tf_op jit(solution)/shard_map/all_to_all | solution.py:499
  139.5 6.3 %near.5.refs_4_ = f32[16,1152]{1,0:T(8,128)S(1)} custom-call(s32[4]{0:T(128)S(1)} %bitcast.30, f32[16,1152]{1,0:T(8,128)S(1)} %get-tuple-element.64.refs_4_.refs_1_, f32[16,1152]{1,0:T(8,128)S(1)} %collective-permute-done.14.refs_5_.refs_2_, f32[16,1152]{1,0:T(8,128)S(1)} %collective-permute-done.15.refs_6_.refs_3_, ...), custom_call_target="tpu_custom_call" | custom-call | flops 4000000000 | bytes 500000 | tf_op jit(solution)/shard_map/near/pallas_call | solution.py:436
  145.9 1.6 all-to-all-done.7.refs_1_
  147.5 1.2 fourth.1
  148.6 22.5 %all_to_all.51 = f32[256,1,128]{2,1,0:T(1,128)S(1)} all-to-all(f32[256,1,128]{2,1,0:T(1,128)S(1)} %bitcast.14), channel_id=1, replica_groups=mesh['y'=4,'core'=2,'x'=4,'z'=8] {'y','core','x','z'}, dimensions={0} | all-to-all | bytes 262144 | tf_op jit(solution)/shard_map/all_to_all | solution.py:622
  171.1 0.9 last.1
  (51 shorter events, 6.8 us)
Async XLA Ops:
  0.6 29.6 %copy-start = (s32[8,4]{0,1:T(4,128)S(1)}, s32[8,4]{0,1:T(4,128)}, u32[]{:S(2)}) copy-start(s32[8,4]{0,1:T(4,128)} %param.18) | copy-start | bytes 388
  0.6 29.7 %copy-start.8 = (s32[4,1]{0,1:T(1,128)S(1)}, s32[4,1]{0,1:T(1,128)}, u32[]{:S(2)}) copy-start(s32[4,1]{0,1:T(1,128)} %param.17) | copy-start | bytes 52
  0.7 29.7 %copy-start.2 = (f32[4,1,64,64]{3,2,1,0:T(8,128)S(1)}, f32[4,1,64,64]{3,2,1,0:T(8,128)}, u32[]{:S(2)}) copy-start(f32[4,1,64,64]{3,2,1,0:T(8,128)} %param.15) | copy-start | bytes 196612
  0.7 29.7 %copy-start.5 = (f32[8,64,64]{2,1,0:T(8,128)S(1)}, f32[8,64,64]{2,1,0:T(8,128)}, u32[]{:S(2)}) copy-start(f32[8,64,64]{2,1,0:T(8,128)} %param.16) | copy-start | bytes 393220
  2.5 17.6 %collective-permute-start = (f32[80,1024]{1,0:T(8,128)S(1)}, f32[80,1024]{1,0:T(8,128)S(1)}, u32[]{:S(2)}, u32[]{:S(2)}) collective-permute-start(f32[80,1024]{1,0:T(8,128)S(1)} %constant_dynamic-update-slice_fusion.refs_1_), channel_id=1, source_target_pairs={{0,2},{1,3},{2,0},{3,1},{4,6},{5,7},{6,4},{7,5},{8,10},{9,11},{10,... | collective-permute-start | bytes 983048 | tf_op jit(solution)/shard_map/ppermute | solution.py:491
  9.9 20.5 %copy-start.9 = (f32[64,64]{1,0:T(8,128)S(1)}, f32[64,64]{1,0:T(8,128)}, u32[]{:S(2)}) copy-start(f32[64,64]{1,0:T(8,128)} %get-tuple-element.41.refs_5_) | copy-start | bytes 49156
  9.9 21.8 %copy-start.10 = (f32[32,128]{1,0:T(8,128)S(1)}, f32[32,128]{1,0:T(8,128)}, u32[]{:S(2)}) copy-start(f32[32,128]{1,0:T(8,128)} %get-tuple-element.38.refs_7_) | copy-start | bytes 49156
  9.9 21.8 %copy-start.11 = (f32[16,128]{1,0:T(8,128)S(1)}, f32[16,128]{1,0:T(8,128)}, u32[]{:S(2)}) copy-start(f32[16,128]{1,0:T(8,128)} %get-tuple-element.42.refs_5_) | copy-start | bytes 24580
  9.9 17.3 %all-to-all-start = ((f32[16,64,128]{2,1,0:T(8,128)}), f32[16,64,128]{2,1,0:T(8,128)S(1)}, u32[]{:S(2)}, u32[]{:S(2)}) async-start(f32[16,64,128]{2,1,0:T(8,128)} %get-tuple-element.36), calls=%async_computation | async-start | bytes 1048576 | tf_op jit(solution)/shard_map/all_to_all | solution.py:503
  16.8 22.8 %collective-permute-start.4 = (f32[80,1024]{1,0:T(8,128)S(1)}, f32[80,1024]{1,0:T(8,128)S(1)}, u32[]{:S(2)}, u32[]{:S(2)}) collective-permute-start(f32[80,1024]{1,0:T(8,128)S(1)} %constant_dynamic-update-slice_fusion.refs_1_), channel_id=1, source_target_pairs={{0,1},{1,0},{2,3},{3,2},{4,5},{5,4},{6,7},{7,6},{8,9},{9,8},{10,11... | collective-permute-start | bytes 983048 | tf_op jit(solution)/shard_map/ppermute | solution.py:491
  18.5 8.3 %collective-permute-start.1 = (f32[32,128]{1,0:T(8,128)}, f32[32,128]{1,0:T(8,128)S(1)}, u32[]{:S(2)}, u32[]{:S(2)}) collective-permute-start(f32[32,128]{1,0:T(8,128)} %get-tuple-element.38.refs_7_), channel_id=1, source_target_pairs={{0,8},{8,0},{16,24},{24,16},{1,9},{9,1},{17,25},{25,17},{2,10},{10... | collective-permute-start | bytes 49160 | tf_op jit(solution)/shard_map/ppermute | solution.py:557
  20.1 19.5 %collective-permute-start.3 = (f32[80,1024]{1,0:T(8,128)S(1)}, f32[80,1024]{1,0:T(8,128)S(1)}, u32[]{:S(2)}, u32[]{:S(2)}) collective-permute-start(f32[80,1024]{1,0:T(8,128)S(1)} %collective-permute-done.refs_2_), channel_id=1, source_target_pairs={{0,1},{1,0},{2,3},{3,2},{4,5},{5,4},{6,7},{7,6},{8,9},{9,8},{10,11... | collective-permute-start | bytes 983048 | tf_op jit(solution)/shard_map/ppermute | solution.py:491
  22.1 0.7 copy-start.7
  27.8 3.9 %collective-permute-start.2 = (f32[64,128]{1,0:T(8,128)S(1)}, f32[64,128]{1,0:T(8,128)S(1)}, u32[]{:S(2)}, u32[]{:S(2)}) collective-permute-start(f32[64,128]{1,0:T(8,128)S(1)} %get-tuple-element.40.refs_2_), channel_id=1, source_target_pairs={{0,32},{32,0},{1,33},{33,1},{2,34},{34,2},{3,35},{35,3},{4,36},{36... | collective-permute-start | bytes 98312 | tf_op jit(solution)/shard_map/ppermute | solution.py:495
  33.3 18.8 %all-to-all-start.1 = ((f32[8,64,128]{2,1,0:T(8,128)}), f32[8,64,128]{2,1,0:T(8,128)S(1)}, u32[]{:S(2)}, u32[]{:S(2)}) async-start(f32[8,64,128]{2,1,0:T(8,128)} %lower.4.refs_5_), calls=%async_computation.1 | async-start | bytes 524288 | tf_op jit(solution)/shard_map/all_to_all | solution.py:499
  39.7 12.4 %copy-start.1 = (bf16[128,1024]{1,0:T(8,128)(2,1)S(1)}, bf16[128,1024]{1,0:T(8,128)(2,1)}, u32[]{:S(2)}) copy-start(bf16[128,1024]{1,0:T(8,128)(2,1)} %get-tuple-element.43.refs_3_.refs_5_) | copy-start | bytes 786436
  39.7 12.3 %copy-start.4 = (bf16[64,512]{1,0:T(8,128)(2,1)S(1)}, bf16[64,512]{1,0:T(8,128)(2,1)}, u32[]{:S(2)}) copy-start(bf16[64,512]{1,0:T(8,128)(2,1)} %get-tuple-element.48.refs_5_.refs_6_) | copy-start | bytes 196612
  43.9 40.7 %copy-start.6 = (bf16[64,128]{1,0:T(8,128)(2,1)S(1)}, bf16[64,128]{1,0:T(8,128)(2,1)}, u32[]{:S(2)}) copy-start(bf16[64,128]{1,0:T(8,128)(2,1)} %get-tuple-element.55.refs_5_) | copy-start | bytes 49156
  54.7 14.0 %all-to-all-start.2 = ((f32[16,32,128]{2,1,0:T(8,128)}), f32[16,32,128]{2,1,0:T(8,128)S(1)}, u32[]{:S(2)}, u32[]{:S(2)}) async-start(f32[16,32,128]{2,1,0:T(8,128)} %get-tuple-element.49), calls=%async_computation.2 | async-start | bytes 524288 | tf_op jit(solution)/shard_map/all_to_all | solution.py:503
  60.7 10.3 %collective-permute-start.8 = (f32[16,1152]{1,0:T(8,128)S(1)}, f32[16,1152]{1,0:T(8,128)S(1)}, u32[]{:S(2)}, u32[]{:S(2)}) collective-permute-start(f32[16,1152]{1,0:T(8,128)S(1)} %get-tuple-element.52.refs_4_.refs_1_.refs_7_.refs_2_), channel_id=1, source_target_pairs={{0,3},{1,2},{2,1},{3,0},{4,7},{5,6},{6,5},{7,4},{8,11},{9,10},{10,... | collective-permute-start | bytes 221192 | tf_op jit(solution)/shard_map/ppermute | solution.py:491
  60.8 10.2 %collective-permute-start.7 = (f32[16,1152]{1,0:T(8,128)S(1)}, f32[16,1152]{1,0:T(8,128)S(1)}, u32[]{:S(2)}, u32[]{:S(2)}) collective-permute-start(f32[16,1152]{1,0:T(8,128)S(1)} %get-tuple-element.52.refs_4_.refs_1_.refs_7_.refs_2_), channel_id=1, source_target_pairs={{0,2},{1,3},{2,0},{3,1},{4,6},{5,7},{6,4},{7,5},{8,10},{9,11},{10,... | collective-permute-start | bytes 221192 | tf_op jit(solution)/shard_map/ppermute | solution.py:491
  60.9 10.1 %collective-permute-start.6 = (f32[16,1152]{1,0:T(8,128)S(1)}, f32[16,1152]{1,0:T(8,128)S(1)}, u32[]{:S(2)}, u32[]{:S(2)}) collective-permute-start(f32[16,1152]{1,0:T(8,128)S(1)} %get-tuple-element.52.refs_4_.refs_1_.refs_7_.refs_2_), channel_id=1, source_target_pairs={{0,1},{1,0},{2,3},{3,2},{4,5},{5,4},{6,7},{7,6},{8,9},{9,8},{10,11... | collective-permute-start | bytes 221192 | tf_op jit(solution)/shard_map/ppermute | solution.py:491
  69.3 2.6 %collective-permute-start.5 = (f32[64,128]{1,0:T(8,128)S(1)}, f32[64,128]{1,0:T(8,128)S(1)}, u32[]{:S(2)}, u32[]{:S(2)}) collective-permute-start(f32[64,128]{1,0:T(8,128)S(1)} %get-tuple-element.51.refs_1_), channel_id=1, source_target_pairs={{0,32},{32,0},{1,33},{33,1},{2,34},{34,2},{3,35},{35,3},{4,36},{36... | collective-permute-start | bytes 98312 | tf_op jit(solution)/shard_map/ppermute | solution.py:495
  72.8 11.7 %all-to-all-start.3 = ((f32[8,32,128]{2,1,0:T(8,128)}), f32[8,32,128]{2,1,0:T(8,128)S(1)}, u32[]{:S(2)}, u32[]{:S(2)}) async-start(f32[8,32,128]{2,1,0:T(8,128)} %lower.5.refs_7_), calls=%async_computation.3 | async-start | bytes 262144 | tf_op jit(solution)/shard_map/all_to_all | solution.py:499
  86.7 11.0 %all-to-all-start.4 = ((f32[16,32,128]{2,1,0:T(8,128)}), f32[16,32,128]{2,1,0:T(8,128)S(1)}, u32[]{:S(2)}, u32[]{:S(2)}) async-start(f32[16,32,128]{2,1,0:T(8,128)} %get-tuple-element.56), calls=%async_computation.4 | async-start | bytes 524288 | tf_op jit(solution)/shard_map/all_to_all | solution.py:503
  90.3 11.9 %collective-permute-start.12 = (f32[16,1152]{1,0:T(8,128)S(1)}, f32[16,1152]{1,0:T(8,128)S(1)}, u32[]{:S(2)}, u32[]{:S(2)}) collective-permute-start(f32[16,1152]{1,0:T(8,128)S(1)} %get-tuple-element.59.refs_4_.refs_1_), channel_id=1, source_target_pairs={{0,3},{1,2},{2,1},{3,0},{4,7},{5,6},{6,5},{7,4},{8,11},{9,10},{10,... | collective-permute-start | bytes 221192 | tf_op jit(solution)/shard_map/ppermute | solution.py:491
  91.5 10.6 %collective-permute-start.11 = (f32[16,1152]{1,0:T(8,128)S(1)}, f32[16,1152]{1,0:T(8,128)S(1)}, u32[]{:S(2)}, u32[]{:S(2)}) collective-permute-start(f32[16,1152]{1,0:T(8,128)S(1)} %get-tuple-element.59.refs_4_.refs_1_), channel_id=1, source_target_pairs={{0,2},{1,3},{2,0},{3,1},{4,6},{5,7},{6,4},{7,5},{8,10},{9,11},{10,... | collective-permute-start | bytes 221192 | tf_op jit(solution)/shard_map/ppermute | solution.py:491
  91.6 10.6 %collective-permute-start.10 = (f32[16,1152]{1,0:T(8,128)S(1)}, f32[16,1152]{1,0:T(8,128)S(1)}, u32[]{:S(2)}, u32[]{:S(2)}) collective-permute-start(f32[16,1152]{1,0:T(8,128)S(1)} %get-tuple-element.59.refs_4_.refs_1_), channel_id=1, source_target_pairs={{0,1},{1,0},{2,3},{3,2},{4,5},{5,4},{6,7},{7,6},{8,9},{9,8},{10,11... | collective-permute-start | bytes 221192 | tf_op jit(solution)/shard_map/ppermute | solution.py:491
  98.4 4.6 %collective-permute-start.9 = (f32[64,128]{1,0:T(8,128)S(1)}, f32[64,128]{1,0:T(8,128)S(1)}, u32[]{:S(2)}, u32[]{:S(2)}) collective-permute-start(f32[64,128]{1,0:T(8,128)S(1)} %get-tuple-element.58.refs_1_), channel_id=1, source_target_pairs={{0,32},{32,0},{1,33},{33,1},{2,34},{34,2},{3,35},{35,3},{4,36},{36... | collective-permute-start | bytes 98312 | tf_op jit(solution)/shard_map/ppermute | solution.py:495
  104.0 12.1 %all-to-all-start.5 = ((f32[8,32,128]{2,1,0:T(8,128)}), f32[8,32,128]{2,1,0:T(8,128)S(1)}, u32[]{:S(2)}, u32[]{:S(2)}) async-start(f32[8,32,128]{2,1,0:T(8,128)} %lower.6.refs_7_), calls=%async_computation.5 | async-start | bytes 262144 | tf_op jit(solution)/shard_map/all_to_all | solution.py:499
  114.5 56.6 %copy-start.3 = (f32[16,1024]{1,0:T(8,128)S(1)}, f32[16,1024]{1,0:T(8,128)}, u32[]{:S(2)}) copy-start(f32[16,1024]{1,0:T(8,128)} %refs_1_.3) | copy-start | bytes 196612
  118.3 11.0 %all-to-all-start.6 = ((f32[16,32,128]{2,1,0:T(8,128)}), f32[16,32,128]{2,1,0:T(8,128)S(1)}, u32[]{:S(2)}, u32[]{:S(2)}) async-start(f32[16,32,128]{2,1,0:T(8,128)} %get-tuple-element.61), calls=%async_computation.6 | async-start | bytes 524288 | tf_op jit(solution)/shard_map/all_to_all | solution.py:503
  121.8 11.7 %collective-permute-start.16 = (f32[16,1152]{1,0:T(8,128)S(1)}, f32[16,1152]{1,0:T(8,128)S(1)}, u32[]{:S(2)}, u32[]{:S(2)}) collective-permute-start(f32[16,1152]{1,0:T(8,128)S(1)} %get-tuple-element.64.refs_4_.refs_1_), channel_id=1, source_target_pairs={{0,3},{1,2},{2,1},{3,0},{4,7},{5,6},{6,5},{7,4},{8,11},{9,10},{10,... | collective-permute-start | bytes 221192 | tf_op jit(solution)/shard_map/ppermute | solution.py:491
  123.6 9.9 %collective-permute-start.15 = (f32[16,1152]{1,0:T(8,128)S(1)}, f32[16,1152]{1,0:T(8,128)S(1)}, u32[]{:S(2)}, u32[]{:S(2)}) collective-permute-start(f32[16,1152]{1,0:T(8,128)S(1)} %get-tuple-element.64.refs_4_.refs_1_), channel_id=1, source_target_pairs={{0,2},{1,3},{2,0},{3,1},{4,6},{5,7},{6,4},{7,5},{8,10},{9,11},{10,... | collective-permute-start | bytes 221192 | tf_op jit(solution)/shard_map/ppermute | solution.py:491
  123.6 9.9 %collective-permute-start.14 = (f32[16,1152]{1,0:T(8,128)S(1)}, f32[16,1152]{1,0:T(8,128)S(1)}, u32[]{:S(2)}, u32[]{:S(2)}) collective-permute-start(f32[16,1152]{1,0:T(8,128)S(1)} %get-tuple-element.64.refs_4_.refs_1_), channel_id=1, source_target_pairs={{0,1},{1,0},{2,3},{3,2},{4,5},{5,4},{6,7},{7,6},{8,9},{9,8},{10,11... | collective-permute-start | bytes 221192 | tf_op jit(solution)/shard_map/ppermute | solution.py:491
  129.9 4.4 %collective-permute-start.13 = (f32[64,128]{1,0:T(8,128)S(1)}, f32[64,128]{1,0:T(8,128)S(1)}, u32[]{:S(2)}, u32[]{:S(2)}) collective-permute-start(f32[64,128]{1,0:T(8,128)S(1)} %get-tuple-element.63.refs_1_), channel_id=1, source_target_pairs={{0,32},{32,0},{1,33},{33,1},{2,34},{34,2},{3,35},{35,3},{4,36},{36... | collective-permute-start | bytes 98312 | tf_op jit(solution)/shard_map/ppermute | solution.py:495
  135.3 12.1 %all-to-all-start.7 = ((f32[8,32,128]{2,1,0:T(8,128)}), f32[8,32,128]{2,1,0:T(8,128)S(1)}, u32[]{:S(2)}, u32[]{:S(2)}) async-start(f32[8,32,128]{2,1,0:T(8,128)} %lower.7.refs_7_), calls=%async_computation.7 | async-start | bytes 262144 | tf_op jit(solution)/shard_map/all_to_all | solution.py:499

commit v8 on v6

--- a/solution.py
+++ b/solution.py
@@ -549,7 +549,7 @@
         )
         return high, mine, other_core(mine)
 
-    kernels, near = build(scalars, both, [], None, None, [two], "build_own")
+    kernels, near = build(scalars, both, [], None, None, [two, one], "build_own")
     from_yx = over_yx(outgoing)
     second_moved = lax.ppermute(second, "x", [(i, i ^ 1) for i in range(4)])
     spread = gather(from_yx, [near, second_moved])

time: 172 us -> 171 us (level)
  no operation moved by 1% of the time
where the time goes in v8:
time: 171 us; the launch traced here: 170 us
  starting transfers between devices  66.9 us (39%)
  Pallas kernels  50.7 us (30%)
  waiting for transfers between devices  27.4 us (16%)
  blocking collectives  21.8 us (13%)
  local copies, waits for them, and re-layouts  2.76 us (2%)
    pallas_call x21, Pallas kernels, call(): pl.pallas_call(body, out_shape=outs, in_specs=[SMEM] * len(scalars) + [VM...  50.7 us
    all_to_all x1, blocking collectives, local(): shares = lax.all_to_all(outgoing, ('y', 'core', 'x', 'z'), 0, 0, tiled=True)  21.8 us
    all_to_all x4, starting transfers between devices, over_yx(): return lax.all_to_all(v, ('y', 'x'), 0, 0)  19.1 us
    ppermute x12, starting transfers between devices, along_z(): return lax.ppermute(v, 'z', [(i, i ^ offset) for i in range(8)])  18.2 us
    all_to_all x4, starting transfers between devices, over_z(): return lax.all_to_all(v, 'z', 0, 0)  16.4 us
    all_to_all x4, waiting for transfers between devices, over_yx(): return lax.all_to_all(v, ('y', 'x'), 0, 0)  13.9 us
    ppermute x4, starting transfers between devices, other_core(): return lax.ppermute(v, 'core', [(0, 1), (1, 0)])  11.9 us
    all_to_all x4, waiting for transfers between devices, over_z(): return lax.all_to_all(v, 'z', 0, 0)  10.5 us
  transfers between devices with their start and end apart: 25, of which 12 were waited for; matrix products, arithmetic and copies ran while one was open for 0% of the time, Pallas kernels for 23%

profile of v8, /device:TPU:1, one launch (start us, length us, event | category | flops | bytes accessed | tf_op | source)
XLA Modules:
  0.0 170.5 jit_solution(4110797281147787291)
XLA Ops:
  0.7 1.0 constant_dynamic-update-slice_fusion.1
  2.5 3.8 %collective-permute-start = (f32[80,1024]{1,0:T(8,128)S(1)}, f32[80,1024]{1,0:T(8,128)S(1)}, u32[]{:S(2)}, u32[]{:S(2)}) collective-permute-start(f32[80,1024]{1,0:T(8,128)S(1)} %constant_dynamic-update-slice_fusion.refs_1_), channel_id=1, source_target_pairs={{0,2},{1,3},{2,0},{3,1},{4,6},{5,7},{6,4},{7,5},{8,10},{9,11},{10,... | collective-permute-start | bytes 983048 | tf_op jit(solution)/shard_map/ppermute | solution.py:488
  6.4 1.6 collective-permute-start.1
  8.0 3.5 %prepare.1 = (bf16[128,1024]{1,0:T(8,128)(2,1)}, bf16[64,512]{1,0:T(8,128)(2,1)}, f32[64,64]{1,0:T(8,128)}, bf16[64,128]{1,0:T(8,128)(2,1)}, f32[16,128]{1,0:T(8...) custom-call(s32[4]{0:T(128)} %bitcast.15, s32[1,1024]{1,0:T(1,128)} %refs_1_.2, f32[64,1024]{1,0:T(8,128)} %refs_2_.1, ...), custom_call_target="tpu_custom_call" | custom-call | flops 100000 | bytes 500000 | tf_op jit(solution)/shard_map/prepare/pallas_call | solution.py:433
  11.6 6.9 %all-to-all-start = ((f32[16,64,128]{2,1,0:T(8,128)}), f32[16,64,128]{2,1,0:T(8,128)S(1)}, u32[]{:S(2)}, u32[]{:S(2)}) async-start(f32[16,64,128]{2,1,0:T(8,128)} %get-tuple-element.36), calls=%async_computation | async-start | bytes 1048576 | tf_op jit(solution)/shard_map/all_to_all | solution.py:500
  18.5 1.4 collective-permute-start.2
  20.2 1.8 %collective-permute-start.4 = (f32[80,1024]{1,0:T(8,128)S(1)}, f32[80,1024]{1,0:T(8,128)S(1)}, u32[]{:S(2)}, u32[]{:S(2)}) collective-permute-start(f32[80,1024]{1,0:T(8,128)S(1)} %collective-permute-done.refs_2_), channel_id=1, source_target_pairs={{0,1},{1,0},{2,3},{3,2},{4,5},{5,4},{6,7},{7,6},{8,9},{9,8},{10,11... | collective-permute-start | bytes 983048 | tf_op jit(solution)/shard_map/ppermute | solution.py:488
  22.7 4.1 %build_own.1 = (bf16[3,2,1024,1024]{3,2,1,0:T(8,128)(2,1)}, f32[16,1024]{1,0:T(8,128)S(1)}) custom-call(s32[4]{0:T(128)S(1)} %bitcast.16, f32[80,1024]{1,0:T(8,128)S(1)} %constant_dynamic-update-slice_fusion.refs_1_, f32[80,1024]{1,0:T(8,128)S(1)} %collective-permute-done.refs_2_, f32[80,1024]{1,0:T(8,128)S(1)} %collective-permute-done.1.refs_3_), custom_call_target="tpu_custom_call" | custom-call | flops 4000000000 | bytes 500000 | tf_op jit(solution)/shard_map/build_own/pallas_call | solution.py:433
  26.8 1.8 %all-to-all-done.refs_1_.refs_3_ = f32[16,64,128]{2,1,0:T(8,128)S(1)} async-done(((f32[16,64,128]{2,1,0:T(8,128)}), f32[16,64,128]{2,1,0:T(8,128)S(1)}, u32[]{:S(2)}, u32[]{:S(2)}) %all-to-all-start) | async-done | bytes 524320 | tf_op jit(solution)/shard_map/all_to_all | solution.py:500
  29.2 2.6 %collective-permute-start.3 = (f32[64,128]{1,0:T(8,128)S(1)}, f32[64,128]{1,0:T(8,128)S(1)}, u32[]{:S(2)}, u32[]{:S(2)}) collective-permute-start(f32[64,128]{1,0:T(8,128)S(1)} %get-tuple-element.40.refs_2_), channel_id=1, source_target_pairs={{0,32},{32,0},{1,33},{33,1},{2,34},{34,2},{3,35},{35,3},{4,36},{36... | collective-permute-start | bytes 98312 | tf_op jit(solution)/shard_map/ppermute | solution.py:492
  32.0 1.3 tops.1.refs_4_.refs_3_
  33.3 1.6 lower.4.refs_5_
  34.9 5.5 %all-to-all-start.1 = ((f32[8,64,128]{2,1,0:T(8,128)}), f32[8,64,128]{2,1,0:T(8,128)S(1)}, u32[]{:S(2)}, u32[]{:S(2)}) async-start(f32[8,64,128]{2,1,0:T(8,128)} %lower.4.refs_5_), calls=%async_computation.1 | async-start | bytes 524288 | tf_op jit(solution)/shard_map/all_to_all | solution.py:496
  40.4 4.2 %build_a.1 = (bf16[3,2,1024,1024]{3,2,1,0:T(8,128)(2,1)}, f32[16,1024]{1,0:T(8,128)S(1)}) custom-call(s32[4]{0:T(128)S(1)} %bitcast.20, f32[80,1024]{1,0:T(8,128)S(1)} %constant_dynamic-update-slice_fusion.refs_1_, f32[80,1024]{1,0:T(8,128)S(1)} %collective-permute-done.refs_2_, ...), custom_call_target="tpu_custom_call", output_to_operand_aliasing={{0}: (7, {})} | custom-call | flops 4000000000 | bytes 500000 | tf_op jit(solution)/shard_map/build_a/pallas_call | solution.py:433
  44.6 4.2 %build_b.1 = (bf16[3,2,1024,1024]{3,2,1,0:T(8,128)(2,1)}, f32[16,1024]{1,0:T(8,128)S(1)}) custom-call(s32[4]{0:T(128)S(1)} %bitcast.21, f32[80,1024]{1,0:T(8,128)S(1)} %constant_dynamic-update-slice_fusion.refs_1_, f32[80,1024]{1,0:T(8,128)S(1)} %collective-permute-done.refs_2_, ...), custom_call_target="tpu_custom_call", output_to_operand_aliasing={{0}: (6, {})} | custom-call | flops 4000000000 | bytes 500000 | tf_op jit(solution)/shard_map/build_b/pallas_call | solution.py:433
  48.8 4.0 %all-to-all-done.1.refs_1_ = f32[8,64,128]{2,1,0:T(8,128)S(1)} async-done(((f32[8,64,128]{2,1,0:T(8,128)}), f32[8,64,128]{2,1,0:T(8,128)S(1)}, u32[]{:S(2)}, u32[]{:S(2)}) %all-to-all-start.1) | async-done | bytes 262176 | tf_op jit(solution)/shard_map/all_to_all | solution.py:496
  52.8 2.7 %first.1 = (bf16[128,256]{1,0:T(8,128)(2,1)S(1)}, f32[16,1152]{1,0:T(8,128)S(1)}, f32[16,32,128]{2,1,0:T(8,128)}) custom-call(s32[4]{0:T(128)S(1)} %bitcast.22, f32[8,64,128]{2,1,0:T(8,128)S(1)} %all-to-all-done.1.refs_1_, f32[4,64,64]{2,1,0:T(8,128)S(1)} %bitcast.11, bf16[128,1024]{1,0:T(8,128)(2,1)S(1)} %copy-done.1, ...), custom_call_target="tpu_custom_call" | custom-call | flops 100000 | bytes 500000 | tf_op jit(solution)/shard_map/first/pallas_call | solution.py:433
  55.5 5.1 %all-to-all-start.2 = ((f32[16,32,128]{2,1,0:T(8,128)}), f32[16,32,128]{2,1,0:T(8,128)S(1)}, u32[]{:S(2)}, u32[]{:S(2)}) async-start(f32[16,32,128]{2,1,0:T(8,128)} %get-tuple-element.49), calls=%async_computation.2 | async-start | bytes 524288 | tf_op jit(solution)/shard_map/all_to_all | solution.py:500
  60.8 3.4 %collective-permute-start.6 = (f32[16,1152]{1,0:T(8,128)S(1)}, f32[16,1152]{1,0:T(8,128)S(1)}, u32[]{:S(2)}, u32[]{:S(2)}) collective-permute-start(f32[16,1152]{1,0:T(8,128)S(1)} %get-tuple-element.52.refs_4_.refs_1_.refs_7_.refs_2_), channel_id=1, source_target_pairs={{0,1},{1,0},{2,3},{3,2},{4,5},{5,4},{6,7},{7,6},{8,9},{9,8},{10,11... | collective-permute-start | bytes 221192 | tf_op jit(solution)/shard_map/ppermute | solution.py:488
  64.2 4.4 %all-to-all-done.2.refs_1_ = f32[16,32,128]{2,1,0:T(8,128)S(1)} async-done(((f32[16,32,128]{2,1,0:T(8,128)}), f32[16,32,128]{2,1,0:T(8,128)S(1)}, u32[]{:S(2)}, u32[]{:S(2)}) %all-to-all-start.2) | async-done | bytes 262176 | tf_op jit(solution)/shard_map/all_to_all | solution.py:500
  69.2 1.7 %collective-permute-start.5 = (f32[64,128]{1,0:T(8,128)S(1)}, f32[64,128]{1,0:T(8,128)S(1)}, u32[]{:S(2)}, u32[]{:S(2)}) collective-permute-start(f32[64,128]{1,0:T(8,128)S(1)} %get-tuple-element.51.refs_1_), channel_id=1, source_target_pairs={{0,32},{32,0},{1,33},{33,1},{2,34},{34,2},{3,35},{35,3},{4,36},{36... | collective-permute-start | bytes 98312 | tf_op jit(solution)/shard_map/ppermute | solution.py:492
  70.9 0.8 collective-permute-done.5.refs_2_
  71.8 1.0 lower.5.refs_7_
  72.7 3.4 %all-to-all-start.3 = ((f32[8,32,128]{2,1,0:T(8,128)}), f32[8,32,128]{2,1,0:T(8,128)S(1)}, u32[]{:S(2)}, u32[]{:S(2)}) async-start(f32[8,32,128]{2,1,0:T(8,128)} %lower.5.refs_7_), calls=%async_computation.3 | async-start | bytes 262144 | tf_op jit(solution)/shard_map/all_to_all | solution.py:496
  76.1 5.9 %near.3.refs_4_ = f32[16,1152]{1,0:T(8,128)S(1)} custom-call(s32[4]{0:T(128)S(1)} %bitcast.24, f32[16,1152]{1,0:T(8,128)S(1)} %get-tuple-element.52.refs_4_.refs_1_.refs_7_.refs_2_, f32[16,1152]{1,0:T(8,128)S(1)} %collective-permute-done.6.refs_5_.refs_2_, f32[16,1152]{1,0:T(8,128)S(1)} %collective-permute-done.7.refs_6_.refs_3_, ...), custom_call_target="tpu_custom_call" | custom-call | flops 4000000000 | bytes 500000 | tf_op jit(solution)/shard_map/near/pallas_call | solution.py:433
  82.0 2.5 %all-to-all-done.3.refs_1_ = f32[8,32,128]{2,1,0:T(8,128)S(1)} async-done(((f32[8,32,128]{2,1,0:T(8,128)}), f32[8,32,128]{2,1,0:T(8,128)S(1)}, u32[]{:S(2)}, u32[]{:S(2)}) %all-to-all-start.3) | async-done | bytes 131104 | tf_op jit(solution)/shard_map/all_to_all | solution.py:496
  84.4 2.2 %second.1 = (f32[16,1024]{1,0:T(8,128)S(1)}, f32[16,1152]{1,0:T(8,128)S(1)}, f32[16,128]{1,0:T(8,128)S(1)}, f32[16,32,128]{2,1,0:T(8,128)}) custom-call(s32[4]{0:T(128)S(1)} %bitcast.25, f32[8,32,128]{2,1,0:T(8,128)S(1)} %all-to-all-done.3.refs_1_, bf16[128,256]{1,0:T(8,128)(2,1)S(1)} %get-tuple-element.53.refs_2_, bf16[128,1024]{1,0:T(8,128)(2,1)S(1)} %copy-done.1, ...), custom_call_target="tpu_custom_call" | custom-call | flops 100000 | bytes 500000 | tf_op jit(solution)/shard_map/second/pallas_call | solution.py:433
  86.6 3.5 %all-to-all-start.4 = ((f32[16,32,128]{2,1,0:T(8,128)}), f32[16,32,128]{2,1,0:T(8,128)S(1)}, u32[]{:S(2)}, u32[]{:S(2)}) async-start(f32[16,32,128]{2,1,0:T(8,128)} %get-tuple-element.56), calls=%async_computation.4 | async-start | bytes 524288 | tf_op jit(solution)/shard_map/all_to_all | solution.py:500
  91.5 2.3 %collective-permute-start.10 = (f32[16,1152]{1,0:T(8,128)S(1)}, f32[16,1152]{1,0:T(8,128)S(1)}, u32[]{:S(2)}, u32[]{:S(2)}) collective-permute-start(f32[16,1152]{1,0:T(8,128)S(1)} %get-tuple-element.59.refs_4_.refs_1_), channel_id=1, source_target_pairs={{0,1},{1,0},{2,3},{3,2},{4,5},{5,4},{6,7},{7,6},{8,9},{9,8},{10,11... | collective-permute-start | bytes 221192 | tf_op jit(solution)/shard_map/ppermute | solution.py:488
  93.8 3.9 %all-to-all-done.4.refs_1_ = f32[16,32,128]{2,1,0:T(8,128)S(1)} async-done(((f32[16,32,128]{2,1,0:T(8,128)}), f32[16,32,128]{2,1,0:T(8,128)S(1)}, u32[]{:S(2)}, u32[]{:S(2)}) %all-to-all-start.4) | async-done | bytes 262176 | tf_op jit(solution)/shard_map/all_to_all | solution.py:500
  98.3 3.8 %collective-permute-start.9 = (f32[64,128]{1,0:T(8,128)S(1)}, f32[64,128]{1,0:T(8,128)S(1)}, u32[]{:S(2)}, u32[]{:S(2)}) collective-permute-start(f32[64,128]{1,0:T(8,128)S(1)} %get-tuple-element.58.refs_1_), channel_id=1, source_target_pairs={{0,32},{32,0},{1,33},{33,1},{2,34},{34,2},{3,35},{35,3},{4,36},{36... | collective-permute-start | bytes 98312 | tf_op jit(solution)/shard_map/ppermute | solution.py:492
  102.9 1.0 lower.6.refs_7_
  103.9 3.8 %all-to-all-start.5 = ((f32[8,32,128]{2,1,0:T(8,128)}), f32[8,32,128]{2,1,0:T(8,128)S(1)}, u32[]{:S(2)}, u32[]{:S(2)}) async-start(f32[8,32,128]{2,1,0:T(8,128)} %lower.6.refs_7_), calls=%async_computation.5 | async-start | bytes 262144 | tf_op jit(solution)/shard_map/all_to_all | solution.py:496
  107.6 5.9 %near.4.refs_4_ = f32[16,1152]{1,0:T(8,128)S(1)} custom-call(s32[4]{0:T(128)S(1)} %bitcast.27, f32[16,1152]{1,0:T(8,128)S(1)} %get-tuple-element.59.refs_4_.refs_1_, f32[16,1152]{1,0:T(8,128)S(1)} %collective-permute-done.10.refs_5_.refs_2_, f32[16,1152]{1,0:T(8,128)S(1)} %collective-permute-done.11.refs_6_.refs_3_, ...), custom_call_target="tpu_custom_call" | custom-call | flops 4000000000 | bytes 500000 | tf_op jit(solution)/shard_map/near/pallas_call | solution.py:433
  113.5 2.0 %all-to-all-done.5.refs_1_ = f32[8,32,128]{2,1,0:T(8,128)S(1)} async-done(((f32[8,32,128]{2,1,0:T(8,128)}), f32[8,32,128]{2,1,0:T(8,128)S(1)}, u32[]{:S(2)}, u32[]{:S(2)}) %all-to-all-start.5) | async-done | bytes 131104 | tf_op jit(solution)/shard_map/all_to_all | solution.py:496
  115.5 2.2 %third.1 = (f32[16,1152]{1,0:T(8,128)S(1)}, f32[16,128]{1,0:T(8,128)S(1)}, f32[16,32,128]{2,1,0:T(8,128)}) custom-call(s32[4]{0:T(128)S(1)} %bitcast.28, f32[8,32,128]{2,1,0:T(8,128)S(1)} %all-to-all-done.5.refs_1_, bf16[128,256]{1,0:T(8,128)(2,1)S(1)} %get-tuple-element.53.refs_2_, bf16[128,1024]{1,0:T(8,128)(2,1)S(1)} %copy-done.1, ...), custom_call_target="tpu_custom_call" | custom-call | flops 100000 | bytes 500000 | tf_op jit(solution)/shard_map/third/pallas_call | solution.py:433
  117.7 3.5 %all-to-all-start.6 = ((f32[16,32,128]{2,1,0:T(8,128)}), f32[16,32,128]{2,1,0:T(8,128)S(1)}, u32[]{:S(2)}, u32[]{:S(2)}) async-start(f32[16,32,128]{2,1,0:T(8,128)} %get-tuple-element.61), calls=%async_computation.6 | async-start | bytes 524288 | tf_op jit(solution)/shard_map/all_to_all | solution.py:500
  121.3 1.3 collective-permute-start.16
  122.6 2.3 %collective-permute-start.14 = (f32[16,1152]{1,0:T(8,128)S(1)}, f32[16,1152]{1,0:T(8,128)S(1)}, u32[]{:S(2)}, u32[]{:S(2)}) collective-permute-start(f32[16,1152]{1,0:T(8,128)S(1)} %get-tuple-element.64.refs_4_.refs_1_), channel_id=1, source_target_pairs={{0,1},{1,0},{2,3},{3,2},{4,5},{5,4},{6,7},{7,6},{8,9},{9,8},{10,11... | collective-permute-start | bytes 221192 | tf_op jit(solution)/shard_map/ppermute | solution.py:488
  124.9 3.9 %all-to-all-done.6.refs_1_ = f32[16,32,128]{2,1,0:T(8,128)S(1)} async-done(((f32[16,32,128]{2,1,0:T(8,128)}), f32[16,32,128]{2,1,0:T(8,128)S(1)}, u32[]{:S(2)}, u32[]{:S(2)}) %all-to-all-start.6) | async-done | bytes 262176 | tf_op jit(solution)/shard_map/all_to_all | solution.py:500
  129.4 3.8 %collective-permute-start.13 = (f32[64,128]{1,0:T(8,128)S(1)}, f32[64,128]{1,0:T(8,128)S(1)}, u32[]{:S(2)}, u32[]{:S(2)}) collective-permute-start(f32[64,128]{1,0:T(8,128)S(1)} %get-tuple-element.63.refs_1_), channel_id=1, source_target_pairs={{0,32},{32,0},{1,33},{33,1},{2,34},{34,2},{3,35},{35,3},{4,36},{36... | collective-permute-start | bytes 98312 | tf_op jit(solution)/shard_map/ppermute | solution.py:492
  134.0 1.0 lower.7.refs_7_
  135.0 3.8 %all-to-all-start.7 = ((f32[8,32,128]{2,1,0:T(8,128)}), f32[8,32,128]{2,1,0:T(8,128)S(1)}, u32[]{:S(2)}, u32[]{:S(2)}) async-start(f32[8,32,128]{2,1,0:T(8,128)} %lower.7.refs_7_), calls=%async_computation.7 | async-start | bytes 262144 | tf_op jit(solution)/shard_map/all_to_all | solution.py:496
  138.7 5.9 %near.5.refs_4_ = f32[16,1152]{1,0:T(8,128)S(1)} custom-call(s32[4]{0:T(128)S(1)} %bitcast.30, f32[16,1152]{1,0:T(8,128)S(1)} %get-tuple-element.64.refs_4_.refs_1_, f32[16,1152]{1,0:T(8,128)S(1)} %collective-permute-done.14.refs_5_.refs_2_, f32[16,1152]{1,0:T(8,128)S(1)} %collective-permute-done.15.refs_6_.refs_3_, ...), custom_call_target="tpu_custom_call" | custom-call | flops 4000000000 | bytes 500000 | tf_op jit(solution)/shard_map/near/pallas_call | solution.py:433
  144.6 2.1 %all-to-all-done.7.refs_1_ = f32[8,32,128]{2,1,0:T(8,128)S(1)} async-done(((f32[8,32,128]{2,1,0:T(8,128)}), f32[8,32,128]{2,1,0:T(8,128)S(1)}, u32[]{:S(2)}, u32[]{:S(2)}) %all-to-all-start.7) | async-done | bytes 131104 | tf_op jit(solution)/shard_map/all_to_all | solution.py:496
  146.7 1.2 fourth.1
  147.8 21.8 %all_to_all.51 = f32[256,1,128]{2,1,0:T(1,128)S(1)} all-to-all(f32[256,1,128]{2,1,0:T(1,128)S(1)} %bitcast.14), channel_id=1, replica_groups=mesh['y'=4,'core'=2,'x'=4,'z'=8] {'y','core','x','z'}, dimensions={0} | all-to-all | bytes 262144 | tf_op jit(solution)/shard_map/all_to_all | solution.py:619
  169.6 0.9 last.1
  (51 shorter events, 7.8 us)
Async XLA Ops:
  0.6 31.2 %copy-start = (s32[8,4]{0,1:T(4,128)S(1)}, s32[8,4]{0,1:T(4,128)}, u32[]{:S(2)}) copy-start(s32[8,4]{0,1:T(4,128)} %param.18) | copy-start | bytes 388
  0.6 31.4 %copy-start.8 = (s32[4,1]{0,1:T(1,128)S(1)}, s32[4,1]{0,1:T(1,128)}, u32[]{:S(2)}) copy-start(s32[4,1]{0,1:T(1,128)} %param.17) | copy-start | bytes 52
  0.7 31.4 %copy-start.2 = (f32[4,1,64,64]{3,2,1,0:T(8,128)S(1)}, f32[4,1,64,64]{3,2,1,0:T(8,128)}, u32[]{:S(2)}) copy-start(f32[4,1,64,64]{3,2,1,0:T(8,128)} %param.15) | copy-start | bytes 196612
  0.7 31.3 %copy-start.5 = (f32[8,64,64]{2,1,0:T(8,128)S(1)}, f32[8,64,64]{2,1,0:T(8,128)}, u32[]{:S(2)}) copy-start(f32[8,64,64]{2,1,0:T(8,128)} %param.16) | copy-start | bytes 393220
  2.5 17.6 %collective-permute-start = (f32[80,1024]{1,0:T(8,128)S(1)}, f32[80,1024]{1,0:T(8,128)S(1)}, u32[]{:S(2)}, u32[]{:S(2)}) collective-permute-start(f32[80,1024]{1,0:T(8,128)S(1)} %constant_dynamic-update-slice_fusion.refs_1_), channel_id=1, source_target_pairs={{0,2},{1,3},{2,0},{3,1},{4,6},{5,7},{6,4},{7,5},{8,10},{9,11},{10,... | collective-permute-start | bytes 983048 | tf_op jit(solution)/shard_map/ppermute | solution.py:488
  6.4 15.6 %collective-permute-start.1 = (f32[80,1024]{1,0:T(8,128)S(1)}, f32[80,1024]{1,0:T(8,128)S(1)}, u32[]{:S(2)}, u32[]{:S(2)}) collective-permute-start(f32[80,1024]{1,0:T(8,128)S(1)} %constant_dynamic-update-slice_fusion.refs_1_), channel_id=1, source_target_pairs={{0,1},{1,0},{2,3},{3,2},{4,5},{5,4},{6,7},{7,6},{8,9},{9,8},{10,11... | collective-permute-start | bytes 983048 | tf_op jit(solution)/shard_map/ppermute | solution.py:488
  11.5 20.5 %copy-start.9 = (f32[64,64]{1,0:T(8,128)S(1)}, f32[64,64]{1,0:T(8,128)}, u32[]{:S(2)}) copy-start(f32[64,64]{1,0:T(8,128)} %get-tuple-element.41.refs_5_) | copy-start | bytes 49156
  11.5 21.8 %copy-start.10 = (f32[32,128]{1,0:T(8,128)S(1)}, f32[32,128]{1,0:T(8,128)}, u32[]{:S(2)}) copy-start(f32[32,128]{1,0:T(8,128)} %get-tuple-element.38.refs_7_) | copy-start | bytes 49156
  11.5 21.8 %copy-start.11 = (f32[16,128]{1,0:T(8,128)S(1)}, f32[16,128]{1,0:T(8,128)}, u32[]{:S(2)}) copy-start(f32[16,128]{1,0:T(8,128)} %get-tuple-element.42.refs_5_) | copy-start | bytes 24580
  11.6 17.0 %all-to-all-start = ((f32[16,64,128]{2,1,0:T(8,128)}), f32[16,64,128]{2,1,0:T(8,128)S(1)}, u32[]{:S(2)}, u32[]{:S(2)}) async-start(f32[16,64,128]{2,1,0:T(8,128)} %get-tuple-element.36), calls=%async_computation | async-start | bytes 1048576 | tf_op jit(solution)/shard_map/all_to_all | solution.py:500
  18.5 8.3 %collective-permute-start.2 = (f32[32,128]{1,0:T(8,128)}, f32[32,128]{1,0:T(8,128)S(1)}, u32[]{:S(2)}, u32[]{:S(2)}) collective-permute-start(f32[32,128]{1,0:T(8,128)} %get-tuple-element.38.refs_7_), channel_id=1, source_target_pairs={{0,8},{8,0},{16,24},{24,16},{1,9},{9,1},{17,25},{25,17},{2,10},{10... | collective-permute-start | bytes 49160 | tf_op jit(solution)/shard_map/ppermute | solution.py:554
  20.2 20.2 %collective-permute-start.4 = (f32[80,1024]{1,0:T(8,128)S(1)}, f32[80,1024]{1,0:T(8,128)S(1)}, u32[]{:S(2)}, u32[]{:S(2)}) collective-permute-start(f32[80,1024]{1,0:T(8,128)S(1)} %collective-permute-done.refs_2_), channel_id=1, source_target_pairs={{0,1},{1,0},{2,3},{3,2},{4,5},{5,4},{6,7},{7,6},{8,9},{9,8},{10,11... | collective-permute-start | bytes 983048 | tf_op jit(solution)/shard_map/ppermute | solution.py:488
  22.0 0.7 copy-start.7
  29.2 4.1 %collective-permute-start.3 = (f32[64,128]{1,0:T(8,128)S(1)}, f32[64,128]{1,0:T(8,128)S(1)}, u32[]{:S(2)}, u32[]{:S(2)}) collective-permute-start(f32[64,128]{1,0:T(8,128)S(1)} %get-tuple-element.40.refs_2_), channel_id=1, source_target_pairs={{0,32},{32,0},{1,33},{33,1},{2,34},{34,2},{3,35},{35,3},{4,36},{36... | collective-permute-start | bytes 98312 | tf_op jit(solution)/shard_map/ppermute | solution.py:492
  34.9 17.9 %all-to-all-start.1 = ((f32[8,64,128]{2,1,0:T(8,128)}), f32[8,64,128]{2,1,0:T(8,128)S(1)}, u32[]{:S(2)}, u32[]{:S(2)}) async-start(f32[8,64,128]{2,1,0:T(8,128)} %lower.4.refs_5_), calls=%async_computation.1 | async-start | bytes 524288 | tf_op jit(solution)/shard_map/all_to_all | solution.py:496
  40.4 12.4 %copy-start.1 = (bf16[128,1024]{1,0:T(8,128)(2,1)S(1)}, bf16[128,1024]{1,0:T(8,128)(2,1)}, u32[]{:S(2)}) copy-start(bf16[128,1024]{1,0:T(8,128)(2,1)} %get-tuple-element.43.refs_3_.refs_5_) | copy-start | bytes 786436
  40.4 12.4 %copy-start.4 = (bf16[64,512]{1,0:T(8,128)(2,1)S(1)}, bf16[64,512]{1,0:T(8,128)(2,1)}, u32[]{:S(2)}) copy-start(bf16[64,512]{1,0:T(8,128)(2,1)} %get-tuple-element.48.refs_5_.refs_6_) | copy-start | bytes 196612
  44.6 39.8 %copy-start.6 = (bf16[64,128]{1,0:T(8,128)(2,1)S(1)}, bf16[64,128]{1,0:T(8,128)(2,1)}, u32[]{:S(2)}) copy-start(bf16[64,128]{1,0:T(8,128)(2,1)} %get-tuple-element.55.refs_5_) | copy-start | bytes 49156
  55.5 13.1 %all-to-all-start.2 = ((f32[16,32,128]{2,1,0:T(8,128)}), f32[16,32,128]{2,1,0:T(8,128)S(1)}, u32[]{:S(2)}, u32[]{:S(2)}) async-start(f32[16,32,128]{2,1,0:T(8,128)} %get-tuple-element.49), calls=%async_computation.2 | async-start | bytes 524288 | tf_op jit(solution)/shard_map/all_to_all | solution.py:500
  60.6 10.3 %collective-permute-start.8 = (f32[16,1152]{1,0:T(8,128)S(1)}, f32[16,1152]{1,0:T(8,128)S(1)}, u32[]{:S(2)}, u32[]{:S(2)}) collective-permute-start(f32[16,1152]{1,0:T(8,128)S(1)} %get-tuple-element.52.refs_4_.refs_1_.refs_7_.refs_2_), channel_id=1, source_target_pairs={{0,3},{1,2},{2,1},{3,0},{4,7},{5,6},{6,5},{7,4},{8,11},{9,10},{10,... | collective-permute-start | bytes 221192 | tf_op jit(solution)/shard_map/ppermute | solution.py:488
  60.7 10.2 %collective-permute-start.7 = (f32[16,1152]{1,0:T(8,128)S(1)}, f32[16,1152]{1,0:T(8,128)S(1)}, u32[]{:S(2)}, u32[]{:S(2)}) collective-permute-start(f32[16,1152]{1,0:T(8,128)S(1)} %get-tuple-element.52.refs_4_.refs_1_.refs_7_.refs_2_), channel_id=1, source_target_pairs={{0,2},{1,3},{2,0},{3,1},{4,6},{5,7},{6,4},{7,5},{8,10},{9,11},{10,... | collective-permute-start | bytes 221192 | tf_op jit(solution)/shard_map/ppermute | solution.py:488
  60.8 10.1 %collective-permute-start.6 = (f32[16,1152]{1,0:T(8,128)S(1)}, f32[16,1152]{1,0:T(8,128)S(1)}, u32[]{:S(2)}, u32[]{:S(2)}) collective-permute-start(f32[16,1152]{1,0:T(8,128)S(1)} %get-tuple-element.52.refs_4_.refs_1_.refs_7_.refs_2_), channel_id=1, source_target_pairs={{0,1},{1,0},{2,3},{3,2},{4,5},{5,4},{6,7},{7,6},{8,9},{9,8},{10,11... | collective-permute-start | bytes 221192 | tf_op jit(solution)/shard_map/ppermute | solution.py:488
  69.2 2.6 %collective-permute-start.5 = (f32[64,128]{1,0:T(8,128)S(1)}, f32[64,128]{1,0:T(8,128)S(1)}, u32[]{:S(2)}, u32[]{:S(2)}) collective-permute-start(f32[64,128]{1,0:T(8,128)S(1)} %get-tuple-element.51.refs_1_), channel_id=1, source_target_pairs={{0,32},{32,0},{1,33},{33,1},{2,34},{34,2},{3,35},{35,3},{4,36},{36... | collective-permute-start | bytes 98312 | tf_op jit(solution)/shard_map/ppermute | solution.py:492
  72.7 11.7 %all-to-all-start.3 = ((f32[8,32,128]{2,1,0:T(8,128)}), f32[8,32,128]{2,1,0:T(8,128)S(1)}, u32[]{:S(2)}, u32[]{:S(2)}) async-start(f32[8,32,128]{2,1,0:T(8,128)} %lower.5.refs_7_), calls=%async_computation.3 | async-start | bytes 262144 | tf_op jit(solution)/shard_map/all_to_all | solution.py:496
  86.6 11.0 %all-to-all-start.4 = ((f32[16,32,128]{2,1,0:T(8,128)}), f32[16,32,128]{2,1,0:T(8,128)S(1)}, u32[]{:S(2)}, u32[]{:S(2)}) async-start(f32[16,32,128]{2,1,0:T(8,128)} %get-tuple-element.56), calls=%async_computation.4 | async-start | bytes 524288 | tf_op jit(solution)/shard_map/all_to_all | solution.py:500
  90.2 11.9 %collective-permute-start.12 = (f32[16,1152]{1,0:T(8,128)S(1)}, f32[16,1152]{1,0:T(8,128)S(1)}, u32[]{:S(2)}, u32[]{:S(2)}) collective-permute-start(f32[16,1152]{1,0:T(8,128)S(1)} %get-tuple-element.59.refs_4_.refs_1_), channel_id=1, source_target_pairs={{0,3},{1,2},{2,1},{3,0},{4,7},{5,6},{6,5},{7,4},{8,11},{9,10},{10,... | collective-permute-start | bytes 221192 | tf_op jit(solution)/shard_map/ppermute | solution.py:488
  91.0 11.1 %collective-permute-start.11 = (f32[16,1152]{1,0:T(8,128)S(1)}, f32[16,1152]{1,0:T(8,128)S(1)}, u32[]{:S(2)}, u32[]{:S(2)}) collective-permute-start(f32[16,1152]{1,0:T(8,128)S(1)} %get-tuple-element.59.refs_4_.refs_1_), channel_id=1, source_target_pairs={{0,2},{1,3},{2,0},{3,1},{4,6},{5,7},{6,4},{7,5},{8,10},{9,11},{10,... | collective-permute-start | bytes 221192 | tf_op jit(solution)/shard_map/ppermute | solution.py:488
  91.5 10.6 %collective-permute-start.10 = (f32[16,1152]{1,0:T(8,128)S(1)}, f32[16,1152]{1,0:T(8,128)S(1)}, u32[]{:S(2)}, u32[]{:S(2)}) collective-permute-start(f32[16,1152]{1,0:T(8,128)S(1)} %get-tuple-element.59.refs_4_.refs_1_), channel_id=1, source_target_pairs={{0,1},{1,0},{2,3},{3,2},{4,5},{5,4},{6,7},{7,6},{8,9},{9,8},{10,11... | collective-permute-start | bytes 221192 | tf_op jit(solution)/shard_map/ppermute | solution.py:488
  98.3 4.6 %collective-permute-start.9 = (f32[64,128]{1,0:T(8,128)S(1)}, f32[64,128]{1,0:T(8,128)S(1)}, u32[]{:S(2)}, u32[]{:S(2)}) collective-permute-start(f32[64,128]{1,0:T(8,128)S(1)} %get-tuple-element.58.refs_1_), channel_id=1, source_target_pairs={{0,32},{32,0},{1,33},{33,1},{2,34},{34,2},{3,35},{35,3},{4,36},{36... | collective-permute-start | bytes 98312 | tf_op jit(solution)/shard_map/ppermute | solution.py:492
  103.9 11.7 %all-to-all-start.5 = ((f32[8,32,128]{2,1,0:T(8,128)}), f32[8,32,128]{2,1,0:T(8,128)S(1)}, u32[]{:S(2)}, u32[]{:S(2)}) async-start(f32[8,32,128]{2,1,0:T(8,128)} %lower.6.refs_7_), calls=%async_computation.5 | async-start | bytes 262144 | tf_op jit(solution)/shard_map/all_to_all | solution.py:496
  113.5 56.1 %copy-start.3 = (f32[16,1024]{1,0:T(8,128)S(1)}, f32[16,1024]{1,0:T(8,128)}, u32[]{:S(2)}) copy-start(f32[16,1024]{1,0:T(8,128)} %refs_1_.3) | copy-start | bytes 196612
  117.7 11.1 %all-to-all-start.6 = ((f32[16,32,128]{2,1,0:T(8,128)}), f32[16,32,128]{2,1,0:T(8,128)S(1)}, u32[]{:S(2)}, u32[]{:S(2)}) async-start(f32[16,32,128]{2,1,0:T(8,128)} %get-tuple-element.61), calls=%async_computation.6 | async-start | bytes 524288 | tf_op jit(solution)/shard_map/all_to_all | solution.py:500
  121.3 11.9 %collective-permute-start.16 = (f32[16,1152]{1,0:T(8,128)S(1)}, f32[16,1152]{1,0:T(8,128)S(1)}, u32[]{:S(2)}, u32[]{:S(2)}) collective-permute-start(f32[16,1152]{1,0:T(8,128)S(1)} %get-tuple-element.64.refs_4_.refs_1_), channel_id=1, source_target_pairs={{0,3},{1,2},{2,1},{3,0},{4,7},{5,6},{6,5},{7,4},{8,11},{9,10},{10,... | collective-permute-start | bytes 221192 | tf_op jit(solution)/shard_map/ppermute | solution.py:488
  122.6 10.6 %collective-permute-start.15 = (f32[16,1152]{1,0:T(8,128)S(1)}, f32[16,1152]{1,0:T(8,128)S(1)}, u32[]{:S(2)}, u32[]{:S(2)}) collective-permute-start(f32[16,1152]{1,0:T(8,128)S(1)} %get-tuple-element.64.refs_4_.refs_1_), channel_id=1, source_target_pairs={{0,2},{1,3},{2,0},{3,1},{4,6},{5,7},{6,4},{7,5},{8,10},{9,11},{10,... | collective-permute-start | bytes 221192 | tf_op jit(solution)/shard_map/ppermute | solution.py:488
  122.6 10.6 %collective-permute-start.14 = (f32[16,1152]{1,0:T(8,128)S(1)}, f32[16,1152]{1,0:T(8,128)S(1)}, u32[]{:S(2)}, u32[]{:S(2)}) collective-permute-start(f32[16,1152]{1,0:T(8,128)S(1)} %get-tuple-element.64.refs_4_.refs_1_), channel_id=1, source_target_pairs={{0,1},{1,0},{2,3},{3,2},{4,5},{5,4},{6,7},{7,6},{8,9},{9,8},{10,11... | collective-permute-start | bytes 221192 | tf_op jit(solution)/shard_map/ppermute | solution.py:488
  129.4 4.6 %collective-permute-start.13 = (f32[64,128]{1,0:T(8,128)S(1)}, f32[64,128]{1,0:T(8,128)S(1)}, u32[]{:S(2)}, u32[]{:S(2)}) collective-permute-start(f32[64,128]{1,0:T(8,128)S(1)} %get-tuple-element.63.refs_1_), channel_id=1, source_target_pairs={{0,32},{32,0},{1,33},{33,1},{2,34},{34,2},{3,35},{35,3},{4,36},{36... | collective-permute-start | bytes 98312 | tf_op jit(solution)/shard_map/ppermute | solution.py:492
  135.0 11.7 %all-to-all-start.7 = ((f32[8,32,128]{2,1,0:T(8,128)}), f32[8,32,128]{2,1,0:T(8,128)S(1)}, u32[]{:S(2)}, u32[]{:S(2)}) async-start(f32[8,32,128]{2,1,0:T(8,128)} %lower.7.refs_7_), calls=%async_computation.7 | async-start | bytes 262144 | tf_op jit(solution)/shard_map/all_to_all | solution.py:496
